TPU v7x, 32 devices: a whole 2x2x4 slice. The times are simulated.
32 devices in a mesh: dp: 4 (over y, core), gx: 4 (over z), gy: 2 (over x).
Axes of the slice: x: 2, y: 2, z: 4, core: 2. Of those that a mesh axis runs over, the one named last changes fastest.
Arguments:
- prompt: bfloat16 [16, 2048, 1088], P(('dp', 'gx'), 'gy'), may hold values from -6 to 6
- continuations: bfloat16 [32, 256, 1088], P(('dp', 'gx', 'gy')), may hold values from -6 to 6
- prefix_len: int32 [32], P(('dp', 'gx', 'gy')), may hold values from 512 to 2048, as said below
- attn_gain: float32 [1088], replicated, may hold values from 0.5 to 1.5
- attn_shift: float32 [1088], replicated, may hold values from -1.25 to 1.25
- qkv_weight: bfloat16 [1088, 3264], P('gx', 'gy'), may hold values from -0.25 to 0.25
- query_bias: float32 [1088], replicated, may hold values from -1.25 to 1.25
- value_bias: float32 [1088], replicated, may hold values from -1.25 to 1.25
- out_weight: bfloat16 [1088, 1088], P('gx', 'gy'), may hold values from -0.75 to 0.75
- out_bias: float32 [1088], replicated, may hold values from -1.25 to 1.25
- mlp_gain: float32 [1088], replicated, may hold values from 0.5 to 1.5
- mlp_shift: float32 [1088], replicated, may hold values from -1.25 to 1.25
- up_weight: bfloat16 [1088, 4352], P('gx', 'gy'), may hold values from -0.1875 to 0.1875
- up_bias: float32 [4352], replicated, may hold values from -1.25 to 1.25
- down_weight: bfloat16 [4352, 1088], P('gy', 'gx'), may hold values from -0.09375 to 0.09375
- down_bias: float32 [1088], replicated, may hold values from -1.25 to 1.25
- grad_prompt: bfloat16 [16, 2048, 1088], P(('dp', 'gx'), 'gy'), may hold values from -6 to 6
- grad_continuations: bfloat16 [32, 256, 1088], P(('dp', 'gx', 'gy')), may hold values from -6 to 6
Outputs:
- prompt_out: bfloat16 [16, 2048, 1088], P(('dp', 'gx'), 'gy')
- continuation_out: bfloat16 [32, 256, 1088], P(('dp', 'gx', 'gy'))
- prompt_grad: float32 [16, 2048, 1088], P(('dp', 'gx'), 'gy')
- continuation_grad: float32 [32, 256, 1088], P(('dp', 'gx', 'gy'))
- attn_gain_grad: float32 [1088], replicated
- attn_shift_grad: float32 [1088], replicated
- qkv_weight_grad: float32 [1088, 3264], P('gx', 'gy')
- query_bias_grad: float32 [1088], replicated
- value_bias_grad: float32 [1088], replicated
- out_weight_grad: float32 [1088, 1088], P('gx', 'gy')
- out_bias_grad: float32 [1088], replicated
- mlp_gain_grad: float32 [1088], replicated
- mlp_shift_grad: float32 [1088], replicated
- up_weight_grad: float32 [1088, 4352], P('gx', 'gy')
- up_bias_grad: float32 [4352], replicated
- down_weight_grad: float32 [4352, 1088], P('gy', 'gx')
- down_bias_grad: float32 [1088], replicated
Inputs may be any that keep to these rules, and one draw needn't show every extreme that they name: `prefix_len`: in every group one continuation reads all 2048 prompt tokens and another reads 2048 // 4.
All inputs are finite; a program needn't handle non-finite values.
Results may differ from a plain program's by a relative error of at most 0.019.
Values may be sent and summed in bfloat16 or wider, within the bound.
No kernel may reach another device: no remote copies, remote signals or barrier semaphores. Data moves between devices by JAX's collectives and lax.ppermute only.
A program may use at most 256 MiB of HBM per device.

v0:
```python
import jax
import jax.numpy as jnp
from jax import lax
from jax.sharding import PartitionSpec as P

HEADS = 17
HEAD_DIM = 64


epsilon = 1e-05
masked_score = -1e30


def layer_norm(values_in, norm_gain, norm_shift):
    centre = jnp.mean(values_in, axis=-1, keepdims=True)
    centred = values_in - centre
    spread = jnp.mean(centred * centred, axis=-1, keepdims=True)
    return centred * lax.rsqrt(spread + epsilon) * norm_gain + norm_shift


def smooth_gate(pre_act):
    return jax.nn.gelu(pre_act, approximate=False)


def fetch_weights(qkv_part, out_part, up_part, down_part):
    by_column = (
        lax.all_gather(qkv_part, "gy", axis=1, tiled=True),
        lax.all_gather(out_part, "gy", axis=1, tiled=True),
        lax.all_gather(up_part, "gy", axis=1, tiled=True),
        lax.all_gather(down_part, "gy", axis=0, tiled=True),
    )
    return (
        lax.all_gather(by_column[0], "gx", axis=0, tiled=True),
        lax.all_gather(by_column[1], "gx", axis=0, tiled=True),
        lax.all_gather(by_column[2], "gx", axis=0, tiled=True),
        lax.all_gather(by_column[3], "gx", axis=1, tiled=True),
    )


def fetch_keys(local_keys):
    return lax.all_gather(local_keys, "gy", axis=1, tiled=True)


def head_cols(tensor, offset):
    return lax.dynamic_slice_in_dim(tensor, offset, HEAD_DIM, tensor.ndim - 1)


def softmax_parts(scores):
    top_score = jnp.max(scores, axis=-1, keepdims=True)
    expo = jnp.exp(scores - top_score)
    total = jnp.sum(expo, axis=-1, keepdims=True)
    return (expo / total, top_score + jnp.log(total))


def branch_pairs(own_keys, branch_keys, offset, width_full):
    key_part = jnp.concatenate(
        [head_cols(own_keys, offset), head_cols(branch_keys, offset)], axis=0
    )
    value_part = jnp.concatenate(
        [head_cols(own_keys, width_full + offset), head_cols(branch_keys, width_full + offset)],
        axis=0,
    )
    return (key_part, value_part)


def attend_forward(prompt_queries, branch_queries, keys_all, branch_keys, prompt_mask, branch_mask):
    groups, shard, width_full = prompt_queries.shape
    length = branch_queries.shape[0]
    scale = HEAD_DIM ** (-0.5)
    own_keys = keys_all[0]

    def head_step(head_index, carry):
        out_prompt, out_branch, stats_prompt, stats_branch = carry
        offset = head_index * HEAD_DIM
        query_p = head_cols(prompt_queries, offset)
        key_p = head_cols(keys_all, offset)
        value_p = head_cols(keys_all, width_full + offset)
        scores_p = jnp.where(
            prompt_mask,
            jnp.einsum("gid,gjd->gij", query_p, key_p, preferred_element_type=jnp.float32) * scale,
            masked_score,
        )
        probs_p, log_p = softmax_parts(scores_p)
        mixed_p = jnp.einsum(
            "gij,gjd->gid",
            probs_p.astype(jnp.bfloat16),
            value_p,
            preferred_element_type=jnp.float32,
        )
        query_b = head_cols(branch_queries, offset)
        key_b, value_b = branch_pairs(own_keys, branch_keys, offset, width_full)
        scores_b = jnp.where(
            branch_mask,
            jnp.einsum("id,jd->ij", query_b, key_b, preferred_element_type=jnp.float32) * scale,
            masked_score,
        )
        probs_b, log_b = softmax_parts(scores_b)
        mixed_b = jnp.einsum(
            "ij,jd->id", probs_b.astype(jnp.bfloat16), value_b, preferred_element_type=jnp.float32
        )
        out_prompt = lax.dynamic_update_slice_in_dim(out_prompt, mixed_p, offset, 2)
        out_branch = lax.dynamic_update_slice_in_dim(out_branch, mixed_b, offset, 1)
        stats_prompt = lax.dynamic_update_index_in_dim(stats_prompt, log_p, head_index, 0)
        stats_branch = lax.dynamic_update_index_in_dim(stats_branch, log_b, head_index, 0)
        return (out_prompt, out_branch, stats_prompt, stats_branch)

    start_carry = (
        jnp.zeros((groups, shard, width_full), jnp.float32),
        jnp.zeros((length, width_full), jnp.float32),
        jnp.zeros((HEADS, groups, shard, 1), jnp.float32),
        jnp.zeros((HEADS, length, 1), jnp.float32),
    )
    return lax.fori_loop(0, HEADS, head_step, start_carry)


def attend_backward(
    prompt_queries,
    branch_queries,
    keys_all,
    branch_keys,
    prompt_mask,
    branch_mask,
    stats_prompt,
    stats_branch,
    grad_mixed_p,
    grad_mixed_b,
):
    groups, shard, width_full = prompt_queries.shape
    length = branch_queries.shape[0]
    prompt_len = keys_all.shape[1]
    scale = HEAD_DIM ** (-0.5)
    own_keys = keys_all[0]

    def head_step(head_index, carry):
        dq_prompt, dq_branch, dkv_prompt, dkv_branch = carry
        offset = head_index * HEAD_DIM
        query_p = head_cols(prompt_queries, offset)
        key_p = head_cols(keys_all, offset)
        value_p = head_cols(keys_all, width_full + offset)
        grad_p = head_cols(grad_mixed_p, offset)
        scores_p = jnp.where(
            prompt_mask,
            jnp.einsum("gid,gjd->gij", query_p, key_p, preferred_element_type=jnp.float32) * scale,
            masked_score,
        )
        probs_p = jnp.exp(
            scores_p - lax.dynamic_index_in_dim(stats_prompt, head_index, 0, keepdims=False)
        )
        dprob_p = jnp.einsum("gid,gjd->gij", grad_p, value_p, preferred_element_type=jnp.float32)
        dscore_p = (
            probs_p * (dprob_p - jnp.sum(probs_p * dprob_p, axis=-1, keepdims=True))
        ).astype(jnp.bfloat16)
        dquery_p = (
            jnp.einsum("gij,gjd->gid", dscore_p, key_p, preferred_element_type=jnp.float32) * scale
        )
        dkey_p = (
            jnp.einsum("gij,gid->gjd", dscore_p, query_p, preferred_element_type=jnp.float32)
            * scale
        )
        dvalue_p = jnp.einsum(
            "gij,gid->gjd", probs_p.astype(jnp.bfloat16), grad_p, preferred_element_type=jnp.float32
        )
        query_b = head_cols(branch_queries, offset)
        key_b, value_b = branch_pairs(own_keys, branch_keys, offset, width_full)
        grad_b = head_cols(grad_mixed_b, offset)
        scores_b = jnp.where(
            branch_mask,
            jnp.einsum("id,jd->ij", query_b, key_b, preferred_element_type=jnp.float32) * scale,
            masked_score,
        )
        probs_b = jnp.exp(
            scores_b - lax.dynamic_index_in_dim(stats_branch, head_index, 0, keepdims=False)
        )
        dprob_b = jnp.einsum("id,jd->ij", grad_b, value_b, preferred_element_type=jnp.float32)
        dscore_b = (
            probs_b * (dprob_b - jnp.sum(probs_b * dprob_b, axis=-1, keepdims=True))
        ).astype(jnp.bfloat16)
        dquery_b = (
            jnp.einsum("ij,jd->id", dscore_b, key_b, preferred_element_type=jnp.float32) * scale
        )
        dkey_b = (
            jnp.einsum("ij,id->jd", dscore_b, query_b, preferred_element_type=jnp.float32) * scale
        )
        dvalue_b = jnp.einsum(
            "ij,id->jd", probs_b.astype(jnp.bfloat16), grad_b, preferred_element_type=jnp.float32
        )
        dkey_p = dkey_p + dkey_b[:prompt_len][None]
        dvalue_p = dvalue_p + dvalue_b[:prompt_len][None]
        dq_prompt = lax.dynamic_update_slice_in_dim(dq_prompt, dquery_p, offset, 2)
        dq_branch = lax.dynamic_update_slice_in_dim(dq_branch, dquery_b, offset, 1)
        dkv_prompt = lax.dynamic_update_slice_in_dim(dkv_prompt, dkey_p, offset, 2)
        dkv_prompt = lax.dynamic_update_slice_in_dim(dkv_prompt, dvalue_p, width_full + offset, 2)
        dkv_branch = lax.dynamic_update_slice_in_dim(dkv_branch, dkey_b[prompt_len:], offset, 1)
        dkv_branch = lax.dynamic_update_slice_in_dim(
            dkv_branch, dvalue_b[prompt_len:], width_full + offset, 1
        )
        return (dq_prompt, dq_branch, dkv_prompt, dkv_branch)

    start_carry = (
        jnp.zeros((groups, shard, width_full), jnp.float32),
        jnp.zeros((length, width_full), jnp.float32),
        jnp.zeros((groups, prompt_len, 2 * width_full), jnp.float32),
        jnp.zeros((length, 2 * width_full), jnp.float32),
    )
    return lax.fori_loop(0, HEADS, head_step, start_carry)


def local(
    prompt,
    continuations,
    prefix_len,
    attn_gain,
    attn_shift,
    qkv_weight,
    query_bias,
    value_bias,
    out_weight,
    out_bias,
    mlp_gain,
    mlp_shift,
    up_weight,
    up_bias,
    down_weight,
    down_bias,
    grad_prompt,
    grad_continuations,
):
    groups, shard, width_full = prompt.shape
    length = continuations.shape[1]
    prompt_count = groups * shard
    first_pos = lax.axis_index("gy") * shard
    limit = prefix_len[0]
    prompt_len = shard * lax.axis_size("gy")
    query_pos = first_pos + lax.broadcasted_iota(jnp.int32, (shard, prompt_len), 0)
    key_pos = lax.broadcasted_iota(jnp.int32, (shard, prompt_len), 1)
    prompt_mask = key_pos <= query_pos
    branch_pos = lax.broadcasted_iota(jnp.int32, (length, prompt_len + length), 0)
    branch_key = lax.broadcasted_iota(jnp.int32, (length, prompt_len + length), 1)
    branch_mask = jnp.where(
        branch_key < prompt_len, branch_key < limit, branch_key - prompt_len <= branch_pos
    )
    gathered = fetch_weights(qkv_weight, out_weight, up_weight, down_weight)
    token_rows = jnp.concatenate(
        [prompt.reshape(prompt_count, width_full), continuations.reshape(length, width_full)],
        axis=0,
    ).astype(jnp.float32)
    normed_one, norm_one_back = jax.vjp(layer_norm, token_rows, attn_gain, attn_shift)
    act_one = normed_one.astype(jnp.bfloat16)
    projected = jnp.dot(act_one, gathered[0], preferred_element_type=jnp.float32)
    queries = (projected[:, :width_full] + query_bias).astype(jnp.bfloat16)
    keys = projected[:, width_full : 2 * width_full].astype(jnp.bfloat16)
    values = (projected[:, 2 * width_full :] + value_bias).astype(jnp.bfloat16)
    local_keys = jnp.concatenate([keys[:prompt_count], values[:prompt_count]], axis=1).reshape(
        groups, shard, 2 * width_full
    )
    branch_keys = jnp.concatenate([keys[prompt_count:], values[prompt_count:]], axis=1)
    keys_all = fetch_keys(local_keys)
    prompt_queries = queries[:prompt_count].reshape(groups, shard, width_full)
    branch_queries = queries[prompt_count:]
    mixed_p, mixed_b, stats_prompt, stats_branch = attend_forward(
        prompt_queries, branch_queries, keys_all, branch_keys, prompt_mask, branch_mask
    )
    mixed = jnp.concatenate([mixed_p.reshape(prompt_count, width_full), mixed_b], axis=0).astype(
        jnp.bfloat16
    )
    resid = token_rows + (
        jnp.dot(mixed, gathered[1], preferred_element_type=jnp.float32) + out_bias
    )
    normed_two, norm_two_back = jax.vjp(layer_norm, resid, mlp_gain, mlp_shift)
    act_two = normed_two.astype(jnp.bfloat16)
    pre_act = jnp.dot(act_two, gathered[2], preferred_element_type=jnp.float32) + up_bias
    hidden_exact, gate_back = jax.vjp(smooth_gate, pre_act)
    hidden = hidden_exact.astype(jnp.bfloat16)
    result = resid + jnp.dot(hidden, gathered[3], preferred_element_type=jnp.float32) + down_bias
    prompt_out = result[:prompt_count].reshape(groups, shard, width_full).astype(jnp.bfloat16)
    continuation_out = result[prompt_count:].reshape(1, length, width_full).astype(jnp.bfloat16)
    back_weights = fetch_weights(qkv_weight, out_weight, up_weight, down_weight)
    back_keys = fetch_keys(local_keys)
    cotangent = jnp.concatenate(
        [
            grad_prompt.reshape(prompt_count, width_full),
            grad_continuations.reshape(length, width_full),
        ],
        axis=0,
    )
    cot_exact = cotangent.astype(jnp.float32)
    down_grad = jnp.einsum("rf,rd->fd", hidden, cotangent, preferred_element_type=jnp.float32)
    down_bias_grad = jnp.sum(cot_exact, axis=0)
    d_hidden = jnp.einsum(
        "rd,fd->rf", cotangent, back_weights[3], preferred_element_type=jnp.float32
    )
    d_pre = gate_back(d_hidden)[0].astype(jnp.bfloat16)
    up_grad = jnp.einsum("rd,rf->df", act_two, d_pre, preferred_element_type=jnp.float32)
    up_bias_grad = jnp.sum(d_pre.astype(jnp.float32), axis=0)
    d_act_two = jnp.einsum("rf,df->rd", d_pre, back_weights[2], preferred_element_type=jnp.float32)
    resid_part, mlp_gain_grad, mlp_shift_grad = norm_two_back(d_act_two)
    d_resid = cot_exact + resid_part
    d_branch = d_resid.astype(jnp.bfloat16)
    out_grad = jnp.einsum("ri,rj->ij", mixed, d_branch, preferred_element_type=jnp.float32)
    out_bias_grad = jnp.sum(d_branch.astype(jnp.float32), axis=0)
    d_mixed = jnp.einsum(
        "rj,ij->ri", d_branch, back_weights[1], preferred_element_type=jnp.float32
    ).astype(jnp.bfloat16)
    dq_prompt, dq_branch, dkv_prompt, dkv_branch = attend_backward(
        prompt_queries,
        branch_queries,
        back_keys,
        branch_keys,
        prompt_mask,
        branch_mask,
        stats_prompt,
        stats_branch,
        d_mixed[:prompt_count].reshape(groups, shard, width_full),
        d_mixed[prompt_count:],
    )
    dkv_local = (
        lax.psum_scatter(dkv_prompt.astype(jnp.bfloat16), "gy", scatter_dimension=1, tiled=True)
        .astype(jnp.float32)
        .reshape(prompt_count, 2 * width_full)
    )
    d_queries = jnp.concatenate(
        [dq_prompt.reshape(prompt_count, width_full), dq_branch], axis=0
    ).astype(jnp.bfloat16)
    d_keys = jnp.concatenate(
        [dkv_local[:, :width_full], dkv_branch[:, :width_full]], axis=0
    ).astype(jnp.bfloat16)
    d_values = jnp.concatenate(
        [dkv_local[:, width_full:], dkv_branch[:, width_full:]], axis=0
    ).astype(jnp.bfloat16)
    d_projected = jnp.concatenate([d_queries, d_keys, d_values], axis=1)
    qkv_grad = jnp.einsum("rd,rc->dc", act_one, d_projected, preferred_element_type=jnp.float32)
    query_bias_grad = jnp.sum(d_queries.astype(jnp.float32), axis=0)
    value_bias_grad = jnp.sum(d_values.astype(jnp.float32), axis=0)
    d_act_one = jnp.einsum(
        "rc,dc->rd", d_projected, back_weights[0], preferred_element_type=jnp.float32
    )
    rows_part, attn_gain_grad, attn_shift_grad = norm_one_back(d_act_one)
    d_rows = d_resid + rows_part
    prompt_grad = d_rows[:prompt_count].reshape(groups, shard, width_full)
    continuation_grad = d_rows[prompt_count:].reshape(1, length, width_full)
    column_sums = (
        lax.psum_scatter(
            qkv_grad.astype(jnp.bfloat16), "gy", scatter_dimension=1, tiled=True
        ).astype(jnp.float32),
        lax.psum_scatter(
            out_grad.astype(jnp.bfloat16), "gy", scatter_dimension=1, tiled=True
        ).astype(jnp.float32),
        lax.psum_scatter(
            up_grad.astype(jnp.bfloat16), "gy", scatter_dimension=1, tiled=True
        ).astype(jnp.float32),
        lax.psum_scatter(
            down_grad.astype(jnp.bfloat16), "gy", scatter_dimension=0, tiled=True
        ).astype(jnp.float32),
    )
    grid_sums = (
        lax.psum_scatter(
            column_sums[0].astype(jnp.bfloat16), "gx", scatter_dimension=0, tiled=True
        ).astype(jnp.float32),
        lax.psum_scatter(
            column_sums[1].astype(jnp.bfloat16), "gx", scatter_dimension=0, tiled=True
        ).astype(jnp.float32),
        lax.psum_scatter(
            column_sums[2].astype(jnp.bfloat16), "gx", scatter_dimension=0, tiled=True
        ).astype(jnp.float32),
        lax.psum_scatter(
            column_sums[3].astype(jnp.bfloat16), "gx", scatter_dimension=1, tiled=True
        ).astype(jnp.float32),
    )
    weight_totals = (
        lax.psum(grid_sums[0].astype(jnp.bfloat16), "dp").astype(jnp.float32),
        lax.psum(grid_sums[1].astype(jnp.bfloat16), "dp").astype(jnp.float32),
        lax.psum(grid_sums[2].astype(jnp.bfloat16), "dp").astype(jnp.float32),
        lax.psum(grid_sums[3].astype(jnp.bfloat16), "dp").astype(jnp.float32),
    )
    vector_totals = lax.psum(
        (
            attn_gain_grad,
            attn_shift_grad,
            query_bias_grad,
            value_bias_grad,
            out_bias_grad,
            mlp_gain_grad,
            mlp_shift_grad,
            up_bias_grad,
            down_bias_grad,
        ),
        ("dp", "gx", "gy"),
    )
    return (
        prompt_out,
        continuation_out,
        prompt_grad,
        continuation_grad,
        vector_totals[0],
        vector_totals[1],
        weight_totals[0],
        vector_totals[2],
        vector_totals[3],
        weight_totals[1],
        vector_totals[4],
        vector_totals[5],
        vector_totals[6],
        weight_totals[2],
        vector_totals[7],
        weight_totals[3],
        vector_totals[8],
    )


def solution(mesh):
    placed = (
        P(("dp", "gx"), "gy", None),
        P(("dp", "gx", "gy"), None, None),
        P(("dp", "gx", "gy")),
        P(),
        P(),
        P("gx", "gy"),
        P(),
        P(),
        P("gx", "gy"),
        P(),
        P(),
        P(),
        P("gx", "gy"),
        P(),
        P("gy", "gx"),
        P(),
        P(("dp", "gx"), "gy", None),
        P(("dp", "gx", "gy"), None, None),
    )
    return jax.shard_map(
        local,
        mesh=mesh,
        in_specs=placed,
        out_specs=(
            P(("dp", "gx"), "gy", None),
            P(("dp", "gx", "gy"), None, None),
            P(("dp", "gx"), "gy", None),
            P(("dp", "gx", "gy"), None, None),
            P(),
            P(),
            P("gx", "gy"),
            P(),
            P(),
            P("gx", "gy"),
            P(),
            P(),
            P(),
            P("gx", "gy"),
            P(),
            P("gy", "gx"),
            P(),
        ),
        check_vma=False,
    )
```

profile of v0, /device:TPU:0, one launch (start us, length us, event | category | flops | bytes accessed | tf_op | source)
XLA Modules:
  0.0 2485.4 jit_solution(11941156708972222016)
XLA Ops:
  8.0 34.2 %all-gather.26.cloned.1.call-done = bf16[2,1632,272]{1,2,0:T(8,128)(2,1)} async-done(((bf16[1,1632,272]{1,2,0:T(8,128)(2,1)}), bf16[2,1632,272]{1,2,0:T(8,128)(2,1)}) %all-gather.26.cloned.1.call-update) | async-done | bytes 1775632 | tf_op jit(solution)/shard_map/all_gather | solution.py:27
  54.5 127.8 %all-gather.12.cloned.1.call-done = bf16[1088,3264]{1,0:T(8,128)(2,1)} async-done(((bf16[272,3264]{1,0:T(8,128)(2,1)}), bf16[1088,3264]{1,0:T(8,128)(2,1)}) %all-gather.12.cloned.1.call-update) | async-done | bytes 7102480 | tf_op jit(solution)/shard_map/all_gather | solution.py:33
  182.3 23.0 fusion.137
  216.4 10.8 all-gather.2
  230.5 26.3 %all-gather.20.cloned.1.call-done = bf16[4352,272]{0,1:T(8,128)(2,1)} async-done(((bf16[2176,272]{0,1:T(8,128)(2,1)}), bf16[4352,272]{0,1:T(8,128)(2,1)}) %all-gather.20.cloned.1.call-update) | async-done | bytes 2367504 | tf_op jit(solution)/shard_map/all_gather | solution.py:30
  267.6 103.5 %all-gather.24.cloned.1.call-done = bf16[2048,2176]{0,1:T(8,128)(2,1)} async-done(((bf16[1024,2176]{0,1:T(8,128)(2,1)}), bf16[2048,2176]{0,1:T(8,128)(2,1)}) %all-gather.24.cloned.1.call-update) | async-done | bytes 8912912 | tf_op jit(solution)/shard_map/all_gather | solution.py:41
  371.1 11.9 copy.65
  383.0 11.8 copy.67
  397.3 367.7 %while.44 = (s32[]{:T(128)}, bf16[1,1024,1088]{1,2,0:T(8,128)(2,1)}, bf16[256,1088]{0,1:T(8,128)(2,1)}, f32[17,1,1024,1]{2,3,1,0:T(1,128)}, f32[17,256,1]{1,2,0:...) while((s32[]{:T(128)}, ...), condition=%wide.region_7.8_spmd.clone, body=%wide.region_2.7_spmd.clone.sunk | while | flops 726399744 | bytes 94815640 | solution.py:113
  777.7 71.8 %multiply_convert_fusion.2 = (bf16[1280,4352]{1,0:T(8,128)(2,1)}, f32[1280,4352]{1,0:T(8,128)}, f32[1280,4352]{1,0:T(8,128)}) fusion(f32[4352]{0:T(1024)S(1)} %copy-done.65, bf16[1088,4352]{1,0:T(8,128)(2,1)} %all-gather.18.cloned.1.call-done, bf16[1280,1088]{0,1:T(8,128)(2,1)} %add_convert_fusion.3.clone.4), kind=kOutput, calls=%fused_computation.129 | convolution fusion | flops 12489195520 | bytes 67978240 | tf_op jit(solution)/shard_map/dot_general | solution.py:271
  849.5 32.8 %convert_reduce_fusion = (f32[4352]{0:T(1024)}, bf16[1280,4352]{1,0:T(8,128)(2,1)}) fusion(f32[1280,4352]{1,0:T(8,128)} %get-tuple-element.1005, f32[1280,4352]{1,0:T(8,128)} %get-tuple-element.1034, bf16[4352,1088]{0,1:T(8,128)(2,1)} %all-gather.22.cloned.1.call-done, bf16[256,1088]{0,1:T(8,128)(2,1)S(1)} %bitcast.200, bf16[1024,1088]{0,1:T(8,128)(2,1)S(1)} %bitcast.181), kind=kOutput, calls=%fused_computation.127 | convolution fusion | flops 12216233984 | bytes 67978240 | tf_op jit(solution)/shard_map/rd,fd->rf/dot_general | solution.py:289
  882.3 21.6 multiply_reduce_fusion.2
  924.2 706.2 %while.45 = (s32[]{:T(128)}, bf16[1,1024,1088]{1,2,0:T(8,128)(2,1)}, bf16[256,1088]{0,1:T(8,128)(2,1)}, bf16[1,2048,2176]{1,2,0:T(8,128)(2,1)}, bf16[256,2176]{0...) while((s32[]{:T(128)}, ...), condition=%wide.region_15.16_spmd.clone, body=%wide.region_12.15_spmd.clone.sunk | while | flops 1749515008 | bytes 114469832 | solution.py:205
  1138.3 9.8 multiply_reduce_fusion.7
  1346.0 9.8 multiply_reduce_fusion.7
  1639.5 20.3 convolution_convert_fusion.1
  1659.7 14.0 copy.82
  1675.5 18.7 convolution_convert_fusion
  1694.1 14.0 copy.84
  1710.7 24.6 reduce-scatter.18.cloned.1.call-done
  1740.2 22.6 convolution_convert_fusion.2
  1762.8 11.1 copy.78
  1777.0 116.7 %reduce-scatter.32.cloned.1.call-done = bf16[2176,1088]{1,0:T(8,128)(2,1)} async-done(((bf16[4352,1088]{1,0:T(8,128)(2,1)}), bf16[2176,1088]{1,0:T(8,128)(2,1)}) %reduce-scatter.32.cloned.1.call-update) | async-done | bytes 4734992
  1902.1 110.8 %reduce-scatter.34.cloned.1.call-done = bf16[2176,1088]{1,0:T(8,128)(2,1)} async-done(((bf16[4352,1088]{1,0:T(8,128)(2,1)}), bf16[2176,1088]{1,0:T(8,128)(2,1)}) %reduce-scatter.34.cloned.1.call-update) | async-done | bytes 4734992
  2021.3 84.4 %reduce-scatter.28.cloned.1.call-done = bf16[1632,1088]{1,0:T(8,128)(2,1)} async-done(((bf16[3264,1088]{1,0:T(8,128)(2,1)}), bf16[1632,1088]{1,0:T(8,128)(2,1)}) %reduce-scatter.28.cloned.1.call-update) | async-done | bytes 3551248
  2112.1 19.4 fusion.109
  2143.2 19.1 fusion.130
  2167.2 61.0 %reduce-scatter.24.cloned.1.call-done = bf16[272,2176]{1,0:T(8,128)(2,1)} async-done(((bf16[1088,2176]{1,0:T(8,128)(2,1)}), bf16[272,2176]{1,0:T(8,128)(2,1)}) %reduce-scatter.24.cloned.1.call-update) | async-done | bytes 1183760 | tf_op jit(solution)/shard_map/reduce_scatter | solution.py:362
  2228.1 88.5 %reduce-scatter.26.cloned.1.call-done = bf16[2176,272]{0,1:T(8,128)(2,1)} async-done(((bf16[2176,1088]{0,1:T(8,128)(2,1)}), bf16[2176,272]{0,1:T(8,128)(2,1)}) %reduce-scatter.26.cloned.1.call-update) | async-done | bytes 1183760 | tf_op jit(solution)/shard_map/reduce_scatter | solution.py:365
  2316.7 71.2 %reduce-scatter.20.cloned.1.call-done = bf16[272,1632]{1,0:T(8,128)(2,1)} async-done(((bf16[1088,1632]{1,0:T(8,128)(2,1)}), bf16[272,1632]{1,0:T(8,128)(2,1)}) %reduce-scatter.20.cloned.1.call-update) | async-done | bytes 887824 | tf_op jit(solution)/shard_map/reduce_scatter | solution.py:356
  2397.5 43.9 %all-reduce = (f32[1088]{0:T(1024)}, f32[1088]{0:T(1024)}, f32[1088]{0:T(1024)}, f32[1088]{0:T(1024)}, f32[1088]{0:T(1024)}, /*index=5*/f32[1088]{0:T(1024)}, f32[1088]{0:T(1024)}, f32[4352]{0:T(1024)}, f32[1088]{0:T(1024)}) all-reduce(f32[1088]{0:T(1024)S(1)} %get-tuple-element.918, ...), channel_id=1, replica_groups=mesh['dp'=4,'gx'=4,'gy'=2] {'dp','gx','gy'}, use_global_device_ids=true, to_apply=%region_20.21 | all-reduce | flops 13056 | bytes 104448 | tf_op jit(solution)/shard_map/psum | solution.py:375
  2448.7 21.4 all-reduce.4.cloned.1.call-done
  (958 shorter events, 1210.6 us)
Async XLA Ops:
  7.2 35.0 %all-gather.26.cloned.1.call-start = ((), (), s32[]{:S(2)}) async-start(), calls=%async_computation.21 | async-start | bytes 2715648 | tf_op jit(solution)/shard_map/all_gather | solution.py:27
  7.9 44.6 %copy-start.4 = (bf16[1,1024,1088]{1,2,0:T(8,128)(2,1)S(1)}, bf16[1,1024,1088]{1,2,0:T(8,128)(2,1)}, u32[]{:S(2)}) copy-start(bf16[1,1024,1088]{1,2,0:T(8,128)(2,1)} %param.22) | copy-start | bytes 6684676
  7.9 174.3 %all-gather.12.cloned.1.call-start = ((), (), s32[]{:S(2)}) async-start(), calls=%async_computation.9 | async-start | bytes 9052160 | tf_op jit(solution)/shard_map/all_gather | solution.py:33
  51.2 131.1 %copy-start.48 = (f32[1088]{0:T(1024)S(1)}, f32[1088]{0:T(1024)}, u32[]{:S(2)}) copy-start(f32[1088]{0:T(1024)} %param.25) | copy-start | bytes 13060
  51.2 131.1 %copy-start.67 = (f32[1088]{0:T(1024)S(1)}, f32[1088]{0:T(1024)}, u32[]{:S(2)}) copy-start(f32[1088]{0:T(1024)} %param.26) | copy-start | bytes 13060
  51.2 177.9 %all-gather.16.cloned.1.call-start = ((), (), s32[]{:S(2)}) async-start(), calls=%async_computation.11 | async-start | bytes 3551232 | tf_op jit(solution)/shard_map/all_gather | solution.py:29
  51.9 204.9 %all-gather.20.cloned.1.call-start = ((), (), s32[]{:S(2)}) async-start(), calls=%async_computation.13 | async-start | bytes 3551232 | tf_op jit(solution)/shard_map/all_gather | solution.py:30
  52.5 318.6 %all-gather.24.cloned.1.call-start = ((), (), s32[]{:S(2)}) async-start(), calls=%async_computation.20 | async-start | bytes 13369344 | tf_op jit(solution)/shard_map/all_gather | solution.py:41
  53.0 152.2 %copy-start.29 = (f32[1280]{0:T(1024)}, f32[1280]{0:T(1024)S(1)}, u32[]{:S(2)}) copy-start(f32[1280]{0:T(1024)S(1)} %broadcast_multiply_fusion.1) | copy-start | bytes 15364
  54.4 150.8 %copy-start.38 = (f32[1280]{0:T(1024)}, f32[1280]{0:T(1024)S(1)}, u32[]{:S(2)}) copy-start(f32[1280]{0:T(1024)S(1)} %fusion.121) | copy-start | bytes 15364
  54.4 150.8 %copy-start.54 = (f32[1088]{0:T(1024)S(1)}, f32[1088]{0:T(1024)}, u32[]{:S(2)}) copy-start(f32[1088]{0:T(1024)} %param.29) | copy-start | bytes 13060
  54.4 150.8 %copy-start.55 = (f32[1088]{0:T(1024)S(1)}, f32[1088]{0:T(1024)}, u32[]{:S(2)}) copy-start(f32[1088]{0:T(1024)} %param.28) | copy-start | bytes 13060
  216.3 548.7 %all-gather.14.cloned.1.call-start = ((), (), s32[]{:S(2)}) async-start(), calls=%async_computation.10 | async-start | bytes 3133440 | tf_op jit(solution)/shard_map/all_gather | solution.py:34
  229.0 548.6 %all-gather.18.cloned.1.call-start = ((), (), s32[]{:S(2)}) async-start(), calls=%async_computation.12 | async-start | bytes 11837440 | tf_op jit(solution)/shard_map/all_gather | solution.py:35
  229.8 619.7 %all-gather.22.cloned.1.call-start = ((), (), s32[]{:S(2)}) async-start(), calls=%async_computation.14 | async-start | bytes 11837440 | tf_op jit(solution)/shard_map/all_gather | solution.py:36
  256.9 1478.4 %reduce-scatter.18.cloned.1.call-start = ((), (), s32[]{:S(2)}) async-start(), calls=%async_computation.15 | async-start | bytes 13369344 | tf_op jit(solution)/shard_map/reduce_scatter | solution.py:317
  397.3 367.7 %copy-start.5 = (bf16[1,1024,1088]{1,2,0:T(8,128)(2,1)S(1)}, bf16[1,1024,1088]{1,2,0:T(8,128)(2,1)}, u32[]{:S(2)}) copy-start(bf16[1,1024,1088]{1,2,0:T(8,128)(2,1)} %param.22) | copy-start | bytes 6684676
  397.3 367.7 %copy-start.11 = (bf16[1,256,1088]{1,2,0:T(8,128)(2,1)S(1)}, bf16[1,256,1088]{1,2,0:T(8,128)(2,1)}, u32[]{:S(2)}) copy-start(bf16[1,256,1088]{1,2,0:T(8,128)(2,1)} %param.23) | copy-start | bytes 1671172
  397.3 367.8 %copy-start.66 = (f32[1088]{0:T(1024)S(1)}, f32[1088]{0:T(1024)}, u32[]{:S(2)}) copy-start(f32[1088]{0:T(1024)} %param.31) | copy-start | bytes 13060
  777.7 71.8 %copy-start.8 = (bf16[1,1024,1088]{1,2,0:T(8,128)(2,1)S(1)}, bf16[1,1024,1088]{1,2,0:T(8,128)(2,1)}, u32[]{:S(2)}) copy-start(bf16[1,1024,1088]{1,2,0:T(8,128)(2,1)} %param.38) | copy-start | bytes 6684676
  777.7 71.8 %copy-start.19 = (bf16[1,256,1088]{1,2,0:T(8,128)(2,1)S(1)}, bf16[1,256,1088]{1,2,0:T(8,128)(2,1)}, u32[]{:S(2)}) copy-start(bf16[1,256,1088]{1,2,0:T(8,128)(2,1)} %param.39) | copy-start | bytes 1671172
  1630.5 143.9 %reduce-scatter.22.cloned.1.call-start = ((), (), s32[]{:S(2)}) async-start(), calls=%async_computation.17 | async-start | bytes 3760128 | tf_op jit(solution)/shard_map/reduce_scatter | solution.py:345
  1639.4 254.4 %reduce-scatter.32.cloned.1.call-start = ((), (), s32[]{:S(2)}) async-start(), calls=%async_computation.24 | async-start | bytes 15040512
  1673.8 339.2 %reduce-scatter.34.cloned.1.call-start = ((), (), s32[]{:S(2)}) async-start(), calls=%async_computation.25 | async-start | bytes 15040512
  1708.2 397.6 %reduce-scatter.28.cloned.1.call-start = ((), (), s32[]{:S(2)}) async-start(), calls=%async_computation.22 | async-start | bytes 11280384
  1773.9 367.4 %reduce-scatter.30.cloned.1.call-start = ((), (), s32[]{:S(2)}) async-start(), calls=%async_computation.23 | async-start | bytes 1740800
  1776.9 451.2 %reduce-scatter.24.cloned.1.call-start = ((), (), s32[]{:S(2)}) async-start(), calls=%async_computation.18 | async-start | bytes 5918720 | tf_op jit(solution)/shard_map/reduce_scatter | solution.py:362
  1902.1 414.6 %reduce-scatter.26.cloned.1.call-start = ((), (), s32[]{:S(2)}) async-start(), calls=%async_computation.19 | async-start | bytes 5918720 | tf_op jit(solution)/shard_map/reduce_scatter | solution.py:365
  2021.3 90.8 %copy-start.69 = (f32[1088]{0:T(1024)S(1)}, f32[1088]{0:T(1024)}, u32[]{:S(2)}) copy-start(f32[1088]{0:T(1024)} %param.37) | copy-start | bytes 13060
  2021.3 366.6 %reduce-scatter.20.cloned.1.call-start = ((), (), s32[]{:S(2)}) async-start(), calls=%async_computation.16 | async-start | bytes 4526080 | tf_op jit(solution)/shard_map/reduce_scatter | solution.py:356
  2112.0 358.1 %all-reduce.4.cloned.1.call-start = ((), (), s32[]{:S(2)}) async-start(), calls=%async_computation.26 | async-start | bytes 7380992 | tf_op jit(solution)/shard_map/psum | solution.py:371
  2162.3 225.6 %copy-start.41 = (f32[1280]{0:T(1024)S(1)}, f32[1280]{0:T(1024)}, u32[]{:S(2)}) copy-start(f32[1280]{0:T(1024)} %copy-done.40) | copy-start | bytes 15364
  (141 other events, 936.6 us)
Sparse Core Ops, SparseCore 0:
  9.6 32.5 all-gather.25
  51.3 130.8 all-gather.11
  183.8 34.3 all-gather.15
  219.6 37.1 all-gather.19
  258.8 112.2 all-gather.23
  373.1 52.9 all-gather.13
  427.6 166.0 all-gather.17
  595.3 165.4 all-gather.21
  1630.5 104.7 reduce-scatter.17
  1738.0 36.3 reduce-scatter.21
  1776.8 116.8 reduce-scatter.31
  1896.0 116.8 reduce-scatter.33
  2015.4 90.3 reduce-scatter.27
  2108.6 32.6 reduce-scatter.29
  2143.6 84.5 reduce-scatter.23
  2230.4 86.1 reduce-scatter.25
  2319.5 68.3 reduce-scatter.19
  2390.9 79.1 all-reduce.3
where the time goes:
time: 2500 us; the launch traced here: 2490 us
  matrix products  952 us (38%)
  waiting for transfers between devices  879 us (35%)
  local copies, waits for them, and re-layouts  371 us (15%)
  other arithmetic  209 us (8%)
  blocking collectives  54.6 us (2%)
    unnamed x22, waiting for transfers between devices  321 us
    dot_general x34, matrix products, head_step(): jnp.einsum('gid,gjd->gij', query_p, key_p, preferred_element_type=jnp.flo...  224 us
    all_gather x1, waiting for transfers between devices, fetch_weights(): lax.all_gather(by_column[0], 'gx', axis=0, tiled=True)  128 us
    unnamed x154, local copies, waits for them, and re-layouts  114 us
    convert_element_type x17, other arithmetic, head_step(): dscore_p = (probs_p * (dprob_p - jnp.sum(probs_p * dprob_p, axis=-1, keep...  111 us
    all_gather x1, waiting for transfers between devices, fetch_keys(): return lax.all_gather(local_keys, 'gy', axis=1, tiled=True)  104 us
    dot_general x17, matrix products, head_step(): jnp.einsum('gid,gjd->gij', grad_p, value_p, preferred_element_type=jnp.fl...  98 us
    reduce_scatter x1, waiting for transfers between devices, local(): lax.psum_scatter(column_sums[3].astype(jnp.bfloat16), 'gx', scatter_dimen...  88.5 us
  transfers between devices with their start and end apart: 18, of which 14 were waited for; matrix products, arithmetic and copies ran while one was open for 27% of the time, Pallas kernels for 0%

commit v1 on v0

v1 whole, which is shorter than its diff:
```python
import functools
import jax
import jax.numpy as jnp
from jax import lax
from jax.sharding import PartitionSpec as P
from jax.experimental import pallas as pl
from jax.experimental.pallas import tpu as pltpu

HEADS = 17
HEAD_DIM = 64
LOG2E = 1.4426950408889634
NEG = -1e30
BK = 512


def nt(a, b):
    return lax.dot_general(a, b, (((1,), (1,)), ((), ())), preferred_element_type=jnp.float32)


def nn(a, b):
    return jnp.dot(a, b, preferred_element_type=jnp.float32)


def tn(a, b):
    return lax.dot_general(a, b, (((0,), (0,)), ((), ())), preferred_element_type=jnp.float32)


def halves(pair, total):
    lane = lax.broadcasted_iota(jnp.int32, (1, 128), 1)
    left = jnp.minimum(total - pair * 128, 128)
    return lane < 64, jnp.logical_and(lane >= 64, lane < left), lane < left


def norm_bounds(ref, valid, spread):
    part = jnp.where(valid, ref[...], jnp.zeros((), jnp.bfloat16))
    return jnp.max(nn(part * part, spread), axis=0, keepdims=True)


def forward_kernel(pos, q, k, v, kb, vb, o, lse, va, vc, vab, vcb, tops, accs, *, block):
    pair = pl.program_id(0)
    scale = HEAD_DIM ** (-0.5) * LOG2E
    low, high, valid = halves(pair, HEADS * HEAD_DIM)
    zero = jnp.zeros((), jnp.bfloat16)
    one = jnp.ones((), jnp.bfloat16)
    for src, first, second in ((v, va, vc), (vb, vab, vcb)):
        whole = src[...]
        first[...] = jnp.where(low, whole, one)
        second[...] = jnp.where(low, one, jnp.where(high, whole, zero))
    spread = (
        (lax.broadcasted_iota(jnp.int32, (128, 128), 0) < 64)
        == (lax.broadcasted_iota(jnp.int32, (128, 128), 1) < 64)
    ).astype(jnp.bfloat16)
    key_bound = jnp.maximum(norm_bounds(k, valid, spread), norm_bounds(kb, valid, spread))
    bound = jnp.max(key_bound * norm_bounds(q, valid, spread)) * (scale * scale)
    plain = bound < 90.0 * 90.0
    rows = q.shape[0]
    branch = kb.shape[0]
    blocks = [(start, block, False) for start in range(0, rows - branch, block)]
    blocks.append((rows - branch, branch, True))

    def finish(start, size, acc_a, acc_b, top):
        total = pltpu.roll(jnp.where(low, acc_b, acc_a), 64, 1)
        o[start : start + size, :] = (jnp.where(low, acc_a, acc_b) / total).astype(o.dtype)
        turned = (top + jnp.log2(total)).T
        lse[0, 0:1, start : start + size] = turned[0:1, :]
        lse[0, 1:2, start : start + size] = turned[64:65, :]

    def setup(number, start, size, is_branch):
        at = pos[number]
        query = q[start : start + size, :]
        queries = (jnp.where(low, query, zero), jnp.where(high, query, zero))
        row = lax.broadcasted_iota(jnp.int32, (size, BK), 0)
        column = lax.broadcasted_iota(jnp.int32, (size, BK), 1)
        triangle = lax.broadcasted_iota(jnp.int32, (size, size), 1) <= lax.broadcasted_iota(
            jnp.int32, (size, size), 0
        )
        whole_blocks = at // BK

        def allowed(index):
            if is_branch:
                return column + index * BK < at
            return column + index * BK <= row + at

        end = (at + BK - 1) // BK if is_branch else whole_blocks + 1
        return queries, triangle, whole_blocks, allowed, end

    def read(index):
        rows_at = pl.ds(pl.multiple_of(index * BK, BK), BK)
        return jnp.where(valid, k[rows_at, :], zero), va[rows_at, :], vc[rows_at, :]

    def own():
        return jnp.where(valid, kb[...], zero), vab[...], vcb[...]

    @pl.when(plain)
    def _():
        for number, (start, size, is_branch) in enumerate(blocks):
            queries, triangle, whole_blocks, allowed, end = setup(number, start, size, is_branch)

            def step(key, first, second, carry, mask):
                out = []
                for query_h, value_h, acc in zip(queries, (first, second), carry):
                    probs = jnp.exp2(nt(query_h, key) * scale)
                    if mask is not None:
                        probs = jnp.where(mask, probs, 0.0)
                    out.append(acc + nn(probs.astype(jnp.bfloat16), value_h))
                return tuple(out)

            carry = (jnp.zeros((size, 128), jnp.float32),) * 2
            carry = lax.fori_loop(0, whole_blocks, lambda i, c: step(*read(i), c, None), carry)
            if is_branch:
                carry = lax.fori_loop(
                    whole_blocks, end, lambda i, c: step(*read(i), c, allowed(i)), carry
                )
                carry = step(*own(), carry, triangle)
            else:
                carry = step(*read(whole_blocks), carry, allowed(whole_blocks))
            finish(start, size, *carry, 0.0)

    @pl.when(jnp.logical_not(plain))
    def _():
        for number, (start, size, is_branch) in enumerate(blocks):
            queries, triangle, whole_blocks, allowed, end = setup(number, start, size, is_branch)

            def step(key, first, second, mask):
                for head, value_h in enumerate((first, second)):
                    top = tops[head, 0:size, :]
                    scores = jnp.where(mask, nt(queries[head], key), NEG)
                    new_top = jnp.maximum(top, jnp.max(scores, axis=1, keepdims=True))
                    probs = jnp.exp2((scores - new_top[:, 0:1]) * scale).astype(jnp.bfloat16)
                    fade = jnp.exp2((top - new_top) * scale)
                    accs[head, 0:size, :] = accs[head, 0:size, :] * fade + nn(probs, value_h)
                    tops[head, 0:size, :] = new_top

            accs[:, 0:size, :] = jnp.zeros((2, size, 128), jnp.float32)
            tops[:, 0:size, :] = jnp.full((2, size, 128), NEG, jnp.float32)

            @pl.loop(0, end)
            def _(index):
                step(*read(index), allowed(index))

            if is_branch:
                step(*own(), triangle)
            top = jnp.where(low, tops[0, 0:size, :], tops[1, 0:size, :]) * scale
            finish(start, size, accs[0, 0:size, :], accs[1, 0:size, :], top)


def attention_forward(pos, q, k, v, kb, vb, block):
    rows, width = q.shape
    branch = kb.shape[0]
    span = k.shape[0]
    pairs = (HEADS + 1) // 2

    def col(n):
        return pl.BlockSpec((n, 128), lambda p, pos: (0, p))

    return pl.pallas_call(
        functools.partial(forward_kernel, block=block),
        grid_spec=pltpu.PrefetchScalarGridSpec(
            num_scalar_prefetch=1,
            grid=(pairs,),
            in_specs=[col(rows), col(span), col(span), col(branch), col(branch)],
            out_specs=[col(rows), pl.BlockSpec((1, 8, rows), lambda p, pos: (p, 0, 0))],
            scratch_shapes=[
                pltpu.VMEM((span, 128), jnp.bfloat16),
                pltpu.VMEM((span, 128), jnp.bfloat16),
                pltpu.VMEM((branch, 128), jnp.bfloat16),
                pltpu.VMEM((branch, 128), jnp.bfloat16),
                pltpu.VMEM((2, max(block, branch), 128), jnp.float32),
                pltpu.VMEM((2, max(block, branch), 128), jnp.float32),
            ],
        ),
        out_shape=[
            jax.ShapeDtypeStruct((rows, width), jnp.bfloat16),
            jax.ShapeDtypeStruct((pairs, 8, rows), jnp.float32),
        ],
        compiler_params=pltpu.CompilerParams(
            dimension_semantics=("arbitrary",), vmem_limit_bytes=50 * 2**20
        ),
        name="attention_forward",
    )(pos, q, k, v, kb, vb)


def backward_kernel(
    pos, q, k, v, kb, vb, o, do, lse, dq, dk, dv, dkb, dvb,
    ka, kc, kta, ktc, kam, vm, kab, kcb, ktab, ktcb, kbm, vbm, dks, dvs, *, block, span, mode
):
    pair = pl.program_id(0)
    scale = HEAD_DIM ** (-0.5)
    low, high, valid = halves(pair, HEADS * HEAD_DIM)
    zero = jnp.zeros((), jnp.bfloat16)
    for src, whole_ref, first, second, turn_a, turn_b in (
        (k, kam, ka, kc, kta, ktc),
        (kb, kbm, kab, kcb, ktab, ktcb),
    ):
        whole = jnp.where(valid, src[...], zero)
        whole_ref[...] = whole
        if mode == "t":
            first[...] = jnp.where(low, whole, zero)
            second[...] = jnp.where(high, whole, zero)
        else:
            turned = whole.T
            turn_a[...] = turned[0:64, :]
            turn_b[...] = turned[64:128, :]
    vm[...] = jnp.where(valid, v[...], zero)
    vbm[...] = jnp.where(valid, vb[...], zero)
    dks[...] = jnp.zeros_like(dks)
    dvs[...] = jnp.zeros_like(dvs)
    rows = q.shape[0]
    branch = kb.shape[0]
    blocks = [(start, block, False) for start in range(0, rows - branch, block)]
    blocks.append((rows - branch, branch, True))
    ones_a = jnp.broadcast_to(low, (8, 128)).astype(jnp.bfloat16)
    ones_b = jnp.broadcast_to(high, (8, 128)).astype(jnp.bfloat16)
    for number, (start, size, is_branch) in enumerate(blocks):
        at = pos[number]
        here = slice(start, start + size)
        query = q[here, :]
        grad = do[here, :]
        queries = (jnp.where(low, query, zero), jnp.where(high, query, zero))
        grads = (jnp.where(low, grad, zero), jnp.where(high, grad, zero))
        product = jnp.where(valid, grad.astype(jnp.float32) * o[here, :].astype(jnp.float32), 0.0)
        upper = product.astype(jnp.bfloat16)
        lower = (product - upper.astype(jnp.float32)).astype(jnp.bfloat16)
        deltas = tuple((nt(m, upper) + nt(m, lower))[0:1, :] for m in (ones_a, ones_b))
        stats = (lse[0, 0:1, here], lse[0, 1:2, here])
        queries_cat = jnp.concatenate(queries, axis=0)
        grads_cat = jnp.concatenate(grads, axis=0)

        def step(key, value, first, second, mask):
            probs, dscores = [], []
            for query_h, grad_h, delta, stat in zip(queries, grads, deltas, stats):
                scores = nt(key, query_h)
                prob = jnp.exp2(scores * (scale * LOG2E) - stat)
                if mask is not None:
                    prob = jnp.where(mask, prob, 0.0)
                dprob = nt(value, grad_h)
                probs.append(prob.astype(jnp.bfloat16))
                dscores.append((prob * (dprob - delta)).astype(jnp.bfloat16))
            dscores_cat = jnp.concatenate(dscores, axis=1)
            dvalue = nn(jnp.concatenate(probs, axis=1), grads_cat)
            dkey = nn(dscores_cat, queries_cat)
            if mode == "t":
                dquery = tn(dscores[0], first) + tn(dscores[1], second)
            else:
                dquery = jnp.concatenate([nn(first, dscores[0]), nn(second, dscores[1])], axis=0)
            return dquery, dkey, dvalue

        def read(base):
            rows_at = pl.ds(pl.multiple_of(base, BK), BK)
            if mode == "t":
                return kam[rows_at, :], vm[rows_at, :], ka[rows_at, :], kc[rows_at, :]
            return kam[rows_at, :], vm[rows_at, :], kta[:, rows_at], ktc[:, rows_at]

        def accumulate(index, carry, mask):
            rows_at = pl.ds(pl.multiple_of(index * BK, BK), BK)
            dquery, dkey, dvalue = step(*read(index * BK), mask)
            dks[rows_at, :] += dkey
            dvs[rows_at, :] += dvalue
            return carry + dquery

        dim = (size, 128) if mode == "t" else (128, size)
        carry = jnp.zeros(dim, jnp.float32)
        whole_blocks = at // BK
        carry = lax.fori_loop(0, whole_blocks, lambda i, c: accumulate(i, c, None), carry)
        row = lax.broadcasted_iota(jnp.int32, (BK, size), 0)
        column = lax.broadcasted_iota(jnp.int32, (BK, size), 1)
        if is_branch:
            carry = lax.fori_loop(
                whole_blocks,
                (at + BK - 1) // BK,
                lambda i, c: accumulate(i, c, row + i * BK < at),
                carry,
            )
            triangle = lax.broadcasted_iota(jnp.int32, (size, size), 0) <= lax.broadcasted_iota(
                jnp.int32, (size, size), 1
            )
            own = (kab[...], kcb[...]) if mode == "t" else (ktab[...], ktcb[...])
            dquery, dkey, dvalue = step(kbm[...], vbm[...], *own, triangle)
            carry = carry + dquery
            dkb[...] = (dkey * scale).astype(dkb.dtype)
            dvb[...] = dvalue.astype(dvb.dtype)
        else:
            carry = accumulate(whole_blocks, carry, row + whole_blocks * BK <= column + at)
        if mode != "t":
            carry = carry.T
        dq[here, :] = (carry * scale).astype(dq.dtype)
    dk[...] = (dks[...] * scale).astype(dk.dtype)
    dv[...] = dvs[...].astype(dv.dtype)


def attention_backward(pos, q, k, v, kb, vb, o, do, lse, block, mode="n"):
    rows, width = q.shape
    branch = kb.shape[0]
    span = k.shape[0]
    pairs = (HEADS + 1) // 2

    def col(n):
        return pl.BlockSpec((n, 128), lambda p, pos: (0, p))

    def scratch(n):
        tall = pltpu.VMEM((n, 128) if mode == "t" else (8, 128), jnp.bfloat16)
        wide = pltpu.VMEM((64, n) if mode != "t" else (8, 128), jnp.bfloat16)
        return [tall, tall, wide, wide, pltpu.VMEM((n, 128), jnp.bfloat16), pltpu.VMEM((n, 128), jnp.bfloat16)]

    def shape(n, t=jnp.bfloat16):
        return jax.ShapeDtypeStruct((n, width), t)

    return pl.pallas_call(
        functools.partial(backward_kernel, block=block, span=span, mode=mode),
        grid_spec=pltpu.PrefetchScalarGridSpec(
            num_scalar_prefetch=1,
            grid=(pairs,),
            in_specs=[col(rows), col(span), col(span), col(branch), col(branch), col(rows), col(rows),
                      pl.BlockSpec((1, 8, rows), lambda p, pos: (p, 0, 0))],
            out_specs=[col(rows), col(span), col(span), col(branch), col(branch)],
            scratch_shapes=scratch(span) + scratch(branch)
            + [pltpu.VMEM((span, 128), jnp.float32), pltpu.VMEM((span, 128), jnp.float32)],
        ),
        out_shape=[shape(rows), shape(span), shape(span), shape(branch), shape(branch)],
        compiler_params=pltpu.CompilerParams(
            dimension_semantics=("arbitrary",), vmem_limit_bytes=56 * 2**20
        ),
        name="attention_backward",
    )(pos, q, k, v, kb, vb, o, do, lse)


epsilon = 1e-05


def layer_norm(values_in, norm_gain, norm_shift):
    centre = jnp.mean(values_in, axis=-1, keepdims=True)
    centred = values_in - centre
    spread = jnp.mean(centred * centred, axis=-1, keepdims=True)
    return centred * lax.rsqrt(spread + epsilon) * norm_gain + norm_shift


def smooth_gate(pre_act):
    return jax.nn.gelu(pre_act, approximate=False)


def swap(value, axis, bit):
    count = lax.axis_size(axis)
    return lax.ppermute(value, axis, [(i, i ^ bit) for i in range(count)])


def ahead(value, axis, step):
    count = lax.axis_size(axis)
    return lax.ppermute(value, axis, [(i, (i + step) % count) for i in range(count)])


def total_over(value, axes):
    for axis in axes:
        count = lax.axis_size(axis)
        if count & (count - 1):
            value = lax.psum(value, axis)
            continue
        bit = 1
        while bit < count:
            value = value + swap(value, axis, bit)
            bit *= 2
    return value


def by_halves():
    return lax.axis_size("dp") % 2 == 0 and lax.axis_size("gy") == 2


def half_index():
    return lax.axis_index("dp") % 2


def pair_rows(mine, theirs):
    first = half_index() == 0
    return jnp.stack([jnp.where(first, mine, theirs), jnp.where(first, theirs, mine)], axis=-3)


def along_gx(block):
    count = lax.axis_size("gx")
    here = lax.axis_index("gx")
    out = jnp.zeros((count,) + block.shape, block.dtype)
    for step in range(count):
        got = block if step == 0 else ahead(block, "gx", step)
        out = lax.dynamic_update_index_in_dim(out, got, (here - step) % count, 0)
    return out


def order_columns(mine, theirs):
    first = lax.axis_index("gy") == 0
    return jnp.concatenate([jnp.where(first, mine, theirs), jnp.where(first, theirs, mine)], axis=-1)


def gather_ordered(part):
    rows, columns = part.shape
    if not by_halves():
        part = lax.all_gather(part, "gy", axis=1, tiled=True)
        return lax.all_gather(part, "gx", axis=0, tiled=True)
    mine = lax.dynamic_index_in_dim(part.reshape(2, rows // 2, columns), half_index(), 0, False)
    both = order_columns(mine, swap(mine, "gy", 1))
    blocks = along_gx(both)
    return pair_rows(blocks, swap(blocks, "dp", 1)).reshape(-1, 2 * columns)


def gather_parts(part):
    rows, columns = part.shape
    if not by_halves():
        part = lax.all_gather(part, "gx", axis=0, tiled=True)
        return [part] + [ahead(part, "gy", step) for step in range(1, lax.axis_size("gy"))]
    mine = lax.dynamic_index_in_dim(part.reshape(2, rows // 2, columns), half_index(), 0, False)
    blocks = along_gx(mine)
    out = []
    for piece in (blocks, swap(blocks, "gy", 1)):
        out.append(pair_rows(piece, swap(piece, "dp", 1)).reshape(-1, columns))
    return out


def scatter_parts(parts):
    rows, columns = parts[0].shape
    count = lax.axis_size("gx")
    here = lax.axis_index("gx")
    if not by_halves():
        total = parts[0].astype(jnp.float32)
        for step in range(1, len(parts)):
            total = total + ahead(parts[step], "gy", -step).astype(jnp.float32)
        total = lax.psum_scatter(
            total.astype(jnp.bfloat16), "gx", scatter_dimension=0, tiled=True
        )
        return lax.psum(total, "dp").astype(jnp.float32)
    wide = [p.reshape(count, 2, rows // count // 2, columns) for p in parts]
    half = half_index()
    sums = []
    for piece in (wide[1], wide[0]):
        keep = lax.dynamic_index_in_dim(piece, half, 1, False)
        give = lax.dynamic_index_in_dim(piece, 1 - half, 1, False)
        sums.append(keep.astype(jnp.float32) + swap(give, "dp", 1).astype(jnp.float32))
    block = sums[1] + swap(sums[0].astype(jnp.bfloat16), "gy", 1).astype(jnp.float32)
    block = block.astype(jnp.bfloat16)
    total = lax.dynamic_index_in_dim(block, here, 0, False).astype(jnp.float32)
    for step in range(1, count):
        give = lax.dynamic_index_in_dim(block, (here + step) % count, 0, False)
        total = total + ahead(give, "gx", step).astype(jnp.float32)
    mine = total.astype(jnp.bfloat16)
    bit = 2
    while bit < lax.axis_size("dp"):
        mine = (mine.astype(jnp.float32) + swap(mine, "dp", bit).astype(jnp.float32)).astype(jnp.bfloat16)
        bit *= 2
    return pair_rows(mine, swap(mine, "dp", 1)).reshape(-1, columns).astype(jnp.float32)


def split_columns(whole):
    count = lax.axis_size("gy")
    here = lax.axis_index("gy")
    columns = whole.shape[1] // count
    if count == 2:
        first, second = whole[:, :columns], whole[:, columns:]
        swapped = here == 1
        return [jnp.where(swapped, second, first), jnp.where(swapped, first, second)]
    return [
        lax.dynamic_slice_in_dim(whole, (here - step) % count * columns, columns, 1)
        for step in range(count)
    ]


def own_vector(vector):
    count = lax.axis_size("gy")
    here = lax.axis_index("gy")
    pieces = vector.reshape(count, -1)
    return [lax.dynamic_index_in_dim(pieces, (here - step) % count, 0, False) for step in range(count)]


def order_vector(pieces):
    count = lax.axis_size("gy")
    here = lax.axis_index("gy")
    out = jnp.zeros((count,) + pieces[0].shape, pieces[0].dtype)
    for step, piece in enumerate(pieces):
        out = lax.dynamic_update_index_in_dim(out, piece, (here - step) % count, 0)
    return out.reshape(-1)


def all_tokens(own):
    count = lax.axis_size("gy")
    here = lax.axis_index("gy")
    if count != 2:
        return lax.all_gather(own, "gy", axis=0, tiled=True)
    other = swap(own, "gy", 1)
    first = here == 0
    return jnp.concatenate([jnp.where(first, own, other), jnp.where(first, other, own)], axis=0)


def own_tokens_sum(whole):
    count = lax.axis_size("gy")
    here = lax.axis_index("gy")
    rows = whole.shape[0] // count
    if count != 2:
        return lax.psum_scatter(
            whole.astype(jnp.bfloat16), "gy", scatter_dimension=0, tiled=True
        ).astype(jnp.float32)
    give = lax.dynamic_slice_in_dim(whole, (1 - here) * rows, rows, 0)
    keep = lax.dynamic_slice_in_dim(whole, here * rows, rows, 0)
    return keep + swap(give.astype(jnp.bfloat16), "gy", 1).astype(jnp.float32)


def dot(a, b):
    return jnp.dot(a, b, preferred_element_type=jnp.float32)


def local(
    prompt,
    continuations,
    prefix_len,
    attn_gain,
    attn_shift,
    qkv_weight,
    query_bias,
    value_bias,
    out_weight,
    out_bias,
    mlp_gain,
    mlp_shift,
    up_weight,
    up_bias,
    down_weight,
    down_bias,
    grad_prompt,
    grad_continuations,
):
    groups, shard, width = prompt.shape
    length = continuations.shape[1]
    first_pos = lax.axis_index("gy") * shard
    prompt_len = shard * lax.axis_size("gy")
    block = min(512, shard)
    places = [first_pos + start for start in range(0, shard, block)] + [prefix_len[0]]
    places = jnp.stack(places).astype(jnp.int32)

    qkv = gather_ordered(qkv_weight)
    qkv_split = [qkv[:, :width], qkv[:, width : 2 * width], qkv[:, 2 * width :]]
    own_prompt = prompt.reshape(shard, width)
    branch = continuations.reshape(length, width)
    whole_prompt = all_tokens(own_prompt)
    out_full = gather_ordered(out_weight)
    up_parts = gather_parts(up_weight)
    down_parts = gather_parts(down_weight.T)

    token_rows = jnp.concatenate([own_prompt, branch], axis=0).astype(jnp.float32)
    normed_one, norm_one_back = jax.vjp(layer_norm, token_rows, attn_gain, attn_shift)
    act_one = normed_one.astype(jnp.bfloat16)
    key_rows = jnp.concatenate([whole_prompt, branch], axis=0).astype(jnp.float32)
    key_act = layer_norm(key_rows, attn_gain, attn_shift).astype(jnp.bfloat16)
    queries = (dot(act_one, qkv_split[0]) + query_bias).astype(jnp.bfloat16)
    keys = dot(key_act, qkv_split[1]).astype(jnp.bfloat16)
    values = (dot(key_act, qkv_split[2]) + value_bias).astype(jnp.bfloat16)
    parts_in = (queries, keys[:prompt_len], values[:prompt_len], keys[prompt_len:], values[prompt_len:])
    mixed, stats = attention_forward(places, *parts_in, block)

    resid = token_rows + (dot(mixed, out_full) + out_bias)
    normed_two, norm_two_back = jax.vjp(layer_norm, resid, mlp_gain, mlp_shift)
    act_two = normed_two.astype(jnp.bfloat16)
    result = resid + down_bias
    hidden_parts, gates_back = [], []
    for up_part, down_part, bias in zip(up_parts, down_parts, own_vector(up_bias)):
        pre_act = dot(act_two, up_part) + bias
        hidden_exact, gate_back = jax.vjp(smooth_gate, pre_act)
        hidden_parts.append(hidden_exact.astype(jnp.bfloat16))
        gates_back.append(gate_back)
        result = result + nt(hidden_parts[-1], down_part)
    prompt_out = result[:shard].reshape(groups, shard, width).astype(jnp.bfloat16)
    continuation_out = result[shard:].reshape(1, length, width).astype(jnp.bfloat16)

    cotangent = jnp.concatenate(
        [grad_prompt.reshape(shard, width), grad_continuations.reshape(length, width)], axis=0
    )
    cot_exact = cotangent.astype(jnp.float32)
    down_bias_grad = jnp.sum(cot_exact, axis=0)
    down_grads, up_grads, bias_grads = [], [], []
    d_act_two = 0.0
    for hidden, gate_back, up_part, down_part in zip(hidden_parts, gates_back, up_parts, down_parts):
        down_grads.append(tn(cotangent, hidden).astype(jnp.bfloat16))
        d_pre = gate_back(dot(cotangent, down_part))[0].astype(jnp.bfloat16)
        up_grads.append(tn(act_two, d_pre).astype(jnp.bfloat16))
        bias_grads.append(jnp.sum(d_pre.astype(jnp.float32), axis=0))
        d_act_two = d_act_two + nt(d_pre, up_part)
    down_total = scatter_parts(down_grads).T
    up_total = scatter_parts(up_grads)
    up_bias_grad = order_vector(bias_grads)
    resid_part, mlp_gain_grad, mlp_shift_grad = norm_two_back(d_act_two)
    d_resid = cot_exact + resid_part
    d_branch = d_resid.astype(jnp.bfloat16)
    out_total = scatter_parts(split_columns(tn(mixed, d_branch).astype(jnp.bfloat16)))
    out_bias_grad = jnp.sum(d_branch.astype(jnp.float32), axis=0)
    d_mixed = nt(d_branch, out_full).astype(jnp.bfloat16)
    d_queries, dk, dv, dkb, dvb = attention_backward(places, *parts_in, mixed, d_mixed, stats, block)

    d_keys = jnp.concatenate([dk, dkb], axis=0)
    d_values = jnp.concatenate([dv, dvb], axis=0)
    d_key_act = nt(d_keys, qkv_split[1]) + nt(d_values, qkv_split[2])
    shared = own_tokens_sum(d_key_act[:prompt_len])
    qkv_grad = jnp.concatenate([tn(act_one, d_queries), tn(key_act, d_keys), tn(key_act, d_values)], axis=1)
    qkv_total = scatter_parts(split_columns(qkv_grad.astype(jnp.bfloat16)))
    query_bias_grad = jnp.sum(d_queries.astype(jnp.float32), axis=0)
    value_bias_grad = jnp.sum(d_values.astype(jnp.float32), axis=0)
    d_act_one = nt(d_queries, qkv_split[0]) + jnp.concatenate([shared, d_key_act[prompt_len:]], axis=0)
    rows_part, attn_gain_grad, attn_shift_grad = norm_one_back(d_act_one)
    d_rows = d_resid + rows_part
    prompt_grad = d_rows[:shard].reshape(groups, shard, width)
    continuation_grad = d_rows[shard:].reshape(1, length, width)
    vectors = (
        attn_gain_grad,
        attn_shift_grad,
        query_bias_grad,
        value_bias_grad,
        out_bias_grad,
        mlp_gain_grad,
        mlp_shift_grad,
        up_bias_grad,
        down_bias_grad,
    )
    joined = total_over(jnp.concatenate(vectors), ("dp", "gy", "gx"))
    totals = []
    at = 0
    for vector in vectors:
        totals.append(joined[at : at + vector.shape[0]])
        at += vector.shape[0]
    return (
        prompt_out,
        continuation_out,
        prompt_grad,
        continuation_grad,
        totals[0],
        totals[1],
        qkv_total,
        totals[2],
        totals[3],
        out_total,
        totals[4],
        totals[5],
        totals[6],
        up_total,
        totals[7],
        down_total,
        totals[8],
    )


def solution(mesh):
    placed = (
        P(("dp", "gx"), "gy", None),
        P(("dp", "gx", "gy"), None, None),
        P(("dp", "gx", "gy")),
        P(),
        P(),
        P("gx", "gy"),
        P(),
        P(),
        P("gx", "gy"),
        P(),
        P(),
        P(),
        P("gx", "gy"),
        P(),
        P("gy", "gx"),
        P(),
        P(("dp", "gx"), "gy", None),
        P(("dp", "gx", "gy"), None, None),
    )
    return jax.shard_map(
        local,
        mesh=mesh,
        in_specs=placed,
        out_specs=(
            P(("dp", "gx"), "gy", None),
            P(("dp", "gx", "gy"), None, None),
            P(("dp", "gx"), "gy", None),
            P(("dp", "gx", "gy"), None, None),
            P(),
            P(),
            P("gx", "gy"),
            P(),
            P(),
            P("gx", "gy"),
            P(),
            P(),
            P(),
            P("gx", "gy"),
            P(),
            P("gy", "gx"),
            P(),
        ),
        check_vma=False,
    )
```

time: 2500 us -> 1240 us (0.50)
  matrix products: 952 us -> 286 us
  waiting for transfers between devices: 879 us -> 396 us
  local copies, waits for them, and re-layouts: 371 us -> 92.3 us
  starting transfers between devices: 0.91 us -> 241 us
  other arithmetic: 209 us -> 90.1 us
  Pallas kernels: 0 us -> 114 us
  blocking collectives: 54.6 us -> 0 us
    dot_general x250 -> x24, matrix products: 952 us -> 286 us  [the longest x8 139 us: dot(): return jnp.dot(a, b, preferred_element_type=jnp.float32)]
    ppermute x0 -> x61, waiting for transfers between devices: none -> 396 us  [the longest x37 216 us: swap(): return lax.ppermute(value, axis, [(i, i ^ bit) for i in range(count)])]
    unnamed x22 -> x0, waiting for transfers between devices: 321 us -> none
    all_gather x8 -> x0, waiting for transfers between devices: 292 us -> none  [the longest x1 128 us: fetch_weights(): lax.all_gather(by_column[0], 'gx', axis=0, tiled=True)]
    reduce_scatter x5 -> x0, waiting for transfers between devices: 246 us -> none  [the longest x1 88.5 us: local(): lax.psum_scatter(column_sums[3].astype(jnp.bfloat16), 'gx', scatter_dimen...]
    ppermute x0 -> x61, starting transfers between devices: none -> 241 us  [the longest x37 155 us: swap(): return lax.ppermute(value, axis, [(i, i ^ bit) for i in range(count)])]
    pallas_call x0 -> x2, Pallas kernels: none -> 114 us  [the longest x1 65.7 us: attention_backward(): pl.pallas_call(functools.partial(backward_kernel, block=block, span=span,...]
    dynamic_slice x102 -> x1, local copies, waits for them, and re-layouts: 110 us -> 1.45 us  [own_vector(): lax.dynamic_index_in_dim(pieces, (here - step) % count, 0, False)]
  transfers between devices with their start and end apart: 18 -> 61, of which waited for: 14 -> 22; matrix products, arithmetic and copies ran while one was open for 27% -> 25% of each run, Pallas kernels for 0% -> 4%
where the time goes in v1:
time: 1240 us; the launch traced here: 1220 us
  waiting for transfers between devices  396 us (32%)
  matrix products  286 us (23%)
  starting transfers between devices  241 us (19%)
  Pallas kernels  114 us (9%)
  local copies, waits for them, and re-layouts  92.3 us (7%)
  other arithmetic  90.1 us (7%)
    ppermute x37, waiting for transfers between devices, swap(): return lax.ppermute(value, axis, [(i, i ^ bit) for i in range(count)])  216 us
    ppermute x24, waiting for transfers between devices, ahead(): lax.ppermute(value, axis, [(i, (i + step) % count) for i in range(count)])  181 us
    ppermute x37, starting transfers between devices, swap(): return lax.ppermute(value, axis, [(i, i ^ bit) for i in range(count)])  155 us
    dot_general x8, matrix products, dot(): return jnp.dot(a, b, preferred_element_type=jnp.float32)  139 us
    ppermute x24, starting transfers between devices, ahead(): lax.ppermute(value, axis, [(i, (i + step) % count) for i in range(count)])  85.5 us
    dot_general x8, matrix products, nt(): lax.dot_general(a, b, (((1,), (1,)), ((), ())), preferred_element_type=jn...  78.4 us
    dot_general x8, matrix products, tn(): lax.dot_general(a, b, (((0,), (0,)), ((), ())), preferred_element_type=jn...  68.3 us
    pallas_call x1, Pallas kernels, attention_backward(): pl.pallas_call(functools.partial(backward_kernel, block=block, span=span,...  65.7 us
  transfers between devices with their start and end apart: 61, of which 22 were waited for; matrix products, arithmetic and copies ran while one was open for 25% of the time, Pallas kernels for 4%

profile of v1, /device:TPU:0, one launch (start us, length us, event | category | flops | bytes accessed | tf_op | source)
XLA Modules:
  0.0 1222.6 jit_solution(2852053163312970289)
XLA Ops:
  27.8 48.3 %collective-permute-done = bf16[136,1632]{1,0:T(8,128)(2,1)S(1)} collective-permute-done((bf16[136,1632]{1,0:T(8,128)(2,1)}, bf16[136,1632]{1,0:T(8,128)(2,1)S(1)}, u32[]{:S(2)}, u32[]{:S(2)}) %collective-permute-start) | collective-permute-done | bytes 443936 | tf_op jit(solution)/shard_map/ppermute | solution.py:343
  86.3 12.4 %collective-permute-done.8 = bf16[136,1088]{1,0:T(8,128)(2,1)S(1)} collective-permute-done((bf16[136,1088]{1,0:T(8,128)(2,1)S(1)}, bf16[136,1088]{1,0:T(8,128)(2,1)S(1)}, u32[]{:S(2)}, u32[]{:S(2)}) %collective-permute-start.8) | collective-permute-done | bytes 295968 | tf_op jit(solution)/shard_map/ppermute | solution.py:348
  98.9 9.1 collective-permute-done.9
  126.2 21.6 %collective-permute-start.2 = (bf16[136,3264]{1,0:T(8,128)(2,1)S(1)}, bf16[136,3264]{1,0:T(8,128)(2,1)S(1)}, u32[]{:S(2)}, u32[]{:S(2)}) collective-permute-start(bf16[136,3264]{1,0:T(8,128)(2,1)S(1)} %pad_maximum_fusion.13), channel_id=1, source_target_pairs={{0,4},{2,6},{4,0},{6,2},{1,5},{3,7},{5,1},{7,3},{8,12},{10,14},{12... | collective-permute-start | bytes 2663432 | tf_op jit(solution)/shard_map/ppermute | solution.py:348
  148.7 38.2 %collective-permute-done.16 = bf16[136,2176]{1,0:T(8,128)(2,1)S(1)} collective-permute-done((bf16[136,2176]{1,0:T(8,128)(2,1)S(1)}, bf16[136,2176]{1,0:T(8,128)(2,1)S(1)}, u32[]{:S(2)}, u32[]{:S(2)}) %collective-permute-start.16) | collective-permute-done | bytes 591904 | tf_op jit(solution)/shard_map/ppermute | solution.py:348
  190.4 30.4 %collective-permute-done.2 = bf16[136,3264]{1,0:T(8,128)(2,1)S(1)} collective-permute-done((bf16[136,3264]{1,0:T(8,128)(2,1)S(1)}, bf16[136,3264]{1,0:T(8,128)(2,1)S(1)}, u32[]{:S(2)}, u32[]{:S(2)}) %collective-permute-start.2) | collective-permute-done | bytes 887840 | tf_op jit(solution)/shard_map/ppermute | solution.py:348
  243.4 50.3 %collective-permute-done.21 = bf16[4,136,2176]{2,1,0:T(8,128)(2,1)} collective-permute-done((bf16[4,136,2176]{2,1,0:T(8,128)(2,1)}, bf16[4,136,2176]{2,1,0:T(8,128)(2,1)}, u32[]{:S(2)}, u32[]{:S(2)}) %collective-permute-start.21) | collective-permute-done | bytes 2367520 | tf_op jit(solution)/shard_map/ppermute | solution.py:343
  304.8 10.6 fusion.2
  337.6 48.7 %attention_forward.1 = (bf16[1280,1088]{1,0:T(8,128)(2,1)}, f32[9,8,1280]{2,1,0:T(8,128)S(1)}) custom-call(s32[3]{0:T(128)S(1)} %pad_add_fusion.pos, bf16[1280,1088]{1,0:T(8,128)(2,1)} %fusion.24.q, bf16[2048,1088]{1,0:T(8,128)(2,1)} %slice.110.k, bf16[2048,1088]{1,0:T(8,128)(2,1)} %slice.112.v, bf16[256,1088]{1,0:T(8,128)(2,1)S(1)} %slice.113.kb, ...), custom_call_target="tpu_custom_call" | custom-call | tf_op jit(solution)/shard_map/attention_forward/pallas_call | solution.py:156
  398.1 33.9 %multiply_convert_fusion.1 = (bf16[1280,2176]{1,0:T(8,128)(2,1)}, f32[1280,2176]{1,0:T(8,128)}, f32[1280,2176]{1,0:T(8,128)}) fusion(f32[2176]{0:T(1024)S(1)} %get-tuple-element.39, bf16[1280,1088]{0,1:T(8,128)(2,1)S(1)} %add_convert_fusion.2, bf16[1088,2176]{1,0:T(8,128)(2,1)S(1)} %bitcast.333), kind=kOutput, calls=%fused_computation.35 | convolution fusion | flops 6244597760 | bytes 35381760 | tf_op jit(solution)/shard_map/dot_general | solution.py:503
  432.0 19.5 %convert_reduce_fusion.2 = (f32[2176]{0:T(1024)S(1)}, bf16[1280,2176]{1,0:T(8,128)(2,1)}) fusion(f32[1280,2176]{1,0:T(8,128)} %get-tuple-element.47, f32[1280,2176]{1,0:T(8,128)} %get-tuple-element.108, bf16[1088,2176]{1,0:T(8,128)(2,1)} %bitcast.326, bf16[256,1088]{0,1:T(8,128)(2,1)S(1)} %bitcast.338, bf16[1024,1088]{0,1:T(8,128)(2,1)S(1)} %bitcast.286), kind=kOutput, calls=%fused_computation.19 | convolution fusion | flops 6110902272 | bytes 35381760 | tf_op jit(solution)/shard_map/dot_general | solution.py:503
  451.5 11.4 convolution_convert_fusion.3
  463.0 10.3 fusion.84
  473.3 8.9 convolution_add_fusion.6
  507.2 34.1 %multiply_convert_fusion = (bf16[1280,2176]{1,0:T(8,128)(2,1)}, f32[1280,2176]{1,0:T(8,128)}, f32[1280,2176]{1,0:T(8,128)}) fusion(f32[2176]{0:T(1024)S(1)} %copy-done.65, bf16[1280,1088]{0,1:T(8,128)(2,1)S(1)} %copy-done.32, bf16[1088,2176]{1,0:T(8,128)(2,1)S(1)} %bitcast.334), kind=kOutput, calls=%fused_computation.22 | convolution fusion | flops 6244597760 | bytes 35381760 | tf_op jit(solution)/shard_map/dot_general | solution.py:503
  541.2 19.8 %convert_reduce_fusion.1 = (f32[2176]{0:T(1024)}, bf16[1280,2176]{1,0:T(8,128)(2,1)}) fusion(f32[1280,2176]{1,0:T(8,128)} %get-tuple-element.45, f32[1280,2176]{1,0:T(8,128)} %get-tuple-element.109, bf16[1088,2176]{1,0:T(8,128)(2,1)} %bitcast.324, bf16[256,1088]{0,1:T(8,128)(2,1)S(1)} %bitcast.340, bf16[1024,1088]{0,1:T(8,128)(2,1)S(1)} %bitcast.288), kind=kOutput, calls=%fused_computation.18 | convolution fusion | flops 6110902272 | bytes 35381760 | tf_op jit(solution)/shard_map/dot_general | solution.py:503
  561.1 11.6 convolution_convert_fusion.2
  572.7 12.7 %multiply_reduce_fusion = (f32[1088]{0:T(1024)}, f32[1280]{0:T(1024)S(1)}, f32[1088]{0:T(1024)}, f32[1280,1088]{0,1:T(8,128)S(1)}) fusion(f32[1280,1088]{0,1:T(8,128)S(1)} %bitcast.268, f32[1280]{0:T(1024)S(1)} %copy-done.57, f32[1280]{0:T(1024)S(1)} %copy-done.47, f32[1088]{0:T(1024)S(1)} %copy-done.63, f32[1280,1088]{0,1:T(8,128)} %fusion.84, ...), kind=kOutput, calls=%fused_computation.88 | convolution fusion | flops 6073299968 | bytes 27045632 | tf_op jit(solution)/shard_map/dot_general | solution.py:17
  606.7 65.7 %attention_backward.1 = (bf16[1280,1088]{1,0:T(8,128)(2,1)}, bf16[2048,1088]{1,0:T(8,128)(2,1)}, bf16[2048,1088]{1,0:T(8,128)(2,1)}, bf16[256,1088]{1,0:T(8,128)(2,1)}, bf16[256,1088]{1,0:T(8,128)(2,1)}) custom-call(s32[3]{0:T(128)} %copy-done.3, bf16[1280,1088]{1,0:T(8,128)(2,1)} %fusion.24.q, bf16[2048,1088]{1,0:T(8,128)(2,1)} %slice.110.k, ...), custom_call_target="tpu_custom_call" | custom-call | tf_op jit(solution)/shard_map/attention_backward/pallas_call | solution.py:308
  687.0 10.7 fusion.45
  699.3 9.4 convolution_convert_fusion
  719.7 10.2 convolution_convert_fusion.8
  744.4 12.4 %convolution_add_fusion = f32[2304,1088]{0,1:T(8,128)} fusion(f32[2304,1088]{0,1:T(8,128)} %fusion.45, bf16[2304,1088]{1,0:T(8,128)(2,1)S(1)} %bitcast.281, bf16[1088,3264]{1,0:T(8,128)(2,1)} %bitcast.294), kind=kOutput, calls=%fused_computation.2 | convolution fusion | flops 5457199104 | bytes 27574272 | tf_op jit(solution)/shard_map/dot_general | solution.py:17
  763.0 117.5 %collective-permute-start.23 = (bf16[1024,1088]{0,1:T(8,128)(2,1)}, bf16[1024,1088]{0,1:T(8,128)(2,1)}, u32[]{:S(2)}, u32[]{:S(2)}) collective-permute-start(bf16[1024,1088]{0,1:T(8,128)(2,1)} %dynamic-slice_convert_fusion), channel_id=1, source_target_pairs={{0,1},{1,0},{2,3},{3,2},{4,5},{5,4},{6,7},{7,6},{8,9},{9,8},{10,11... | collective-permute-start | bytes 6684680 | tf_op jit(solution)/shard_map/ppermute | solution.py:343
  880.5 11.0 fusion.25
  897.3 47.0 %collective-permute-done.39 = bf16[4,136,544]{2,1,0:T(8,128)(2,1)S(1)} collective-permute-done((bf16[4,136,544]{2,1,0:T(8,128)(2,1)S(1)}, bf16[4,136,544]{2,1,0:T(8,128)(2,1)S(1)}, u32[]{:S(2)}, u32[]{:S(2)}) %collective-permute-start.39) | collective-permute-done | bytes 591904 | tf_op jit(solution)/shard_map/ppermute | solution.py:343
  945.4 25.3 %collective-permute-start.40 = (bf16[136,544]{1,0:T(8,128)(2,1)}, bf16[136,544]{1,0:T(8,128)(2,1)}, u32[]{:S(2)}, u32[]{:S(2)}) collective-permute-start(bf16[136,544]{1,0:T(8,128)(2,1)} %get-tuple-element.91), channel_id=1, source_target_pairs={{0,2},{2,4},{4,6},{6,0},{1,3},{3,5},{5,7},{7,1},{8,10},{10,12},{12... | collective-permute-start | bytes 443912 | tf_op jit(solution)/shard_map/ppermute | solution.py:348
  1065.5 17.1 %collective-permute-done.33 = bf16[136,1632]{1,0:T(8,128)(2,1)S(1)} collective-permute-done((bf16[136,1632]{1,0:T(8,128)(2,1)S(1)}, bf16[136,1632]{1,0:T(8,128)(2,1)S(1)}, u32[]{:S(2)}, u32[]{:S(2)}) %collective-permute-start.33) | collective-permute-done | bytes 443936 | tf_op jit(solution)/shard_map/ppermute | solution.py:348
  1112.7 31.7 %collective-permute-done.55 = bf16[4,136,2176]{2,1,0:T(8,128)(2,1)S(1)} collective-permute-done((bf16[4,136,2176]{2,1,0:T(8,128)(2,1)S(1)}, bf16[4,136,2176]{2,1,0:T(8,128)(2,1)S(1)}, u32[]{:S(2)}, u32[]{:S(2)}) %collective-permute-start.55) | collective-permute-done | bytes 2367520 | tf_op jit(solution)/shard_map/ppermute | solution.py:343
  1157.5 10.3 collective-permute-done.56
  1167.8 33.7 %collective-permute-done.57 = bf16[136,2176]{1,0:T(8,128)(2,1)S(1)} collective-permute-done((bf16[136,2176]{1,0:T(8,128)(2,1)S(1)}, bf16[136,2176]{1,0:T(8,128)(2,1)S(1)}, u32[]{:S(2)}, u32[]{:S(2)}) %collective-permute-start.57) | collective-permute-done | bytes 591904 | tf_op jit(solution)/shard_map/ppermute | solution.py:348
  1203.7 13.5 %collective-permute-done.59 = bf16[136,2176]{1,0:T(8,128)(2,1)S(1)} collective-permute-done((bf16[136,2176]{1,0:T(8,128)(2,1)S(1)}, bf16[136,2176]{1,0:T(8,128)(2,1)S(1)}, u32[]{:S(2)}, u32[]{:S(2)}) %collective-permute-start.59) | collective-permute-done | bytes 591904 | tf_op jit(solution)/shard_map/ppermute | solution.py:343
  (476 shorter events, 371.9 us)
Async XLA Ops:
  4.6 103.5 %collective-permute-start.11 = (bf16[136,2176]{1,0:T(8,128)(2,1)}, bf16[136,2176]{1,0:T(8,128)(2,1)}, u32[]{:S(2)}, u32[]{:S(2)}) collective-permute-start(bf16[136,2176]{1,0:T(8,128)(2,1)} %get-tuple-element.85), channel_id=1, source_target_pairs={{0,2},{2,4},{4,6},{6,0},{1,3},{3,5},{5,7},{7,1},{8,10},{10,12},{12... | collective-permute-start | bytes 1775624 | tf_op jit(solution)/shard_map/ppermute | solution.py:348
  7.6 105.1 %collective-permute-start.12 = (bf16[136,2176]{1,0:T(8,128)(2,1)}, bf16[136,2176]{1,0:T(8,128)(2,1)}, u32[]{:S(2)}, u32[]{:S(2)}) collective-permute-start(bf16[136,2176]{1,0:T(8,128)(2,1)} %get-tuple-element.85), channel_id=1, source_target_pairs={{0,4},{2,6},{4,0},{6,2},{1,5},{3,7},{5,1},{7,3},{8,12},{10,14},{12... | collective-permute-start | bytes 1775624 | tf_op jit(solution)/shard_map/ppermute | solution.py:348
  10.2 105.7 %collective-permute-start.13 = (bf16[136,2176]{1,0:T(8,128)(2,1)}, bf16[136,2176]{1,0:T(8,128)(2,1)S(1)}, u32[]{:S(2)}, u32[]{:S(2)}) collective-permute-start(bf16[136,2176]{1,0:T(8,128)(2,1)} %get-tuple-element.85), channel_id=1, source_target_pairs={{0,6},{2,0},{4,2},{6,4},{1,7},{3,1},{5,3},{7,5},{8,14},{10,8},{12,... | collective-permute-start | bytes 1775624 | tf_op jit(solution)/shard_map/ppermute | solution.py:348
  14.6 210.2 %collective-permute-start.5 = (bf16[1024,1088]{0,1:T(8,128)(2,1)}, bf16[1024,1088]{0,1:T(8,128)(2,1)}, u32[]{:S(2)}, u32[]{:S(2)}) collective-permute-start(bf16[1024,1088]{0,1:T(8,128)(2,1)} %bitcast.256), channel_id=1, source_target_pairs={{0,1},{1,0},{2,3},{3,2},{4,5},{5,4},{6,7},{7,6},{8,9},{9,8},{10,11... | collective-permute-start | bytes 6684680 | tf_op jit(solution)/shard_map/ppermute | solution.py:343
  25.0 51.1 %collective-permute-start = (bf16[136,1632]{1,0:T(8,128)(2,1)}, bf16[136,1632]{1,0:T(8,128)(2,1)S(1)}, u32[]{:S(2)}, u32[]{:S(2)}) collective-permute-start(bf16[136,1632]{1,0:T(8,128)(2,1)} %dynamic-slice_bitcast_fusion.19), channel_id=1, source_target_pairs={{0,1},{1,0},{2,3},{3,2},{4,5},{5,4},{6,7},{7,6},{8,9},{9,8},{10,11... | collective-permute-start | bytes 1331720 | tf_op jit(solution)/shard_map/ppermute | solution.py:343
  108.1 78.9 %collective-permute-start.16 = (bf16[136,2176]{1,0:T(8,128)(2,1)S(1)}, bf16[136,2176]{1,0:T(8,128)(2,1)S(1)}, u32[]{:S(2)}, u32[]{:S(2)}) collective-permute-start(bf16[136,2176]{1,0:T(8,128)(2,1)S(1)} %copy-done.40), channel_id=1, source_target_pairs={{0,4},{2,6},{4,0},{6,2},{1,5},{3,7},{5,1},{7,3},{8,12},{10,14},{12... | collective-permute-start | bytes 1775624 | tf_op jit(solution)/shard_map/ppermute | solution.py:348
  112.7 75.3 %collective-permute-start.17 = (bf16[136,2176]{1,0:T(8,128)(2,1)S(1)}, bf16[136,2176]{1,0:T(8,128)(2,1)S(1)}, u32[]{:S(2)}, u32[]{:S(2)}) collective-permute-start(bf16[136,2176]{1,0:T(8,128)(2,1)S(1)} %copy-done.40), channel_id=1, source_target_pairs={{0,6},{2,0},{4,2},{6,4},{1,7},{3,1},{5,3},{7,5},{8,14},{10,8},{12,... | collective-permute-start | bytes 1775624 | tf_op jit(solution)/shard_map/ppermute | solution.py:348
  115.8 73.0 %collective-permute-start.1 = (bf16[136,3264]{1,0:T(8,128)(2,1)S(1)}, bf16[136,3264]{1,0:T(8,128)(2,1)S(1)}, u32[]{:S(2)}, u32[]{:S(2)}) collective-permute-start(bf16[136,3264]{1,0:T(8,128)(2,1)S(1)} %pad_maximum_fusion.13), channel_id=1, source_target_pairs={{0,2},{2,4},{4,6},{6,0},{1,3},{3,5},{5,7},{7,1},{8,10},{10,12},{12... | collective-permute-start | bytes 2663432 | tf_op jit(solution)/shard_map/ppermute | solution.py:348
  126.2 94.5 %collective-permute-start.2 = (bf16[136,3264]{1,0:T(8,128)(2,1)S(1)}, bf16[136,3264]{1,0:T(8,128)(2,1)S(1)}, u32[]{:S(2)}, u32[]{:S(2)}) collective-permute-start(bf16[136,3264]{1,0:T(8,128)(2,1)S(1)} %pad_maximum_fusion.13), channel_id=1, source_target_pairs={{0,4},{2,6},{4,0},{6,2},{1,5},{3,7},{5,1},{7,3},{8,12},{10,14},{12... | collective-permute-start | bytes 2663432 | tf_op jit(solution)/shard_map/ppermute | solution.py:348
  188.8 54.5 %collective-permute-start.19 = (bf16[4,136,2176]{2,1,0:T(8,128)(2,1)}, bf16[4,136,2176]{2,1,0:T(8,128)(2,1)}, u32[]{:S(2)}, u32[]{:S(2)}) collective-permute-start(bf16[4,136,2176]{2,1,0:T(8,128)(2,1)} %bitcast_dynamic-update-slice_fusion.7), channel_id=1, source_target_pairs={{0,1},{1,0},{2,3},{3,2},{4,5},{5,4},{6,7},{7,6},{8,9},{9,8},{10,11... | collective-permute-start | bytes 7102472 | tf_op jit(solution)/shard_map/ppermute | solution.py:343
  220.8 73.0 %collective-permute-start.14 = (bf16[4,136,2176]{2,1,0:T(8,128)(2,1)}, bf16[4,136,2176]{2,1,0:T(8,128)(2,1)S(1)}, u32[]{:S(2)}, u32[]{:S(2)}) collective-permute-start(bf16[4,136,2176]{2,1,0:T(8,128)(2,1)} %bitcast_dynamic-update-slice_fusion.7), channel_id=1, source_target_pairs={{0,8},{8,0},{16,24},{24,16},{1,9},{9,1},{17,25},{25,17},{2,10},{10... | collective-permute-start | bytes 7102472 | tf_op jit(solution)/shard_map/ppermute | solution.py:343
  220.9 72.9 %collective-permute-start.21 = (bf16[4,136,2176]{2,1,0:T(8,128)(2,1)}, bf16[4,136,2176]{2,1,0:T(8,128)(2,1)}, u32[]{:S(2)}, u32[]{:S(2)}) collective-permute-start(bf16[4,136,2176]{2,1,0:T(8,128)(2,1)} %bitcast_dynamic-update-slice_fusion.4), channel_id=1, source_target_pairs={{0,1},{1,0},{2,3},{3,2},{4,5},{5,4},{6,7},{7,6},{8,9},{9,8},{10,11... | collective-permute-start | bytes 7102472 | tf_op jit(solution)/shard_map/ppermute | solution.py:343
  224.8 73.8 %collective-permute-start.4 = (bf16[4,136,3264]{2,1,0:T(8,128)(2,1)S(1)}, bf16[4,136,3264]{2,1,0:T(8,128)(2,1)}, u32[]{:S(2)}, u32[]{:S(2)}) collective-permute-start(bf16[4,136,3264]{2,1,0:T(8,128)(2,1)S(1)} %bitcast_dynamic-update-slice_fusion), channel_id=1, source_target_pairs={{0,8},{8,0},{16,24},{24,16},{1,9},{9,1},{17,25},{25,17},{2,10},{10... | collective-permute-start | bytes 10653704 | tf_op jit(solution)/shard_map/ppermute | solution.py:343
  243.4 252.2 %collective-permute-start.20 = (bf16[4,136,2176]{2,1,0:T(8,128)(2,1)}, bf16[4,136,2176]{2,1,0:T(8,128)(2,1)}, u32[]{:S(2)}, u32[]{:S(2)}) collective-permute-start(bf16[4,136,2176]{2,1,0:T(8,128)(2,1)} %collective-permute-done.19), channel_id=1, source_target_pairs={{0,8},{8,0},{16,24},{24,16},{1,9},{9,1},{17,25},{25,17},{2,10},{10... | collective-permute-start | bytes 7102472 | tf_op jit(solution)/shard_map/ppermute | solution.py:343
  293.7 205.5 %collective-permute-start.22 = (bf16[4,136,2176]{2,1,0:T(8,128)(2,1)}, bf16[4,136,2176]{2,1,0:T(8,128)(2,1)}, u32[]{:S(2)}, u32[]{:S(2)}) collective-permute-start(bf16[4,136,2176]{2,1,0:T(8,128)(2,1)} %collective-permute-done.21), channel_id=1, source_target_pairs={{0,8},{8,0},{16,24},{24,16},{1,9},{9,1},{17,25},{25,17},{2,10},{10... | collective-permute-start | bytes 7102472 | tf_op jit(solution)/shard_map/ppermute | solution.py:343
  716.1 176.3 %collective-permute-start.38 = (bf16[4,136,544]{2,1,0:T(8,128)(2,1)S(1)}, bf16[4,136,544]{2,1,0:T(8,128)(2,1)}, u32[]{:S(2)}, u32[]{:S(2)}) collective-permute-start(bf16[4,136,544]{2,1,0:T(8,128)(2,1)S(1)} %dynamic-slice_bitcast_fusion.6), channel_id=1, source_target_pairs={{0,8},{8,0},{16,24},{24,16},{1,9},{9,1},{17,25},{25,17},{2,10},{10... | collective-permute-start | bytes 1775624 | tf_op jit(solution)/shard_map/ppermute | solution.py:343
  718.7 178.6 %collective-permute-start.37 = (bf16[4,136,544]{2,1,0:T(8,128)(2,1)S(1)}, bf16[4,136,544]{2,1,0:T(8,128)(2,1)S(1)}, u32[]{:S(2)}, u32[]{:S(2)}) collective-permute-start(bf16[4,136,544]{2,1,0:T(8,128)(2,1)S(1)} %dynamic-slice_bitcast_fusion.7), channel_id=1, source_target_pairs={{0,8},{8,0},{16,24},{24,16},{1,9},{9,1},{17,25},{25,17},{2,10},{10... | collective-permute-start | bytes 1775624 | tf_op jit(solution)/shard_map/ppermute | solution.py:343
  743.9 251.0 %collective-permute-start.30 = (bf16[4,136,1632]{2,1,0:T(8,128)(2,1)}, bf16[4,136,1632]{2,1,0:T(8,128)(2,1)}, u32[]{:S(2)}, u32[]{:S(2)}) collective-permute-start(bf16[4,136,1632]{2,1,0:T(8,128)(2,1)} %dynamic-slice_bitcast_fusion.4), channel_id=1, source_target_pairs={{0,8},{8,0},{16,24},{24,16},{1,9},{9,1},{17,25},{25,17},{2,10},{10... | collective-permute-start | bytes 5326856 | tf_op jit(solution)/shard_map/ppermute | solution.py:343
  763.0 236.6 %collective-permute-start.23 = (bf16[1024,1088]{0,1:T(8,128)(2,1)}, bf16[1024,1088]{0,1:T(8,128)(2,1)}, u32[]{:S(2)}, u32[]{:S(2)}) collective-permute-start(bf16[1024,1088]{0,1:T(8,128)(2,1)} %dynamic-slice_convert_fusion), channel_id=1, source_target_pairs={{0,1},{1,0},{2,3},{3,2},{4,5},{5,4},{6,7},{7,6},{8,9},{9,8},{10,11... | collective-permute-start | bytes 6684680 | tf_op jit(solution)/shard_map/ppermute | solution.py:343
  893.7 50.5 %collective-permute-start.39 = (bf16[4,136,544]{2,1,0:T(8,128)(2,1)S(1)}, bf16[4,136,544]{2,1,0:T(8,128)(2,1)S(1)}, u32[]{:S(2)}, u32[]{:S(2)}) collective-permute-start(bf16[4,136,544]{2,1,0:T(8,128)(2,1)S(1)} %fusion.53), channel_id=1, source_target_pairs={{0,1},{1,0},{2,3},{3,2},{4,5},{5,4},{6,7},{7,6},{8,9},{9,8},{10,11... | collective-permute-start | bytes 1775624 | tf_op jit(solution)/shard_map/ppermute | solution.py:343
  976.5 51.9 %collective-permute-start.46 = (bf16[4,136,2176]{2,1,0:T(8,128)(2,1)}, bf16[4,136,2176]{2,1,0:T(8,128)(2,1)}, u32[]{:S(2)}, u32[]{:S(2)}) collective-permute-start(bf16[4,136,2176]{2,1,0:T(8,128)(2,1)} %dynamic-slice_bitcast_fusion.2), channel_id=1, source_target_pairs={{0,8},{8,0},{16,24},{24,16},{1,9},{9,1},{17,25},{25,17},{2,10},{10... | collective-permute-start | bytes 7102472 | tf_op jit(solution)/shard_map/ppermute | solution.py:343
  983.0 67.4 %collective-permute-start.54 = (bf16[4,136,2176]{2,1,0:T(8,128)(2,1)}, bf16[4,136,2176]{2,1,0:T(8,128)(2,1)}, u32[]{:S(2)}, u32[]{:S(2)}) collective-permute-start(bf16[4,136,2176]{2,1,0:T(8,128)(2,1)} %dynamic-slice_bitcast_fusion), channel_id=1, source_target_pairs={{0,8},{8,0},{16,24},{24,16},{1,9},{9,1},{17,25},{25,17},{2,10},{10... | collective-permute-start | bytes 7102472 | tf_op jit(solution)/shard_map/ppermute | solution.py:343
  993.5 48.8 %collective-permute-start.29 = (bf16[4,136,1632]{2,1,0:T(8,128)(2,1)}, bf16[4,136,1632]{2,1,0:T(8,128)(2,1)}, u32[]{:S(2)}, u32[]{:S(2)}) collective-permute-start(bf16[4,136,1632]{2,1,0:T(8,128)(2,1)} %dynamic-slice_bitcast_fusion.5), channel_id=1, source_target_pairs={{0,8},{8,0},{16,24},{24,16},{1,9},{9,1},{17,25},{25,17},{2,10},{10... | collective-permute-start | bytes 5326856 | tf_op jit(solution)/shard_map/ppermute | solution.py:343
  998.1 49.3 %collective-permute-start.31 = (bf16[4,136,1632]{2,1,0:T(8,128)(2,1)}, bf16[4,136,1632]{2,1,0:T(8,128)(2,1)}, u32[]{:S(2)}, u32[]{:S(2)}) collective-permute-start(bf16[4,136,1632]{2,1,0:T(8,128)(2,1)} %fusion.39), channel_id=1, source_target_pairs={{0,1},{1,0},{2,3},{3,2},{4,5},{5,4},{6,7},{7,6},{8,9},{9,8},{10,11... | collective-permute-start | bytes 5326856 | tf_op jit(solution)/shard_map/ppermute | solution.py:343
  1028.2 77.3 %collective-permute-start.45 = (bf16[4,136,2176]{2,1,0:T(8,128)(2,1)}, bf16[4,136,2176]{2,1,0:T(8,128)(2,1)S(1)}, u32[]{:S(2)}, u32[]{:S(2)}) collective-permute-start(bf16[4,136,2176]{2,1,0:T(8,128)(2,1)} %dynamic-slice_bitcast_fusion.3), channel_id=1, source_target_pairs={{0,8},{8,0},{16,24},{24,16},{1,9},{9,1},{17,25},{25,17},{2,10},{10... | collective-permute-start | bytes 7102472 | tf_op jit(solution)/shard_map/ppermute | solution.py:343
  1040.9 64.6 %collective-permute-start.47 = (bf16[4,136,2176]{2,1,0:T(8,128)(2,1)}, bf16[4,136,2176]{2,1,0:T(8,128)(2,1)S(1)}, u32[]{:S(2)}, u32[]{:S(2)}) collective-permute-start(bf16[4,136,2176]{2,1,0:T(8,128)(2,1)} %fusion.36), channel_id=1, source_target_pairs={{0,1},{1,0},{2,3},{3,2},{4,5},{5,4},{6,7},{7,6},{8,9},{9,8},{10,11... | collective-permute-start | bytes 7102472 | tf_op jit(solution)/shard_map/ppermute | solution.py:343
  1065.5 46.3 %collective-permute-start.53 = (bf16[4,136,2176]{2,1,0:T(8,128)(2,1)S(1)}, bf16[4,136,2176]{2,1,0:T(8,128)(2,1)S(1)}, u32[]{:S(2)}, u32[]{:S(2)}) collective-permute-start(bf16[4,136,2176]{2,1,0:T(8,128)(2,1)S(1)} %copy-done.37), channel_id=1, source_target_pairs={{0,8},{8,0},{16,24},{24,16},{1,9},{9,1},{17,25},{25,17},{2,10},{10... | collective-permute-start | bytes 7102472 | tf_op jit(solution)/shard_map/ppermute | solution.py:343
  1082.7 61.8 %collective-permute-start.55 = (bf16[4,136,2176]{2,1,0:T(8,128)(2,1)S(1)}, bf16[4,136,2176]{2,1,0:T(8,128)(2,1)S(1)}, u32[]{:S(2)}, u32[]{:S(2)}) collective-permute-start(bf16[4,136,2176]{2,1,0:T(8,128)(2,1)S(1)} %fusion.33), channel_id=1, source_target_pairs={{0,1},{1,0},{2,3},{3,2},{4,5},{5,4},{6,7},{7,6},{8,9},{9,8},{10,11... | collective-permute-start | bytes 7102472 | tf_op jit(solution)/shard_map/ppermute | solution.py:343
  1106.6 49.0 %collective-permute-start.48 = (bf16[136,2176]{1,0:T(8,128)(2,1)S(1)}, bf16[136,2176]{1,0:T(8,128)(2,1)S(1)}, u32[]{:S(2)}, u32[]{:S(2)}) collective-permute-start(bf16[136,2176]{1,0:T(8,128)(2,1)S(1)} %get-tuple-element.73), channel_id=1, source_target_pairs={{0,2},{2,4},{4,6},{6,0},{1,3},{3,5},{5,7},{7,1},{8,10},{10,12},{12... | collective-permute-start | bytes 1775624 | tf_op jit(solution)/shard_map/ppermute | solution.py:348
  1150.6 50.9 %collective-permute-start.57 = (bf16[136,2176]{1,0:T(8,128)(2,1)S(1)}, bf16[136,2176]{1,0:T(8,128)(2,1)S(1)}, u32[]{:S(2)}, u32[]{:S(2)}) collective-permute-start(bf16[136,2176]{1,0:T(8,128)(2,1)S(1)} %get-tuple-element.72), channel_id=1, source_target_pairs={{0,4},{2,6},{4,0},{6,2},{1,5},{3,7},{5,1},{7,3},{8,12},{10,14},{12... | collective-permute-start | bytes 1775624 | tf_op jit(solution)/shard_map/ppermute | solution.py:348
  1155.6 45.9 %collective-permute-start.58 = (bf16[136,2176]{1,0:T(8,128)(2,1)S(1)}, bf16[136,2176]{1,0:T(8,128)(2,1)S(1)}, u32[]{:S(2)}, u32[]{:S(2)}) collective-permute-start(bf16[136,2176]{1,0:T(8,128)(2,1)S(1)} %get-tuple-element.71), channel_id=1, source_target_pairs={{0,6},{2,0},{4,2},{6,4},{1,7},{3,1},{5,3},{7,5},{8,14},{10,8},{12,... | collective-permute-start | bytes 1775624 | tf_op jit(solution)/shard_map/ppermute | solution.py:348
  1155.9 47.5 %collective-permute-start.51 = (bf16[136,2176]{1,0:T(8,128)(2,1)S(1)}, bf16[136,2176]{1,0:T(8,128)(2,1)S(1)}, u32[]{:S(2)}, u32[]{:S(2)}) collective-permute-start(bf16[136,2176]{1,0:T(8,128)(2,1)S(1)} %fusion.61), channel_id=1, source_target_pairs={{0,16},{8,24},{16,0},{24,8},{1,17},{9,25},{17,1},{25,9},{2,18},{10... | collective-permute-start | bytes 1775624 | tf_op jit(solution)/shard_map/ppermute | solution.py:343
  (133 other events, 2723.8 us)

commit v2 on v1

v2 whole, which is shorter than its diff:
```python
import functools
import jax
import jax.numpy as jnp
from jax import lax
from jax.sharding import PartitionSpec as P
from jax.experimental import pallas as pl
from jax.experimental.pallas import tpu as pltpu

HEAD_DIM = 64
LOG2E = 1.4426950408889634
NEG = -1e30
BK = 512


def nt(a, b):
    return lax.dot_general(a, b, (((1,), (1,)), ((), ())), preferred_element_type=jnp.float32)


def nn(a, b):
    return jnp.dot(a, b, preferred_element_type=jnp.float32)


def tn(a, b):
    return lax.dot_general(a, b, (((0,), (0,)), ((), ())), preferred_element_type=jnp.float32)


def halves(pair, total):
    lane = lax.broadcasted_iota(jnp.int32, (1, 128), 1)
    left = jnp.minimum(total - pair * 128, 128)
    return lane < 64, jnp.logical_and(lane >= 64, lane < left), lane < left


def norm_bounds(ref, valid, spread):
    part = jnp.where(valid, ref[...], jnp.zeros((), jnp.bfloat16))
    return jnp.max(nn(part * part, spread), axis=0, keepdims=True)


def query_rows(pos, number, size, span, is_branch):
    if is_branch:
        return pl.ds(span, size)
    return pl.ds(pl.multiple_of(pos[number], size), size)


def forward_kernel(pos, q, k, v, *rest, block, branch, width):
    o, lse, va, vc, vab, vcb, tops, accs = rest[-8:]
    pair = pl.program_id(0)
    scale = HEAD_DIM ** (-0.5) * LOG2E
    low, high, valid = halves(pair, width)
    zero = jnp.zeros((), jnp.bfloat16)
    one = jnp.ones((), jnp.bfloat16)
    span = k.shape[0] - branch
    for part, first, second in ((slice(0, span), va, vc), (slice(span, None), vab, vcb)):
        whole = v[part, :]
        first[...] = jnp.where(low, whole, one)
        second[...] = jnp.where(low, one, jnp.where(high, whole, zero))
    spread = (
        (lax.broadcasted_iota(jnp.int32, (128, 128), 0) < 64)
        == (lax.broadcasted_iota(jnp.int32, (128, 128), 1) < 64)
    ).astype(jnp.bfloat16)
    bound = jnp.max(norm_bounds(k, valid, spread) * norm_bounds(q, valid, spread)) * (scale * scale)
    plain = bound < 90.0 * 90.0
    rows = o.shape[0]
    blocks = [(start, block, False) for start in range(0, rows - branch, block)]
    blocks.append((rows - branch, branch, True))

    def finish(start, size, acc_a, acc_b, top):
        total = pltpu.roll(jnp.where(low, acc_b, acc_a), 64, 1)
        o[start : start + size, :] = (jnp.where(low, acc_a, acc_b) / total).astype(o.dtype)
        turned = (top + jnp.log2(total)).T
        lse[0, 0:1, start : start + size] = turned[0:1, :]
        lse[0, 1:2, start : start + size] = turned[64:65, :]

    def setup(number, start, size, is_branch):
        at = pos[number]
        query = q[query_rows(pos, number, size, span, is_branch), :]
        queries = (jnp.where(low, query, zero), jnp.where(high, query, zero))
        row = lax.broadcasted_iota(jnp.int32, (size, BK), 0)
        column = lax.broadcasted_iota(jnp.int32, (size, BK), 1)
        triangle = lax.broadcasted_iota(jnp.int32, (size, size), 1) <= lax.broadcasted_iota(
            jnp.int32, (size, size), 0
        )
        whole_blocks = at // BK

        def allowed(index):
            if is_branch:
                return column + index * BK < at
            return column + index * BK <= row + at

        end = (at + BK - 1) // BK if is_branch else whole_blocks + 1
        return queries, triangle, whole_blocks, allowed, end

    def read(index):
        rows_at = pl.ds(pl.multiple_of(index * BK, BK), BK)
        return jnp.where(valid, k[rows_at, :], zero), va[rows_at, :], vc[rows_at, :]

    def own():
        return jnp.where(valid, k[span:, :], zero), vab[...], vcb[...]

    @pl.when(plain)
    def _():
        for number, (start, size, is_branch) in enumerate(blocks):
            queries, triangle, whole_blocks, allowed, end = setup(number, start, size, is_branch)

            def step(key, first, second, carry, mask):
                out = []
                for query_h, value_h, acc in zip(queries, (first, second), carry):
                    probs = jnp.exp2(nt(query_h, key) * scale)
                    if mask is not None:
                        probs = jnp.where(mask, probs, 0.0)
                    out.append(acc + nn(probs.astype(jnp.bfloat16), value_h))
                return tuple(out)

            carry = (jnp.zeros((size, 128), jnp.float32),) * 2
            carry = lax.fori_loop(0, whole_blocks, lambda i, c: step(*read(i), c, None), carry)
            if is_branch:
                carry = lax.fori_loop(
                    whole_blocks, end, lambda i, c: step(*read(i), c, allowed(i)), carry
                )
                carry = step(*own(), carry, triangle)
            else:
                carry = step(*read(whole_blocks), carry, allowed(whole_blocks))
            finish(start, size, *carry, 0.0)

    @pl.when(jnp.logical_not(plain))
    def _():
        for number, (start, size, is_branch) in enumerate(blocks):
            queries, triangle, whole_blocks, allowed, end = setup(number, start, size, is_branch)

            def step(key, first, second, mask):
                for head, value_h in enumerate((first, second)):
                    top = tops[head, 0:size, :]
                    scores = jnp.where(mask, nt(queries[head], key), NEG)
                    new_top = jnp.maximum(top, jnp.max(scores, axis=1, keepdims=True))
                    probs = jnp.exp2((scores - new_top[:, 0:1]) * scale).astype(jnp.bfloat16)
                    fade = jnp.exp2((top - new_top) * scale)
                    accs[head, 0:size, :] = accs[head, 0:size, :] * fade + nn(probs, value_h)
                    tops[head, 0:size, :] = new_top

            accs[:, 0:size, :] = jnp.zeros((2, size, 128), jnp.float32)
            tops[:, 0:size, :] = jnp.full((2, size, 128), NEG, jnp.float32)

            @pl.loop(0, end)
            def _(index):
                step(*read(index), allowed(index))

            if is_branch:
                step(*own(), triangle)
            top = jnp.where(low, tops[0, 0:size, :], tops[1, 0:size, :]) * scale
            finish(start, size, accs[0, 0:size, :], accs[1, 0:size, :], top)


def busy(microseconds):
    return pl.CostEstimate(
        flops=int(microseconds * 1.0e9), bytes_accessed=int(microseconds * 1.0e6), transcendentals=0
    )


def attention_forward(pos, q, k, v, block, branch, after=()):
    total, width = q.shape
    span = total - branch
    rows = block * (pos.shape[0] - 1) + branch
    pairs = pl.cdiv(width, 128)

    def col(n):
        return pl.BlockSpec((n, 128), lambda p, pos: (0, p))

    return pl.pallas_call(
        functools.partial(forward_kernel, block=block, branch=branch, width=width),
        grid_spec=pltpu.PrefetchScalarGridSpec(
            num_scalar_prefetch=1,
            grid=(pairs,),
            in_specs=[col(total)] * 3 + [pl.BlockSpec(memory_space=pl.ANY)] * len(after),
            out_specs=[col(rows), pl.BlockSpec((1, 8, rows), lambda p, pos: (p, 0, 0))],
            scratch_shapes=[
                pltpu.VMEM((span, 128), jnp.bfloat16),
                pltpu.VMEM((span, 128), jnp.bfloat16),
                pltpu.VMEM((branch, 128), jnp.bfloat16),
                pltpu.VMEM((branch, 128), jnp.bfloat16),
                pltpu.VMEM((2, max(block, branch), 128), jnp.float32),
                pltpu.VMEM((2, max(block, branch), 128), jnp.float32),
            ],
        ),
        out_shape=[
            jax.ShapeDtypeStruct((rows, width), jnp.bfloat16),
            jax.ShapeDtypeStruct((pairs, 8, rows), jnp.float32),
        ],
        compiler_params=pltpu.CompilerParams(
            dimension_semantics=("arbitrary",), vmem_limit_bytes=32 * 2**20
        ),
        cost_estimate=busy(7 * pairs),
        name="attention_forward",
    )(pos, q, k, v, *after)


def backward_kernel(pos, q, k, v, o, do, lse, *rest, block, branch, width):
    dq, dk, dv = rest[-13:-10]
    kta, ktc, kam, vm, ktab, ktcb, kbm, vbm, dks, dvs = rest[-10:]
    pair = pl.program_id(0)
    scale = HEAD_DIM ** (-0.5)
    low, high, valid = halves(pair, width)
    zero = jnp.zeros((), jnp.bfloat16)
    span = k.shape[0] - branch
    prompt_part, branch_part = slice(0, span), slice(span, None)
    for part, whole_ref, turn_a, turn_b in ((prompt_part, kam, kta, ktc), (branch_part, kbm, ktab, ktcb)):
        whole = jnp.where(valid, k[part, :], zero)
        whole_ref[...] = whole
        turned = whole.T
        turn_a[...] = turned[0:64, :]
        turn_b[...] = turned[64:128, :]
    vm[...] = jnp.where(valid, v[prompt_part, :], zero)
    vbm[...] = jnp.where(valid, v[branch_part, :], zero)
    dq[...] = jnp.zeros_like(dq)
    dks[...] = jnp.zeros_like(dks)
    dvs[...] = jnp.zeros_like(dvs)
    rows = o.shape[0]
    blocks = [(start, block, False) for start in range(0, rows - branch, block)]
    blocks.append((rows - branch, branch, True))
    ones_a = jnp.broadcast_to(low, (8, 128)).astype(jnp.bfloat16)
    ones_b = jnp.broadcast_to(high, (8, 128)).astype(jnp.bfloat16)
    for number, (start, size, is_branch) in enumerate(blocks):
        at = pos[number]
        here = slice(start, start + size)
        query_at = query_rows(pos, number, size, span, is_branch)
        query = q[query_at, :]
        grad = do[here, :]
        queries = (jnp.where(low, query, zero), jnp.where(high, query, zero))
        grads = (jnp.where(low, grad, zero), jnp.where(high, grad, zero))
        product = jnp.where(valid, grad.astype(jnp.float32) * o[here, :].astype(jnp.float32), 0.0)
        upper = product.astype(jnp.bfloat16)
        lower = (product - upper.astype(jnp.float32)).astype(jnp.bfloat16)
        deltas = tuple((nt(m, upper) + nt(m, lower))[0:1, :] for m in (ones_a, ones_b))
        stats = (lse[0, 0:1, here], lse[0, 1:2, here])
        queries_cat = jnp.concatenate(queries, axis=0)
        grads_cat = jnp.concatenate(grads, axis=0)

        def step(key, value, first, second, mask):
            probs, dscores = [], []
            for query_h, grad_h, delta, stat in zip(queries, grads, deltas, stats):
                scores = nt(key, query_h)
                prob = jnp.exp2(scores * (scale * LOG2E) - stat)
                if mask is not None:
                    prob = jnp.where(mask, prob, 0.0)
                dprob = nt(value, grad_h)
                probs.append(prob.astype(jnp.bfloat16))
                dscores.append((prob * (dprob - delta)).astype(jnp.bfloat16))
            dscores_cat = jnp.concatenate(dscores, axis=1)
            dvalue = nn(jnp.concatenate(probs, axis=1), grads_cat)
            dkey = nn(dscores_cat, queries_cat)
            dquery = jnp.concatenate([nn(first, dscores[0]), nn(second, dscores[1])], axis=0)
            return dquery, dkey, dvalue

        def read(base):
            rows_at = pl.ds(pl.multiple_of(base, BK), BK)
            return kam[rows_at, :], vm[rows_at, :], kta[:, rows_at], ktc[:, rows_at]

        def accumulate(index, carry, mask):
            rows_at = pl.ds(pl.multiple_of(index * BK, BK), BK)
            dquery, dkey, dvalue = step(*read(index * BK), mask)
            dks[rows_at, :] += dkey
            dvs[rows_at, :] += dvalue
            return carry + dquery

        carry = jnp.zeros((128, size), jnp.float32)
        whole_blocks = at // BK
        carry = lax.fori_loop(0, whole_blocks, lambda i, c: accumulate(i, c, None), carry)
        row = lax.broadcasted_iota(jnp.int32, (BK, size), 0)
        column = lax.broadcasted_iota(jnp.int32, (BK, size), 1)
        if is_branch:
            carry = lax.fori_loop(
                whole_blocks,
                (at + BK - 1) // BK,
                lambda i, c: accumulate(i, c, row + i * BK < at),
                carry,
            )
            triangle = lax.broadcasted_iota(jnp.int32, (size, size), 0) <= lax.broadcasted_iota(
                jnp.int32, (size, size), 1
            )
            dquery, dkey, dvalue = step(kbm[...], vbm[...], ktab[...], ktcb[...], triangle)
            carry = carry + dquery
            dk[branch_part, :] = (dkey * scale).astype(dk.dtype)
            dv[branch_part, :] = dvalue.astype(dv.dtype)
        else:
            carry = accumulate(whole_blocks, carry, row + whole_blocks * BK <= column + at)
        dq[query_at, :] = (carry.T * scale).astype(dq.dtype)
    dk[prompt_part, :] = (dks[...] * scale).astype(dk.dtype)
    dv[prompt_part, :] = dvs[...].astype(dv.dtype)


def attention_backward(pos, q, k, v, o, do, lse, block, branch, after=()):
    total, width = q.shape
    span = total - branch
    rows = o.shape[0]
    pairs = pl.cdiv(width, 128)

    def col(n):
        return pl.BlockSpec((n, 128), lambda p, pos: (0, p))

    def scratch(n):
        wide = pltpu.VMEM((64, n), jnp.bfloat16)
        tall = pltpu.VMEM((n, 128), jnp.bfloat16)
        return [wide, wide, tall, tall]

    return pl.pallas_call(
        functools.partial(backward_kernel, block=block, branch=branch, width=width),
        grid_spec=pltpu.PrefetchScalarGridSpec(
            num_scalar_prefetch=1,
            grid=(pairs,),
            in_specs=[col(total)] * 3
            + [col(rows)] * 2
            + [pl.BlockSpec((1, 8, rows), lambda p, pos: (p, 0, 0))]
            + [pl.BlockSpec(memory_space=pl.ANY)] * len(after),
            out_specs=[col(total)] * 3,
            scratch_shapes=scratch(span)
            + scratch(branch)
            + [pltpu.VMEM((span, 128), jnp.float32), pltpu.VMEM((span, 128), jnp.float32)],
        ),
        out_shape=[jax.ShapeDtypeStruct((total, width), jnp.bfloat16)] * 3,
        compiler_params=pltpu.CompilerParams(
            dimension_semantics=("arbitrary",), vmem_limit_bytes=40 * 2**20
        ),
        cost_estimate=busy(10 * pairs),
        name="attention_backward",
    )(pos, q, k, v, o, do, lse, *after)


TILE = 256


def mlp_forward_kernel(act, resid, up, up_bias, down, down_bias, *rest):
    hidden, slope, result, acc = rest[-4:]
    step = pl.program_id(0)

    @pl.when(step == 0)
    def _():
        acc[...] = resid[...] + down_bias[...]

    rows = act.shape[0]
    size = 256 if rows % 256 == 0 else rows
    for start in range(0, rows, size):
        here = slice(start, start + size)
        pre = nn(act[here, :], up[...]) + up_bias[...]
        bell = jnp.exp(pre * pre * -0.5)
        t = 1.0 / (1.0 + (0.3275911 * 0.7071067811865476) * jnp.abs(pre))
        series = t * (
            0.127414796 + t * (-0.142248368 + t * (0.7107068705 + t * (-0.7265760135 + t * 0.5307027145)))
        )
        tail = series * bell
        below = jnp.where(pre >= 0.0, 1.0 - tail, tail)
        exact = (pre * below).astype(jnp.bfloat16)
        hidden[here, :] = exact
        slope[here, :] = (below + pre * bell * 0.3989422804014327).astype(jnp.bfloat16)
        acc[here, :] += nt(exact, down[...])

    @pl.when(step == pl.num_programs(0) - 1)
    def _():
        result[...] = acc[...].astype(result.dtype)


def whole_block(shape):
    return pl.BlockSpec(shape, lambda j: (0,) * len(shape))


def mlp_forward(act, resid, up, up_bias, down, down_bias, after=()):
    rows, width = act.shape
    inner = up.shape[1]
    column = pl.BlockSpec((width, TILE), lambda j: (0, j))
    tall = pl.BlockSpec((rows, TILE), lambda j: (0, j))
    return pl.pallas_call(
        mlp_forward_kernel,
        grid=(inner // TILE,),
        in_specs=[
            whole_block((rows, width)),
            whole_block((rows, width)),
            column,
            pl.BlockSpec((1, TILE), lambda j: (0, j)),
            column,
            whole_block((1, width)),
        ]
        + [pl.BlockSpec(memory_space=pl.ANY)] * len(after),
        out_specs=[tall, tall, whole_block((rows, width))],
        out_shape=[
            jax.ShapeDtypeStruct((rows, inner), jnp.bfloat16),
            jax.ShapeDtypeStruct((rows, inner), jnp.bfloat16),
            jax.ShapeDtypeStruct((rows, width), jnp.bfloat16),
        ],
        scratch_shapes=[pltpu.VMEM((rows, width), jnp.float32)],
        compiler_params=pltpu.CompilerParams(
            dimension_semantics=("arbitrary",), vmem_limit_bytes=44 * 2**20
        ),
        cost_estimate=busy(40),
        name="mlp_forward",
    )(act, resid, up, up_bias.reshape(1, inner), down, down_bias.reshape(1, width), *after)


def mlp_backward_kernel(act, cot, hidden, slope, up, down, *rest):
    d_act, up_grad, down_grad, bias_grad, act_turned, cot_turned = rest[-6:]
    step = pl.program_id(0)

    @pl.when(step == 0)
    def _():
        act_turned[...] = act[...].T
        cot_turned[...] = cot[...].T
        d_act[...] = jnp.zeros_like(d_act)

    rows = act.shape[0]
    size = 256 if rows % 256 == 0 else rows
    bias = jnp.zeros((1, TILE), jnp.float32)
    pieces = []
    for start in range(0, rows, size):
        here = slice(start, start + size)
        d_pre = (nn(cot[here, :], down[...]) * slope[here, :].astype(jnp.float32)).astype(jnp.bfloat16)
        bias = bias + jnp.sum(d_pre.astype(jnp.float32), axis=0, keepdims=True)
        d_act[here, :] += nt(d_pre, up[...])
        pieces.append(d_pre)
    bias_grad[...] = bias
    up_grad[...] = nn(act_turned[...], jnp.concatenate(pieces, axis=0)).astype(jnp.bfloat16)
    down_grad[...] = nn(cot_turned[...], hidden[...]).astype(jnp.bfloat16)


def mlp_backward(act, cot, hidden, slope, up, down, after=()):
    rows, width = act.shape
    inner = up.shape[1]
    column = pl.BlockSpec((width, TILE), lambda j: (0, j))
    tall = pl.BlockSpec((rows, TILE), lambda j: (0, j))
    return pl.pallas_call(
        mlp_backward_kernel,
        grid=(inner // TILE,),
        in_specs=[whole_block((rows, width)), whole_block((rows, width)), tall, tall, column, column]
        + [pl.BlockSpec(memory_space=pl.ANY)] * len(after),
        out_specs=[
            whole_block((rows, width)),
            column,
            column,
            pl.BlockSpec((1, TILE), lambda j: (0, j)),
        ],
        out_shape=[
            jax.ShapeDtypeStruct((rows, width), jnp.float32),
            jax.ShapeDtypeStruct((width, inner), jnp.bfloat16),
            jax.ShapeDtypeStruct((width, inner), jnp.bfloat16),
            jax.ShapeDtypeStruct((1, inner), jnp.float32),
        ],
        scratch_shapes=[
            pltpu.VMEM((width, rows), jnp.bfloat16),
            pltpu.VMEM((width, rows), jnp.bfloat16),
        ],
        compiler_params=pltpu.CompilerParams(
            dimension_semantics=("arbitrary",), vmem_limit_bytes=48 * 2**20
        ),
        cost_estimate=busy(60),
        name="mlp_backward",
    )(act, cot, hidden, slope, up, down, *after)


def gate_kernel(*refs):
    pass


def gate(value, after):
    if not after:
        return value
    anywhere = pl.BlockSpec(memory_space=pl.ANY)
    return pl.pallas_call(
        gate_kernel,
        in_specs=[anywhere] * (1 + len(after)),
        out_specs=anywhere,
        out_shape=jax.ShapeDtypeStruct(value.shape, value.dtype),
        input_output_aliases={0: 0},
        cost_estimate=busy(1),
        name="gate",
    )(value, *after)


GROUP = 512

epsilon = 1e-05


def normalise(values_in):
    centre = jnp.mean(values_in, axis=-1, keepdims=True)
    centred = values_in - centre
    spread = jnp.mean(centred * centred, axis=-1, keepdims=True)
    pace = lax.rsqrt(spread + epsilon)
    return centred * pace, pace


def norm_back(grad, norm, pace, gain):
    scaled = grad * gain
    return pace * (
        scaled
        - jnp.mean(scaled, axis=-1, keepdims=True)
        - norm * jnp.mean(scaled * norm, axis=-1, keepdims=True)
    )


def swap(value, axis, bit):
    count = lax.axis_size(axis)
    return lax.ppermute(value, axis, [(i, i ^ bit) for i in range(count)])


def ahead(value, axis, step):
    count = lax.axis_size(axis)
    return lax.ppermute(value, axis, [(i, (i + step) % count) for i in range(count)])


def total_over(value, axes):
    for axis in axes:
        count = lax.axis_size(axis)
        if count & (count - 1):
            value = lax.psum(value, axis)
            continue
        bit = 1
        while bit < count:
            value = value + swap(value, axis, bit)
            bit *= 2
    return value


def by_halves(half_width):
    return lax.axis_size("dp") == 4 and lax.axis_size("gy") == 2 and half_width > GROUP


def half_index():
    return lax.axis_index("dp") % 2


def pair_rows(mine, theirs):
    first = half_index() == 0
    return jnp.stack([jnp.where(first, mine, theirs), jnp.where(first, theirs, mine)], axis=-3)


def gather_plain(part):
    part = lax.all_gather(part, "gy", axis=1, tiled=True)
    return lax.all_gather(part, "gx", axis=0, tiled=True)


def gather_quarters(part):
    rows, columns = part.shape
    copies, gx, gy = (lax.axis_size(axis) for axis in ("dp", "gx", "gy"))
    size = columns // copies
    mine = lax.dynamic_slice_in_dim(part, lax.axis_index("dp") * size, size, 1)
    raw = lax.all_gather(mine, ("dp", "gx", "gy"))
    got = raw.reshape(copies, gx, gy, rows, size)
    return raw, [
        [got[quarter, :, side].reshape(gx * rows, size) for quarter in range(copies)]
        for side in range(gy)
    ]


def gather_projections(qkv_part, out_part, width):
    rows = qkv_part.shape[0]
    half = width // 2
    first_side = lax.axis_index("gy") == 0
    key_at = width - half
    here = jnp.where(
        first_side,
        qkv_part[:, :GROUP],
        qkv_part[:, half : half + GROUP],
    )
    keys_here = jnp.where(first_side, qkv_part[:, width : width + GROUP], qkv_part[:, :GROUP])
    raw, one = gather_quarters(jnp.concatenate([here, keys_here], axis=1))
    rest = width - GROUP
    spare = half - GROUP
    queries_rest = jnp.where(first_side, qkv_part[:, GROUP:width], qkv_part[:, half + GROUP :])
    keys_rest = jnp.where(first_side, qkv_part[:, width + GROUP :], qkv_part[:, GROUP:half])

    def pad(value, size):
        return jnp.pad(value, ((0, 0), (0, size - value.shape[1])))

    outer = pl.cdiv(rest + spare, 128) * 128
    out_size = pl.cdiv(half, 128) * 128
    total = pl.cdiv(outer + out_size, 512) * 512
    packed = pad(jnp.concatenate([queries_rest, keys_rest], axis=1), outer)
    packed = pad(jnp.concatenate([packed, pad(out_part, out_size)], axis=1), total)
    two = [jnp.concatenate(side, axis=1) for side in gather_quarters(packed)[1]]
    first = [
        jnp.concatenate(one[0][:2], axis=1),
        jnp.concatenate(one[0][2:], axis=1),
        jnp.concatenate(one[1][:2], axis=1),
    ]
    second = [
        two[0][:, :rest],
        jnp.concatenate(
            [two[0][:, rest : rest + spare]] + one[1][2:] + [two[1][:, rest : rest + spare]], axis=1
        ),
        two[1][:, :rest],
    ]
    out_full = jnp.concatenate([side[:, outer : outer + half] for side in two], axis=1)
    return [first, second], out_full, raw


def gather_feed_forward(up_part, down_part, after):
    columns = up_part.shape[1]
    shared = columns // 2 // 512 * 512
    _, quarters = gather_quarters(jnp.concatenate([up_part[:, :shared], down_part[:, :shared]], axis=1))
    first_half = half_index() == 0
    first_side = lax.axis_index("gy") == 0
    mine = gate(jnp.where(first_half, up_part[:, shared:], down_part[:, shared:]), after)
    rows, size = mine.shape
    count = lax.axis_size("gx")
    here = lax.axis_index("gx")
    blocks = jnp.zeros((count, rows, size), mine.dtype)
    for step in range(count):
        got = mine if step == 0 else ahead(mine, "gx", step)
        blocks = lax.dynamic_update_index_in_dim(blocks, got, (here - step) % count, 0)
    own = blocks.reshape(count * rows, size)
    theirs = swap(own, "gy", 1)
    sides = (jnp.where(first_side, own, theirs), jnp.where(first_side, theirs, own))
    others = [swap(side, "dp", 1) for side in sides]
    ups = [jnp.where(first_half, a, b) for a, b in zip(sides, others)]
    downs = [jnp.where(first_half, b, a) for a, b in zip(sides, others)]
    wholes = []
    for pieces, rest in ((slice(0, 2), ups), (slice(2, 4), downs)):
        wholes.append(
            jnp.concatenate([p for side in range(2) for p in quarters[side][pieces] + [rest[side]]], axis=1)
        )
    return wholes, own


def core_step(whole):
    count = lax.axis_size("gx")
    rows, columns = whole.shape
    pieces = whole.reshape(count, 2, rows // count // 2, columns)
    half = half_index()
    keep = lax.dynamic_index_in_dim(pieces, half, 1, False)
    give = lax.dynamic_index_in_dim(pieces, 1 - half, 1, False)
    return add(keep, swap(give, "dp", 1))


def add(a, b):
    return (a.astype(jnp.float32) + b.astype(jnp.float32)).astype(jnp.bfloat16)


def halves_step(value, axis, bit, here):
    size = value.shape[-1] // 2
    first, second = value[..., :size], value[..., size:]
    own_first = here == 0
    keep = jnp.where(own_first, first, second)
    give = jnp.where(own_first, second, first)
    return add(keep, swap(give, axis, bit))


def columns_step(value):
    return halves_step(value, "gy", 1, lax.axis_index("gy"))


def overlap_step(value):
    columns = value.shape[-1] // 2
    size = pl.cdiv(columns // 128, 2) * 128
    first, second = (
        jnp.concatenate([value[..., at : at + size], value[..., columns + at : columns + at + size]], axis=-1)
        for at in (0, columns - size)
    )
    own_first = lax.axis_index("dp") // 2 == 0
    return add(jnp.where(own_first, first, second), swap(jnp.where(own_first, second, first), "dp", 2))


def overlap_join(value, columns):
    size = value.shape[-1]
    other = swap(value, "dp", 2)
    own_first = lax.axis_index("dp") // 2 == 0
    first, second = jnp.where(own_first, value, other), jnp.where(own_first, other, value)
    return jnp.concatenate([first, second[..., 2 * size - columns :]], axis=-1)


def blocks_step(value):
    count = lax.axis_size("gx")
    here = lax.axis_index("gx")
    total = lax.dynamic_index_in_dim(value, here, 0, False).astype(jnp.float32)
    for step in range(1, count):
        give = lax.dynamic_index_in_dim(value, (here + step) % count, 0, False)
        total = total + ahead(give, "gx", step).astype(jnp.float32)
    return total.astype(jnp.bfloat16)


def copies_step(value):
    bit = 2
    while bit < lax.axis_size("dp"):
        value = add(value, swap(value, "dp", bit))
        bit *= 2
    return value


def join_step(value):
    columns = value.shape[-1]
    return pair_rows(value, swap(value, "dp", 1)).reshape(-1, columns).astype(jnp.float32)


def side_exchange(first, second):
    first_side = lax.axis_index("gy") == 0
    keep = jnp.where(first_side, first, second)
    return add(keep, swap(jnp.where(first_side, second, first), "gy", 1))


def rest_exchange(rest_flow, out_flow, width):
    rest = width - GROUP
    spare = width // 2 - GROUP
    query, key, value = (rest_flow[..., rest * kind : rest * (kind + 1)] for kind in range(3))
    return side_exchange(
        jnp.concatenate([query, key[..., :spare], out_flow[..., : width // 2]], axis=-1),
        jnp.concatenate([value, key[..., rest - spare :], out_flow[..., width // 2 :]], axis=-1),
    )


def first_exchange(first_flow, rest_flow, width):
    rest = width - GROUP
    spare = width // 2 - GROUP
    query, key, value = (first_flow[..., GROUP * kind : GROUP * (kind + 1)] for kind in range(3))
    return side_exchange(
        jnp.concatenate([query, key], axis=-1),
        jnp.concatenate([value, rest_flow[..., rest + spare : 2 * rest - spare]], axis=-1),
    )


def join_projections(first, second, width):
    rest = width - GROUP
    one, two = first[:, :GROUP], first[:, GROUP:]
    three, four = second[:, :rest], second[:, rest:]
    return jnp.where(
        lax.axis_index("gy") == 0,
        jnp.concatenate([one, three, two, four], axis=1),
        jnp.concatenate([two, four, one, three], axis=1),
    )


def scatter_plain(whole):
    part = lax.psum_scatter(whole, "gy", scatter_dimension=1, tiled=True)
    part = lax.psum_scatter(part, "gx", scatter_dimension=0, tiled=True)
    return lax.psum(part, "dp").astype(jnp.float32)


def all_tokens(own):
    count = lax.axis_size("gy")
    here = lax.axis_index("gy")
    if count != 2:
        return lax.all_gather(own, "gy", axis=0, tiled=True)
    other = swap(own, "gy", 1)
    first = here == 0
    return jnp.concatenate([jnp.where(first, own, other), jnp.where(first, other, own)], axis=0)


def own_tokens_sum(whole):
    count = lax.axis_size("gy")
    here = lax.axis_index("gy")
    rows = whole.shape[0] // count
    if count != 2:
        return lax.psum_scatter(
            whole.astype(jnp.bfloat16), "gy", scatter_dimension=0, tiled=True
        ).astype(jnp.float32)
    give = lax.dynamic_slice_in_dim(whole, (1 - here) * rows, rows, 0)
    keep = lax.dynamic_slice_in_dim(whole, here * rows, rows, 0)
    return keep + swap(give.astype(jnp.bfloat16), "gy", 1).astype(jnp.float32)


def dot(a, b):
    return jnp.dot(a, b, preferred_element_type=jnp.float32)


def local(
    prompt,
    continuations,
    prefix_len,
    attn_gain,
    attn_shift,
    qkv_weight,
    query_bias,
    value_bias,
    out_weight,
    out_bias,
    mlp_gain,
    mlp_shift,
    up_weight,
    up_bias,
    down_weight,
    down_bias,
    grad_prompt,
    grad_continuations,
):
    groups, shard, width = prompt.shape
    length = continuations.shape[1]
    first_pos = lax.axis_index("gy") * shard
    prompt_len = shard * lax.axis_size("gy")
    block = shard // 2
    halved = by_halves(width // 2)
    spans = [slice(0, GROUP), slice(GROUP, width)]

    if halved:
        limit, other_limit = prefix_len[0], swap(prefix_len, "gy", 1)[0]
        is_first = first_pos == 0
        is_long = jnp.logical_or(limit > other_limit, jnp.logical_and(limit == other_limit, is_first))
        kept_at = jnp.where(is_long, 0, block)
        places = [first_pos + kept_at, shard - first_pos + kept_at, limit]
    else:
        places = [first_pos, first_pos + block, prefix_len[0]]
    places = jnp.stack(places).astype(jnp.int32)

    def kept_rows(own):
        return lax.dynamic_slice_in_dim(own, kept_at, block, 0)

    def given_rows(own):
        return lax.dynamic_slice_in_dim(own, block - kept_at, block, 0)

    def back_home(done):
        if not halved:
            return done
        kept, home = done[:block], swap(done[block:], "gy", 1)
        return jnp.concatenate([jnp.where(is_long, kept, home), jnp.where(is_long, home, kept)], axis=0)

    own_prompt = prompt.reshape(shard, width)
    branch = continuations.reshape(length, width)
    own_cot = grad_prompt.reshape(shard, width)
    branch_cot = grad_continuations.reshape(length, width)
    whole_prompt = all_tokens(own_prompt)
    if halved:
        weights, out_full, raw = gather_projections(qkv_weight, out_weight, width)
        (up_full, down_full), fetched = gather_feed_forward(up_weight, down_weight.T, (raw,))
        fetched = (fetched,)
        other_cot = swap(gate(given_rows(own_cot), (raw,)), "gy", 1)
        cotangent = jnp.concatenate([kept_rows(own_cot), other_cot, branch_cot], axis=0)
    else:
        qkv = gather_plain(qkv_weight)
        weights = [[qkv[:, c.start + s : c.stop + s] for s in (0, width, 2 * width)] for c in spans]
        out_full, up_full, down_full = (gather_plain(w) for w in (out_weight, up_weight, down_weight.T))
        fetched = ()
        cotangent = jnp.concatenate([own_cot, branch_cot], axis=0)

    all_rows = jnp.concatenate([whole_prompt, branch], axis=0)
    norm_all, _ = normalise(all_rows.astype(jnp.float32))
    act_all = (norm_all * attn_gain + attn_shift).astype(jnp.bfloat16)
    projected, mixed, stats = [], [], []
    for number, (cols, (w_query, w_key, w_value)) in enumerate(zip(spans, weights)):
        projected.append(
            (
                (dot(act_all, w_query) + query_bias[cols]).astype(jnp.bfloat16),
                dot(act_all, w_key).astype(jnp.bfloat16),
                (dot(act_all, w_value) + value_bias[cols]).astype(jnp.bfloat16),
            )
        )
        got, stat = attention_forward(
            places, *projected[-1], block, length, fetched if number == 1 else ()
        )
        mixed.append(got)
        stats.append(stat)

    token_rows = jnp.concatenate(
        [lax.dynamic_slice_in_dim(whole_prompt, places[n], block, 0) for n in range(2)] + [branch], axis=0
    ).astype(jnp.float32)
    resid = token_rows + (sum(dot(m, out_full[c]) for m, c in zip(mixed, spans)) + out_bias)
    norm_two, pace_two = normalise(resid)
    act_two = (norm_two * mlp_gain + mlp_shift).astype(jnp.bfloat16)
    hidden, slope, result = mlp_forward(act_two, resid, up_full, up_bias, down_full, down_bias)
    prompt_out = back_home(result[:shard]).reshape(groups, shard, width)
    continuation_out = result[shard:].reshape(1, length, width)

    cot_exact = cotangent.astype(jnp.float32)
    down_bias_grad = jnp.sum(cot_exact, axis=0)
    d_act_two, up_grad, down_grad, up_bias_grad = mlp_backward(
        act_two, cotangent, hidden, slope, up_full, down_full
    )
    up_bias_grad = up_bias_grad.reshape(-1)
    after = ()
    if halved:
        up_flow, down_flow = core_step(up_grad), core_step(down_grad)
        after = (up_flow, down_flow)
    mlp_gain_grad = jnp.sum(d_act_two * norm_two, axis=0)
    mlp_shift_grad = jnp.sum(d_act_two, axis=0)
    d_resid = cot_exact + norm_back(d_act_two, norm_two, pace_two, mlp_gain)
    d_branch = d_resid.astype(jnp.bfloat16)
    out_grad = jnp.concatenate([tn(m, d_branch) for m in mixed], axis=0).astype(jnp.bfloat16)
    out_bias_grad = jnp.sum(d_branch.astype(jnp.float32), axis=0)
    d_act_all = 0.0
    grads, flows, bias_grads = [None, None], [None, None], [None, None]
    for number in (1, 0):
        cols = spans[number]
        d_mixed = nt(d_branch, out_full[cols]).astype(jnp.bfloat16)
        d_parts = list(
            attention_backward(
                places, *projected[number], mixed[number], d_mixed, stats[number], block, length, after
            )
        )
        if halved and number == 0:
            d_parts[0] = gate(d_parts[0], (up_flow, down_flow, rest_flow))
        for d_part, weight in zip(d_parts, weights[number]):
            d_act_all = d_act_all + nt(d_part, weight)
        grads[number] = jnp.concatenate([tn(act_all, d).astype(jnp.bfloat16) for d in d_parts], axis=1)
        bias_grads[number] = [jnp.sum(d_parts[n].astype(jnp.float32), axis=0) for n in (0, 2)]
        if halved and number == 1:
            joint = core_step(jnp.concatenate([grads[1], out_grad], axis=1))
            flows[1], out_flow = joint[..., :-width], joint[..., -width:]
            up_flow, down_flow = columns_step(up_flow), overlap_step(down_flow)
            after = (up_flow, down_flow, joint)
            up_flow, down_flow = blocks_step(up_flow), columns_step(down_flow)
            rest_flow = rest_exchange(flows[1], out_flow, width)
    shared = own_tokens_sum(d_act_all[:prompt_len])
    if halved:
        flows[0] = core_step(grads[0])
        first_flow = first_exchange(flows[0], flows[1], width)
        up_total = join_step(copies_step(up_flow))
        down_total = join_step(overlap_join(blocks_step(down_flow), up_weight.shape[1]))
        first_total, rest_total = (
            join_step(copies_step(blocks_step(f))) for f in (first_flow, rest_flow)
        )
        qkv_total = join_projections(first_total, rest_total[:, : -(width // 2)], width)
        out_total = rest_total[:, -(width // 2) :]
    else:
        qkv_grad = jnp.concatenate(
            [
                grads[n][:, kind * (c.stop - c.start) : (kind + 1) * (c.stop - c.start)]
                for kind in range(3)
                for n, c in enumerate(spans)
            ],
            axis=1,
        )
        up_total, down_total, out_total, qkv_total = (
            scatter_plain(g) for g in (up_grad, down_grad, out_grad, qkv_grad)
        )
    query_bias_grad, value_bias_grad = (
        jnp.concatenate([bias_grads[n][kind] for n in range(2)]) for kind in range(2)
    )
    attn_gain_grad = jnp.sum(d_act_all * norm_all, axis=0)
    attn_shift_grad = jnp.sum(d_act_all, axis=0)
    norm_own, pace_own = normalise(jnp.concatenate([own_prompt, branch], axis=0).astype(jnp.float32))
    d_act_own = jnp.concatenate([shared, d_act_all[prompt_len:]], axis=0)
    rows_part = norm_back(d_act_own, norm_own, pace_own, attn_gain)
    prompt_resid = d_resid[:shard]
    if halved:
        home = back_home(d_branch[:shard]).astype(jnp.float32)
        kept = jnp.where(is_long, prompt_resid[:block], home[:block]), jnp.where(
            is_long, home[block:], prompt_resid[:block]
        )
        prompt_resid = jnp.concatenate(kept, axis=0)
    d_rows = jnp.concatenate([prompt_resid, d_resid[shard:]], axis=0) + rows_part
    prompt_grad = d_rows[:shard].reshape(groups, shard, width)
    continuation_grad = d_rows[shard:].reshape(1, length, width)
    vectors = (
        attn_gain_grad,
        attn_shift_grad,
        query_bias_grad,
        value_bias_grad,
        out_bias_grad,
        mlp_gain_grad,
        mlp_shift_grad,
        up_bias_grad,
        down_bias_grad,
    )
    joined = total_over(jnp.concatenate(vectors), ("dp", "gy", "gx"))
    totals = []
    at = 0
    for vector in vectors:
        totals.append(joined[at : at + vector.shape[0]])
        at += vector.shape[0]
    return (
        prompt_out,
        continuation_out,
        prompt_grad,
        continuation_grad,
        totals[0],
        totals[1],
        qkv_total,
        totals[2],
        totals[3],
        out_total,
        totals[4],
        totals[5],
        totals[6],
        up_total,
        totals[7],
        down_total.T,
        totals[8],
    )


def solution(mesh):
    placed = (
        P(("dp", "gx"), "gy", None),
        P(("dp", "gx", "gy"), None, None),
        P(("dp", "gx", "gy")),
        P(),
        P(),
        P("gx", "gy"),
        P(),
        P(),
        P("gx", "gy"),
        P(),
        P(),
        P(),
        P("gx", "gy"),
        P(),
        P("gy", "gx"),
        P(),
        P(("dp", "gx"), "gy", None),
        P(("dp", "gx", "gy"), None, None),
    )
    return jax.shard_map(
        local,
        mesh=mesh,
        in_specs=placed,
        out_specs=(
            P(("dp", "gx"), "gy", None),
            P(("dp", "gx", "gy"), None, None),
            P(("dp", "gx"), "gy", None),
            P(("dp", "gx", "gy"), None, None),
            P(),
            P(),
            P("gx", "gy"),
            P(),
            P(),
            P("gx", "gy"),
            P(),
            P(),
            P(),
            P("gx", "gy"),
            P(),
            P("gy", "gx"),
            P(),
        ),
        check_vma=False,
    )
```

time: 1240 us -> 1110 us (0.90)
  Pallas kernels: 114 us -> 304 us
  starting transfers between devices: 241 us -> 87.9 us
  waiting for transfers between devices: 396 us -> 244 us
  matrix products: 286 us -> 145 us
  local copies, waits for them, and re-layouts: 92.3 us -> 168 us
  other arithmetic: 90.1 us -> 133 us
  between operations: 3.15 us -> 18.4 us
    pallas_call x2 -> x9, Pallas kernels: 114 us -> 304 us  [the longest x2 104 us: attention_backward(): pl.pallas_call(functools.partial(backward_kernel, block=block, branch=bra...]
    ppermute x37 -> x31, starting transfers between devices: 155 us -> 34.9 us  [swap(): return lax.ppermute(value, axis, [(i, i ^ bit) for i in range(count)])]
    dot_general x8, matrix products: 139 us -> 39.4 us  [dot(): return jnp.dot(a, b, preferred_element_type=jnp.float32)]
    ppermute x24 -> x15, waiting for transfers between devices: 181 us -> 101 us  [ahead(): lax.ppermute(value, axis, [(i, (i + step) % count) for i in range(count)])]
    ppermute x37 -> x31, waiting for transfers between devices: 216 us -> 143 us  [swap(): return lax.ppermute(value, axis, [(i, i ^ bit) for i in range(count)])]
    ppermute x24 -> x15, starting transfers between devices: 85.5 us -> 52.9 us  [ahead(): lax.ppermute(value, axis, [(i, (i + step) % count) for i in range(count)])]
    unnamed x208 -> x298, local copies, waits for them, and re-layouts: 17.7 us -> 47.4 us
    another operation x20 -> x8, other arithmetic: 25.3 us -> 0.85 us  [pair_rows(): jnp.stack([jnp.where(first, mine, theirs), jnp.where(first, theirs, mine)...]
  transfers between devices with their start and end apart: 61 -> 49, of which waited for: 22 -> 15; matrix products, arithmetic and copies ran while one was open for 25% -> 33% of each run, Pallas kernels for 4% -> 11%
where the time goes in v2:
time: 1110 us; the launch traced here: 1100 us
  Pallas kernels  304 us (27%)
  waiting for transfers between devices  244 us (22%)
  local copies, waits for them, and re-layouts  168 us (15%)
  matrix products  145 us (13%)
  other arithmetic  133 us (12%)
  starting transfers between devices  87.9 us (8%)
  between operations  18.4 us (2%)
    ppermute x31, waiting for transfers between devices, swap(): return lax.ppermute(value, axis, [(i, i ^ bit) for i in range(count)])  143 us
    pallas_call x2, Pallas kernels, attention_backward(): pl.pallas_call(functools.partial(backward_kernel, block=block, branch=bra...  104 us
    ppermute x15, waiting for transfers between devices, ahead(): lax.ppermute(value, axis, [(i, (i + step) % count) for i in range(count)])  101 us
    pallas_call x2, Pallas kernels, attention_forward(): pl.pallas_call(functools.partial(forward_kernel, block=block, branch=bran...  73.9 us
    pallas_call x1, Pallas kernels, mlp_backward(): pl.pallas_call(mlp_backward_kernel, grid=(inner // TILE,), in_specs=[whol...  70.8 us
    pallas_call x1, Pallas kernels, mlp_forward(): pl.pallas_call(mlp_forward_kernel, grid=(inner // TILE,), in_specs=[whole...  55.4 us
    dot_general x8, matrix products, nt(): lax.dot_general(a, b, (((1,), (1,)), ((), ())), preferred_element_type=jn...  54.8 us
    ppermute x15, starting transfers between devices, ahead(): lax.ppermute(value, axis, [(i, (i + step) % count) for i in range(count)])  52.9 us
  transfers between devices with their start and end apart: 49, of which 15 were waited for; matrix products, arithmetic and copies ran while one was open for 33% of the time, Pallas kernels for 11%

profile of v2, /device:TPU:0, one launch (start us, length us, event | category | flops | bytes accessed | tf_op | source)
XLA Modules:
  0.0 1101.3 jit_solution(2092249153155588878)
XLA Ops:
  29.1 46.5 %collective-permute-done = s32[1]{0:T(128)} collective-permute-done((s32[1]{0:T(128)}, s32[1]{0:T(128)}, u32[]{:S(2)}, u32[]{:S(2)}) %collective-permute-start) | collective-permute-done | bytes 36 | tf_op jit(solution)/shard_map/ppermute | solution.py:497
  102.5 6.6 fusion.5
  129.8 6.9 fusion.25.v
  144.7 17.1 %collective-permute-done.3 = bf16[272,1152]{1,0:T(8,128)(2,1)} collective-permute-done((bf16[272,1152]{1,0:T(8,128)(2,1)}, bf16[272,1152]{1,0:T(8,128)(2,1)}, u32[]{:S(2)}, u32[]{:S(2)}) %collective-permute-start.3) | collective-permute-done | bytes 626720 | tf_op jit(solution)/shard_map/ppermute | solution.py:502
  170.6 32.7 %attention_forward.2 = (bf16[1280,512]{1,0:T(8,128)(2,1)S(1)}, f32[4,8,1280]{2,1,0:T(8,128)S(1)}) custom-call(s32[3]{0:T(128)S(1)} %pad_add_fusion.pos, bf16[2304,512]{1,0:T(8,128)(2,1)S(1)} %fusion.24.q, bf16[2304,512]{1,0:T(8,128)(2,1)S(1)} %convolution_convert_fusion.1.k, bf16[2304,512]{1,0:T(8,128)(2,1)S(1)} %fusion.25.v), custom_call_target="tpu_custom_call" | custom-call | flops 28000000000 | bytes 28000000 | tf_op jit(solution)/shard_map/attention_forward/pallas_call | solution.py:167
  210.4 22.2 %collective-permute-done.5 = bf16[1088,1152]{1,0:T(8,128)(2,1)} collective-permute-done((bf16[1088,1152]{1,0:T(8,128)(2,1)}, bf16[1088,1152]{1,0:T(8,128)(2,1)}, u32[]{:S(2)}, u32[]{:S(2)}) %collective-permute-start.5) | collective-permute-done | bytes 2506784 | tf_op jit(solution)/shard_map/ppermute | solution.py:497
  242.4 8.3 convolution_convert_fusion.k
  262.3 41.2 %attention_forward.3 = (bf16[1280,576]{1,0:T(8,128)(2,1)S(1)}, f32[5,8,1280]{2,1,0:T(8,128)S(1)}) custom-call(s32[3]{0:T(128)S(1)} %pad_add_fusion.pos, bf16[2304,576]{1,0:T(8,128)(2,1)S(1)} %add_convert_fusion.2.q, bf16[2304,576]{1,0:T(8,128)(2,1)S(1)} %convolution_convert_fusion.k, bf16[2304,576]{1,0:T(8,128)(2,1)S(1)} %add_convert_fusion.1.v, ...), custom_call_target="tpu_custom_call" | custom-call | flops 35000000512 | bytes 35000000 | tf_op jit(solution)/shard_map/attention_forward/pallas_call | solution.py:167
  334.2 55.4 %mlp_forward.1 = (bf16[1280,4352]{1,0:T(8,128)(2,1)}, bf16[1280,4352]{1,0:T(8,128)(2,1)}, bf16[1280,1088]{1,0:T(8,128)(2,1)S(1)}) custom-call(bf16[1280,1088]{1,0:T(8,128)(2,1)S(1)} %copy-done.5, f32[1280,1088]{1,0:T(8,128)} %copy-done.25, bf16[1088,4352]{1,0:T(8,128)(2,1)} %copy-done.107, f32[1,4352]{1,0:T(1,128)S(1)} %reshape.188.up_bias, ...), custom_call_target="tpu_custom_call" | custom-call | flops 40000000000 | bytes 40000000 | tf_op jit(solution)/shard_map/mlp_forward/pallas_call | solution.py:368
  392.5 70.8 %mlp_backward.1 = (f32[1280,1088]{1,0:T(8,128)}, bf16[1088,4352]{1,0:T(8,128)(2,1)}, bf16[1088,4352]{1,0:T(8,128)(2,1)}, f32[1,4352]{1,0:T(1,128)S(1)}) custom-call(bf16[1280,1088]{1,0:T(8,128)(2,1)S(1)} %copy-done.5, bf16[1280,1088]{1,0:T(8,128)(2,1)S(1)} %get-tuple-element.128.cot, bf16[1280,4352]{1,0:T(8,128)(2,1)} %get-tuple-element.37.hidden, ...), custom_call_target="tpu_custom_call" | custom-call | flops 60000002048 | bytes 60000000 | tf_op jit(solution)/shard_map/mlp_backward/pallas_call | solution.py:425
  519.1 11.3 %collective-permute-done.10 = bf16[512,1088]{0,1:T(8,128)(2,1)} collective-permute-done((bf16[512,1088]{0,1:T(8,128)(2,1)}, bf16[512,1088]{0,1:T(8,128)(2,1)}, u32[]{:S(2)}, u32[]{:S(2)}) %collective-permute-start.10) | collective-permute-done | bytes 1114144 | tf_op jit(solution)/shard_map/ppermute | solution.py:497
  555.3 57.4 %attention_backward.2 = (bf16[2304,576]{1,0:T(8,128)(2,1)S(1)}, bf16[2304,576]{1,0:T(8,128)(2,1)S(1)}, bf16[2304,576]{1,0:T(8,128)(2,1)S(1)}) custom-call(s32[3]{0:T(128)S(1)} %pad_add_fusion.pos, bf16[2304,576]{1,0:T(8,128)(2,1)} %copy-done.23, bf16[2304,576]{1,0:T(8,128)(2,1)} %copy-done.19, bf16[2304,576]{1,0:T(8,128)(2,1)} %copy-done.24, ...), custom_call_target="tpu_custom_call" | custom-call | flops 49999998976 | bytes 50000000 | tf_op jit(solution)/shard_map/attention_backward/pallas_call | solution.py:303
  612.7 7.6 fusion.43
  620.3 7.2 convolution_convert_fusion.5
  638.2 8.1 convolution_convert_fusion.4
  649.1 7.3 convolution_convert_fusion.3
  658.9 11.3 %concatenate.142 = bf16[1088,2816]{1,0:T(8,128)(2,1)} concatenate(bf16[1088,576]{1,0:T(8,128)(2,1)} %copy.194, bf16[1088,576]{1,0:T(8,128)(2,1)} %copy.195, bf16[1088,576]{1,0:T(8,128)(2,1)} %copy.196, bf16[1088,1088]{1,0:T(8,128)(2,1)} %pad_maximum_fusion.8), dimensions={1} | concatenate | bytes 12255232 | tf_op jit(solution)/shard_map/concatenate | solution.py:887
  674.1 7.9 convolution_add_fusion.4
  683.4 7.5 convolution_add_fusion.3
  693.9 37.7 %collective-permute-start.18 = (bf16[136,2176]{1,0:T(8,128)(2,1)S(1)}, bf16[136,2176]{1,0:T(8,128)(2,1)S(1)}, u32[]{:S(2)}, u32[]{:S(2)}) collective-permute-start(bf16[136,2176]{1,0:T(8,128)(2,1)S(1)} %get-tuple-element.179), channel_id=1, source_target_pairs={{0,6},{2,0},{4,2},{6,4},{1,7},{3,1},{5,3},{7,5},{8,14},{10,8},{12,... | collective-permute-start | bytes 1775624 | tf_op jit(solution)/shard_map/ppermute | solution.py:502
  738.2 7.3 collective-permute-done.18
  745.5 37.9 %collective-permute-done.17 = bf16[136,2176]{1,0:T(8,128)(2,1)S(1)} collective-permute-done((bf16[136,2176]{1,0:T(8,128)(2,1)S(1)}, bf16[136,2176]{1,0:T(8,128)(2,1)S(1)}, u32[]{:S(2)}, u32[]{:S(2)}) %collective-permute-start.17) | collective-permute-done | bytes 591904 | tf_op jit(solution)/shard_map/ppermute | solution.py:502
  801.3 46.7 %attention_backward.3 = (bf16[2304,512]{1,0:T(8,128)(2,1)S(1)}, bf16[2304,512]{1,0:T(8,128)(2,1)S(1)}, bf16[2304,512]{1,0:T(8,128)(2,1)S(1)}) custom-call(s32[3]{0:T(128)S(1)} %pad_add_fusion.pos, bf16[2304,512]{1,0:T(8,128)(2,1)S(1)} %copy-done.21, bf16[2304,512]{1,0:T(8,128)(2,1)S(1)} %copy-done.18, bf16[2304,512]{1,0:T(8,128)(2,1)} %copy-done.22, ...), custom_call_target="tpu_custom_call" | custom-call | flops 40000000000 | bytes 40000000 | tf_op jit(solution)/shard_map/attention_backward/pallas_call | solution.py:303
  848.1 8.0 convolution_convert_fusion.7
  856.1 6.5 convolution_convert_fusion.8
  873.1 19.0 %collective-permute-done.42 = bf16[136,1152]{1,0:T(8,128)(2,1)S(1)} collective-permute-done((bf16[136,1152]{1,0:T(8,128)(2,1)S(1)}, bf16[136,1152]{1,0:T(8,128)(2,1)S(1)}, u32[]{:S(2)}, u32[]{:S(2)}) %collective-permute-start.42) | collective-permute-done | bytes 313376 | tf_op jit(solution)/shard_map/ppermute | solution.py:502
  901.2 7.2 convolution_convert_fusion.9
  921.0 13.1 %fusion.71 = (f32[1088]{0:T(1024)S(1)}, f32[1088]{0:T(1024)S(1)}, f32[2304,1088]{1,0:T(8,128)}) fusion(f32[2304]{0:T(1024)S(1)} %copy-done.117, f32[2304]{0:T(1024)S(1)} %copy-done.110, bf16[256,1088]{1,0:T(8,128)(2,1)S(1)} %bitcast.223, bf16[1024,1088]{1,0:T(8,128)(2,1)S(1)} %copy-done.31, bf16[1024,1088]{1,0:T(8,128)(2,1)S(1)} %copy-done.29, ...), kind=kOutput, calls=%fused_computation.249 | convolution fusion | flops 2599221248 | bytes 28568064 | tf_op jit(solution)/shard_map/dot_general | solution.py:16
  956.4 38.5 %collective-permute-done.24 = f32[13056]{0:T(1024)S(1)} collective-permute-done((f32[13056]{0:T(1024)S(1)}, f32[13056]{0:T(1024)S(1)}, u32[]{:S(2)}, u32[]{:S(2)}) %collective-permute-start.24) | collective-permute-done | bytes 52256 | tf_op jit(solution)/shard_map/ppermute | solution.py:497
  1031.8 14.5 %collective-permute-done.28 = bf16[4,136,1024]{2,1,0:T(8,128)(2,1)} collective-permute-done((bf16[4,136,1024]{2,1,0:T(8,128)(2,1)}, bf16[4,136,1024]{2,1,0:T(8,128)(2,1)}, u32[]{:S(2)}, u32[]{:S(2)}) %collective-permute-start.28) | collective-permute-done | bytes 1114144 | tf_op jit(solution)/shard_map/ppermute | solution.py:497
  1051.4 6.5 fusion.20
  1058.2 16.6 %collective-permute-done.30 = bf16[136,1024]{1,0:T(8,128)(2,1)S(1)} collective-permute-done((bf16[136,1024]{1,0:T(8,128)(2,1)}, bf16[136,1024]{1,0:T(8,128)(2,1)S(1)}, u32[]{:S(2)}, u32[]{:S(2)}) %collective-permute-start.30) | collective-permute-done | bytes 278560 | tf_op jit(solution)/shard_map/ppermute | solution.py:502
  (572 shorter events, 390.2 us)
Async XLA Ops:
  7.2 101.9 %all-gather.7.cloned.1.call-start = ((), (), s32[]{:S(2)}) async-start(), calls=%async_computation | async-start | bytes 4595712 | tf_op jit(solution)/shard_map/all_gather | solution.py:541
  9.5 228.7 %all-gather.9.cloned.1.call-start = ((), (), s32[]{:S(2)}) async-start(), calls=%async_computation.1 | async-start | bytes 6893568 | tf_op jit(solution)/shard_map/all_gather | solution.py:541
  11.7 301.7 %all-gather.11.cloned.1.call-start = ((), (), s32[]{:S(2)}) async-start(), calls=%async_computation.2 | async-start | bytes 9191424 | tf_op jit(solution)/shard_map/all_gather | solution.py:541
  11.7 73.2 %collective-permute-start.1 = (bf16[1024,1088]{0,1:T(8,128)(2,1)}, bf16[1024,1088]{0,1:T(8,128)(2,1)}, u32[]{:S(2)}, u32[]{:S(2)}) collective-permute-start(bf16[1024,1088]{0,1:T(8,128)(2,1)} %bitcast.3), channel_id=1, source_target_pairs={{0,1},{1,0},{2,3},{3,2},{4,5},{5,4},{6,7},{7,6},{8,9},{9,8},{10,11... | collective-permute-start | bytes 6684680 | tf_op jit(solution)/shard_map/ppermute | solution.py:497
  14.8 60.9 %collective-permute-start = (s32[1]{0:T(128)}, s32[1]{0:T(128)}, u32[]{:S(2)}, u32[]{:S(2)}) collective-permute-start(s32[1]{0:T(128)} %param.20), channel_id=1, source_target_pairs={{0,1},{1,0},{2,3},{3,2},{4,5},{5,4},{6,7},{7,6},{8,9},{9,8},{10,11... | collective-permute-start | bytes 20 | tf_op jit(solution)/shard_map/ppermute | solution.py:497
  109.1 33.7 %collective-permute-start.2 = (bf16[272,1152]{1,0:T(8,128)(2,1)}, bf16[272,1152]{1,0:T(8,128)(2,1)}, u32[]{:S(2)}, u32[]{:S(2)}) collective-permute-start(bf16[272,1152]{1,0:T(8,128)(2,1)} %gate.3), channel_id=1, source_target_pairs={{0,2},{2,4},{4,6},{6,0},{1,3},{3,5},{5,7},{7,1},{8,10},{10,12},{12... | collective-permute-start | bytes 1880072 | tf_op jit(solution)/shard_map/ppermute | solution.py:502
  110.8 50.9 %collective-permute-start.3 = (bf16[272,1152]{1,0:T(8,128)(2,1)}, bf16[272,1152]{1,0:T(8,128)(2,1)}, u32[]{:S(2)}, u32[]{:S(2)}) collective-permute-start(bf16[272,1152]{1,0:T(8,128)(2,1)} %gate.3), channel_id=1, source_target_pairs={{0,4},{2,6},{4,0},{6,2},{1,5},{3,7},{5,1},{7,3},{8,12},{10,14},{12... | collective-permute-start | bytes 1880072 | tf_op jit(solution)/shard_map/ppermute | solution.py:502
  113.7 50.0 %collective-permute-start.4 = (bf16[272,1152]{1,0:T(8,128)(2,1)}, bf16[272,1152]{1,0:T(8,128)(2,1)}, u32[]{:S(2)}, u32[]{:S(2)}) collective-permute-start(bf16[272,1152]{1,0:T(8,128)(2,1)} %gate.3), channel_id=1, source_target_pairs={{0,6},{2,0},{4,2},{6,4},{1,7},{3,1},{5,3},{7,5},{8,14},{10,8},{12,... | collective-permute-start | bytes 1880072 | tf_op jit(solution)/shard_map/ppermute | solution.py:502
  121.1 83.3 %collective-permute-start.9 = (bf16[512,1088]{0,1:T(8,128)(2,1)S(1)}, bf16[512,1088]{0,1:T(8,128)(2,1)}, u32[]{:S(2)}, u32[]{:S(2)}) collective-permute-start(bf16[512,1088]{0,1:T(8,128)(2,1)S(1)} %copy.181), channel_id=1, source_target_pairs={{0,1},{1,0},{2,3},{3,2},{4,5},{5,4},{6,7},{7,6},{8,9},{9,8},{10,11... | collective-permute-start | bytes 3342344 | tf_op jit(solution)/shard_map/ppermute | solution.py:497
  165.7 66.9 %collective-permute-start.5 = (bf16[1088,1152]{1,0:T(8,128)(2,1)}, bf16[1088,1152]{1,0:T(8,128)(2,1)}, u32[]{:S(2)}, u32[]{:S(2)}) collective-permute-start(bf16[1088,1152]{1,0:T(8,128)(2,1)} %bitcast.31.rest_0_), channel_id=1, source_target_pairs={{0,1},{1,0},{2,3},{3,2},{4,5},{5,4},{6,7},{7,6},{8,9},{9,8},{10,11... | collective-permute-start | bytes 7520264 | tf_op jit(solution)/shard_map/ppermute | solution.py:497
  237.7 80.0 %collective-permute-start.6 = (bf16[1088,1152]{1,0:T(8,128)(2,1)}, bf16[1088,1152]{1,0:T(8,128)(2,1)}, u32[]{:S(2)}, u32[]{:S(2)}) collective-permute-start(bf16[1088,1152]{1,0:T(8,128)(2,1)} %get-tuple-element.155), channel_id=1, source_target_pairs={{0,8},{8,0},{16,24},{24,16},{1,9},{9,1},{17,25},{25,17},{2,10},{10... | collective-permute-start | bytes 7520264 | tf_op jit(solution)/shard_map/ppermute | solution.py:497
  237.7 87.7 %collective-permute-start.7 = (bf16[1088,1152]{1,0:T(8,128)(2,1)}, bf16[1088,1152]{1,0:T(8,128)(2,1)}, u32[]{:S(2)}, u32[]{:S(2)}) collective-permute-start(bf16[1088,1152]{1,0:T(8,128)(2,1)} %get-tuple-element.154), channel_id=1, source_target_pairs={{0,8},{8,0},{16,24},{24,16},{1,9},{9,1},{17,25},{25,17},{2,10},{10... | collective-permute-start | bytes 7520264 | tf_op jit(solution)/shard_map/ppermute | solution.py:497
  479.8 33.5 %collective-permute-start.8 = (bf16[512,1088]{0,1:T(8,128)(2,1)}, bf16[512,1088]{0,1:T(8,128)(2,1)}, u32[]{:S(2)}, u32[]{:S(2)}) collective-permute-start(bf16[512,1088]{0,1:T(8,128)(2,1)} %copy.176), channel_id=1, source_target_pairs={{0,1},{1,0},{2,3},{3,2},{4,5},{5,4},{6,7},{7,6},{8,9},{9,8},{10,11... | collective-permute-start | bytes 3342344 | tf_op jit(solution)/shard_map/ppermute | solution.py:497
  485.7 44.8 %collective-permute-start.10 = (bf16[512,1088]{0,1:T(8,128)(2,1)}, bf16[512,1088]{0,1:T(8,128)(2,1)}, u32[]{:S(2)}, u32[]{:S(2)}) collective-permute-start(bf16[512,1088]{0,1:T(8,128)(2,1)} %copy.184), channel_id=1, source_target_pairs={{0,1},{1,0},{2,3},{3,2},{4,5},{5,4},{6,7},{7,6},{8,9},{9,8},{10,11... | collective-permute-start | bytes 3342344 | tf_op jit(solution)/shard_map/ppermute | solution.py:497
  491.5 46.8 %collective-permute-start.11 = (bf16[4,136,4352]{2,1,0:T(8,128)(2,1)}, bf16[4,136,4352]{2,1,0:T(8,128)(2,1)}, u32[]{:S(2)}, u32[]{:S(2)}) collective-permute-start(bf16[4,136,4352]{2,1,0:T(8,128)(2,1)} %dynamic-slice_bitcast_fusion.1), channel_id=1, source_target_pairs={{0,8},{8,0},{16,24},{24,16},{1,9},{9,1},{17,25},{25,17},{2,10},{10... | collective-permute-start | bytes 14204936 | tf_op jit(solution)/shard_map/ppermute | solution.py:497
  500.4 45.7 %collective-permute-start.12 = (bf16[4,136,4352]{2,1,0:T(8,128)(2,1)}, bf16[4,136,4352]{2,1,0:T(8,128)(2,1)}, u32[]{:S(2)}, u32[]{:S(2)}) collective-permute-start(bf16[4,136,4352]{2,1,0:T(8,128)(2,1)} %dynamic-slice_bitcast_fusion), channel_id=1, source_target_pairs={{0,8},{8,0},{16,24},{24,16},{1,9},{9,1},{17,25},{25,17},{2,10},{10... | collective-permute-start | bytes 14204936 | tf_op jit(solution)/shard_map/ppermute | solution.py:497
  628.7 62.3 %collective-permute-start.13 = (bf16[4,136,2176]{2,1,0:T(8,128)(2,1)}, bf16[4,136,2176]{2,1,0:T(8,128)(2,1)}, u32[]{:S(2)}, u32[]{:S(2)}) collective-permute-start(bf16[4,136,2176]{2,1,0:T(8,128)(2,1)} %broadcast_select_fusion.3), channel_id=1, source_target_pairs={{0,1},{1,0},{2,3},{3,2},{4,5},{5,4},{6,7},{7,6},{8,9},{9,8},{10,11... | collective-permute-start | bytes 7102472 | tf_op jit(solution)/shard_map/ppermute | solution.py:497
  634.5 97.8 %collective-permute-start.14 = (bf16[4,136,2304]{2,1,0:T(8,128)(2,1)}, bf16[4,136,2304]{2,1,0:T(8,128)(2,1)}, u32[]{:S(2)}, u32[]{:S(2)}) collective-permute-start(bf16[4,136,2304]{2,1,0:T(8,128)(2,1)} %broadcast_select_fusion), channel_id=1, source_target_pairs={{0,16},{8,24},{16,0},{24,8},{1,17},{9,25},{17,1},{25,9},{2,18},{10... | collective-permute-start | bytes 7520264 | tf_op jit(solution)/shard_map/ppermute | solution.py:497
  682.6 103.9 %collective-permute-start.15 = (bf16[4,136,2816]{2,1,0:T(8,128)(2,1)}, bf16[4,136,2816]{2,1,0:T(8,128)(2,1)}, u32[]{:S(2)}, u32[]{:S(2)}) collective-permute-start(bf16[4,136,2816]{2,1,0:T(8,128)(2,1)} %dynamic-slice_bitcast_fusion.2), channel_id=1, source_target_pairs={{0,8},{8,0},{16,24},{24,16},{1,9},{9,1},{17,25},{25,17},{2,10},{10... | collective-permute-start | bytes 9191432 | tf_op jit(solution)/shard_map/ppermute | solution.py:497
  693.9 51.5 %collective-permute-start.18 = (bf16[136,2176]{1,0:T(8,128)(2,1)S(1)}, bf16[136,2176]{1,0:T(8,128)(2,1)S(1)}, u32[]{:S(2)}, u32[]{:S(2)}) collective-permute-start(bf16[136,2176]{1,0:T(8,128)(2,1)S(1)} %get-tuple-element.179), channel_id=1, source_target_pairs={{0,6},{2,0},{4,2},{6,4},{1,7},{3,1},{5,3},{7,5},{8,14},{10,8},{12,... | collective-permute-start | bytes 1775624 | tf_op jit(solution)/shard_map/ppermute | solution.py:502
  731.6 51.7 %collective-permute-start.17 = (bf16[136,2176]{1,0:T(8,128)(2,1)S(1)}, bf16[136,2176]{1,0:T(8,128)(2,1)S(1)}, u32[]{:S(2)}, u32[]{:S(2)}) collective-permute-start(bf16[136,2176]{1,0:T(8,128)(2,1)S(1)} %get-tuple-element.180), channel_id=1, source_target_pairs={{0,4},{2,6},{4,0},{6,2},{1,5},{3,7},{5,1},{7,3},{8,12},{10,14},{12... | collective-permute-start | bytes 1775624 | tf_op jit(solution)/shard_map/ppermute | solution.py:502
  732.3 51.1 %collective-permute-start.16 = (bf16[136,2176]{1,0:T(8,128)(2,1)S(1)}, bf16[136,2176]{1,0:T(8,128)(2,1)S(1)}, u32[]{:S(2)}, u32[]{:S(2)}) collective-permute-start(bf16[136,2176]{1,0:T(8,128)(2,1)S(1)} %get-tuple-element.178), channel_id=1, source_target_pairs={{0,2},{2,4},{4,6},{6,0},{1,3},{3,5},{5,7},{7,1},{8,10},{10,12},{12... | collective-permute-start | bytes 1775624 | tf_op jit(solution)/shard_map/ppermute | solution.py:502
  736.3 126.3 %collective-permute-start.19 = (bf16[4,136,1152]{2,1,0:T(8,128)(2,1)}, bf16[4,136,1152]{2,1,0:T(8,128)(2,1)}, u32[]{:S(2)}, u32[]{:S(2)}) collective-permute-start(bf16[4,136,1152]{2,1,0:T(8,128)(2,1)} %broadcast_select_fusion.7), channel_id=1, source_target_pairs={{0,1},{1,0},{2,3},{3,2},{4,5},{5,4},{6,7},{7,6},{8,9},{9,8},{10,11... | collective-permute-start | bytes 3760136 | tf_op jit(solution)/shard_map/ppermute | solution.py:497
  784.5 82.4 %collective-permute-start.39 = (bf16[136,2176]{1,0:T(8,128)(2,1)}, bf16[136,2176]{1,0:T(8,128)(2,1)}, u32[]{:S(2)}, u32[]{:S(2)}) collective-permute-start(bf16[136,2176]{1,0:T(8,128)(2,1)} %fusion.35.refs_1_), channel_id=1, source_target_pairs={{0,16},{8,24},{16,0},{24,8},{1,17},{9,25},{17,1},{25,9},{2,18},{10... | collective-permute-start | bytes 1775624 | tf_op jit(solution)/shard_map/ppermute | solution.py:497
  796.5 100.7 %collective-permute-start.20 = (bf16[4,136,1152]{2,1,0:T(8,128)(2,1)S(1)}, bf16[4,136,1152]{2,1,0:T(8,128)(2,1)S(1)}, u32[]{:S(2)}, u32[]{:S(2)}) collective-permute-start(bf16[4,136,1152]{2,1,0:T(8,128)(2,1)S(1)} %broadcast_select_fusion.6), channel_id=1, source_target_pairs={{0,1},{1,0},{2,3},{3,2},{4,5},{5,4},{6,7},{7,6},{8,9},{9,8},{10,11... | collective-permute-start | bytes 3760136 | tf_op jit(solution)/shard_map/ppermute | solution.py:497
  864.5 27.5 %collective-permute-start.42 = (bf16[136,1152]{1,0:T(8,128)(2,1)S(1)}, bf16[136,1152]{1,0:T(8,128)(2,1)S(1)}, u32[]{:S(2)}, u32[]{:S(2)}) collective-permute-start(bf16[136,1152]{1,0:T(8,128)(2,1)S(1)} %get-tuple-element.185), channel_id=1, source_target_pairs={{0,4},{2,6},{4,0},{6,2},{1,5},{3,7},{5,1},{7,3},{8,12},{10,14},{12... | collective-permute-start | bytes 940040 | tf_op jit(solution)/shard_map/ppermute | solution.py:502
  892.3 63.3 %collective-permute-start.44 = (bf16[136,1152]{1,0:T(8,128)(2,1)S(1)}, bf16[136,1152]{1,0:T(8,128)(2,1)}, u32[]{:S(2)}, u32[]{:S(2)}) collective-permute-start(bf16[136,1152]{1,0:T(8,128)(2,1)S(1)} %fusion.49), channel_id=1, source_target_pairs={{0,16},{8,24},{16,0},{24,8},{1,17},{9,25},{17,1},{25,9},{2,18},{10... | collective-permute-start | bytes 940040 | tf_op jit(solution)/shard_map/ppermute | solution.py:497
  944.7 74.8 %collective-permute-start.21 = (bf16[1024,1088]{0,1:T(8,128)(2,1)}, bf16[1024,1088]{0,1:T(8,128)(2,1)}, u32[]{:S(2)}, u32[]{:S(2)}) collective-permute-start(bf16[1024,1088]{0,1:T(8,128)(2,1)} %copy.201), channel_id=1, source_target_pairs={{0,1},{1,0},{2,3},{3,2},{4,5},{5,4},{6,7},{7,6},{8,9},{9,8},{10,11... | collective-permute-start | bytes 6684680 | tf_op jit(solution)/shard_map/ppermute | solution.py:497
  951.7 47.4 %collective-permute-start.36 = (bf16[136,1152]{1,0:T(8,128)(2,1)S(1)}, bf16[136,1152]{1,0:T(8,128)(2,1)S(1)}, u32[]{:S(2)}, u32[]{:S(2)}) collective-permute-start(bf16[136,1152]{1,0:T(8,128)(2,1)S(1)} %get-tuple-element.187), channel_id=1, source_target_pairs={{0,6},{2,0},{4,2},{6,4},{1,7},{3,1},{5,3},{7,5},{8,14},{10,8},{12,... | collective-permute-start | bytes 940040 | tf_op jit(solution)/shard_map/ppermute | solution.py:502
  951.7 50.2 %collective-permute-start.35 = (bf16[136,1152]{1,0:T(8,128)(2,1)S(1)}, bf16[136,1152]{1,0:T(8,128)(2,1)S(1)}, u32[]{:S(2)}, u32[]{:S(2)}) collective-permute-start(bf16[136,1152]{1,0:T(8,128)(2,1)S(1)} %get-tuple-element.188), channel_id=1, source_target_pairs={{0,4},{2,6},{4,0},{6,2},{1,5},{3,7},{5,1},{7,3},{8,12},{10,14},{12... | collective-permute-start | bytes 940040 | tf_op jit(solution)/shard_map/ppermute | solution.py:502
  953.5 48.5 %collective-permute-start.34 = (bf16[136,1152]{1,0:T(8,128)(2,1)S(1)}, bf16[136,1152]{1,0:T(8,128)(2,1)S(1)}, u32[]{:S(2)}, u32[]{:S(2)}) collective-permute-start(bf16[136,1152]{1,0:T(8,128)(2,1)S(1)} %get-tuple-element.186), channel_id=1, source_target_pairs={{0,2},{2,4},{4,6},{6,0},{1,3},{3,5},{5,7},{7,1},{8,10},{10,12},{12... | collective-permute-start | bytes 940040 | tf_op jit(solution)/shard_map/ppermute | solution.py:502
  955.5 39.3 %collective-permute-start.24 = (f32[13056]{0:T(1024)S(1)}, f32[13056]{0:T(1024)S(1)}, u32[]{:S(2)}, u32[]{:S(2)}) collective-permute-start(f32[13056]{0:T(1024)S(1)} %add.428), channel_id=1, source_target_pairs={{0,1},{1,0},{2,3},{3,2},{4,5},{5,4},{6,7},{7,6},{8,9},{9,8},{10,11... | collective-permute-start | bytes 156680 | tf_op jit(solution)/shard_map/ppermute | solution.py:497
  (162 other events, 2265.0 us)
Sparse Core Ops, SparseCore 0:
  11.5 74.2 all-gather.6
  88.8 99.4 all-gather.8
  191.7 96.6 all-gather.10

commit v3 on v2

--- a/solution.py
+++ b/solution.py
@@ -10,6 +10,8 @@
 LOG2E = 1.4426950408889634
 NEG = -1e30
 BK = 512
+GROUP = 512
+epsilon = 1e-05
 
 
 def nt(a, b):
@@ -326,18 +328,55 @@
 TILE = 256
 
 
-def mlp_forward_kernel(act, resid, up, up_bias, down, down_bias, *rest):
-    hidden, slope, result, acc = rest[-4:]
+def row_chunks(rows, size=256):
+    return [slice(at, min(at + size, rows)) for at in range(0, rows, size)]
+
+
+def fixed(shape):
+    return pl.BlockSpec(shape, lambda *_: (0,) * len(shape), pipeline_mode=pl.Buffered(1))
+
+
+def steady(shape):
+    return pl.BlockSpec(shape, lambda *_: (0,) * len(shape))
+
+
+def store_halves(value, half, keep, give):
+    count, size = keep.shape[0], keep.shape[1]
+    for block in range(count):
+        first = value[2 * block * size : (2 * block + 1) * size, :]
+        second = value[(2 * block + 1) * size : (2 * block + 2) * size, :]
+        keep[block, :, :] = jnp.where(half == 0, first, second).astype(keep.dtype)
+        give[block, :, :] = jnp.where(half == 0, second, first).astype(give.dtype)
+
+
+def mlp_forward_kernel(
+    mixed_a, mixed_b, tokens, out_w, out_bias, gain, shift, up, up_bias, down, down_bias, *rest
+):
+    hidden, slope, result, act_turned, norm, pace, act, acc = rest[-8:]
     step = pl.program_id(0)
+    rows = tokens.shape[0]
+    first = mixed_a.shape[1]
 
     @pl.when(step == 0)
     def _():
-        acc[...] = resid[...] + down_bias[...]
-
-    rows = act.shape[0]
-    size = 256 if rows % 256 == 0 else rows
-    for start in range(0, rows, size):
-        here = slice(start, start + size)
+        for here in row_chunks(rows):
+            resid = (
+                tokens[here, :].astype(jnp.float32)
+                + nn(mixed_a[here, :], out_w[:first, :])
+                + nn(mixed_b[here, :], out_w[first:, :])
+                + out_bias[...]
+            )
+            centred = resid - jnp.mean(resid, axis=1, keepdims=True)
+            speed = lax.rsqrt(jnp.mean(centred * centred, axis=1, keepdims=True) + epsilon)
+            normed = centred * speed
+            acting = (normed * gain[...] + shift[...]).astype(jnp.bfloat16)
+            act[here, :] = acting
+            act_turned[:, here] = acting.T
+            norm[here, :] = normed.astype(norm.dtype)
+            pace[here, :] = jnp.broadcast_to(speed, (speed.shape[0], 128))
+            acc[here, :] = resid + down_bias[...]
+
+    for here in row_chunks(rows):
         pre = nn(act[here, :], up[...]) + up_bias[...]
         bell = jnp.exp(pre * pre * -0.5)
         t = 1.0 / (1.0 + (0.3275911 * 0.7071067811865476) * jnp.abs(pre))
@@ -356,99 +395,305 @@
         result[...] = acc[...].astype(result.dtype)
 
 
-def whole_block(shape):
-    return pl.BlockSpec(shape, lambda j: (0,) * len(shape))
-
-
-def mlp_forward(act, resid, up, up_bias, down, down_bias, after=()):
-    rows, width = act.shape
+def mlp_forward(
+    mixed, tokens, out_w, out_bias, gain, shift, up, up_bias, down, down_bias, after=()
+):
+    rows, width = tokens.shape
     inner = up.shape[1]
     column = pl.BlockSpec((width, TILE), lambda j: (0, j))
     tall = pl.BlockSpec((rows, TILE), lambda j: (0, j))
+    line = fixed((1, width))
+    like = jax.ShapeDtypeStruct
     return pl.pallas_call(
         mlp_forward_kernel,
         grid=(inner // TILE,),
         in_specs=[
-            whole_block((rows, width)),
-            whole_block((rows, width)),
+            fixed(mixed[0].shape),
+            fixed(mixed[1].shape),
+            fixed((rows, width)),
+            fixed((width, width)),
+            line,
+            line,
+            line,
             column,
             pl.BlockSpec((1, TILE), lambda j: (0, j)),
             column,
-            whole_block((1, width)),
+            line,
         ]
         + [pl.BlockSpec(memory_space=pl.ANY)] * len(after),
-        out_specs=[tall, tall, whole_block((rows, width))],
+        out_specs=[
+            tall,
+            tall,
+            steady((rows, width)),
+            steady((width, rows)),
+            steady((rows, width)),
+            steady((rows, 128)),
+        ],
         out_shape=[
-            jax.ShapeDtypeStruct((rows, inner), jnp.bfloat16),
-            jax.ShapeDtypeStruct((rows, inner), jnp.bfloat16),
-            jax.ShapeDtypeStruct((rows, width), jnp.bfloat16),
+            like((rows, inner), jnp.bfloat16),
+            like((rows, inner), jnp.bfloat16),
+            like((rows, width), jnp.bfloat16),
+            like((width, rows), jnp.bfloat16),
+            like((rows, width), jnp.bfloat16),
+            like((rows, 128), jnp.float32),
         ],
-        scratch_shapes=[pltpu.VMEM((rows, width), jnp.float32)],
+        scratch_shapes=[pltpu.VMEM((rows, width), jnp.bfloat16), pltpu.VMEM((rows, width), jnp.float32)],
         compiler_params=pltpu.CompilerParams(
-            dimension_semantics=("arbitrary",), vmem_limit_bytes=44 * 2**20
+            dimension_semantics=("arbitrary",), vmem_limit_bytes=52 * 2**20
         ),
-        cost_estimate=busy(40),
+        cost_estimate=busy(50),
         name="mlp_forward",
-    )(act, resid, up, up_bias.reshape(1, inner), down, down_bias.reshape(1, width), *after)
-
-
-def mlp_backward_kernel(act, cot, hidden, slope, up, down, *rest):
-    d_act, up_grad, down_grad, bias_grad, act_turned, cot_turned = rest[-6:]
+    )(
+        *mixed,
+        tokens,
+        out_w,
+        *(v.reshape(1, width) for v in (out_bias, gain, shift)),
+        up,
+        up_bias.reshape(1, inner),
+        down,
+        down_bias.reshape(1, width),
+        *after,
+    )
+
+
+def mlp_backward_kernel(
+    half, act_turned, cot, norm, pace, gain, mixed_a, mixed_b, out_w, hidden, slope, up, down, *rest
+):
+    outs = rest[-14:]
+    d_resid, d_mixed_a, d_mixed_b, up_keep, up_give, down_keep, down_give, out_keep, out_give = outs[:9]
+    bias_grad, lines, cot_turned, d_branch, piece = outs[9:]
     step = pl.program_id(0)
+    rows, width = cot.shape
+    first = mixed_a.shape[1]
 
     @pl.when(step == 0)
     def _():
-        act_turned[...] = act[...].T
         cot_turned[...] = cot[...].T
-        d_act[...] = jnp.zeros_like(d_act)
-
-    rows = act.shape[0]
-    size = 256 if rows % 256 == 0 else rows
+        d_resid[...] = jnp.zeros_like(d_resid)
+
     bias = jnp.zeros((1, TILE), jnp.float32)
     pieces = []
-    for start in range(0, rows, size):
-        here = slice(start, start + size)
+    for here in row_chunks(rows):
         d_pre = (nn(cot[here, :], down[...]) * slope[here, :].astype(jnp.float32)).astype(jnp.bfloat16)
         bias = bias + jnp.sum(d_pre.astype(jnp.float32), axis=0, keepdims=True)
-        d_act[here, :] += nt(d_pre, up[...])
+        d_resid[here, :] += nt(d_pre, up[...])
         pieces.append(d_pre)
     bias_grad[...] = bias
-    up_grad[...] = nn(act_turned[...], jnp.concatenate(pieces, axis=0)).astype(jnp.bfloat16)
-    down_grad[...] = nn(cot_turned[...], hidden[...]).astype(jnp.bfloat16)
-
-
-def mlp_backward(act, cot, hidden, slope, up, down, after=()):
-    rows, width = act.shape
+    store_halves(nn(act_turned[...], jnp.concatenate(pieces, axis=0)), half[0], up_keep, up_give)
+    store_halves(nn(cot_turned[...], hidden[...]), half[0], down_keep, down_give)
+
+    @pl.when(step == pl.num_programs(0) - 1)
+    def _():
+        sums = [jnp.zeros((1, width), jnp.float32)] * 4
+        for here in row_chunks(rows):
+            grad = d_resid[here, :]
+            normed = norm[here, :].astype(jnp.float32)
+            scaled = grad * gain[...]
+            inner = (
+                scaled
+                - jnp.mean(scaled, axis=1, keepdims=True)
+                - normed * jnp.mean(scaled * normed, axis=1, keepdims=True)
+            )
+            exact = cot[here, :].astype(jnp.float32)
+            total = exact + pace[here, 0:1] * inner
+            d_resid[here, :] = total
+            rounded = total.astype(jnp.bfloat16)
+            d_branch[here, :] = rounded
+            d_mixed_a[here, :] = nt(rounded, out_w[:first, :]).astype(d_mixed_a.dtype)
+            d_mixed_b[here, :] = nt(rounded, out_w[first:, :]).astype(d_mixed_b.dtype)
+            for n, term in enumerate((grad * normed, grad, rounded.astype(jnp.float32), exact)):
+                sums[n] = sums[n] + jnp.sum(term, axis=0, keepdims=True)
+        for n in range(4):
+            lines[n : n + 1, :] = sums[n]
+        for columns in row_chunks(width):
+            size = columns.stop - columns.start
+            piece[:first, :size] = tn(mixed_a[...], d_branch[:, columns])
+            piece[first:, :size] = tn(mixed_b[...], d_branch[:, columns])
+            value = piece[:, :size]
+            store_halves(value, half[0], out_keep.at[:, :, columns], out_give.at[:, :, columns])
+
+
+def mlp_backward(half, count, act_turned, cot, norm, pace, gain, mixed, out_w, hidden, slope, up, down):
+    rows, width = cot.shape
     inner = up.shape[1]
-    column = pl.BlockSpec((width, TILE), lambda j: (0, j))
-    tall = pl.BlockSpec((rows, TILE), lambda j: (0, j))
+    block = width // count // 2
+    column = pl.BlockSpec((width, TILE), lambda j, half: (0, j))
+    tall = pl.BlockSpec((rows, TILE), lambda j, half: (0, j))
+    split = pl.BlockSpec((count, block, TILE), lambda j, half: (0, 0, j))
+    like = jax.ShapeDtypeStruct
     return pl.pallas_call(
         mlp_backward_kernel,
-        grid=(inner // TILE,),
-        in_specs=[whole_block((rows, width)), whole_block((rows, width)), tall, tall, column, column]
-        + [pl.BlockSpec(memory_space=pl.ANY)] * len(after),
-        out_specs=[
-            whole_block((rows, width)),
-            column,
-            column,
-            pl.BlockSpec((1, TILE), lambda j: (0, j)),
-        ],
-        out_shape=[
-            jax.ShapeDtypeStruct((rows, width), jnp.float32),
-            jax.ShapeDtypeStruct((width, inner), jnp.bfloat16),
-            jax.ShapeDtypeStruct((width, inner), jnp.bfloat16),
-            jax.ShapeDtypeStruct((1, inner), jnp.float32),
-        ],
-        scratch_shapes=[
-            pltpu.VMEM((width, rows), jnp.bfloat16),
-            pltpu.VMEM((width, rows), jnp.bfloat16),
-        ],
+        grid_spec=pltpu.PrefetchScalarGridSpec(
+            num_scalar_prefetch=1,
+            grid=(inner // TILE,),
+            in_specs=[
+                fixed((width, rows)),
+                fixed((rows, width)),
+                fixed((rows, width)),
+                fixed((rows, 128)),
+                fixed((1, width)),
+                fixed(mixed[0].shape),
+                fixed(mixed[1].shape),
+                fixed((width, width)),
+                tall,
+                tall,
+                column,
+                column,
+            ],
+            out_specs=[
+                steady((rows, width)),
+                steady(mixed[0].shape),
+                steady(mixed[1].shape),
+                split,
+                split,
+                split,
+                split,
+                steady((count, block, width)),
+                steady((count, block, width)),
+                pl.BlockSpec((1, TILE), lambda j, half: (0, j)),
+                steady((8, width)),
+            ],
+            scratch_shapes=[
+                pltpu.VMEM((width, rows), jnp.bfloat16),
+                pltpu.VMEM((rows, width), jnp.bfloat16),
+                pltpu.VMEM((width, TILE), jnp.float32),
+            ],
+        ),
+        out_shape=[like((rows, width), jnp.float32)]
+        + [like(m.shape, jnp.bfloat16) for m in mixed]
+        + [like((count, block, inner), jnp.bfloat16)] * 4
+        + [like((count, block, width), jnp.bfloat16)] * 2
+        + [like((1, inner), jnp.float32), like((8, width), jnp.float32)],
         compiler_params=pltpu.CompilerParams(
-            dimension_semantics=("arbitrary",), vmem_limit_bytes=48 * 2**20
+            dimension_semantics=("arbitrary",), vmem_limit_bytes=58 * 2**20
         ),
-        cost_estimate=busy(60),
+        cost_estimate=busy(80),
         name="mlp_backward",
-    )(act, cot, hidden, slope, up, down, *after)
+    )(half, act_turned, cot, norm, pace, gain.reshape(1, width), *mixed, out_w, hidden, slope, up, down)
+
+
+def projection_tiles(widths):
+    first, second = (pl.cdiv(w, TILE) for w in widths)
+    return first, second, [
+        lambda t, *_: jnp.minimum(t, first - 1),
+        lambda t, *_: jnp.maximum(t - first, 0),
+    ]
+
+
+def tile_of(ref, place, width):
+    value = ref[...]
+    if width % TILE == 0:
+        return value
+    lane = lax.broadcasted_iota(jnp.int32, (1, TILE), 1)
+    return jnp.where(lane < width - place * TILE, value, jnp.zeros((), value.dtype))
+
+
+def tokens_back_kernel(*refs, widths):
+    grads, weights = (refs[0:3], refs[3:6]), (refs[6:9], refs[9:12])
+    out, acc = refs[-2:]
+    step = pl.program_id(0)
+    first, second, _ = projection_tiles(widths)
+
+    @pl.when(step == 0)
+    def _():
+        acc[...] = jnp.zeros_like(acc)
+
+    for group in range(2):
+
+        @pl.when(step < first if group == 0 else step >= first)
+        def _():
+            place = step if group == 0 else step - first
+            weight = jnp.concatenate([tile_of(w, place, widths[group]) for w in weights[group]], axis=1)
+            lane = lax.broadcasted_iota(jnp.int32, (1, TILE), 1)
+            for here in row_chunks(acc.shape[0]):
+                parts = []
+                for ref in grads[group]:
+                    part = ref[here, :]
+                    if widths[group] % TILE:
+                        part = jnp.where(lane < widths[group] - place * TILE, part, jnp.zeros((), part.dtype))
+                    parts.append(part)
+                acc[here, :] += nt(jnp.concatenate(parts, axis=1), weight)
+
+    @pl.when(step == pl.num_programs(0) - 1)
+    def _():
+        out[...] = acc[...].astype(out.dtype)
+
+
+def tokens_back(grads, weights, after=()):
+    total = grads[0][0].shape[0]
+    width = weights[0][0].shape[0]
+    widths = [group[0].shape[1] for group in grads]
+    first, second, places = projection_tiles(widths)
+
+    def tiles(rows):
+        return [pl.BlockSpec((rows, TILE), lambda t, at=at: (0, at(t))) for at in places for _ in range(3)]
+
+    return pl.pallas_call(
+        functools.partial(tokens_back_kernel, widths=widths),
+        grid=(first + second,),
+        in_specs=tiles(total) + tiles(width) + [pl.BlockSpec(memory_space=pl.ANY)] * len(after),
+        out_specs=steady((total, width)),
+        out_shape=jax.ShapeDtypeStruct((total, width), jnp.bfloat16),
+        scratch_shapes=[pltpu.VMEM((total, width), jnp.float32)],
+        compiler_params=pltpu.CompilerParams(
+            dimension_semantics=("arbitrary",), vmem_limit_bytes=52 * 2**20
+        ),
+        cost_estimate=busy(20),
+        name="tokens_back",
+    )(*grads[0], *grads[1], *weights[0], *weights[1], *after)
+
+
+def weights_back_kernel(half, turned, *refs, widths):
+    grads = (refs[0:3], refs[3:6])
+    outs = refs[-16:]
+    step = pl.program_id(0)
+    first, second, _ = projection_tiles(widths)
+    for group in range(2):
+        keeps = outs[group * 8 : group * 8 + 3]
+        gives = outs[group * 8 + 3 : group * 8 + 6]
+        biases = outs[group * 8 + 6 : group * 8 + 8]
+
+        @pl.when(step < first if group == 0 else step >= first)
+        def _():
+            for kind in range(3):
+                part = grads[group][kind][...]
+                store_halves(nn(turned[...], part), half[0], keeps[kind], gives[kind])
+                if kind != 1:
+                    biases[kind // 2][...] = jnp.sum(part.astype(jnp.float32), axis=0, keepdims=True)
+
+
+def weights_back(half, count, turned, grads, after=()):
+    width, total = turned.shape
+    widths = [group[0].shape[1] for group in grads]
+    first, second, places = projection_tiles(widths)
+    block = width // count // 2
+    like = jax.ShapeDtypeStruct
+    out_specs, out_shape = [], []
+    for at, w in zip(places, widths):
+        out_specs += [pl.BlockSpec((count, block, TILE), lambda t, half, at=at: (0, 0, at(t)))] * 6
+        out_specs += [pl.BlockSpec((1, TILE), lambda t, half, at=at: (0, at(t)))] * 2
+        out_shape += [like((count, block, w), jnp.bfloat16)] * 6 + [like((1, w), jnp.float32)] * 2
+    return pl.pallas_call(
+        functools.partial(weights_back_kernel, widths=widths),
+        grid_spec=pltpu.PrefetchScalarGridSpec(
+            num_scalar_prefetch=1,
+            grid=(first + second,),
+            in_specs=[fixed((width, total))]
+            + [
+                pl.BlockSpec((total, TILE), lambda t, half, at=at: (0, at(t)))
+                for at in places
+                for _ in range(3)
+            ]
+            + [pl.BlockSpec(memory_space=pl.ANY)] * len(after),
+            out_specs=out_specs,
+        ),
+        out_shape=out_shape,
+        compiler_params=pltpu.CompilerParams(
+            dimension_semantics=("arbitrary",), vmem_limit_bytes=52 * 2**20
+        ),
+        cost_estimate=busy(20),
+        name="weights_back",
+    )(half, turned, *grads[0], *grads[1], *after)
 
 
 def gate_kernel(*refs):
@@ -468,11 +713,6 @@
         cost_estimate=busy(1),
         name="gate",
     )(value, *after)
-
-
-GROUP = 512
-
-epsilon = 1e-05
 
 
 def normalise(values_in):
@@ -616,42 +856,28 @@
     return wholes, own
 
 
-def core_step(whole):
-    count = lax.axis_size("gx")
-    rows, columns = whole.shape
-    pieces = whole.reshape(count, 2, rows // count // 2, columns)
-    half = half_index()
-    keep = lax.dynamic_index_in_dim(pieces, half, 1, False)
-    give = lax.dynamic_index_in_dim(pieces, 1 - half, 1, False)
+def core_step(keep, give):
     return add(keep, swap(give, "dp", 1))
+
+
+def both_halves(keep, give):
+    count, size, columns = keep.shape
+    return jnp.stack([keep, give], axis=1).reshape(2 * count * size, columns)
 
 
 def add(a, b):
     return (a.astype(jnp.float32) + b.astype(jnp.float32)).astype(jnp.bfloat16)
 
 
-def halves_step(value, axis, bit, here):
-    size = value.shape[-1] // 2
-    first, second = value[..., :size], value[..., size:]
-    own_first = here == 0
-    keep = jnp.where(own_first, first, second)
-    give = jnp.where(own_first, second, first)
-    return add(keep, swap(give, axis, bit))
-
-
-def columns_step(value):
-    return halves_step(value, "gy", 1, lax.axis_index("gy"))
-
-
-def overlap_step(value):
-    columns = value.shape[-1] // 2
-    size = pl.cdiv(columns // 128, 2) * 128
+def overlap_step(sides):
+    columns = sides[0].shape[-1]
+    size = pl.cdiv(pl.cdiv(columns, 128), 2) * 128
+    own_first = lax.axis_index("dp") // 2 == 0
     first, second = (
-        jnp.concatenate([value[..., at : at + size], value[..., columns + at : columns + at + size]], axis=-1)
-        for at in (0, columns - size)
-    )
-    own_first = lax.axis_index("dp") // 2 == 0
-    return add(jnp.where(own_first, first, second), swap(jnp.where(own_first, second, first), "dp", 2))
+        jnp.concatenate([side[..., at : at + size] for side in sides], axis=-1) for at in (0, columns - size)
+    )
+    done = add(jnp.where(own_first, first, second), swap(jnp.where(own_first, second, first), "dp", 2))
+    return done[..., :size], done[..., size:]
 
 
 def overlap_join(value, columns):
@@ -691,34 +917,31 @@
     return add(keep, swap(jnp.where(first_side, second, first), "gy", 1))
 
 
-def rest_exchange(rest_flow, out_flow, width):
+def projection_sides(first, rest, width):
+    size = width - GROUP
+    spare = width // 2 - GROUP
+    query, key, value = first
+    query_rest, key_rest, value_rest = rest
+    return (
+        jnp.concatenate([query, key, query_rest, key_rest[..., :spare]], axis=-1),
+        jnp.concatenate(
+            [value, key_rest[..., spare : size - spare], value_rest, key_rest[..., size - spare :]], axis=-1
+        ),
+    )
+
+
+def join_projections(whole, width):
     rest = width - GROUP
-    spare = width // 2 - GROUP
-    query, key, value = (rest_flow[..., rest * kind : rest * (kind + 1)] for kind in range(3))
-    return side_exchange(
-        jnp.concatenate([query, key[..., :spare], out_flow[..., : width // 2]], axis=-1),
-        jnp.concatenate([value, key[..., rest - spare :], out_flow[..., width // 2 :]], axis=-1),
-    )
-
-
-def first_exchange(first_flow, rest_flow, width):
-    rest = width - GROUP
-    spare = width // 2 - GROUP
-    query, key, value = (first_flow[..., GROUP * kind : GROUP * (kind + 1)] for kind in range(3))
-    return side_exchange(
-        jnp.concatenate([query, key], axis=-1),
-        jnp.concatenate([value, rest_flow[..., rest + spare : 2 * rest - spare]], axis=-1),
-    )
-
-
-def join_projections(first, second, width):
-    rest = width - GROUP
-    one, two = first[:, :GROUP], first[:, GROUP:]
-    three, four = second[:, :rest], second[:, rest:]
+    pieces = [
+        whole[:, :GROUP],
+        whole[:, GROUP : 2 * GROUP],
+        whole[:, 2 * GROUP : 2 * GROUP + rest],
+        whole[:, 2 * GROUP + rest :],
+    ]
     return jnp.where(
         lax.axis_index("gy") == 0,
-        jnp.concatenate([one, three, two, four], axis=1),
-        jnp.concatenate([two, four, one, three], axis=1),
+        jnp.concatenate([pieces[n] for n in (0, 2, 1, 3)], axis=1),
+        jnp.concatenate([pieces[n] for n in (1, 3, 0, 2)], axis=1),
     )
 
 
@@ -748,7 +971,7 @@
         ).astype(jnp.float32)
     give = lax.dynamic_slice_in_dim(whole, (1 - here) * rows, rows, 0)
     keep = lax.dynamic_slice_in_dim(whole, here * rows, rows, 0)
-    return keep + swap(give.astype(jnp.bfloat16), "gy", 1).astype(jnp.float32)
+    return keep.astype(jnp.float32) + swap(give.astype(jnp.bfloat16), "gy", 1).astype(jnp.float32)
 
 
 def dot(a, b):
@@ -841,89 +1064,109 @@
         mixed.append(got)
         stats.append(stat)
 
-    token_rows = jnp.concatenate(
+    tokens = jnp.concatenate(
         [lax.dynamic_slice_in_dim(whole_prompt, places[n], block, 0) for n in range(2)] + [branch], axis=0
-    ).astype(jnp.float32)
-    resid = token_rows + (sum(dot(m, out_full[c]) for m, c in zip(mixed, spans)) + out_bias)
-    norm_two, pace_two = normalise(resid)
-    act_two = (norm_two * mlp_gain + mlp_shift).astype(jnp.bfloat16)
-    hidden, slope, result = mlp_forward(act_two, resid, up_full, up_bias, down_full, down_bias)
+    )
+    hidden, slope, result, act_turned, norm_two, pace_two = mlp_forward(
+        mixed, tokens, out_full, out_bias, mlp_gain, mlp_shift, up_full, up_bias, down_full, down_bias
+    )
     prompt_out = back_home(result[:shard]).reshape(groups, shard, width)
     continuation_out = result[shard:].reshape(1, length, width)
 
-    cot_exact = cotangent.astype(jnp.float32)
-    down_bias_grad = jnp.sum(cot_exact, axis=0)
-    d_act_two, up_grad, down_grad, up_bias_grad = mlp_backward(
-        act_two, cotangent, hidden, slope, up_full, down_full
-    )
-    up_bias_grad = up_bias_grad.reshape(-1)
+    count = lax.axis_size("gx")
+    half = jnp.reshape(half_index() if halved else 0, (1,)).astype(jnp.int32)
+    (
+        d_resid,
+        *d_mixed,
+        up_keep,
+        up_give,
+        down_keep,
+        down_give,
+        out_keep,
+        out_give,
+        up_bias_grad,
+        lines,
+    ) = mlp_backward(
+        half,
+        count,
+        act_turned,
+        cotangent,
+        norm_two,
+        pace_two,
+        mlp_gain,
+        mixed,
+        out_full,
+        hidden,
+        slope,
+        up_full,
+        down_full,
+    )
+    mlp_gain_grad, mlp_shift_grad, out_bias_grad, down_bias_grad = (lines[n] for n in range(4))
     after = ()
     if halved:
-        up_flow, down_flow = core_step(up_grad), core_step(down_grad)
-        after = (up_flow, down_flow)
-    mlp_gain_grad = jnp.sum(d_act_two * norm_two, axis=0)
-    mlp_shift_grad = jnp.sum(d_act_two, axis=0)
-    d_resid = cot_exact + norm_back(d_act_two, norm_two, pace_two, mlp_gain)
-    d_branch = d_resid.astype(jnp.bfloat16)
-    out_grad = jnp.concatenate([tn(m, d_branch) for m in mixed], axis=0).astype(jnp.bfloat16)
-    out_bias_grad = jnp.sum(d_branch.astype(jnp.float32), axis=0)
-    d_act_all = 0.0
-    grads, flows, bias_grads = [None, None], [None, None], [None, None]
+        up_flow, down_flow, out_flow = (
+            core_step(*pair)
+            for pair in ((up_keep, up_give), (down_keep, down_give), (out_keep, out_give))
+        )
+        after = (up_flow, down_flow, out_flow)
+    d_parts = [None, None]
     for number in (1, 0):
-        cols = spans[number]
-        d_mixed = nt(d_branch, out_full[cols]).astype(jnp.bfloat16)
-        d_parts = list(
-            attention_backward(
-                places, *projected[number], mixed[number], d_mixed, stats[number], block, length, after
+        d_parts[number] = attention_backward(
+            places, *projected[number], mixed[number], d_mixed[number], stats[number], block, length, after
+        )
+        if halved and number == 1:
+            side = up_weight.shape[1]
+            up_flow = side_exchange(
+                jnp.concatenate([up_flow[..., :side], out_flow[..., : width // 2]], axis=-1),
+                jnp.concatenate([up_flow[..., side:], out_flow[..., width // 2 :]], axis=-1),
+            )
+            down_sides = overlap_step((down_flow[..., :side], down_flow[..., side:]))
+            after = (up_flow, *down_sides)
+        if halved and number == 0:
+            up_flow, down_flow = blocks_step(up_flow), side_exchange(*down_sides)
+            after = (up_flow, down_flow)
+    d_act_all = tokens_back(d_parts, weights, after)
+    shared = own_tokens_sum(d_act_all[:prompt_len])
+    grads = weights_back(half, count, act_all.T, d_parts, (d_act_all,))
+    keeps, gives = (grads[0:3], grads[8:11]), (grads[3:6], grads[11:14])
+    query_bias_grad, value_bias_grad = (
+        jnp.concatenate([grads[6 + n], grads[14 + n]], axis=1).reshape(-1) for n in range(2)
+    )
+    if halved:
+        sides = [
+            core_step(keep, give)
+            for keep, give in zip(projection_sides(*keeps, width), projection_sides(*gives, width))
+        ]
+        qkv_flow = side_exchange(*overlap_step(sides))
+        qkv_total = join_projections(
+            join_step(overlap_join(blocks_step(qkv_flow), qkv_weight.shape[1])),
+            width,
+        )
+        up_total = join_step(copies_step(up_flow))
+        up_total, out_total = up_total[:, :side], up_total[:, side:]
+        down_total = join_step(overlap_join(blocks_step(down_flow), side))
+    else:
+        qkv_grad = jnp.concatenate(
+            [both_halves(keeps[n][kind], gives[n][kind]) for kind in range(3) for n in range(2)], axis=1
+        )
+        up_total, down_total, out_total, qkv_total = (
+            scatter_plain(g)
+            for g in (
+                both_halves(up_keep, up_give),
+                both_halves(down_keep, down_give),
+                both_halves(out_keep, out_give),
+                qkv_grad,
             )
         )
-        if halved and number == 0:
-            d_parts[0] = gate(d_parts[0], (up_flow, down_flow, rest_flow))
-        for d_part, weight in zip(d_parts, weights[number]):
-            d_act_all = d_act_all + nt(d_part, weight)
-        grads[number] = jnp.concatenate([tn(act_all, d).astype(jnp.bfloat16) for d in d_parts], axis=1)
-        bias_grads[number] = [jnp.sum(d_parts[n].astype(jnp.float32), axis=0) for n in (0, 2)]
-        if halved and number == 1:
-            joint = core_step(jnp.concatenate([grads[1], out_grad], axis=1))
-            flows[1], out_flow = joint[..., :-width], joint[..., -width:]
-            up_flow, down_flow = columns_step(up_flow), overlap_step(down_flow)
-            after = (up_flow, down_flow, joint)
-            up_flow, down_flow = blocks_step(up_flow), columns_step(down_flow)
-            rest_flow = rest_exchange(flows[1], out_flow, width)
-    shared = own_tokens_sum(d_act_all[:prompt_len])
-    if halved:
-        flows[0] = core_step(grads[0])
-        first_flow = first_exchange(flows[0], flows[1], width)
-        up_total = join_step(copies_step(up_flow))
-        down_total = join_step(overlap_join(blocks_step(down_flow), up_weight.shape[1]))
-        first_total, rest_total = (
-            join_step(copies_step(blocks_step(f))) for f in (first_flow, rest_flow)
-        )
-        qkv_total = join_projections(first_total, rest_total[:, : -(width // 2)], width)
-        out_total = rest_total[:, -(width // 2) :]
-    else:
-        qkv_grad = jnp.concatenate(
-            [
-                grads[n][:, kind * (c.stop - c.start) : (kind + 1) * (c.stop - c.start)]
-                for kind in range(3)
-                for n, c in enumerate(spans)
-            ],
-            axis=1,
-        )
-        up_total, down_total, out_total, qkv_total = (
-            scatter_plain(g) for g in (up_grad, down_grad, out_grad, qkv_grad)
-        )
-    query_bias_grad, value_bias_grad = (
-        jnp.concatenate([bias_grads[n][kind] for n in range(2)]) for kind in range(2)
-    )
-    attn_gain_grad = jnp.sum(d_act_all * norm_all, axis=0)
-    attn_shift_grad = jnp.sum(d_act_all, axis=0)
+    d_act_exact = d_act_all.astype(jnp.float32)
+    attn_gain_grad = jnp.sum(d_act_exact * norm_all, axis=0)
+    attn_shift_grad = jnp.sum(d_act_exact, axis=0)
     norm_own, pace_own = normalise(jnp.concatenate([own_prompt, branch], axis=0).astype(jnp.float32))
     d_act_own = jnp.concatenate([shared, d_act_all[prompt_len:]], axis=0)
     rows_part = norm_back(d_act_own, norm_own, pace_own, attn_gain)
     prompt_resid = d_resid[:shard]
     if halved:
-        home = back_home(d_branch[:shard]).astype(jnp.float32)
+        home = back_home(prompt_resid.astype(jnp.bfloat16)).astype(jnp.float32)
         kept = jnp.where(is_long, prompt_resid[:block], home[:block]), jnp.where(
             is_long, home[block:], prompt_resid[:block]
         )
@@ -939,7 +1182,7 @@
         out_bias_grad,
         mlp_gain_grad,
         mlp_shift_grad,
-        up_bias_grad,
+        up_bias_grad.reshape(-1),
         down_bias_grad,
     )
     joined = total_over(jnp.concatenate(vectors), ("dp", "gy", "gx"))

time: 1110 us -> 995 us (0.90)
  matrix products: 145 us -> 34.3 us
  Pallas kernels: 304 us -> 391 us
  local copies, waits for them, and re-layouts: 168 us -> 132 us
  waiting for transfers between devices: 244 us -> 211 us
  other arithmetic: 133 us -> 119 us
    dot_general x16 -> x0, matrix products: 106 us -> none  [the longest x8 54.8 us: nt(): lax.dot_general(a, b, (((1,), (1,)), ((), ())), preferred_element_type=jn...]
    pallas_call x2 -> x4, Pallas kernels: 126 us -> 211 us  [the longest x1 87.8 us: mlp_backward(): pl.pallas_call(mlp_backward_kernel, grid_spec=pltpu.PrefetchScalarGridSpe...]
    ppermute x15 -> x12, waiting for transfers between devices: 101 us -> 27.2 us  [ahead(): lax.ppermute(value, axis, [(i, (i + step) % count) for i in range(count)])]
    ppermute x31 -> x30, waiting for transfers between devices: 143 us -> 184 us  [swap(): return lax.ppermute(value, axis, [(i, i ^ bit) for i in range(count)])]
    unnamed x298 -> x212, local copies, waits for them, and re-layouts: 47.4 us -> 26.7 us
    pallas_call x0 -> x3, local copies, waits for them, and re-layouts: none -> 19.9 us  [the longest x1 8.46 us: tokens_back(): pl.pallas_call(functools.partial(tokens_back_kernel, widths=widths), grid...]
    squeeze x4 -> x0, local copies, waits for them, and re-layouts: 13.9 us -> none  [core_step(): give = lax.dynamic_index_in_dim(pieces, 1 - half, 1, False)]
    convert_element_type x6 -> x0, local copies, waits for them, and re-layouts: 12.2 us -> none  [the longest x3 7.8 us: local(): tn(act_all, d).astype(jnp.bfloat16)]
  transfers between devices with their start and end apart: 49 -> 45, of which waited for: 15 -> 15; matrix products, arithmetic and copies ran while one was open for 33% -> 25% of each run, Pallas kernels for 11% -> 24%
where the time goes in v3:
time: 995 us; the launch traced here: 983 us
  Pallas kernels  391 us (39%)
  waiting for transfers between devices  211 us (21%)
  local copies, waits for them, and re-layouts  132 us (13%)
  other arithmetic  119 us (12%)
  starting transfers between devices  77.7 us (8%)
  matrix products  34.3 us (3%)
  between operations  17.9 us (2%)
    ppermute x30, waiting for transfers between devices, swap(): return lax.ppermute(value, axis, [(i, i ^ bit) for i in range(count)])  184 us
    pallas_call x2, Pallas kernels, attention_backward(): pl.pallas_call(functools.partial(backward_kernel, block=block, branch=bra...  109 us
    pallas_call x1, Pallas kernels, mlp_backward(): pl.pallas_call(mlp_backward_kernel, grid_spec=pltpu.PrefetchScalarGridSpe...  87.8 us
    pallas_call x2, Pallas kernels, attention_forward(): pl.pallas_call(functools.partial(forward_kernel, block=block, branch=bran...  71.4 us
    pallas_call x1, Pallas kernels, mlp_forward(): pl.pallas_call(mlp_forward_kernel, grid=(inner // TILE,), in_specs=[fixed...  63.1 us
    ppermute x12, starting transfers between devices, ahead(): lax.ppermute(value, axis, [(i, (i + step) % count) for i in range(count)])  52 us
    dot_general x6, matrix products, dot(): return jnp.dot(a, b, preferred_element_type=jnp.float32)  34.3 us
    pallas_call x1, Pallas kernels, tokens_back(): pl.pallas_call(functools.partial(tokens_back_kernel, widths=widths), grid...  32.4 us
  transfers between devices with their start and end apart: 45, of which 15 were waited for; matrix products, arithmetic and copies ran while one was open for 25% of the time, Pallas kernels for 24%

profile of v3, /device:TPU:0, one launch (start us, length us, event | category | flops | bytes accessed | tf_op | source)
XLA Modules:
  0.0 982.9 jit_solution(9702428945192560429)
XLA Ops:
  27.5 49.4 %collective-permute-done = s32[1]{0:T(128)} collective-permute-done((s32[1]{0:T(128)}, s32[1]{0:T(128)}, u32[]{:S(2)}, u32[]{:S(2)}) %collective-permute-start) | collective-permute-done | bytes 36 | tf_op jit(solution)/shard_map/ppermute | solution.py:737
  94.5 5.4 copy.104.tokens
  100.0 5.6 fusion.4
  120.2 6.0 fusion.19.v
  126.2 6.9 fusion.18.q
  139.5 16.8 %collective-permute-done.3 = bf16[272,1152]{1,0:T(8,128)(2,1)} collective-permute-done((bf16[272,1152]{1,0:T(8,128)(2,1)}, bf16[272,1152]{1,0:T(8,128)(2,1)}, u32[]{:S(2)}, u32[]{:S(2)}) %collective-permute-start.3) | collective-permute-done | bytes 626720 | tf_op jit(solution)/shard_map/ppermute | solution.py:742
  161.1 31.8 %attention_forward.2 = (bf16[1280,512]{1,0:T(8,128)(2,1)S(1)}, f32[4,8,1280]{2,1,0:T(8,128)S(1)}) custom-call(s32[3]{0:T(128)S(1)} %pad_add_fusion.pos, bf16[2304,512]{1,0:T(8,128)(2,1)S(1)} %fusion.18.q, bf16[2304,512]{1,0:T(8,128)(2,1)S(1)} %convolution_convert_fusion.1.k, bf16[2304,512]{1,0:T(8,128)(2,1)S(1)} %fusion.19.v), custom_call_target="tpu_custom_call" | custom-call | flops 28000000000 | bytes 28000000 | tf_op jit(solution)/shard_map/attention_forward/pallas_call | solution.py:169
  200.3 28.9 %collective-permute-done.5 = bf16[1088,1152]{1,0:T(8,128)(2,1)} collective-permute-done((bf16[1088,1152]{1,0:T(8,128)(2,1)S(1)}, bf16[1088,1152]{1,0:T(8,128)(2,1)}, u32[]{:S(2)}, u32[]{:S(2)}) %collective-permute-start.5) | collective-permute-done | bytes 2506784 | tf_op jit(solution)/shard_map/ppermute | solution.py:737
  240.6 8.0 convolution_convert_fusion.k
  248.7 4.9 add_convert_fusion.3.v
  253.6 4.9 add_convert_fusion.4.q
  258.6 39.6 %attention_forward.3 = (bf16[1280,576]{1,0:T(8,128)(2,1)S(1)}, f32[5,8,1280]{2,1,0:T(8,128)S(1)}) custom-call(s32[3]{0:T(128)S(1)} %pad_add_fusion.pos, bf16[2304,576]{1,0:T(8,128)(2,1)S(1)} %add_convert_fusion.4.q, bf16[2304,576]{1,0:T(8,128)(2,1)S(1)} %convolution_convert_fusion.k, bf16[2304,576]{1,0:T(8,128)(2,1)S(1)} %add_convert_fusion.3.v, ...), custom_call_target="tpu_custom_call" | custom-call | flops 35000000512 | bytes 35000000 | tf_op jit(solution)/shard_map/attention_forward/pallas_call | solution.py:169
  314.6 5.1 select_dynamic-update-slice_fusion
  323.3 63.1 %mlp_forward.1 = (bf16[1280,4352]{1,0:T(8,128)(2,1)}, bf16[1280,4352]{1,0:T(8,128)(2,1)}, bf16[1280,1088]{1,0:T(8,128)(2,1)}, bf16[1088,1280]{1,0:T(8,128)(2,1)}...) custom-call(bf16[1280,512]{1,0:T(8,128)(2,1)S(1)} %copy-done.14, bf16[1280,576]{1,0:T(8,128)(2,1)} %copy-done.16, ...), custom_call_target="tpu_custom_call" | custom-call | flops 49999998976 | bytes 50000000 | tf_op jit(solution)/shard_map/mlp_forward/pallas_call | solution.py:407
  387.2 87.8 %mlp_backward.1 = (f32[1280,1088]{1,0:T(8,128)}, bf16[1280,512]{1,0:T(8,128)(2,1)}, bf16[1280,576]{1,0:T(8,128)(2,1)}, bf16[4,136,4352]{2,1,0:T(8,128)(2,1)}, bf...) custom-call(s32[1]{0:T(128)} %bitcast.42.half, ...), custom_call_target="tpu_custom_call" | custom-call | flops 80000000000 | bytes 80000000 | tf_op jit(solution)/shard_map/mlp_backward/pallas_call | solution.py:524
  477.2 7.6 copy.112
  505.4 12.5 %collective-permute-done.10 = bf16[512,1088]{0,1:T(8,128)(2,1)} collective-permute-done((bf16[512,1088]{0,1:T(8,128)(2,1)}, bf16[512,1088]{0,1:T(8,128)(2,1)}, u32[]{:S(2)}, u32[]{:S(2)}) %collective-permute-start.10) | collective-permute-done | bytes 1114144 | tf_op jit(solution)/shard_map/ppermute | solution.py:737
  517.9 23.5 %collective-permute-done.8 = bf16[512,1088]{0,1:T(8,128)(2,1)} collective-permute-done((bf16[512,1088]{0,1:T(8,128)(2,1)}, bf16[512,1088]{0,1:T(8,128)(2,1)}, u32[]{:S(2)}, u32[]{:S(2)}) %collective-permute-start.8) | collective-permute-done | bytes 1114144 | tf_op jit(solution)/shard_map/ppermute | solution.py:737
  572.0 60.5 %attention_backward.3 = (bf16[2304,576]{1,0:T(8,128)(2,1)S(1)}, bf16[2304,576]{1,0:T(8,128)(2,1)S(1)}, bf16[2304,576]{1,0:T(8,128)(2,1)S(1)}) custom-call(s32[3]{0:T(128)S(1)} %pad_add_fusion.pos, bf16[2304,576]{1,0:T(8,128)(2,1)} %copy-done.6, bf16[2304,576]{1,0:T(8,128)(2,1)} %copy-done.4, bf16[2304,576]{1,0:T(8,128)(2,1)} %copy-done.5, ...), custom_call_target="tpu_custom_call" | custom-call | flops 49999998976 | bytes 50000000 | tf_op jit(solution)/shard_map/attention_backward/pallas_call | solution.py:305
  634.1 5.0 add_convert_fusion.5
  644.1 13.7 %collective-permute-start.16 = (bf16[136,2720]{1,0:T(8,128)(2,1)}, bf16[136,2720]{1,0:T(8,128)(2,1)S(1)}, u32[]{:S(2)}, u32[]{:S(2)}) collective-permute-start(bf16[136,2720]{1,0:T(8,128)(2,1)} %get-tuple-element.191), channel_id=1, source_target_pairs={{0,2},{2,4},{4,6},{6,0},{1,3},{3,5},{5,7},{7,1},{8,10},{10,12},{12... | collective-permute-start | bytes 2219528 | tf_op jit(solution)/shard_map/ppermute | solution.py:742
  660.7 48.6 %attention_backward.2 = (bf16[2304,512]{1,0:T(8,128)(2,1)S(1)}, bf16[2304,512]{1,0:T(8,128)(2,1)S(1)}, bf16[2304,512]{1,0:T(8,128)(2,1)S(1)}) custom-call(s32[3]{0:T(128)S(1)} %pad_add_fusion.pos, bf16[2304,512]{1,0:T(8,128)(2,1)} %copy-done.3, bf16[2304,512]{1,0:T(8,128)(2,1)} %copy-done.1, bf16[2304,512]{1,0:T(8,128)(2,1)} %copy-done.2, ...), custom_call_target="tpu_custom_call" | custom-call | flops 40000000000 | bytes 40000000 | tf_op jit(solution)/shard_map/attention_backward/pallas_call | solution.py:305
  715.2 32.4 %tokens_back.1.refs_6_ = bf16[2304,1088]{1,0:T(8,128)(2,1)} custom-call(bf16[2304,512]{1,0:T(8,128)(2,1)} %copy-done.10, bf16[2304,512]{1,0:T(8,128)(2,1)} %copy-done.11, bf16[2304,512]{1,0:T(8,128)(2,1)} %copy-done.12, bf16[2304,576]{1,0:T(8,128)(2,1)} %copy-done.7, bf16[2304,576]{1,0:T(8,128)(2,1)} %copy-done.8, bf16[2304,576]{1,0:T(8,128)(2,1)} %copy-done.9, ...), custom_call_target="tpu_custom_call" | custom-call | flops 20000000000 | bytes 20000000 | tf_op jit(solution)/shard_map/tokens_back/pallas_call | solution.py:631
  747.6 8.5 copy.115
  756.0 27.7 %weights_back.1 = (bf16[4,136,512]{2,1,0:T(8,128)(2,1)S(1)}, bf16[4,136,512]{2,1,0:T(8,128)(2,1)S(1)}, bf16[4,136,512]{2,1,0:T(8,128)(2,1)S(1)}, bf16[4,136,512]...) custom-call(s32[1]{0:T(128)} %bitcast.42.half, ...), custom_call_target="tpu_custom_call" | custom-call | flops 20000000000 | bytes 20000000 | tf_op jit(solution)/shard_map/weights_back/pallas_call | solution.py:676
  783.9 7.1 convert_reduce_fusion
  800.0 16.3 %collective-permute-start.37 = (bf16[136,1152]{1,0:T(8,128)(2,1)}, bf16[136,1152]{1,0:T(8,128)(2,1)}, u32[]{:S(2)}, u32[]{:S(2)}) collective-permute-start(bf16[136,1152]{1,0:T(8,128)(2,1)} %get-tuple-element.207), channel_id=1, source_target_pairs={{0,2},{2,4},{4,6},{6,0},{1,3},{3,5},{5,7},{7,1},{8,10},{10,12},{12... | collective-permute-start | bytes 940040 | tf_op jit(solution)/shard_map/ppermute | solution.py:742
  833.8 5.3 collective-permute-done.24
  871.6 38.5 %collective-permute-done.28 = bf16[4,136,1792]{2,1,0:T(8,128)(2,1)S(1)} collective-permute-done((bf16[4,136,1792]{2,1,0:T(8,128)(2,1)S(1)}, bf16[4,136,1792]{2,1,0:T(8,128)(2,1)S(1)}, u32[]{:S(2)}, u32[]{:S(2)}) %collective-permute-start.28) | collective-permute-done | bytes 1949728 | tf_op jit(solution)/shard_map/ppermute | solution.py:737
  915.6 18.8 %collective-permute-done.29 = bf16[4,136,896]{2,1,0:T(8,128)(2,1)S(1)} collective-permute-done((bf16[4,136,896]{2,1,0:T(8,128)(2,1)S(1)}, bf16[4,136,896]{2,1,0:T(8,128)(2,1)S(1)}, u32[]{:S(2)}, u32[]{:S(2)}) %collective-permute-start.29) | collective-permute-done | bytes 974880 | tf_op jit(solution)/shard_map/ppermute | solution.py:737
  934.9 7.8 collective-permute-start.30
  949.0 8.5 collective-permute-done.31
  (449 shorter events, 258.4 us)
Async XLA Ops:
  7.2 98.4 %all-gather.7.cloned.1.call-start = ((), (), s32[]{:S(2)}) async-start(), calls=%async_computation | async-start | bytes 4595712 | tf_op jit(solution)/shard_map/all_gather | solution.py:781
  9.4 224.7 %all-gather.9.cloned.1.call-start = ((), (), s32[]{:S(2)}) async-start(), calls=%async_computation.1 | async-start | bytes 6893568 | tf_op jit(solution)/shard_map/all_gather | solution.py:781
  12.9 289.2 %all-gather.11.cloned.1.call-start = ((), (), s32[]{:S(2)}) async-start(), calls=%async_computation.2 | async-start | bytes 9191424 | tf_op jit(solution)/shard_map/all_gather | solution.py:781
  13.0 73.1 %collective-permute-start.1 = (bf16[1024,1088]{0,1:T(8,128)(2,1)S(1)}, bf16[1024,1088]{0,1:T(8,128)(2,1)}, u32[]{:S(2)}, u32[]{:S(2)}) collective-permute-start(bf16[1024,1088]{0,1:T(8,128)(2,1)S(1)} %bitcast.170), channel_id=1, source_target_pairs={{0,1},{1,0},{2,3},{3,2},{4,5},{5,4},{6,7},{7,6},{8,9},{9,8},{10,11... | collective-permute-start | bytes 6684680 | tf_op jit(solution)/shard_map/ppermute | solution.py:737
  16.0 60.9 %collective-permute-start = (s32[1]{0:T(128)}, s32[1]{0:T(128)}, u32[]{:S(2)}, u32[]{:S(2)}) collective-permute-start(s32[1]{0:T(128)} %param.20), channel_id=1, source_target_pairs={{0,1},{1,0},{2,3},{3,2},{4,5},{5,4},{6,7},{7,6},{8,9},{9,8},{10,11... | collective-permute-start | bytes 20 | tf_op jit(solution)/shard_map/ppermute | solution.py:737
  105.6 32.8 %collective-permute-start.2 = (bf16[272,1152]{1,0:T(8,128)(2,1)}, bf16[272,1152]{1,0:T(8,128)(2,1)}, u32[]{:S(2)}, u32[]{:S(2)}) collective-permute-start(bf16[272,1152]{1,0:T(8,128)(2,1)} %gate.2), channel_id=1, source_target_pairs={{0,2},{2,4},{4,6},{6,0},{1,3},{3,5},{5,7},{7,1},{8,10},{10,12},{12... | collective-permute-start | bytes 1880072 | tf_op jit(solution)/shard_map/ppermute | solution.py:742
  107.8 48.6 %collective-permute-start.3 = (bf16[272,1152]{1,0:T(8,128)(2,1)}, bf16[272,1152]{1,0:T(8,128)(2,1)}, u32[]{:S(2)}, u32[]{:S(2)}) collective-permute-start(bf16[272,1152]{1,0:T(8,128)(2,1)} %gate.2), channel_id=1, source_target_pairs={{0,4},{2,6},{4,0},{6,2},{1,5},{3,7},{5,1},{7,3},{8,12},{10,14},{12... | collective-permute-start | bytes 1880072 | tf_op jit(solution)/shard_map/ppermute | solution.py:742
  110.4 47.1 %collective-permute-start.4 = (bf16[272,1152]{1,0:T(8,128)(2,1)}, bf16[272,1152]{1,0:T(8,128)(2,1)}, u32[]{:S(2)}, u32[]{:S(2)}) collective-permute-start(bf16[272,1152]{1,0:T(8,128)(2,1)} %gate.2), channel_id=1, source_target_pairs={{0,6},{2,0},{4,2},{6,4},{1,7},{3,1},{5,3},{7,5},{8,14},{10,8},{12,... | collective-permute-start | bytes 1880072 | tf_op jit(solution)/shard_map/ppermute | solution.py:742
  118.7 75.2 %collective-permute-start.9 = (bf16[512,1088]{0,1:T(8,128)(2,1)}, bf16[512,1088]{0,1:T(8,128)(2,1)}, u32[]{:S(2)}, u32[]{:S(2)}) collective-permute-start(bf16[512,1088]{0,1:T(8,128)(2,1)} %copy.109), channel_id=1, source_target_pairs={{0,1},{1,0},{2,3},{3,2},{4,5},{5,4},{6,7},{7,6},{8,9},{9,8},{10,11... | collective-permute-start | bytes 3342344 | tf_op jit(solution)/shard_map/ppermute | solution.py:737
  158.7 70.6 %collective-permute-start.5 = (bf16[1088,1152]{1,0:T(8,128)(2,1)S(1)}, bf16[1088,1152]{1,0:T(8,128)(2,1)}, u32[]{:S(2)}, u32[]{:S(2)}) collective-permute-start(bf16[1088,1152]{1,0:T(8,128)(2,1)S(1)} %bitcast.168), channel_id=1, source_target_pairs={{0,1},{1,0},{2,3},{3,2},{4,5},{5,4},{6,7},{7,6},{8,9},{9,8},{10,11... | collective-permute-start | bytes 7520264 | tf_op jit(solution)/shard_map/ppermute | solution.py:737
  233.6 73.4 %collective-permute-start.6 = (bf16[1088,1152]{1,0:T(8,128)(2,1)}, bf16[1088,1152]{1,0:T(8,128)(2,1)}, u32[]{:S(2)}, u32[]{:S(2)}) collective-permute-start(bf16[1088,1152]{1,0:T(8,128)(2,1)} %get-tuple-element.168), channel_id=1, source_target_pairs={{0,8},{8,0},{16,24},{24,16},{1,9},{9,1},{17,25},{25,17},{2,10},{10... | collective-permute-start | bytes 7520264 | tf_op jit(solution)/shard_map/ppermute | solution.py:737
  233.6 81.0 %collective-permute-start.7 = (bf16[1088,1152]{1,0:T(8,128)(2,1)}, bf16[1088,1152]{1,0:T(8,128)(2,1)}, u32[]{:S(2)}, u32[]{:S(2)}) collective-permute-start(bf16[1088,1152]{1,0:T(8,128)(2,1)} %get-tuple-element.167), channel_id=1, source_target_pairs={{0,8},{8,0},{16,24},{24,16},{1,9},{9,1},{17,25},{25,17},{2,10},{10... | collective-permute-start | bytes 7520264 | tf_op jit(solution)/shard_map/ppermute | solution.py:737
  475.0 77.1 %collective-permute-start.14 = (bf16[4,136,4352]{2,1,0:T(8,128)(2,1)}, bf16[4,136,4352]{2,1,0:T(8,128)(2,1)}, u32[]{:S(2)}, u32[]{:S(2)}) collective-permute-start(bf16[4,136,4352]{2,1,0:T(8,128)(2,1)} %get-tuple-element.76), channel_id=1, source_target_pairs={{0,8},{8,0},{16,24},{24,16},{1,9},{9,1},{17,25},{25,17},{2,10},{10... | collective-permute-start | bytes 14204936 | tf_op jit(solution)/shard_map/ppermute | solution.py:737
  490.2 27.7 %collective-permute-start.10 = (bf16[512,1088]{0,1:T(8,128)(2,1)}, bf16[512,1088]{0,1:T(8,128)(2,1)}, u32[]{:S(2)}, u32[]{:S(2)}) collective-permute-start(bf16[512,1088]{0,1:T(8,128)(2,1)} %slice.456), channel_id=1, source_target_pairs={{0,1},{1,0},{2,3},{3,2},{4,5},{5,4},{6,7},{7,6},{8,9},{9,8},{10,11... | collective-permute-start | bytes 3342344 | tf_op jit(solution)/shard_map/ppermute | solution.py:737
  497.0 44.4 %collective-permute-start.8 = (bf16[512,1088]{0,1:T(8,128)(2,1)}, bf16[512,1088]{0,1:T(8,128)(2,1)}, u32[]{:S(2)}, u32[]{:S(2)}) collective-permute-start(bf16[512,1088]{0,1:T(8,128)(2,1)} %slice.453), channel_id=1, source_target_pairs={{0,1},{1,0},{2,3},{3,2},{4,5},{5,4},{6,7},{7,6},{8,9},{9,8},{10,11... | collective-permute-start | bytes 3342344 | tf_op jit(solution)/shard_map/ppermute | solution.py:737
  501.4 59.8 %collective-permute-start.11 = (bf16[4,136,4352]{2,1,0:T(8,128)(2,1)}, bf16[4,136,4352]{2,1,0:T(8,128)(2,1)}, u32[]{:S(2)}, u32[]{:S(2)}) collective-permute-start(bf16[4,136,4352]{2,1,0:T(8,128)(2,1)} %get-tuple-element.72), channel_id=1, source_target_pairs={{0,8},{8,0},{16,24},{24,16},{1,9},{9,1},{17,25},{25,17},{2,10},{10... | collective-permute-start | bytes 14204936 | tf_op jit(solution)/shard_map/ppermute | solution.py:737
  501.6 48.5 %collective-permute-start.12 = (bf16[4,136,1088]{2,1,0:T(8,128)(2,1)}, bf16[4,136,1088]{2,1,0:T(8,128)(2,1)}, u32[]{:S(2)}, u32[]{:S(2)}) collective-permute-start(bf16[4,136,1088]{2,1,0:T(8,128)(2,1)} %get-tuple-element.74), channel_id=1, source_target_pairs={{0,8},{8,0},{16,24},{24,16},{1,9},{9,1},{17,25},{25,17},{2,10},{10... | collective-permute-start | bytes 3551240 | tf_op jit(solution)/shard_map/ppermute | solution.py:737
  560.0 74.1 %collective-permute-start.15 = (bf16[4,136,2304]{2,1,0:T(8,128)(2,1)}, bf16[4,136,2304]{2,1,0:T(8,128)(2,1)}, u32[]{:S(2)}, u32[]{:S(2)}) collective-permute-start(bf16[4,136,2304]{2,1,0:T(8,128)(2,1)} %broadcast_select_fusion.1), channel_id=1, source_target_pairs={{0,16},{8,24},{16,0},{24,8},{1,17},{9,25},{17,1},{25,9},{2,18},{10... | collective-permute-start | bytes 7520264 | tf_op jit(solution)/shard_map/ppermute | solution.py:737
  570.2 70.2 %collective-permute-start.13 = (bf16[4,136,2720]{2,1,0:T(8,128)(2,1)}, bf16[4,136,2720]{2,1,0:T(8,128)(2,1)}, u32[]{:S(2)}, u32[]{:S(2)}) collective-permute-start(bf16[4,136,2720]{2,1,0:T(8,128)(2,1)} %broadcast_select_fusion), channel_id=1, source_target_pairs={{0,1},{1,0},{2,3},{3,2},{4,5},{5,4},{6,7},{7,6},{8,9},{9,8},{10,11... | collective-permute-start | bytes 8878088 | tf_op jit(solution)/shard_map/ppermute | solution.py:737
  640.5 71.9 %collective-permute-start.19 = (bf16[4,136,1152]{2,1,0:T(8,128)(2,1)}, bf16[4,136,1152]{2,1,0:T(8,128)(2,1)}, u32[]{:S(2)}, u32[]{:S(2)}) collective-permute-start(bf16[4,136,1152]{2,1,0:T(8,128)(2,1)} %get-tuple-element.194), channel_id=1, source_target_pairs={{0,1},{1,0},{2,3},{3,2},{4,5},{5,4},{6,7},{7,6},{8,9},{9,8},{10,11... | collective-permute-start | bytes 3760136 | tf_op jit(solution)/shard_map/ppermute | solution.py:737
  644.1 65.2 %collective-permute-start.16 = (bf16[136,2720]{1,0:T(8,128)(2,1)}, bf16[136,2720]{1,0:T(8,128)(2,1)S(1)}, u32[]{:S(2)}, u32[]{:S(2)}) collective-permute-start(bf16[136,2720]{1,0:T(8,128)(2,1)} %get-tuple-element.191), channel_id=1, source_target_pairs={{0,2},{2,4},{4,6},{6,0},{1,3},{3,5},{5,7},{7,1},{8,10},{10,12},{12... | collective-permute-start | bytes 2219528 | tf_op jit(solution)/shard_map/ppermute | solution.py:742
  657.8 51.9 %collective-permute-start.17 = (bf16[136,2720]{1,0:T(8,128)(2,1)S(1)}, bf16[136,2720]{1,0:T(8,128)(2,1)S(1)}, u32[]{:S(2)}, u32[]{:S(2)}) collective-permute-start(bf16[136,2720]{1,0:T(8,128)(2,1)S(1)} %get-tuple-element.193), channel_id=1, source_target_pairs={{0,4},{2,6},{4,0},{6,2},{1,5},{3,7},{5,1},{7,3},{8,12},{10,14},{12... | collective-permute-start | bytes 2219528 | tf_op jit(solution)/shard_map/ppermute | solution.py:742
  660.7 49.0 %collective-permute-start.18 = (bf16[136,2720]{1,0:T(8,128)(2,1)S(1)}, bf16[136,2720]{1,0:T(8,128)(2,1)S(1)}, u32[]{:S(2)}, u32[]{:S(2)}) collective-permute-start(bf16[136,2720]{1,0:T(8,128)(2,1)S(1)} %get-tuple-element.192), channel_id=1, source_target_pairs={{0,6},{2,0},{4,2},{6,4},{1,7},{3,1},{5,3},{7,5},{8,14},{10,8},{12,... | collective-permute-start | bytes 2219528 | tf_op jit(solution)/shard_map/ppermute | solution.py:742
  711.8 144.1 %collective-permute-start.35 = (bf16[136,2720]{1,0:T(8,128)(2,1)S(1)}, bf16[136,2720]{1,0:T(8,128)(2,1)}, u32[]{:S(2)}, u32[]{:S(2)}) collective-permute-start(bf16[136,2720]{1,0:T(8,128)(2,1)S(1)} %fusion.27.refs_12_), channel_id=1, source_target_pairs={{0,16},{8,24},{16,0},{24,8},{1,17},{9,25},{17,1},{25,9},{2,18},{10... | collective-permute-start | bytes 2219528 | tf_op jit(solution)/shard_map/ppermute | solution.py:737
  793.4 25.4 %collective-permute-start.22 = (f32[13056]{0:T(1024)S(1)}, f32[13056]{0:T(1024)S(1)}, u32[]{:S(2)}, u32[]{:S(2)}) collective-permute-start(f32[13056]{0:T(1024)S(1)} %add.325), channel_id=1, source_target_pairs={{0,16},{8,24},{16,0},{24,8},{1,17},{9,25},{17,1},{25,9},{2,18},{10... | collective-permute-start | bytes 156680 | tf_op jit(solution)/shard_map/ppermute | solution.py:737
  800.0 40.0 %collective-permute-start.37 = (bf16[136,1152]{1,0:T(8,128)(2,1)}, bf16[136,1152]{1,0:T(8,128)(2,1)}, u32[]{:S(2)}, u32[]{:S(2)}) collective-permute-start(bf16[136,1152]{1,0:T(8,128)(2,1)} %get-tuple-element.207), channel_id=1, source_target_pairs={{0,2},{2,4},{4,6},{6,0},{1,3},{3,5},{5,7},{7,1},{8,10},{10,12},{12... | collective-permute-start | bytes 940040 | tf_op jit(solution)/shard_map/ppermute | solution.py:742
  816.4 24.2 %collective-permute-start.38 = (bf16[136,1152]{1,0:T(8,128)(2,1)}, bf16[136,1152]{1,0:T(8,128)(2,1)}, u32[]{:S(2)}, u32[]{:S(2)}) collective-permute-start(bf16[136,1152]{1,0:T(8,128)(2,1)} %get-tuple-element.209), channel_id=1, source_target_pairs={{0,4},{2,6},{4,0},{6,2},{1,5},{3,7},{5,1},{7,3},{8,12},{10,14},{12... | collective-permute-start | bytes 940040 | tf_op jit(solution)/shard_map/ppermute | solution.py:742
  817.0 24.2 %collective-permute-start.39 = (bf16[136,1152]{1,0:T(8,128)(2,1)}, bf16[136,1152]{1,0:T(8,128)(2,1)}, u32[]{:S(2)}, u32[]{:S(2)}) collective-permute-start(bf16[136,1152]{1,0:T(8,128)(2,1)} %get-tuple-element.208), channel_id=1, source_target_pairs={{0,6},{2,0},{4,2},{6,4},{1,7},{3,1},{5,3},{7,5},{8,14},{10,8},{12,... | collective-permute-start | bytes 940040 | tf_op jit(solution)/shard_map/ppermute | solution.py:742
  840.0 21.3 %collective-permute-start.27 = (bf16[4,136,1632]{2,1,0:T(8,128)(2,1)}, bf16[4,136,1632]{2,1,0:T(8,128)(2,1)}, u32[]{:S(2)}, u32[]{:S(2)}) collective-permute-start(bf16[4,136,1632]{2,1,0:T(8,128)(2,1)} %concatenate.160), channel_id=1, source_target_pairs={{0,8},{8,0},{16,24},{24,16},{1,9},{9,1},{17,25},{25,17},{2,10},{10... | collective-permute-start | bytes 5326856 | tf_op jit(solution)/shard_map/ppermute | solution.py:737
  852.0 60.7 %collective-permute-start.20 = (bf16[1024,1088]{0,1:T(8,128)(2,1)}, bf16[1024,1088]{0,1:T(8,128)(2,1)S(1)}, u32[]{:S(2)}, u32[]{:S(2)}) collective-permute-start(bf16[1024,1088]{0,1:T(8,128)(2,1)} %constant_dynamic-slice_fusion), channel_id=1, source_target_pairs={{0,1},{1,0},{2,3},{3,2},{4,5},{5,4},{6,7},{7,6},{8,9},{9,8},{10,11... | collective-permute-start | bytes 6684680 | tf_op jit(solution)/shard_map/ppermute | solution.py:737
  865.2 44.9 %collective-permute-start.28 = (bf16[4,136,1792]{2,1,0:T(8,128)(2,1)S(1)}, bf16[4,136,1792]{2,1,0:T(8,128)(2,1)S(1)}, u32[]{:S(2)}, u32[]{:S(2)}) collective-permute-start(bf16[4,136,1792]{2,1,0:T(8,128)(2,1)S(1)} %broadcast_select_fusion.6), channel_id=1, source_target_pairs={{0,16},{8,24},{16,0},{24,8},{1,17},{9,25},{17,1},{25,9},{2,18},{10... | collective-permute-start | bytes 5849096 | tf_op jit(solution)/shard_map/ppermute | solution.py:737
  911.0 23.4 %collective-permute-start.29 = (bf16[4,136,896]{2,1,0:T(8,128)(2,1)S(1)}, bf16[4,136,896]{2,1,0:T(8,128)(2,1)S(1)}, u32[]{:S(2)}, u32[]{:S(2)}) collective-permute-start(bf16[4,136,896]{2,1,0:T(8,128)(2,1)S(1)} %broadcast_select_fusion.12), channel_id=1, source_target_pairs={{0,1},{1,0},{2,3},{3,2},{4,5},{5,4},{6,7},{7,6},{8,9},{9,8},{10,11... | collective-permute-start | bytes 2924552 | tf_op jit(solution)/shard_map/ppermute | solution.py:737
  (117 other events, 1537.9 us)
Sparse Core Ops, SparseCore 0:
  11.4 75.1 all-gather.6
  89.7 112.7 all-gather.8
  205.4 84.2 all-gather.10

commit v4 on v3

--- a/solution.py
+++ b/solution.py
@@ -378,8 +378,10 @@
 
     for here in row_chunks(rows):
         pre = nn(act[here, :], up[...]) + up_bias[...]
-        bell = jnp.exp(pre * pre * -0.5)
-        t = 1.0 / (1.0 + (0.3275911 * 0.7071067811865476) * jnp.abs(pre))
+        bell = jnp.exp2(pre * pre * (-0.5 * LOG2E))
+        base = 1.0 + (0.3275911 * 0.7071067811865476) * jnp.abs(pre)
+        t = pl.reciprocal(base, approx=True)
+        t = t * (2.0 - base * t)
         series = t * (
             0.127414796 + t * (-0.142248368 + t * (0.7107068705 + t * (-0.7265760135 + t * 0.5307027145)))
         )
@@ -456,31 +458,66 @@
     )
 
 
-def mlp_backward_kernel(
-    half, act_turned, cot, norm, pace, gain, mixed_a, mixed_b, out_w, hidden, slope, up, down, *rest
+def down_back_kernel(half, cot_turned, hidden, keep, give):
+    store_halves(nn(cot_turned[...], hidden[...]), half[0], keep, give)
+
+
+def down_back(half, count, cot_turned, hidden):
+    width, rows = cot_turned.shape
+    inner = hidden.shape[1]
+    block = width // count // 2
+    split = pl.BlockSpec((count, block, TILE), lambda j, half: (0, 0, j))
+    return pl.pallas_call(
+        down_back_kernel,
+        grid_spec=pltpu.PrefetchScalarGridSpec(
+            num_scalar_prefetch=1,
+            grid=(inner // TILE,),
+            in_specs=[fixed((width, rows)), pl.BlockSpec((rows, TILE), lambda j, half: (0, j))],
+            out_specs=[split, split],
+        ),
+        out_shape=[jax.ShapeDtypeStruct((count, block, inner), jnp.bfloat16)] * 2,
+        compiler_params=pltpu.CompilerParams(
+            dimension_semantics=("arbitrary",), vmem_limit_bytes=32 * 2**20
+        ),
+        cost_estimate=busy(15),
+        name="down_back",
+    )(half, cot_turned, hidden)
+
+
+def up_back_step(half, act_turned, cot, slope, up, down, total, keep, give, bias_grad):
+    bias = jnp.zeros((1, TILE), jnp.float32)
+    pieces = []
+    for here in row_chunks(cot.shape[0]):
+        d_pre = (nn(cot[here, :], down[...]) * slope[here, :].astype(jnp.float32)).astype(jnp.bfloat16)
+        bias = bias + jnp.sum(d_pre.astype(jnp.float32), axis=0, keepdims=True)
+        total[here, :] += nt(d_pre, up[...])
+        pieces.append(d_pre)
+    bias_grad[...] = bias
+    store_halves(nn(act_turned[...], jnp.concatenate(pieces, axis=0)), half[0], keep, give)
+
+
+def up_back_first_kernel(half, act_turned, cot, slope, up, down, total, keep, give, bias_grad):
+    @pl.when(pl.program_id(0) == 0)
+    def _():
+        total[...] = jnp.zeros_like(total)
+
+    up_back_step(half, act_turned, cot, slope, up, down, total, keep, give, bias_grad)
+
+
+def up_back_last_kernel(
+    half, act_turned, cot, slope, up, down, so_far, norm, pace, gain, mixed_a, mixed_b, out_w, *rest
 ):
-    outs = rest[-14:]
-    d_resid, d_mixed_a, d_mixed_b, up_keep, up_give, down_keep, down_give, out_keep, out_give = outs[:9]
-    bias_grad, lines, cot_turned, d_branch, piece = outs[9:]
+    d_resid, d_mixed_a, d_mixed_b, keep, give, out_keep, out_give, bias_grad, lines = rest[-11:-2]
+    d_branch, piece = rest[-2:]
     step = pl.program_id(0)
     rows, width = cot.shape
     first = mixed_a.shape[1]
 
     @pl.when(step == 0)
     def _():
-        cot_turned[...] = cot[...].T
-        d_resid[...] = jnp.zeros_like(d_resid)
-
-    bias = jnp.zeros((1, TILE), jnp.float32)
-    pieces = []
-    for here in row_chunks(rows):
-        d_pre = (nn(cot[here, :], down[...]) * slope[here, :].astype(jnp.float32)).astype(jnp.bfloat16)
-        bias = bias + jnp.sum(d_pre.astype(jnp.float32), axis=0, keepdims=True)
-        d_resid[here, :] += nt(d_pre, up[...])
-        pieces.append(d_pre)
-    bias_grad[...] = bias
-    store_halves(nn(act_turned[...], jnp.concatenate(pieces, axis=0)), half[0], up_keep, up_give)
-    store_halves(nn(cot_turned[...], hidden[...]), half[0], down_keep, down_give)
+        d_resid[...] = so_far[...]
+
+    up_back_step(half, act_turned, cot, slope, up, down, d_resid, keep, give, bias_grad)
 
     @pl.when(step == pl.num_programs(0) - 1)
     def _():
@@ -513,63 +550,68 @@
             store_halves(value, half[0], out_keep.at[:, :, columns], out_give.at[:, :, columns])
 
 
-def mlp_backward(half, count, act_turned, cot, norm, pace, gain, mixed, out_w, hidden, slope, up, down):
+def up_back(half, count, tiles, act_turned, cot, slope, up, down, final=None, after=()):
     rows, width = cot.shape
-    inner = up.shape[1]
     block = width // count // 2
-    column = pl.BlockSpec((width, TILE), lambda j, half: (0, j))
-    tall = pl.BlockSpec((rows, TILE), lambda j, half: (0, j))
+    low, high = tiles
+    inner = (high - low) * TILE
     split = pl.BlockSpec((count, block, TILE), lambda j, half: (0, 0, j))
+    column = pl.BlockSpec((width, TILE), lambda j, half: (0, j + low))
     like = jax.ShapeDtypeStruct
+    in_specs = [
+        fixed((width, rows)),
+        fixed((rows, width)),
+        pl.BlockSpec((rows, TILE), lambda j, half: (0, j + low)),
+        column,
+        column,
+    ]
+    operands = [half, act_turned, cot, slope, up, down]
+    out_specs = [steady((rows, width))]
+    out_shape = [like((rows, width), jnp.float32)]
+    scratch = []
+    if final is not None:
+        so_far, norm, pace, gain, mixed, out_w = final
+        in_specs += [
+            fixed((rows, width)),
+            fixed((rows, width)),
+            fixed((rows, 128)),
+            fixed((1, width)),
+            fixed(mixed[0].shape),
+            fixed(mixed[1].shape),
+            fixed((width, width)),
+        ]
+        operands += [so_far, norm, pace, gain.reshape(1, width), *mixed, out_w]
+        out_specs += [steady(m.shape) for m in mixed]
+        out_shape += [like(m.shape, jnp.bfloat16) for m in mixed]
+        scratch = [pltpu.VMEM((rows, width), jnp.bfloat16), pltpu.VMEM((width, TILE), jnp.float32)]
+    out_specs += [split] * 2
+    out_shape += [like((count, block, inner), jnp.bfloat16)] * 2
+    if final is not None:
+        out_specs += [steady((count, block, width))] * 2
+        out_shape += [like((count, block, width), jnp.bfloat16)] * 2
+    out_specs += [pl.BlockSpec((1, TILE), lambda j, half: (0, j))]
+    out_shape += [like((1, inner), jnp.float32)]
+    if final is not None:
+        out_specs += [steady((8, width))]
+        out_shape += [like((8, width), jnp.float32)]
+        in_specs += [pl.BlockSpec(memory_space=pl.ANY)] * len(after)
+        operands += after
     return pl.pallas_call(
-        mlp_backward_kernel,
+        up_back_first_kernel if final is None else up_back_last_kernel,
         grid_spec=pltpu.PrefetchScalarGridSpec(
             num_scalar_prefetch=1,
-            grid=(inner // TILE,),
-            in_specs=[
-                fixed((width, rows)),
-                fixed((rows, width)),
-                fixed((rows, width)),
-                fixed((rows, 128)),
-                fixed((1, width)),
-                fixed(mixed[0].shape),
-                fixed(mixed[1].shape),
-                fixed((width, width)),
-                tall,
-                tall,
-                column,
-                column,
-            ],
-            out_specs=[
-                steady((rows, width)),
-                steady(mixed[0].shape),
-                steady(mixed[1].shape),
-                split,
-                split,
-                split,
-                split,
-                steady((count, block, width)),
-                steady((count, block, width)),
-                pl.BlockSpec((1, TILE), lambda j, half: (0, j)),
-                steady((8, width)),
-            ],
-            scratch_shapes=[
-                pltpu.VMEM((width, rows), jnp.bfloat16),
-                pltpu.VMEM((rows, width), jnp.bfloat16),
-                pltpu.VMEM((width, TILE), jnp.float32),
-            ],
-        ),
-        out_shape=[like((rows, width), jnp.float32)]
-        + [like(m.shape, jnp.bfloat16) for m in mixed]
-        + [like((count, block, inner), jnp.bfloat16)] * 4
-        + [like((count, block, width), jnp.bfloat16)] * 2
-        + [like((1, inner), jnp.float32), like((8, width), jnp.float32)],
+            grid=(high - low,),
+            in_specs=in_specs,
+            out_specs=out_specs,
+            scratch_shapes=scratch,
+        ),
+        out_shape=out_shape,
         compiler_params=pltpu.CompilerParams(
             dimension_semantics=("arbitrary",), vmem_limit_bytes=58 * 2**20
         ),
-        cost_estimate=busy(80),
-        name="mlp_backward",
-    )(half, act_turned, cot, norm, pace, gain.reshape(1, width), *mixed, out_w, hidden, slope, up, down)
+        cost_estimate=busy(30 if final is None else 50),
+        name="up_back_first" if final is None else "up_back_last",
+    )(*operands)
 
 
 def projection_tiles(widths):
@@ -643,47 +685,53 @@
     )(*grads[0], *grads[1], *weights[0], *weights[1], *after)
 
 
-def weights_back_kernel(half, turned, *refs, widths):
-    grads = (refs[0:3], refs[3:6])
-    outs = refs[-16:]
+def weights_back_kernel(half, turned, *refs, tiles):
+    outs = refs[-6:]
     step = pl.program_id(0)
-    first, second, _ = projection_tiles(widths)
     for group in range(2):
-        keeps = outs[group * 8 : group * 8 + 3]
-        gives = outs[group * 8 + 3 : group * 8 + 6]
-        biases = outs[group * 8 + 6 : group * 8 + 8]
-
-        @pl.when(step < first if group == 0 else step >= first)
-        def _():
-            for kind in range(3):
-                part = grads[group][kind][...]
-                store_halves(nn(turned[...], part), half[0], keeps[kind], gives[kind])
-                if kind != 1:
-                    biases[kind // 2][...] = jnp.sum(part.astype(jnp.float32), axis=0, keepdims=True)
+        keep, give, bias = outs[group * 3 : group * 3 + 3]
+        start, size = group * 3 * tiles[0], tiles[group]
+        for kind in range(3):
+            grad = refs[group * 3 + kind]
+
+            @pl.when(jnp.logical_and(step >= start + kind * size, step < start + (kind + 1) * size))
+            def _():
+                part = grad[...]
+                store_halves(nn(turned[...], part), half[0], keep, give)
+                bias[...] = jnp.sum(part.astype(jnp.float32), axis=0, keepdims=True)
 
 
 def weights_back(half, count, turned, grads, after=()):
     width, total = turned.shape
-    widths = [group[0].shape[1] for group in grads]
-    first, second, places = projection_tiles(widths)
+    tiles = [pl.cdiv(group[0].shape[1], TILE) for group in grads]
     block = width // count // 2
     like = jax.ShapeDtypeStruct
-    out_specs, out_shape = [], []
-    for at, w in zip(places, widths):
-        out_specs += [pl.BlockSpec((count, block, TILE), lambda t, half, at=at: (0, 0, at(t)))] * 6
-        out_specs += [pl.BlockSpec((1, TILE), lambda t, half, at=at: (0, at(t)))] * 2
-        out_shape += [like((count, block, w), jnp.bfloat16)] * 6 + [like((1, w), jnp.float32)] * 2
+    in_specs, out_specs, out_shape = [], [], []
+    for group in range(2):
+        start, size = group * 3 * tiles[0], tiles[group]
+        for kind in range(3):
+            at = start + kind * size
+            in_specs.append(
+                pl.BlockSpec(
+                    (total, TILE), lambda t, half, at=at, size=size: (0, jnp.clip(t - at, 0, size - 1))
+                )
+            )
+
+        def place(t, start=start, size=size):
+            return jnp.clip(t - start, 0, 3 * size - 1)
+
+        out_specs += [
+            pl.BlockSpec((count, block, TILE), lambda t, half, place=place: (0, 0, place(t)))
+        ] * 2 + [pl.BlockSpec((1, TILE), lambda t, half, place=place: (0, place(t)))]
+        columns = 3 * size * TILE
+        out_shape += [like((count, block, columns), jnp.bfloat16)] * 2 + [like((1, columns), jnp.float32)]
     return pl.pallas_call(
-        functools.partial(weights_back_kernel, widths=widths),
+        functools.partial(weights_back_kernel, tiles=tiles),
         grid_spec=pltpu.PrefetchScalarGridSpec(
             num_scalar_prefetch=1,
-            grid=(first + second,),
+            grid=(3 * sum(tiles),),
             in_specs=[fixed((width, total))]
-            + [
-                pl.BlockSpec((total, TILE), lambda t, half, at=at: (0, at(t)))
-                for at in places
-                for _ in range(3)
-            ]
+            + in_specs
             + [pl.BlockSpec(memory_space=pl.ANY)] * len(after),
             out_specs=out_specs,
         ),
@@ -691,9 +739,65 @@
         compiler_params=pltpu.CompilerParams(
             dimension_semantics=("arbitrary",), vmem_limit_bytes=52 * 2**20
         ),
-        cost_estimate=busy(20),
+        cost_estimate=busy(25),
         name="weights_back",
     )(half, turned, *grads[0], *grads[1], *after)
+
+
+def rows_back_kernel(others, own, rows, resid, gain, prompt_out, branch_out):
+    step = pl.program_id(0)
+    last = pl.num_programs(0) - 1
+    values = rows[...].astype(jnp.float32)
+    centred = values - jnp.mean(values, axis=1, keepdims=True)
+    pace = lax.rsqrt(jnp.mean(centred * centred, axis=1, keepdims=True) + epsilon)
+    normed = centred * pace
+    grad = own[...].astype(jnp.float32) + jnp.where(step == last, 0.0, others[...].astype(jnp.float32))
+    scaled = grad * gain[...]
+    inner = (
+        scaled
+        - jnp.mean(scaled, axis=1, keepdims=True)
+        - normed * jnp.mean(scaled * normed, axis=1, keepdims=True)
+    )
+    turned = (resid[...] + pace * inner).T
+
+    @pl.when(step < last)
+    def _():
+        prompt_out[...] = turned
+
+    @pl.when(step == last)
+    def _():
+        branch_out[...] = turned
+
+
+def rows_back(others, own, rows, resid, gain, branch):
+    total, width = own.shape
+    shard = total - branch
+    steps = shard // branch
+    tall = pl.BlockSpec((branch, width), lambda t: (t, 0))
+    return pl.pallas_call(
+        rows_back_kernel,
+        grid=(steps + 1,),
+        in_specs=[
+            pl.BlockSpec((branch, width), lambda t: (jnp.minimum(t, steps - 1), 0)),
+            tall,
+            tall,
+            tall,
+            fixed((1, width)),
+        ],
+        out_specs=[
+            pl.BlockSpec((width, branch), lambda t: (0, jnp.minimum(t, steps - 1))),
+            pl.BlockSpec((width, branch), lambda t: (0, 0)),
+        ],
+        out_shape=[
+            jax.ShapeDtypeStruct((width, shard), jnp.float32),
+            jax.ShapeDtypeStruct((width, branch), jnp.float32),
+        ],
+        compiler_params=pltpu.CompilerParams(
+            dimension_semantics=("arbitrary",), vmem_limit_bytes=40 * 2**20
+        ),
+        cost_estimate=busy(10),
+        name="rows_back",
+    )(others, own, rows, resid, gain.reshape(1, width))
 
 
 def gate_kernel(*refs):
@@ -721,15 +825,6 @@
     spread = jnp.mean(centred * centred, axis=-1, keepdims=True)
     pace = lax.rsqrt(spread + epsilon)
     return centred * pace, pace
-
-
-def norm_back(grad, norm, pace, gain):
-    scaled = grad * gain
-    return pace * (
-        scaled
-        - jnp.mean(scaled, axis=-1, keepdims=True)
-        - norm * jnp.mean(scaled * norm, axis=-1, keepdims=True)
-    )
 
 
 def swap(value, axis, bit):
@@ -869,15 +964,19 @@
     return (a.astype(jnp.float32) + b.astype(jnp.float32)).astype(jnp.bfloat16)
 
 
-def overlap_step(sides):
+def chips_step(sides):
     columns = sides[0].shape[-1]
-    size = pl.cdiv(pl.cdiv(columns, 128), 2) * 128
+    size = pl.cdiv(columns // 128, 2) * 128
     own_first = lax.axis_index("dp") // 2 == 0
     first, second = (
         jnp.concatenate([side[..., at : at + size] for side in sides], axis=-1) for at in (0, columns - size)
     )
-    done = add(jnp.where(own_first, first, second), swap(jnp.where(own_first, second, first), "dp", 2))
-    return done[..., :size], done[..., size:]
+    return add(jnp.where(own_first, first, second), swap(jnp.where(own_first, second, first), "dp", 2))
+
+
+def two(value):
+    size = value.shape[-1] // 2
+    return value[..., :size], value[..., size:]
 
 
 def overlap_join(value, columns):
@@ -917,31 +1016,30 @@
     return add(keep, swap(jnp.where(first_side, second, first), "gy", 1))
 
 
-def projection_sides(first, rest, width):
-    size = width - GROUP
-    spare = width // 2 - GROUP
-    query, key, value = first
-    query_rest, key_rest, value_rest = rest
+def projection_sides(first, rest):
+    query, key, value = (first[..., n * GROUP : (n + 1) * GROUP] for n in range(3))
+    size = rest.shape[-1] // 3
+    query_rest, key_rest, value_rest = (rest[..., n * size : n * size + GROUP + 128] for n in range(3))
     return (
-        jnp.concatenate([query, key, query_rest, key_rest[..., :spare]], axis=-1),
-        jnp.concatenate(
-            [value, key_rest[..., spare : size - spare], value_rest, key_rest[..., size - spare :]], axis=-1
-        ),
+        jnp.concatenate([query, key, query_rest, key_rest[..., :128]], axis=-1),
+        jnp.concatenate([value, key_rest, value_rest], axis=-1),
     )
 
 
 def join_projections(whole, width):
     rest = width - GROUP
-    pieces = [
-        whole[:, :GROUP],
-        whole[:, GROUP : 2 * GROUP],
-        whole[:, 2 * GROUP : 2 * GROUP + rest],
-        whole[:, 2 * GROUP + rest :],
-    ]
+    spare = width // 2 - GROUP
+    wide = GROUP + 128
+    query, key = whole[:, :GROUP], whole[:, GROUP : 2 * GROUP]
+    query_rest = whole[:, 2 * GROUP : 2 * GROUP + rest]
+    key_spare = whole[:, 2 * GROUP + wide : 2 * GROUP + wide + spare]
+    value = whole[:, :GROUP]
+    key_rest = whole[:, GROUP + spare : GROUP + rest]
+    value_rest = whole[:, GROUP + wide : GROUP + wide + rest]
     return jnp.where(
         lax.axis_index("gy") == 0,
-        jnp.concatenate([pieces[n] for n in (0, 2, 1, 3)], axis=1),
-        jnp.concatenate([pieces[n] for n in (1, 3, 0, 2)], axis=1),
+        jnp.concatenate([query, query_rest, key, key_spare], axis=1),
+        jnp.concatenate([key_rest, value, value_rest], axis=1),
     )
 
 
@@ -961,17 +1059,15 @@
     return jnp.concatenate([jnp.where(first, own, other), jnp.where(first, other, own)], axis=0)
 
 
-def own_tokens_sum(whole):
+def others_tokens(whole):
     count = lax.axis_size("gy")
     here = lax.axis_index("gy")
     rows = whole.shape[0] // count
     if count != 2:
-        return lax.psum_scatter(
-            whole.astype(jnp.bfloat16), "gy", scatter_dimension=0, tiled=True
-        ).astype(jnp.float32)
-    give = lax.dynamic_slice_in_dim(whole, (1 - here) * rows, rows, 0)
-    keep = lax.dynamic_slice_in_dim(whole, here * rows, rows, 0)
-    return keep.astype(jnp.float32) + swap(give.astype(jnp.bfloat16), "gy", 1).astype(jnp.float32)
+        keep = lax.dynamic_slice_in_dim(whole, here * rows, rows, 0)
+        total = lax.psum_scatter(whole, "gy", scatter_dimension=0, tiled=True)
+        return (total.astype(jnp.float32) - keep.astype(jnp.float32)).astype(jnp.bfloat16)
+    return swap(lax.dynamic_slice_in_dim(whole, (1 - here) * rows, rows, 0), "gy", 1)
 
 
 def dot(a, b):
@@ -1075,84 +1171,85 @@
 
     count = lax.axis_size("gx")
     half = jnp.reshape(half_index() if halved else 0, (1,)).astype(jnp.int32)
-    (
-        d_resid,
-        *d_mixed,
-        up_keep,
-        up_give,
-        down_keep,
-        down_give,
-        out_keep,
-        out_give,
-        up_bias_grad,
-        lines,
-    ) = mlp_backward(
+    tiles = up_full.shape[1] // TILE
+    part = tiles // 2
+    down_keep, down_give = down_back(half, count, cotangent.T, hidden)
+    after = ()
+    if halved:
+        down_flow = core_step(down_keep, down_give)
+        after = (down_flow,)
+    so_far, up_keep, up_give, up_bias_grad = up_back(
+        half, count, (0, part), act_turned, cotangent, slope, up_full, down_full
+    )
+    d_resid, *d_mixed, keep_rest, give_rest, out_keep, out_give, bias_rest, lines = up_back(
         half,
         count,
+        (part, tiles),
         act_turned,
         cotangent,
-        norm_two,
-        pace_two,
-        mlp_gain,
-        mixed,
-        out_full,
-        hidden,
         slope,
         up_full,
         down_full,
-    )
+        (so_far, norm_two, pace_two, mlp_gain, mixed, out_full),
+        after,
+    )
+    up_bias_grad = jnp.concatenate([up_bias_grad, bias_rest], axis=1)
     mlp_gain_grad, mlp_shift_grad, out_bias_grad, down_bias_grad = (lines[n] for n in range(4))
-    after = ()
     if halved:
-        up_flow, down_flow, out_flow = (
-            core_step(*pair)
-            for pair in ((up_keep, up_give), (down_keep, down_give), (out_keep, out_give))
-        )
-        after = (up_flow, down_flow, out_flow)
+        side = up_weight.shape[1]
+        down_flow = chips_step((down_flow[..., :side], down_flow[..., side:]))
+        up_flow = jnp.concatenate([core_step(up_keep, up_give), core_step(keep_rest, give_rest)], axis=-1)
+        out_flow = core_step(out_keep, out_give)
+        after = (down_flow, up_flow, out_flow)
     d_parts = [None, None]
     for number in (1, 0):
         d_parts[number] = attention_backward(
             places, *projected[number], mixed[number], d_mixed[number], stats[number], block, length, after
         )
         if halved and number == 1:
-            side = up_weight.shape[1]
             up_flow = side_exchange(
                 jnp.concatenate([up_flow[..., :side], out_flow[..., : width // 2]], axis=-1),
                 jnp.concatenate([up_flow[..., side:], out_flow[..., width // 2 :]], axis=-1),
             )
-            down_sides = overlap_step((down_flow[..., :side], down_flow[..., side:]))
-            after = (up_flow, *down_sides)
+            down_flow = blocks_step(down_flow)
+            after = (up_flow, down_flow)
         if halved and number == 0:
-            up_flow, down_flow = blocks_step(up_flow), side_exchange(*down_sides)
+            up_flow, down_flow = blocks_step(up_flow), side_exchange(*two(down_flow))
             after = (up_flow, down_flow)
-    d_act_all = tokens_back(d_parts, weights, after)
-    shared = own_tokens_sum(d_act_all[:prompt_len])
-    grads = weights_back(half, count, act_all.T, d_parts, (d_act_all,))
-    keeps, gives = (grads[0:3], grads[8:11]), (grads[3:6], grads[11:14])
+    keep_a, give_a, bias_a, keep_b, give_b, bias_b = weights_back(half, count, act_all.T, d_parts, after)
+    d_act_all = tokens_back(d_parts, weights, (keep_a,))
+    others = others_tokens(d_act_all[:prompt_len])
+    size = bias_b.shape[1] // 3
     query_bias_grad, value_bias_grad = (
-        jnp.concatenate([grads[6 + n], grads[14 + n]], axis=1).reshape(-1) for n in range(2)
+        jnp.concatenate(
+            [bias_a[0, n * GROUP : (n + 1) * GROUP], bias_b[0, n * size : n * size + width - GROUP]]
+        )
+        for n in (0, 2)
     )
     if halved:
-        sides = [
-            core_step(keep, give)
-            for keep, give in zip(projection_sides(*keeps, width), projection_sides(*gives, width))
-        ]
-        qkv_flow = side_exchange(*overlap_step(sides))
-        qkv_total = join_projections(
-            join_step(overlap_join(blocks_step(qkv_flow), qkv_weight.shape[1])),
-            width,
-        )
+        sides = projection_sides(core_step(keep_a, give_a), core_step(keep_b, give_b))
+        qkv_flow = blocks_step(side_exchange(*two(chips_step(sides))))
+        qkv_total = join_projections(join_step(overlap_join(qkv_flow, sides[0].shape[-1])), width)
         up_total = join_step(copies_step(up_flow))
         up_total, out_total = up_total[:, :side], up_total[:, side:]
-        down_total = join_step(overlap_join(blocks_step(down_flow), side))
+        down_total = join_step(overlap_join(down_flow, side))
     else:
+        whole_a, whole_b = both_halves(keep_a, give_a), both_halves(keep_b, give_b)
         qkv_grad = jnp.concatenate(
-            [both_halves(keeps[n][kind], gives[n][kind]) for kind in range(3) for n in range(2)], axis=1
+            [
+                piece
+                for n in range(3)
+                for piece in (
+                    whole_a[:, n * GROUP : (n + 1) * GROUP],
+                    whole_b[:, n * size : n * size + width - GROUP],
+                )
+            ],
+            axis=1,
         )
         up_total, down_total, out_total, qkv_total = (
             scatter_plain(g)
             for g in (
-                both_halves(up_keep, up_give),
+                jnp.concatenate([both_halves(up_keep, up_give), both_halves(keep_rest, give_rest)], axis=1),
                 both_halves(down_keep, down_give),
                 both_halves(out_keep, out_give),
                 qkv_grad,
@@ -1161,9 +1258,6 @@
     d_act_exact = d_act_all.astype(jnp.float32)
     attn_gain_grad = jnp.sum(d_act_exact * norm_all, axis=0)
     attn_shift_grad = jnp.sum(d_act_exact, axis=0)
-    norm_own, pace_own = normalise(jnp.concatenate([own_prompt, branch], axis=0).astype(jnp.float32))
-    d_act_own = jnp.concatenate([shared, d_act_all[prompt_len:]], axis=0)
-    rows_part = norm_back(d_act_own, norm_own, pace_own, attn_gain)
     prompt_resid = d_resid[:shard]
     if halved:
         home = back_home(prompt_resid.astype(jnp.bfloat16)).astype(jnp.float32)
@@ -1171,9 +1265,14 @@
             is_long, home[block:], prompt_resid[:block]
         )
         prompt_resid = jnp.concatenate(kept, axis=0)
-    d_rows = jnp.concatenate([prompt_resid, d_resid[shard:]], axis=0) + rows_part
-    prompt_grad = d_rows[:shard].reshape(groups, shard, width)
-    continuation_grad = d_rows[shard:].reshape(1, length, width)
+    own_rows = jnp.concatenate([own_prompt, branch], axis=0)
+    own_grad = jnp.concatenate(
+        [lax.dynamic_slice_in_dim(d_act_all, first_pos, shard, 0), d_act_all[prompt_len:]], axis=0
+    )
+    resid_rows = jnp.concatenate([prompt_resid, d_resid[shard:]], axis=0)
+    prompt_grad, branch_grad = rows_back(others, own_grad, own_rows, resid_rows, attn_gain, length)
+    prompt_grad = prompt_grad.T.reshape(groups, shard, width)
+    continuation_grad = branch_grad.T.reshape(1, length, width)
     vectors = (
         attn_gain_grad,
         attn_shift_grad,

time: 995 us -> 1110 us (1.12)
  waiting for transfers between devices: 211 us -> 292 us
  Pallas kernels: 391 us -> 415 us
    ppermute x12, waiting for transfers between devices: 27.2 us -> 105 us  [ahead(): lax.ppermute(value, axis, [(i, (i + step) % count) for i in range(count)])]
    pallas_call x2 -> x5, Pallas kernels: 116 us -> 140 us  [the longest x2 81.7 us: up_back(): pl.pallas_call(up_back_first_kernel if final is None else up_back_last_ke...]
    concatenate x7 -> x2, local copies, waits for them, and re-layouts: 24.6 us -> 4.15 us  [the longest x1 2.4 us: join_projections(): jnp.concatenate([query, query_rest, key, key_spare], axis=1)]
    pallas_call x3 -> x0, local copies, waits for them, and re-layouts: 19.9 us -> none  [the longest x1 8.46 us: tokens_back(): pl.pallas_call(functools.partial(tokens_back_kernel, widths=widths), grid...]
    transpose x0 -> x2, local copies, waits for them, and re-layouts: none -> 14 us  [the longest x1 8.52 us: local(): keep_a, give_a, bias_a, keep_b, give_b, bias_b = weights_back(half, count...]
    unnamed x212 -> x230, local copies, waits for them, and re-layouts: 26.7 us -> 40.3 us
    ppermute x1 -> x5, local copies, waits for them, and re-layouts: 2.81 us -> 15 us  [swap(): return lax.ppermute(value, axis, [(i, i ^ bit) for i in range(count)])]
    concatenate x4 -> x6, other arithmetic: 5.29 us -> 16.9 us  [the longest x1 8.48 us: local(): own_rows = jnp.concatenate([own_prompt, branch], axis=0)]
  transfers between devices with their start and end apart: 45 -> 46, of which waited for: 15 -> 20; matrix products, arithmetic and copies ran while one was open for 25% -> 21% of each run, Pallas kernels for 24% -> 23%
where the time goes in v4:
time: 1110 us; the launch traced here: 1090 us
  Pallas kernels  415 us (37%)
  waiting for transfers between devices  292 us (26%)
  local copies, waits for them, and re-layouts  129 us (12%)
  other arithmetic  129 us (12%)
  starting transfers between devices  76.8 us (7%)
  matrix products  35 us (3%)
  between operations  18.2 us (2%)
    ppermute x31, waiting for transfers between devices, swap(): return lax.ppermute(value, axis, [(i, i ^ bit) for i in range(count)])  187 us
    ppermute x12, waiting for transfers between devices, ahead(): lax.ppermute(value, axis, [(i, (i + step) % count) for i in range(count)])  105 us
    pallas_call x2, Pallas kernels, attention_backward(): pl.pallas_call(functools.partial(backward_kernel, block=block, branch=bra...  104 us
    pallas_call x2, Pallas kernels, up_back(): pl.pallas_call(up_back_first_kernel if final is None else up_back_last_ke...  81.7 us
    pallas_call x2, Pallas kernels, attention_forward(): pl.pallas_call(functools.partial(forward_kernel, block=block, branch=bran...  74.1 us
    pallas_call x1, Pallas kernels, mlp_forward(): pl.pallas_call(mlp_forward_kernel, grid=(inner // TILE,), in_specs=[fixed...  65 us
    ppermute x12, starting transfers between devices, ahead(): lax.ppermute(value, axis, [(i, (i + step) % count) for i in range(count)])  54 us
    unnamed x230, local copies, waits for them, and re-layouts  40.3 us
  transfers between devices with their start and end apart: 46, of which 20 were waited for; matrix products, arithmetic and copies ran while one was open for 21% of the time, Pallas kernels for 23%

profile of v4, /device:TPU:0, one launch (start us, length us, event | category | flops | bytes accessed | tf_op | source)
XLA Modules:
  0.0 1094.9 jit_solution(9988522475684637835)
XLA Ops:
  26.6 49.1 %collective-permute-done = s32[1]{0:T(128)} collective-permute-done((s32[1]{0:T(128)}, s32[1]{0:T(128)}, u32[]{:S(2)}, u32[]{:S(2)}) %collective-permute-start) | collective-permute-done | bytes 36 | tf_op jit(solution)/shard_map/ppermute | solution.py:832
  101.2 6.5 fusion.4
  107.7 8.5 pad_maximum_fusion.3
  137.3 6.9 fusion.10.v
  150.5 23.6 %collective-permute-done.3 = bf16[272,1152]{1,0:T(8,128)(2,1)} collective-permute-done((bf16[272,1152]{1,0:T(8,128)(2,1)}, bf16[272,1152]{1,0:T(8,128)(2,1)}, u32[]{:S(2)}, u32[]{:S(2)}) %collective-permute-start.3) | collective-permute-done | bytes 626720 | tf_op jit(solution)/shard_map/ppermute | solution.py:837
  177.4 32.9 %attention_forward.2 = (bf16[1280,512]{1,0:T(8,128)(2,1)S(1)}, f32[4,8,1280]{2,1,0:T(8,128)S(1)}) custom-call(s32[3]{0:T(128)S(1)} %pad_add_fusion.pos, bf16[2304,512]{1,0:T(8,128)(2,1)S(1)} %fusion.9.q, bf16[2304,512]{1,0:T(8,128)(2,1)S(1)} %convolution_convert_fusion.1.k, bf16[2304,512]{1,0:T(8,128)(2,1)S(1)} %fusion.10.v), custom_call_target="tpu_custom_call" | custom-call | flops 28000000000 | bytes 28000000 | tf_op jit(solution)/shard_map/attention_forward/pallas_call | solution.py:169
  223.9 15.0 %collective-permute-done.5 = bf16[1088,1152]{1,0:T(8,128)(2,1)} collective-permute-done((bf16[1088,1152]{1,0:T(8,128)(2,1)S(1)}, bf16[1088,1152]{1,0:T(8,128)(2,1)}, u32[]{:S(2)}, u32[]{:S(2)}) %collective-permute-start.5) | collective-permute-done | bytes 2506784 | tf_op jit(solution)/shard_map/ppermute | solution.py:832
  249.8 8.8 convolution_convert_fusion.k
  268.4 41.2 %attention_forward.3 = (bf16[1280,576]{1,0:T(8,128)(2,1)S(1)}, f32[5,8,1280]{2,1,0:T(8,128)S(1)}) custom-call(s32[3]{0:T(128)S(1)} %pad_add_fusion.pos, bf16[2304,576]{1,0:T(8,128)(2,1)S(1)} %add_convert_fusion.3.q, bf16[2304,576]{1,0:T(8,128)(2,1)S(1)} %convolution_convert_fusion.k, bf16[2304,576]{1,0:T(8,128)(2,1)S(1)} %add_convert_fusion.2.v, ...), custom_call_target="tpu_custom_call" | custom-call | flops 35000000512 | bytes 35000000 | tf_op jit(solution)/shard_map/attention_forward/pallas_call | solution.py:169
  334.7 65.0 %mlp_forward.1 = (bf16[1280,4352]{1,0:T(8,128)(2,1)}, bf16[1280,4352]{1,0:T(8,128)(2,1)}, bf16[1280,1088]{1,0:T(8,128)(2,1)}, bf16[1088,1280]{1,0:T(8,128)(2,1)}...) custom-call(bf16[1280,512]{1,0:T(8,128)(2,1)S(1)} %copy-done.20, bf16[1280,576]{1,0:T(8,128)(2,1)} %copy-done.22, ...), custom_call_target="tpu_custom_call" | custom-call | flops 49999998976 | bytes 50000000 | tf_op jit(solution)/shard_map/mlp_forward/pallas_call | solution.py:409
  399.7 20.1 %down_back.1 = (bf16[4,136,4352]{2,1,0:T(8,128)(2,1)S(1)}, bf16[4,136,4352]{2,1,0:T(8,128)(2,1)}) custom-call(s32[1]{0:T(128)} %bitcast.43.half, bf16[1088,1280]{1,0:T(8,128)(2,1)S(1)} %copy-done.4, bf16[1280,4352]{1,0:T(8,128)(2,1)} %get-tuple-element.64.hidden), custom_call_target="tpu_custom_call" | custom-call | flops 15000000512 | bytes 15000000 | tf_op jit(solution)/shard_map/down_back/pallas_call | solution.py:470
  422.0 29.8 %up_back_first.1 = (f32[1280,1088]{1,0:T(8,128)}, bf16[4,136,2048]{2,1,0:T(8,128)(2,1)}, bf16[4,136,2048]{2,1,0:T(8,128)(2,1)}, f32[1,2048]{1,0:T(1,128)}) custom-call(s32[1]{0:T(128)} %bitcast.43.half, bf16[1088,1280]{1,0:T(8,128)(2,1)} %get-tuple-element.59.act_turned, bf16[1280,1088]{1,0:T(8,128)(2,1)} %get-tuple-element.185.cot, ...), custom_call_target="tpu_custom_call" | custom-call | flops 30000001024 | bytes 30000000 | tf_op jit(solution)/shard_map/up_back_first/pallas_call | solution.py:599
  454.6 8.5 copy.114.turned
  468.4 12.7 %collective-permute-done.8 = bf16[512,1088]{0,1:T(8,128)(2,1)} collective-permute-done((bf16[512,1088]{0,1:T(8,128)(2,1)S(1)}, bf16[512,1088]{0,1:T(8,128)(2,1)}, u32[]{:S(2)}, u32[]{:S(2)}) %collective-permute-start.8) | collective-permute-done | bytes 1114144 | tf_op jit(solution)/shard_map/ppermute | solution.py:832
  494.8 7.1 add_convert_fusion.rest_0_
  501.9 51.9 %up_back_last.1 = (f32[1280,1088]{1,0:T(8,128)}, bf16[1280,512]{1,0:T(8,128)(2,1)}, bf16[1280,576]{1,0:T(8,128)(2,1)}, bf16[4,136,2304]{2,1,0:T(8,128)(2,1)}, bf...) custom-call(s32[1]{0:T(128)} %bitcast.43.half, ...), custom_call_target="tpu_custom_call" | custom-call | flops 49999998976 | bytes 50000000 | tf_op jit(solution)/shard_map/up_back_last/pallas_call | solution.py:599
  570.0 18.1 %collective-permute-done.24 = bf16[512,1088]{0,1:T(8,128)(2,1)} collective-permute-done((bf16[512,1088]{0,1:T(8,128)(2,1)}, bf16[512,1088]{0,1:T(8,128)(2,1)}, u32[]{:S(2)}, u32[]{:S(2)}) %collective-permute-start.24) | collective-permute-done | bytes 1114144 | tf_op jit(solution)/shard_map/ppermute | solution.py:832
  600.1 24.0 %collective-permute-done.15 = bf16[4,136,2304]{2,1,0:T(8,128)(2,1)} collective-permute-done((bf16[4,136,2304]{2,1,0:T(8,128)(2,1)}, bf16[4,136,2304]{2,1,0:T(8,128)(2,1)}, u32[]{:S(2)}, u32[]{:S(2)}) %collective-permute-start.15) | collective-permute-done | bytes 2506784 | tf_op jit(solution)/shard_map/ppermute | solution.py:832
  626.5 37.3 %collective-permute-start.18 = (bf16[136,2304]{1,0:T(8,128)(2,1)S(1)}, bf16[136,2304]{1,0:T(8,128)(2,1)S(1)}, u32[]{:S(2)}, u32[]{:S(2)}) collective-permute-start(bf16[136,2304]{1,0:T(8,128)(2,1)S(1)} %get-tuple-element.190), channel_id=1, source_target_pairs={{0,6},{2,0},{4,2},{6,4},{1,7},{3,1},{5,3},{7,5},{8,14},{10,8},{12,... | collective-permute-start | bytes 1880072 | tf_op jit(solution)/shard_map/ppermute | solution.py:837
  667.5 10.9 collective-permute-done.18
  678.4 38.1 %collective-permute-done.17 = bf16[136,2304]{1,0:T(8,128)(2,1)S(1)} collective-permute-done((bf16[136,2304]{1,0:T(8,128)(2,1)S(1)}, bf16[136,2304]{1,0:T(8,128)(2,1)S(1)}, u32[]{:S(2)}, u32[]{:S(2)}) %collective-permute-start.17) | collective-permute-done | bytes 626720 | tf_op jit(solution)/shard_map/ppermute | solution.py:837
  731.3 57.5 %attention_backward.3 = (bf16[2304,576]{1,0:T(8,128)(2,1)S(1)}, bf16[2304,576]{1,0:T(8,128)(2,1)S(1)}, bf16[2304,576]{1,0:T(8,128)(2,1)}) custom-call(s32[3]{0:T(128)S(1)} %pad_add_fusion.pos, bf16[2304,576]{1,0:T(8,128)(2,1)} %copy-done.12, bf16[2304,576]{1,0:T(8,128)(2,1)} %copy-done.11, bf16[2304,576]{1,0:T(8,128)(2,1)} %copy-done.13, ...), custom_call_target="tpu_custom_call" | custom-call | flops 49999998976 | bytes 50000000 | tf_op jit(solution)/shard_map/attention_backward/pallas_call | solution.py:305
  794.8 6.3 collective-permute-start.20
  803.1 46.6 %attention_backward.2 = (bf16[2304,512]{1,0:T(8,128)(2,1)S(1)}, bf16[2304,512]{1,0:T(8,128)(2,1)S(1)}, bf16[2304,512]{1,0:T(8,128)(2,1)S(1)}) custom-call(s32[3]{0:T(128)S(1)} %pad_add_fusion.pos, bf16[2304,512]{1,0:T(8,128)(2,1)S(1)} %copy-done.9, bf16[2304,512]{1,0:T(8,128)(2,1)} %copy-done.7, bf16[2304,512]{1,0:T(8,128)(2,1)} %copy-done.10, ...), custom_call_target="tpu_custom_call" | custom-call | flops 40000000000 | bytes 40000000 | tf_op jit(solution)/shard_map/attention_backward/pallas_call | solution.py:305
  852.6 14.8 %collective-permute-done.20 = bf16[136,2720]{1,0:T(8,128)(2,1)S(1)} collective-permute-done((bf16[136,2720]{1,0:T(8,128)(2,1)S(1)}, bf16[136,2720]{1,0:T(8,128)(2,1)S(1)}, u32[]{:S(2)}, u32[]{:S(2)}) %collective-permute-start.20) | collective-permute-done | bytes 739872 | tf_op jit(solution)/shard_map/ppermute | solution.py:837
  868.9 30.9 %weights_back.1 = (bf16[4,136,1536]{2,1,0:T(8,128)(2,1)}, bf16[4,136,1536]{2,1,0:T(8,128)(2,1)}, f32[1,1536]{1,0:T(1,128)S(1)}, bf16[4,136,2304]{2,1,0:T(8,128)(...) custom-call(s32[1]{0:T(128)} %bitcast.43.half, bf16[1088,2304]{1,0:T(8,128)(2,1)} %copy.114.turned, ...), custom_call_target="tpu_custom_call" | custom-call | flops 24999999488 | bytes 25000000 | tf_op jit(solution)/shard_map/weights_back/pallas_call | solution.py:728
  900.4 32.3 %tokens_back.1 = bf16[2304,1088]{1,0:T(8,128)(2,1)} custom-call(bf16[2304,512]{1,0:T(8,128)(2,1)} %copy-done.16, bf16[2304,512]{1,0:T(8,128)(2,1)} %copy-done.17, bf16[2304,512]{1,0:T(8,128)(2,1)} %copy-done.18, bf16[2304,576]{1,0:T(8,128)(2,1)} %copy-done.14, bf16[2304,576]{1,0:T(8,128)(2,1)} %copy-done.15, bf16[2304,576]{1,0:T(8,128)(2,1)} %get-tuple-element.82.refs_5_, ...), custom_call_target="tpu_custom_call" | custom-call | flops 20000000000 | bytes 20000000 | tf_op jit(solution)/shard_map/tokens_back/pallas_call | solution.py:673
  932.9 7.5 convert_reduce_fusion
  976.1 29.7 %collective-permute-done.32 = bf16[4,136,1792]{2,1,0:T(8,128)(2,1)} collective-permute-done((bf16[4,136,1792]{2,1,0:T(8,128)(2,1)}, bf16[4,136,1792]{2,1,0:T(8,128)(2,1)}, u32[]{:S(2)}, u32[]{:S(2)}) %collective-permute-start.32) | collective-permute-done | bytes 1949728 | tf_op jit(solution)/shard_map/ppermute | solution.py:832
  1010.5 24.0 %collective-permute-done.33 = bf16[4,136,896]{2,1,0:T(8,128)(2,1)S(1)} collective-permute-done((bf16[4,136,896]{2,1,0:T(8,128)(2,1)S(1)}, bf16[4,136,896]{2,1,0:T(8,128)(2,1)S(1)}, u32[]{:S(2)}, u32[]{:S(2)}) %collective-permute-start.33) | collective-permute-done | bytes 974880 | tf_op jit(solution)/shard_map/ppermute | solution.py:832
  1042.8 11.7 %collective-permute-done.35 = bf16[136,896]{1,0:T(8,128)(2,1)S(1)} collective-permute-done((bf16[136,896]{1,0:T(8,128)(2,1)S(1)}, bf16[136,896]{1,0:T(8,128)(2,1)S(1)}, u32[]{:S(2)}, u32[]{:S(2)}) %collective-permute-start.35) | collective-permute-done | bytes 243744 | tf_op jit(solution)/shard_map/ppermute | solution.py:837
  1070.5 6.8 rows_back.1
  (467 shorter events, 292.5 us)
Async XLA Ops:
  7.2 109.0 %all-gather.7.cloned.1.call-start = ((), (), s32[]{:S(2)}) async-start(), calls=%async_computation | async-start | bytes 4595712 | tf_op jit(solution)/shard_map/all_gather | solution.py:876
  9.5 234.4 %all-gather.9.cloned.1.call-start = ((), (), s32[]{:S(2)}) async-start(), calls=%async_computation.1 | async-start | bytes 6893568 | tf_op jit(solution)/shard_map/all_gather | solution.py:876
  11.7 301.9 %all-gather.11.cloned.1.call-start = ((), (), s32[]{:S(2)}) async-start(), calls=%async_computation.2 | async-start | bytes 9191424 | tf_op jit(solution)/shard_map/all_gather | solution.py:876
  11.8 73.3 %collective-permute-start.1 = (bf16[1024,1088]{0,1:T(8,128)(2,1)}, bf16[1024,1088]{0,1:T(8,128)(2,1)}, u32[]{:S(2)}, u32[]{:S(2)}) collective-permute-start(bf16[1024,1088]{0,1:T(8,128)(2,1)} %bitcast.5), channel_id=1, source_target_pairs={{0,1},{1,0},{2,3},{3,2},{4,5},{5,4},{6,7},{7,6},{8,9},{9,8},{10,11... | collective-permute-start | bytes 6684680 | tf_op jit(solution)/shard_map/ppermute | solution.py:832
  14.8 60.9 %collective-permute-start = (s32[1]{0:T(128)}, s32[1]{0:T(128)}, u32[]{:S(2)}, u32[]{:S(2)}) collective-permute-start(s32[1]{0:T(128)} %param.20), channel_id=1, source_target_pairs={{0,1},{1,0},{2,3},{3,2},{4,5},{5,4},{6,7},{7,6},{8,9},{9,8},{10,11... | collective-permute-start | bytes 20 | tf_op jit(solution)/shard_map/ppermute | solution.py:832
  116.2 33.2 %collective-permute-start.2 = (bf16[272,1152]{1,0:T(8,128)(2,1)}, bf16[272,1152]{1,0:T(8,128)(2,1)}, u32[]{:S(2)}, u32[]{:S(2)}) collective-permute-start(bf16[272,1152]{1,0:T(8,128)(2,1)} %gate.2), channel_id=1, source_target_pairs={{0,2},{2,4},{4,6},{6,0},{1,3},{3,5},{5,7},{7,1},{8,10},{10,12},{12... | collective-permute-start | bytes 1880072 | tf_op jit(solution)/shard_map/ppermute | solution.py:837
  117.9 56.3 %collective-permute-start.3 = (bf16[272,1152]{1,0:T(8,128)(2,1)}, bf16[272,1152]{1,0:T(8,128)(2,1)}, u32[]{:S(2)}, u32[]{:S(2)}) collective-permute-start(bf16[272,1152]{1,0:T(8,128)(2,1)} %gate.2), channel_id=1, source_target_pairs={{0,4},{2,6},{4,0},{6,2},{1,5},{3,7},{5,1},{7,3},{8,12},{10,14},{12... | collective-permute-start | bytes 1880072 | tf_op jit(solution)/shard_map/ppermute | solution.py:837
  120.7 54.6 %collective-permute-start.4 = (bf16[272,1152]{1,0:T(8,128)(2,1)}, bf16[272,1152]{1,0:T(8,128)(2,1)}, u32[]{:S(2)}, u32[]{:S(2)}) collective-permute-start(bf16[272,1152]{1,0:T(8,128)(2,1)} %gate.2), channel_id=1, source_target_pairs={{0,6},{2,0},{4,2},{6,4},{1,7},{3,1},{5,3},{7,5},{8,14},{10,8},{12,... | collective-permute-start | bytes 1880072 | tf_op jit(solution)/shard_map/ppermute | solution.py:837
  128.7 82.7 %collective-permute-start.9 = (bf16[512,1088]{0,1:T(8,128)(2,1)}, bf16[512,1088]{0,1:T(8,128)(2,1)}, u32[]{:S(2)}, u32[]{:S(2)}) collective-permute-start(bf16[512,1088]{0,1:T(8,128)(2,1)} %copy.110), channel_id=1, source_target_pairs={{0,1},{1,0},{2,3},{3,2},{4,5},{5,4},{6,7},{7,6},{8,9},{9,8},{10,11... | collective-permute-start | bytes 3342344 | tf_op jit(solution)/shard_map/ppermute | solution.py:832
  176.5 62.4 %collective-permute-start.5 = (bf16[1088,1152]{1,0:T(8,128)(2,1)S(1)}, bf16[1088,1152]{1,0:T(8,128)(2,1)}, u32[]{:S(2)}, u32[]{:S(2)}) collective-permute-start(bf16[1088,1152]{1,0:T(8,128)(2,1)S(1)} %bitcast.175), channel_id=1, source_target_pairs={{0,1},{1,0},{2,3},{3,2},{4,5},{5,4},{6,7},{7,6},{8,9},{9,8},{10,11... | collective-permute-start | bytes 7520264 | tf_op jit(solution)/shard_map/ppermute | solution.py:832
  243.4 74.8 %collective-permute-start.6 = (bf16[1088,1152]{1,0:T(8,128)(2,1)}, bf16[1088,1152]{1,0:T(8,128)(2,1)}, u32[]{:S(2)}, u32[]{:S(2)}) collective-permute-start(bf16[1088,1152]{1,0:T(8,128)(2,1)} %get-tuple-element.160), channel_id=1, source_target_pairs={{0,8},{8,0},{16,24},{24,16},{1,9},{9,1},{17,25},{25,17},{2,10},{10... | collective-permute-start | bytes 7520264 | tf_op jit(solution)/shard_map/ppermute | solution.py:832
  243.4 82.5 %collective-permute-start.7 = (bf16[1088,1152]{1,0:T(8,128)(2,1)}, bf16[1088,1152]{1,0:T(8,128)(2,1)}, u32[]{:S(2)}, u32[]{:S(2)}) collective-permute-start(bf16[1088,1152]{1,0:T(8,128)(2,1)} %get-tuple-element.159), channel_id=1, source_target_pairs={{0,8},{8,0},{16,24},{24,16},{1,9},{9,1},{17,25},{25,17},{2,10},{10... | collective-permute-start | bytes 7520264 | tf_op jit(solution)/shard_map/ppermute | solution.py:832
  422.0 72.8 %collective-permute-start.10 = (bf16[4,136,4352]{2,1,0:T(8,128)(2,1)}, bf16[4,136,4352]{2,1,0:T(8,128)(2,1)}, u32[]{:S(2)}, u32[]{:S(2)}) collective-permute-start(bf16[4,136,4352]{2,1,0:T(8,128)(2,1)} %get-tuple-element.66), channel_id=1, source_target_pairs={{0,8},{8,0},{16,24},{24,16},{1,9},{9,1},{17,25},{25,17},{2,10},{10... | collective-permute-start | bytes 14204936 | tf_op jit(solution)/shard_map/ppermute | solution.py:832
  451.9 38.3 %collective-permute-start.11 = (bf16[4,136,2048]{2,1,0:T(8,128)(2,1)}, bf16[4,136,2048]{2,1,0:T(8,128)(2,1)}, u32[]{:S(2)}, u32[]{:S(2)}) collective-permute-start(bf16[4,136,2048]{2,1,0:T(8,128)(2,1)} %get-tuple-element.70), channel_id=1, source_target_pairs={{0,8},{8,0},{16,24},{24,16},{1,9},{9,1},{17,25},{25,17},{2,10},{10... | collective-permute-start | bytes 6684680 | tf_op jit(solution)/shard_map/ppermute | solution.py:832
  454.4 26.7 %collective-permute-start.8 = (bf16[512,1088]{0,1:T(8,128)(2,1)S(1)}, bf16[512,1088]{0,1:T(8,128)(2,1)}, u32[]{:S(2)}, u32[]{:S(2)}) collective-permute-start(bf16[512,1088]{0,1:T(8,128)(2,1)S(1)} %copy.105), channel_id=1, source_target_pairs={{0,1},{1,0},{2,3},{3,2},{4,5},{5,4},{6,7},{7,6},{8,9},{9,8},{10,11... | collective-permute-start | bytes 3342344 | tf_op jit(solution)/shard_map/ppermute | solution.py:832
  559.1 38.8 %collective-permute-start.13 = (bf16[4,136,1088]{2,1,0:T(8,128)(2,1)}, bf16[4,136,1088]{2,1,0:T(8,128)(2,1)}, u32[]{:S(2)}, u32[]{:S(2)}) collective-permute-start(bf16[4,136,1088]{2,1,0:T(8,128)(2,1)} %get-tuple-element.74), channel_id=1, source_target_pairs={{0,8},{8,0},{16,24},{24,16},{1,9},{9,1},{17,25},{25,17},{2,10},{10... | collective-permute-start | bytes 3551240 | tf_op jit(solution)/shard_map/ppermute | solution.py:832
  559.2 105.3 %collective-permute-start.12 = (bf16[4,136,2304]{2,1,0:T(8,128)(2,1)}, bf16[4,136,2304]{2,1,0:T(8,128)(2,1)}, u32[]{:S(2)}, u32[]{:S(2)}) collective-permute-start(bf16[4,136,2304]{2,1,0:T(8,128)(2,1)} %get-tuple-element.72), channel_id=1, source_target_pairs={{0,8},{8,0},{16,24},{24,16},{1,9},{9,1},{17,25},{25,17},{2,10},{10... | collective-permute-start | bytes 7520264 | tf_op jit(solution)/shard_map/ppermute | solution.py:832
  568.1 56.0 %collective-permute-start.15 = (bf16[4,136,2304]{2,1,0:T(8,128)(2,1)}, bf16[4,136,2304]{2,1,0:T(8,128)(2,1)}, u32[]{:S(2)}, u32[]{:S(2)}) collective-permute-start(bf16[4,136,2304]{2,1,0:T(8,128)(2,1)} %broadcast_select_fusion.1), channel_id=1, source_target_pairs={{0,16},{8,24},{16,0},{24,8},{1,17},{9,25},{17,1},{25,9},{2,18},{10... | collective-permute-start | bytes 7520264 | tf_op jit(solution)/shard_map/ppermute | solution.py:832
  626.5 51.9 %collective-permute-start.18 = (bf16[136,2304]{1,0:T(8,128)(2,1)S(1)}, bf16[136,2304]{1,0:T(8,128)(2,1)S(1)}, u32[]{:S(2)}, u32[]{:S(2)}) collective-permute-start(bf16[136,2304]{1,0:T(8,128)(2,1)S(1)} %get-tuple-element.190), channel_id=1, source_target_pairs={{0,6},{2,0},{4,2},{6,4},{1,7},{3,1},{5,3},{7,5},{8,14},{10,8},{12,... | collective-permute-start | bytes 1880072 | tf_op jit(solution)/shard_map/ppermute | solution.py:837
  663.8 52.7 %collective-permute-start.17 = (bf16[136,2304]{1,0:T(8,128)(2,1)S(1)}, bf16[136,2304]{1,0:T(8,128)(2,1)S(1)}, u32[]{:S(2)}, u32[]{:S(2)}) collective-permute-start(bf16[136,2304]{1,0:T(8,128)(2,1)S(1)} %get-tuple-element.191), channel_id=1, source_target_pairs={{0,4},{2,6},{4,0},{6,2},{1,5},{3,7},{5,1},{7,3},{8,12},{10,14},{12... | collective-permute-start | bytes 1880072 | tf_op jit(solution)/shard_map/ppermute | solution.py:837
  664.2 52.3 %collective-permute-start.16 = (bf16[136,2304]{1,0:T(8,128)(2,1)S(1)}, bf16[136,2304]{1,0:T(8,128)(2,1)S(1)}, u32[]{:S(2)}, u32[]{:S(2)}) collective-permute-start(bf16[136,2304]{1,0:T(8,128)(2,1)S(1)} %get-tuple-element.189), channel_id=1, source_target_pairs={{0,2},{2,4},{4,6},{6,0},{1,3},{3,5},{5,7},{7,1},{8,10},{10,12},{12... | collective-permute-start | bytes 1880072 | tf_op jit(solution)/shard_map/ppermute | solution.py:837
  727.6 64.2 %collective-permute-start.14 = (bf16[4,136,2720]{2,1,0:T(8,128)(2,1)}, bf16[4,136,2720]{2,1,0:T(8,128)(2,1)}, u32[]{:S(2)}, u32[]{:S(2)}) collective-permute-start(bf16[4,136,2720]{2,1,0:T(8,128)(2,1)} %broadcast_select_fusion), channel_id=1, source_target_pairs={{0,1},{1,0},{2,3},{3,2},{4,5},{5,4},{6,7},{7,6},{8,9},{9,8},{10,11... | collective-permute-start | bytes 8878088 | tf_op jit(solution)/shard_map/ppermute | solution.py:832
  731.2 57.7 %collective-permute-start.42 = (bf16[136,2176]{1,0:T(8,128)(2,1)S(1)}, bf16[136,2176]{1,0:T(8,128)(2,1)S(1)}, u32[]{:S(2)}, u32[]{:S(2)}) collective-permute-start(bf16[136,2176]{1,0:T(8,128)(2,1)S(1)} %pad_maximum_fusion.24), channel_id=1, source_target_pairs={{0,8},{8,0},{16,24},{24,16},{1,9},{9,1},{17,25},{25,17},{2,10},{10... | collective-permute-start | bytes 1775624 | tf_op jit(solution)/shard_map/ppermute | solution.py:832
  794.7 57.8 %collective-permute-start.21 = (bf16[136,2720]{1,0:T(8,128)(2,1)S(1)}, bf16[136,2720]{1,0:T(8,128)(2,1)S(1)}, u32[]{:S(2)}, u32[]{:S(2)}) collective-permute-start(bf16[136,2720]{1,0:T(8,128)(2,1)S(1)} %get-tuple-element.182), channel_id=1, source_target_pairs={{0,6},{2,0},{4,2},{6,4},{1,7},{3,1},{5,3},{7,5},{8,14},{10,8},{12,... | collective-permute-start | bytes 2219528 | tf_op jit(solution)/shard_map/ppermute | solution.py:837
  794.8 72.6 %collective-permute-start.20 = (bf16[136,2720]{1,0:T(8,128)(2,1)S(1)}, bf16[136,2720]{1,0:T(8,128)(2,1)S(1)}, u32[]{:S(2)}, u32[]{:S(2)}) collective-permute-start(bf16[136,2720]{1,0:T(8,128)(2,1)S(1)} %get-tuple-element.183), channel_id=1, source_target_pairs={{0,4},{2,6},{4,0},{6,2},{1,5},{3,7},{5,1},{7,3},{8,12},{10,14},{12... | collective-permute-start | bytes 2219528 | tf_op jit(solution)/shard_map/ppermute | solution.py:837
  801.1 66.2 %collective-permute-start.19 = (bf16[136,2720]{1,0:T(8,128)(2,1)S(1)}, bf16[136,2720]{1,0:T(8,128)(2,1)S(1)}, u32[]{:S(2)}, u32[]{:S(2)}) collective-permute-start(bf16[136,2720]{1,0:T(8,128)(2,1)S(1)} %get-tuple-element.181), channel_id=1, source_target_pairs={{0,2},{2,4},{4,6},{6,0},{1,3},{3,5},{5,7},{7,1},{8,10},{10,12},{12... | collective-permute-start | bytes 2219528 | tf_op jit(solution)/shard_map/ppermute | solution.py:837
  899.9 49.6 %collective-permute-start.31 = (bf16[4,136,2304]{2,1,0:T(8,128)(2,1)}, bf16[4,136,2304]{2,1,0:T(8,128)(2,1)}, u32[]{:S(2)}, u32[]{:S(2)}) collective-permute-start(bf16[4,136,2304]{2,1,0:T(8,128)(2,1)} %get-tuple-element.94), channel_id=1, source_target_pairs={{0,8},{8,0},{16,24},{24,16},{1,9},{9,1},{17,25},{25,17},{2,10},{10... | collective-permute-start | bytes 7520264 | tf_op jit(solution)/shard_map/ppermute | solution.py:832
  899.9 47.4 %collective-permute-start.30 = (bf16[4,136,1536]{2,1,0:T(8,128)(2,1)}, bf16[4,136,1536]{2,1,0:T(8,128)(2,1)}, u32[]{:S(2)}, u32[]{:S(2)}) collective-permute-start(bf16[4,136,1536]{2,1,0:T(8,128)(2,1)} %get-tuple-element.92), channel_id=1, source_target_pairs={{0,8},{8,0},{16,24},{24,16},{1,9},{9,1},{17,25},{25,17},{2,10},{10... | collective-permute-start | bytes 5013512 | tf_op jit(solution)/shard_map/ppermute | solution.py:832
  945.0 29.6 %collective-permute-start.39 = (bf16[136,2720]{1,0:T(8,128)(2,1)S(1)}, bf16[136,2720]{1,0:T(8,128)(2,1)}, u32[]{:S(2)}, u32[]{:S(2)}) collective-permute-start(bf16[136,2720]{1,0:T(8,128)(2,1)S(1)} %fusion.22.refs_6_), channel_id=1, source_target_pairs={{0,16},{8,24},{16,0},{24,8},{1,17},{9,25},{17,1},{25,9},{2,18},{10... | collective-permute-start | bytes 2219528 | tf_op jit(solution)/shard_map/ppermute | solution.py:832
  956.0 49.8 %collective-permute-start.32 = (bf16[4,136,1792]{2,1,0:T(8,128)(2,1)}, bf16[4,136,1792]{2,1,0:T(8,128)(2,1)}, u32[]{:S(2)}, u32[]{:S(2)}) collective-permute-start(bf16[4,136,1792]{2,1,0:T(8,128)(2,1)} %broadcast_select_fusion.6), channel_id=1, source_target_pairs={{0,16},{8,24},{16,0},{24,8},{1,17},{9,25},{17,1},{25,9},{2,18},{10... | collective-permute-start | bytes 5849096 | tf_op jit(solution)/shard_map/ppermute | solution.py:832
  963.9 94.9 %collective-permute-start.23 = (bf16[1024,1088]{0,1:T(8,128)(2,1)}, bf16[1024,1088]{0,1:T(8,128)(2,1)}, u32[]{:S(2)}, u32[]{:S(2)}) collective-permute-start(bf16[1024,1088]{0,1:T(8,128)(2,1)} %copy.115), channel_id=1, source_target_pairs={{0,1},{1,0},{2,3},{3,2},{4,5},{5,4},{6,7},{7,6},{8,9},{9,8},{10,11... | collective-permute-start | bytes 6684680 | tf_op jit(solution)/shard_map/ppermute | solution.py:832
  976.0 34.4 %collective-permute-start.40 = (bf16[136,2720]{1,0:T(8,128)(2,1)S(1)}, bf16[136,2720]{1,0:T(8,128)(2,1)S(1)}, u32[]{:S(2)}, u32[]{:S(2)}) collective-permute-start(bf16[136,2720]{1,0:T(8,128)(2,1)S(1)} %add_convert_fusion.12), channel_id=1, source_target_pairs={{0,8},{8,0},{16,24},{24,16},{1,9},{9,1},{17,25},{25,17},{2,10},{10... | collective-permute-start | bytes 2219528 | tf_op jit(solution)/shard_map/ppermute | solution.py:832
  (129 other events, 1748.1 us)
Sparse Core Ops, SparseCore 0:
  11.5 74.2 all-gather.6
  88.8 104.2 all-gather.8
  196.0 96.5 all-gather.10

commit v5 on v4

--- a/solution.py
+++ b/solution.py
@@ -614,75 +614,42 @@
     )(*operands)
 
 
-def projection_tiles(widths):
-    first, second = (pl.cdiv(w, TILE) for w in widths)
-    return first, second, [
-        lambda t, *_: jnp.minimum(t, first - 1),
-        lambda t, *_: jnp.maximum(t - first, 0),
-    ]
-
-
-def tile_of(ref, place, width):
-    value = ref[...]
-    if width % TILE == 0:
-        return value
-    lane = lax.broadcasted_iota(jnp.int32, (1, TILE), 1)
-    return jnp.where(lane < width - place * TILE, value, jnp.zeros((), value.dtype))
-
-
-def tokens_back_kernel(*refs, widths):
-    grads, weights = (refs[0:3], refs[3:6]), (refs[6:9], refs[9:12])
-    out, acc = refs[-2:]
-    step = pl.program_id(0)
-    first, second, _ = projection_tiles(widths)
-
-    @pl.when(step == 0)
+def tokens_back_kernel(*refs):
+    grads, weights, norm = refs[0:6], refs[6:12], refs[12]
+    out, lines = refs[-2:]
+    total = sum(nt(grad[...], weight[...]) for grad, weight in zip(grads, weights))
+    out[...] = total.astype(out.dtype)
+
+    @pl.when(pl.program_id(0) == 0)
     def _():
-        acc[...] = jnp.zeros_like(acc)
-
-    for group in range(2):
-
-        @pl.when(step < first if group == 0 else step >= first)
-        def _():
-            place = step if group == 0 else step - first
-            weight = jnp.concatenate([tile_of(w, place, widths[group]) for w in weights[group]], axis=1)
-            lane = lax.broadcasted_iota(jnp.int32, (1, TILE), 1)
-            for here in row_chunks(acc.shape[0]):
-                parts = []
-                for ref in grads[group]:
-                    part = ref[here, :]
-                    if widths[group] % TILE:
-                        part = jnp.where(lane < widths[group] - place * TILE, part, jnp.zeros((), part.dtype))
-                    parts.append(part)
-                acc[here, :] += nt(jnp.concatenate(parts, axis=1), weight)
-
-    @pl.when(step == pl.num_programs(0) - 1)
-    def _():
-        out[...] = acc[...].astype(out.dtype)
-
-
-def tokens_back(grads, weights, after=()):
-    total = grads[0][0].shape[0]
-    width = weights[0][0].shape[0]
-    widths = [group[0].shape[1] for group in grads]
-    first, second, places = projection_tiles(widths)
-
-    def tiles(rows):
-        return [pl.BlockSpec((rows, TILE), lambda t, at=at: (0, at(t))) for at in places for _ in range(3)]
-
+        lines[...] = jnp.zeros_like(lines)
+
+    lines[0:1, :] += jnp.sum(total * norm[...].astype(jnp.float32), axis=0, keepdims=True)
+    lines[1:2, :] += jnp.sum(total, axis=0, keepdims=True)
+
+
+def tokens_back(grads, weights, norm, size, after=()):
+    total, width = norm.shape
+    flat_grads, flat_weights = [g for group in grads for g in group], [w for group in weights for w in group]
+    tall = pl.BlockSpec((size, width), lambda t: (t, 0))
     return pl.pallas_call(
-        functools.partial(tokens_back_kernel, widths=widths),
-        grid=(first + second,),
-        in_specs=tiles(total) + tiles(width) + [pl.BlockSpec(memory_space=pl.ANY)] * len(after),
-        out_specs=steady((total, width)),
-        out_shape=jax.ShapeDtypeStruct((total, width), jnp.bfloat16),
-        scratch_shapes=[pltpu.VMEM((total, width), jnp.float32)],
+        tokens_back_kernel,
+        grid=(total // size,),
+        in_specs=[pl.BlockSpec((size, g.shape[1]), lambda t: (t, 0)) for g in flat_grads]
+        + [fixed(w.shape) for w in flat_weights]
+        + [tall]
+        + [pl.BlockSpec(memory_space=pl.ANY)] * len(after),
+        out_specs=[tall, steady((8, width))],
+        out_shape=[
+            jax.ShapeDtypeStruct((total, width), jnp.bfloat16),
+            jax.ShapeDtypeStruct((8, width), jnp.float32),
+        ],
         compiler_params=pltpu.CompilerParams(
-            dimension_semantics=("arbitrary",), vmem_limit_bytes=52 * 2**20
+            dimension_semantics=("arbitrary",), vmem_limit_bytes=40 * 2**20
         ),
         cost_estimate=busy(20),
         name="tokens_back",
-    )(*grads[0], *grads[1], *weights[0], *weights[1], *after)
+    )(*flat_grads, *flat_weights, norm, *after)
 
 
 def weights_back_kernel(half, turned, *refs, tiles):
@@ -928,7 +895,6 @@
     shared = columns // 2 // 512 * 512
     _, quarters = gather_quarters(jnp.concatenate([up_part[:, :shared], down_part[:, :shared]], axis=1))
     first_half = half_index() == 0
-    first_side = lax.axis_index("gy") == 0
     mine = gate(jnp.where(first_half, up_part[:, shared:], down_part[:, shared:]), after)
     rows, size = mine.shape
     count = lax.axis_size("gx")
@@ -937,8 +903,12 @@
     for step in range(count):
         got = mine if step == 0 else ahead(mine, "gx", step)
         blocks = lax.dynamic_update_index_in_dim(blocks, got, (here - step) % count, 0)
-    own = blocks.reshape(count * rows, size)
-    theirs = swap(own, "gy", 1)
+    return quarters, blocks.reshape(count * rows, size)
+
+
+def finish_feed_forward(quarters, own, theirs):
+    first_half = half_index() == 0
+    first_side = lax.axis_index("gy") == 0
     sides = (jnp.where(first_side, own, theirs), jnp.where(first_side, theirs, own))
     others = [swap(side, "dp", 1) for side in sides]
     ups = [jnp.where(first_half, a, b) for a, b in zip(sides, others)]
@@ -948,7 +918,7 @@
         wholes.append(
             jnp.concatenate([p for side in range(2) for p in quarters[side][pieces] + [rest[side]]], axis=1)
         )
-    return wholes, own
+    return wholes
 
 
 def core_step(keep, give):
@@ -964,14 +934,19 @@
     return (a.astype(jnp.float32) + b.astype(jnp.float32)).astype(jnp.bfloat16)
 
 
-def chips_step(sides):
+def chips_parts(sides):
     columns = sides[0].shape[-1]
     size = pl.cdiv(columns // 128, 2) * 128
     own_first = lax.axis_index("dp") // 2 == 0
     first, second = (
         jnp.concatenate([side[..., at : at + size] for side in sides], axis=-1) for at in (0, columns - size)
     )
-    return add(jnp.where(own_first, first, second), swap(jnp.where(own_first, second, first), "dp", 2))
+    return jnp.where(own_first, first, second), jnp.where(own_first, second, first)
+
+
+def chips_step(parts, end=()):
+    keep, give = parts
+    return add(keep, gate(swap(give, "dp", 2), end))
 
 
 def two(value):
@@ -987,7 +962,8 @@
     return jnp.concatenate([first, second[..., 2 * size - columns :]], axis=-1)
 
 
-def blocks_step(value):
+def blocks_step(value, begin=()):
+    value = gate(value, begin)
     count = lax.axis_size("gx")
     here = lax.axis_index("gx")
     total = lax.dynamic_index_in_dim(value, here, 0, False).astype(jnp.float32)
@@ -1010,10 +986,10 @@
     return pair_rows(value, swap(value, "dp", 1)).reshape(-1, columns).astype(jnp.float32)
 
 
-def side_exchange(first, second):
+def side_exchange(first, second, begin=()):
     first_side = lax.axis_index("gy") == 0
     keep = jnp.where(first_side, first, second)
-    return add(keep, swap(jnp.where(first_side, second, first), "gy", 1))
+    return add(keep, swap(gate(jnp.where(first_side, second, first), begin), "gy", 1))
 
 
 def projection_sides(first, rest):
@@ -1118,10 +1094,10 @@
     def given_rows(own):
         return lax.dynamic_slice_in_dim(own, block - kept_at, block, 0)
 
-    def back_home(done):
+    def back_home(done, end=()):
         if not halved:
             return done
-        kept, home = done[:block], swap(done[block:], "gy", 1)
+        kept, home = done[:block], gate(swap(done[block:], "gy", 1), end)
         return jnp.concatenate([jnp.where(is_long, kept, home), jnp.where(is_long, home, kept)], axis=0)
 
     own_prompt = prompt.reshape(shard, width)
@@ -1131,15 +1107,13 @@
     whole_prompt = all_tokens(own_prompt)
     if halved:
         weights, out_full, raw = gather_projections(qkv_weight, out_weight, width)
-        (up_full, down_full), fetched = gather_feed_forward(up_weight, down_weight.T, (raw,))
-        fetched = (fetched,)
+        quarters, fetched = gather_feed_forward(up_weight, down_weight.T, (raw,))
         other_cot = swap(gate(given_rows(own_cot), (raw,)), "gy", 1)
         cotangent = jnp.concatenate([kept_rows(own_cot), other_cot, branch_cot], axis=0)
     else:
         qkv = gather_plain(qkv_weight)
         weights = [[qkv[:, c.start + s : c.stop + s] for s in (0, width, 2 * width)] for c in spans]
         out_full, up_full, down_full = (gather_plain(w) for w in (out_weight, up_weight, down_weight.T))
-        fetched = ()
         cotangent = jnp.concatenate([own_cot, branch_cot], axis=0)
 
     all_rows = jnp.concatenate([whole_prompt, branch], axis=0)
@@ -1154,9 +1128,12 @@
                 (dot(act_all, w_value) + value_bias[cols]).astype(jnp.bfloat16),
             )
         )
-        got, stat = attention_forward(
-            places, *projected[-1], block, length, fetched if number == 1 else ()
-        )
+        got, stat = attention_forward(places, *projected[-1], block, length)
+        if halved and number == 0:
+            fetched = gate(fetched, (got, cotangent))
+            theirs = swap(fetched, "gy", 1)
+        if halved and number == 1:
+            up_full, down_full = finish_feed_forward(quarters, fetched, gate(theirs, (got,)))
         mixed.append(got)
         stats.append(stat)
 
@@ -1166,18 +1143,17 @@
     hidden, slope, result, act_turned, norm_two, pace_two = mlp_forward(
         mixed, tokens, out_full, out_bias, mlp_gain, mlp_shift, up_full, up_bias, down_full, down_bias
     )
-    prompt_out = back_home(result[:shard]).reshape(groups, shard, width)
-    continuation_out = result[shard:].reshape(1, length, width)
-
     count = lax.axis_size("gx")
     half = jnp.reshape(half_index() if halved else 0, (1,)).astype(jnp.int32)
     tiles = up_full.shape[1] // TILE
     part = tiles // 2
+    prompt_out = back_home(result[:shard]).reshape(groups, shard, width)
+    continuation_out = result[shard:].reshape(1, length, width)
     down_keep, down_give = down_back(half, count, cotangent.T, hidden)
     after = ()
     if halved:
         down_flow = core_step(down_keep, down_give)
-        after = (down_flow,)
+        after = (down_flow, prompt_out)
     so_far, up_keep, up_give, up_bias_grad = up_back(
         half, count, (0, part), act_turned, cotangent, slope, up_full, down_full
     )
@@ -1197,9 +1173,14 @@
     mlp_gain_grad, mlp_shift_grad, out_bias_grad, down_bias_grad = (lines[n] for n in range(4))
     if halved:
         side = up_weight.shape[1]
-        down_flow = chips_step((down_flow[..., :side], down_flow[..., side:]))
-        up_flow = jnp.concatenate([core_step(up_keep, up_give), core_step(keep_rest, give_rest)], axis=-1)
-        out_flow = core_step(out_keep, out_give)
+        up_flow = core_step(up_keep, gate(up_give, (down_flow,)))
+        keep, give = chips_parts((down_flow[..., :side], down_flow[..., side:]))
+        down_flow = chips_step((keep, gate(give, (so_far,))))
+        ready = (down_flow, up_flow)
+        rest_flow, out_flow = core_step(keep_rest, gate(give_rest, ready)), core_step(out_keep, gate(out_give, ready))
+        ready = (rest_flow, out_flow)
+        up_flow = jnp.concatenate([up_flow, rest_flow], axis=-1)
+        down_flow = gate(down_flow, ready)
         after = (down_flow, up_flow, out_flow)
     d_parts = [None, None]
     for number in (1, 0):
@@ -1212,13 +1193,29 @@
                 jnp.concatenate([up_flow[..., side:], out_flow[..., width // 2 :]], axis=-1),
             )
             down_flow = blocks_step(down_flow)
-            after = (up_flow, down_flow)
+            d_home = gate(d_resid.astype(jnp.bfloat16), (d_parts[1][0],))
+            after = (up_flow, down_flow, d_home)
         if halved and number == 0:
-            up_flow, down_flow = blocks_step(up_flow), side_exchange(*two(down_flow))
-            after = (up_flow, down_flow)
+            up_flow = blocks_step(up_flow)
+            home = back_home(d_home[:shard], (d_parts[0][0],)).astype(jnp.float32)
+            after = (up_flow,)
     keep_a, give_a, bias_a, keep_b, give_b, bias_b = weights_back(half, count, act_all.T, d_parts, after)
-    d_act_all = tokens_back(d_parts, weights, (keep_a,))
+    if halved:
+        sides = projection_sides(core_step(keep_a, give_a), core_step(keep_b, give_b))
+        parts = chips_parts(sides)
+        after = parts
+    else:
+        after = (keep_a,)
+    d_act_all, act_lines = tokens_back(d_parts, weights, norm_all.astype(jnp.bfloat16), length, after)
+    attn_gain_grad, attn_shift_grad = act_lines[0], act_lines[1]
     others = others_tokens(d_act_all[:prompt_len])
+    if halved:
+        qkv_flow = chips_step(parts, (d_act_all,))
+        down_flow = side_exchange(*two(down_flow), (qkv_flow,))
+        qkv_flow = blocks_step(qkv_flow)
+        others = gate(others, (qkv_flow,))
+        summed = qkv_flow
+        up_flow = gate(up_flow, (summed,))
     size = bias_b.shape[1] // 3
     query_bias_grad, value_bias_grad = (
         jnp.concatenate(
@@ -1227,8 +1224,7 @@
         for n in (0, 2)
     )
     if halved:
-        sides = projection_sides(core_step(keep_a, give_a), core_step(keep_b, give_b))
-        qkv_flow = blocks_step(side_exchange(*two(chips_step(sides))))
+        qkv_flow = side_exchange(*two(qkv_flow))
         qkv_total = join_projections(join_step(overlap_join(qkv_flow, sides[0].shape[-1])), width)
         up_total = join_step(copies_step(up_flow))
         up_total, out_total = up_total[:, :side], up_total[:, side:]
@@ -1255,12 +1251,8 @@
                 qkv_grad,
             )
         )
-    d_act_exact = d_act_all.astype(jnp.float32)
-    attn_gain_grad = jnp.sum(d_act_exact * norm_all, axis=0)
-    attn_shift_grad = jnp.sum(d_act_exact, axis=0)
     prompt_resid = d_resid[:shard]
     if halved:
-        home = back_home(prompt_resid.astype(jnp.bfloat16)).astype(jnp.float32)
         kept = jnp.where(is_long, prompt_resid[:block], home[:block]), jnp.where(
             is_long, home[block:], prompt_resid[:block]
         )
@@ -1284,7 +1276,8 @@
         up_bias_grad.reshape(-1),
         down_bias_grad,
     )
-    joined = total_over(jnp.concatenate(vectors), ("dp", "gy", "gx"))
+    joined = gate(jnp.concatenate(vectors), (summed,) if halved else ())
+    joined = total_over(joined, ("dp", "gy", "gx"))
     totals = []
     at = 0
     for vector in vectors:

time: 1110 us -> 965 us (0.87)
  waiting for transfers between devices: 292 us -> 140 us
  local copies, waits for them, and re-layouts: 129 us -> 148 us
    ppermute x12, waiting for transfers between devices: 105 us -> 0.03 us  [ahead(): lax.ppermute(value, axis, [(i, (i + step) % count) for i in range(count)])]
    ppermute x31, waiting for transfers between devices: 187 us -> 112 us  [swap(): return lax.ppermute(value, axis, [(i, i ^ bit) for i in range(count)])]
    all_gather x3, waiting for transfers between devices: 0.01 us -> 28.1 us  [gather_quarters(): raw = lax.all_gather(mine, ('dp', 'gx', 'gy'))]
    ppermute x12, starting transfers between devices: 54 us -> 28.2 us  [ahead(): lax.ppermute(value, axis, [(i, (i + step) % count) for i in range(count)])]
    ppermute x31, starting transfers between devices: 22.6 us -> 40.9 us  [swap(): return lax.ppermute(value, axis, [(i, i ^ bit) for i in range(count)])]
    unnamed x230 -> x236, local copies, waits for them, and re-layouts: 40.3 us -> 45.7 us
  transfers between devices with their start and end apart: 46 -> 46, of which waited for: 20 -> 12; matrix products, arithmetic and copies ran while one was open for 21% -> 25% of each run, Pallas kernels for 23% -> 31%
where the time goes in v5:
time: 965 us; the launch traced here: 954 us
  Pallas kernels  412 us (43%)
  local copies, waits for them, and re-layouts  148 us (15%)
  waiting for transfers between devices  140 us (15%)
  other arithmetic  135 us (14%)
  starting transfers between devices  69.2 us (7%)
  matrix products  31 us (3%)
  between operations  17.9 us (2%)
    ppermute x31, waiting for transfers between devices, swap(): return lax.ppermute(value, axis, [(i, i ^ bit) for i in range(count)])  112 us
    pallas_call x2, Pallas kernels, attention_backward(): pl.pallas_call(functools.partial(backward_kernel, block=block, branch=bra...  104 us
    pallas_call x2, Pallas kernels, up_back(): pl.pallas_call(up_back_first_kernel if final is None else up_back_last_ke...  81.6 us
    pallas_call x2, Pallas kernels, attention_forward(): pl.pallas_call(functools.partial(forward_kernel, block=block, branch=bran...  74.3 us
    pallas_call x1, Pallas kernels, mlp_forward(): pl.pallas_call(mlp_forward_kernel, grid=(inner // TILE,), in_specs=[fixed...  64.8 us
    unnamed x236, local copies, waits for them, and re-layouts  45.7 us
    ppermute x31, starting transfers between devices, swap(): return lax.ppermute(value, axis, [(i, i ^ bit) for i in range(count)])  40.9 us
    pallas_call x1, Pallas kernels, weights_back(): pl.pallas_call(functools.partial(weights_back_kernel, tiles=tiles), grid_...  31.1 us
  transfers between devices with their start and end apart: 46, of which 12 were waited for; matrix products, arithmetic and copies ran while one was open for 25% of the time, Pallas kernels for 31%

profile of v5, /device:TPU:0, one launch (start us, length us, event | category | flops | bytes accessed | tf_op | source)
XLA Modules:
  0.0 953.6 jit_solution(4864065684383232047)
XLA Ops:
  26.5 49.2 %collective-permute-done = s32[1]{0:T(128)} collective-permute-done((s32[1]{0:T(128)}, s32[1]{0:T(128)}, u32[]{:S(2)}, u32[]{:S(2)}) %collective-permute-start) | collective-permute-done | bytes 36 | tf_op jit(solution)/shard_map/ppermute | solution.py:799
  92.6 5.4 fusion.6
  101.1 7.3 fusion.2
  108.4 8.2 pad_maximum_fusion.3
  131.5 6.2 fusion.10.v
  144.7 33.1 %attention_forward.2 = (bf16[1280,512]{1,0:T(8,128)(2,1)S(1)}, f32[4,8,1280]{2,1,0:T(8,128)S(1)}) custom-call(s32[3]{0:T(128)S(1)} %pad_add_fusion.pos, bf16[2304,512]{1,0:T(8,128)(2,1)S(1)} %fusion.9.q, bf16[2304,512]{1,0:T(8,128)(2,1)S(1)} %convolution_convert_fusion.1.k, bf16[2304,512]{1,0:T(8,128)(2,1)S(1)} %fusion.10.v), custom_call_target="tpu_custom_call" | custom-call | flops 28000000000 | bytes 28000000 | tf_op jit(solution)/shard_map/attention_forward/pallas_call | solution.py:169
  186.1 5.0 fusion.38
  195.2 5.0 fusion.40
  203.4 8.2 convolution_convert_fusion.k
  211.7 4.9 add_convert_fusion.2.v
  216.6 4.9 add_convert_fusion.3.q
  221.5 41.2 %attention_forward.3 = (bf16[1280,576]{1,0:T(8,128)(2,1)S(1)}, f32[5,8,1280]{2,1,0:T(8,128)S(1)}) custom-call(s32[3]{0:T(128)S(1)} %pad_add_fusion.pos, bf16[2304,576]{1,0:T(8,128)(2,1)S(1)} %add_convert_fusion.3.q, bf16[2304,576]{1,0:T(8,128)(2,1)S(1)} %convolution_convert_fusion.k, bf16[2304,576]{1,0:T(8,128)(2,1)S(1)} %add_convert_fusion.2.v), custom_call_target="tpu_custom_call" | custom-call | flops 35000000512 | bytes 35000000 | tf_op jit(solution)/shard_map/attention_forward/pallas_call | solution.py:169
  263.9 5.3 broadcast_select_fusion.2
  272.6 28.1 %all-gather.11.cloned.1.call-done = bf16[8704,512]{1,0:T(8,128)(2,1)} async-done(((bf16[272,512]{1,0:T(8,128)(2,1)}), bf16[8704,512]{1,0:T(8,128)(2,1)}) %all-gather.11.cloned.1.call-update) | async-done | bytes 8912912 | tf_op jit(solution)/shard_map/all_gather | solution.py:843
  313.0 5.2 select_dynamic-update-slice_fusion
  321.8 64.8 %mlp_forward.1 = (bf16[1280,4352]{1,0:T(8,128)(2,1)}, bf16[1280,4352]{1,0:T(8,128)(2,1)}, bf16[1280,1088]{1,0:T(8,128)(2,1)}, bf16[1088,1280]{1,0:T(8,128)(2,1)}...) custom-call(bf16[1280,512]{1,0:T(8,128)(2,1)S(1)} %copy-done.22, bf16[1280,576]{1,0:T(8,128)(2,1)} %copy-done.13, ...), custom_call_target="tpu_custom_call" | custom-call | flops 49999998976 | bytes 50000000 | tf_op jit(solution)/shard_map/mlp_forward/pallas_call | solution.py:409
  386.5 20.0 %down_back.1 = (bf16[4,136,4352]{2,1,0:T(8,128)(2,1)S(1)}, bf16[4,136,4352]{2,1,0:T(8,128)(2,1)}) custom-call(s32[1]{0:T(128)} %bitcast.46.half, bf16[1088,1280]{1,0:T(8,128)(2,1)S(1)} %copy.127.cot_turned, bf16[1280,4352]{1,0:T(8,128)(2,1)} %get-tuple-element.66.hidden), custom_call_target="tpu_custom_call" | custom-call | flops 15000000512 | bytes 15000000 | tf_op jit(solution)/shard_map/down_back/pallas_call | solution.py:470
  412.4 29.8 %up_back_first.1 = (f32[1280,1088]{1,0:T(8,128)}, bf16[4,136,2048]{2,1,0:T(8,128)(2,1)}, bf16[4,136,2048]{2,1,0:T(8,128)(2,1)}, f32[1,2048]{1,0:T(1,128)}) custom-call(s32[1]{0:T(128)} %bitcast.46.half, bf16[1088,1280]{1,0:T(8,128)(2,1)} %get-tuple-element.61.act_turned, bf16[1280,1088]{1,0:T(8,128)(2,1)} %get-tuple-element.193.refs_2_.cot, ...), custom_call_target="tpu_custom_call" | custom-call | flops 30000001024 | bytes 30000000 | tf_op jit(solution)/shard_map/up_back_first/pallas_call | solution.py:599
  458.1 51.8 %up_back_last.1 = (f32[1280,1088]{1,0:T(8,128)}, bf16[1280,512]{1,0:T(8,128)(2,1)}, bf16[1280,576]{1,0:T(8,128)(2,1)}, bf16[4,136,2304]{2,1,0:T(8,128)(2,1)}, bf...) custom-call(s32[1]{0:T(128)} %bitcast.46.half, ...), custom_call_target="tpu_custom_call" | custom-call | flops 49999998976 | bytes 50000000 | tf_op jit(solution)/shard_map/up_back_last/pallas_call | solution.py:599
  510.0 4.8 add_convert_fusion.7.refs_2_
  517.5 8.4 copy.128.turned
  536.4 4.6 convert_element_type.249.refs_0_
  568.8 57.6 %attention_backward.2 = (bf16[2304,576]{1,0:T(8,128)(2,1)S(1)}, bf16[2304,576]{1,0:T(8,128)(2,1)S(1)}, bf16[2304,576]{1,0:T(8,128)(2,1)}) custom-call(s32[3]{0:T(128)S(1)} %pad_add_fusion.pos, bf16[2304,576]{1,0:T(8,128)(2,1)} %copy-done.36, bf16[2304,576]{1,0:T(8,128)(2,1)} %copy-done.34, bf16[2304,576]{1,0:T(8,128)(2,1)} %copy-done.35, ...), custom_call_target="tpu_custom_call" | custom-call | flops 49999998976 | bytes 50000000 | tf_op jit(solution)/shard_map/attention_backward/pallas_call | solution.py:305
  634.5 4.7 collective-permute-start.29
  641.7 21.6 %collective-permute-done.29 = bf16[512,1088]{0,1:T(8,128)(2,1)} collective-permute-done((bf16[512,1088]{0,1:T(8,128)(2,1)}, bf16[512,1088]{0,1:T(8,128)(2,1)}, u32[]{:S(2)}, u32[]{:S(2)}) %collective-permute-start.29) | collective-permute-done | bytes 1114144 | tf_op jit(solution)/shard_map/ppermute | solution.py:799
  674.5 46.6 %attention_backward.3 = (bf16[2304,512]{1,0:T(8,128)(2,1)S(1)}, bf16[2304,512]{1,0:T(8,128)(2,1)S(1)}, bf16[2304,512]{1,0:T(8,128)(2,1)S(1)}) custom-call(s32[3]{0:T(128)S(1)} %copy-done.29, bf16[2304,512]{1,0:T(8,128)(2,1)S(1)} %copy-done.33, bf16[2304,512]{1,0:T(8,128)(2,1)} %copy-done.30, bf16[2304,512]{1,0:T(8,128)(2,1)} %copy-done.31, ...), custom_call_target="tpu_custom_call" | custom-call | flops 40000000000 | bytes 40000000 | tf_op jit(solution)/shard_map/attention_backward/pallas_call | solution.py:305
  729.4 31.1 %weights_back.1 = (bf16[4,136,1536]{2,1,0:T(8,128)(2,1)}, bf16[4,136,1536]{2,1,0:T(8,128)(2,1)}, f32[1,1536]{1,0:T(1,128)S(1)}, bf16[4,136,2304]{2,1,0:T(8,128)(...) custom-call(s32[1]{0:T(128)} %bitcast.46.half, bf16[1088,2304]{1,0:T(8,128)(2,1)} %copy.128.turned, ...), custom_call_target="tpu_custom_call" | custom-call | flops 24999999488 | bytes 25000000 | tf_op jit(solution)/shard_map/weights_back/pallas_call | solution.py:695
  777.5 29.6 %tokens_back.1 = (bf16[2304,1088]{1,0:T(8,128)(2,1)}, f32[8,1088]{1,0:T(8,128)S(1)}) custom-call(bf16[2304,512]{1,0:T(8,128)(2,1)S(1)} %copy-done.12, bf16[2304,512]{1,0:T(8,128)(2,1)} %copy-done.38, bf16[2304,512]{1,0:T(8,128)(2,1)} %copy-done.39, bf16[2304,576]{1,0:T(8,128)(2,1)} %copy-done.9, bf16[2304,576]{1,0:T(8,128)(2,1)} %copy-done.37, ...), custom_call_target="tpu_custom_call" | custom-call | flops 20000000000 | bytes 20000000 | tf_op jit(solution)/shard_map/tokens_back/pallas_call | solution.py:635
  829.6 10.1 %collective-permute-start.26 = (bf16[136,1792]{1,0:T(8,128)(2,1)}, bf16[136,1792]{1,0:T(8,128)(2,1)}, u32[]{:S(2)}, u32[]{:S(2)}) collective-permute-start(bf16[136,1792]{1,0:T(8,128)(2,1)} %get-tuple-element.208), channel_id=1, source_target_pairs={{0,2},{2,4},{4,6},{6,0},{1,3},{3,5},{5,7},{7,1},{8,10},{10,12},{12... | collective-permute-start | bytes 1462280 | tf_op jit(solution)/shard_map/ppermute | solution.py:804
  842.1 26.3 %collective-permute-done.24 = bf16[1024,1088]{0,1:T(8,128)(2,1)} collective-permute-done((bf16[1024,1088]{0,1:T(8,128)(2,1)}, bf16[1024,1088]{0,1:T(8,128)(2,1)}, u32[]{:S(2)}, u32[]{:S(2)}) %collective-permute-start.24) | collective-permute-done | bytes 2228256 | tf_op jit(solution)/shard_map/ppermute | solution.py:799
  891.7 6.8 rows_back.1
  906.5 10.3 %collective-permute-start.33 = (f32[13056]{0:T(1024)S(1)}, f32[13056]{0:T(1024)S(1)}, u32[]{:S(2)}, u32[]{:S(2)}) collective-permute-start(f32[13056]{0:T(1024)S(1)} %add.319), channel_id=1, source_target_pairs={{0,2},{2,0},{4,6},{6,4},{1,3},{3,1},{5,7},{7,5},{8,10},{10,8},{12,... | collective-permute-start | bytes 156680 | tf_op jit(solution)/shard_map/ppermute | solution.py:799
  (490 shorter events, 289.7 us)
Async XLA Ops:
  7.2 109.5 %all-gather.7.cloned.1.call-start = ((), (), s32[]{:S(2)}) async-start(), calls=%async_computation | async-start | bytes 4595712 | tf_op jit(solution)/shard_map/all_gather | solution.py:843
  9.5 185.7 %all-gather.9.cloned.1.call-start = ((), (), s32[]{:S(2)}) async-start(), calls=%async_computation.1 | async-start | bytes 6893568 | tf_op jit(solution)/shard_map/all_gather | solution.py:843
  11.7 289.0 %all-gather.11.cloned.1.call-start = ((), (), s32[]{:S(2)}) async-start(), calls=%async_computation.2 | async-start | bytes 9191424 | tf_op jit(solution)/shard_map/all_gather | solution.py:843
  11.7 73.2 %collective-permute-start.1 = (bf16[1024,1088]{0,1:T(8,128)(2,1)}, bf16[1024,1088]{0,1:T(8,128)(2,1)}, u32[]{:S(2)}, u32[]{:S(2)}) collective-permute-start(bf16[1024,1088]{0,1:T(8,128)(2,1)} %bitcast.5), channel_id=1, source_target_pairs={{0,1},{1,0},{2,3},{3,2},{4,5},{5,4},{6,7},{7,6},{8,9},{9,8},{10,11... | collective-permute-start | bytes 6684680 | tf_op jit(solution)/shard_map/ppermute | solution.py:799
  14.7 60.9 %collective-permute-start = (s32[1]{0:T(128)}, s32[1]{0:T(128)}, u32[]{:S(2)}, u32[]{:S(2)}) collective-permute-start(s32[1]{0:T(128)} %param.20), channel_id=1, source_target_pairs={{0,1},{1,0},{2,3},{3,2},{4,5},{5,4},{6,7},{7,6},{8,9},{9,8},{10,11... | collective-permute-start | bytes 20 | tf_op jit(solution)/shard_map/ppermute | solution.py:799
  116.7 62.8 %collective-permute-start.2 = (bf16[272,1152]{1,0:T(8,128)(2,1)}, bf16[272,1152]{1,0:T(8,128)(2,1)}, u32[]{:S(2)}, u32[]{:S(2)}) collective-permute-start(bf16[272,1152]{1,0:T(8,128)(2,1)} %gate.16), channel_id=1, source_target_pairs={{0,2},{2,4},{4,6},{6,0},{1,3},{3,5},{5,7},{7,1},{8,10},{10,12},{12... | collective-permute-start | bytes 1880072 | tf_op jit(solution)/shard_map/ppermute | solution.py:804
  118.3 62.3 %collective-permute-start.3 = (bf16[272,1152]{1,0:T(8,128)(2,1)}, bf16[272,1152]{1,0:T(8,128)(2,1)}, u32[]{:S(2)}, u32[]{:S(2)}) collective-permute-start(bf16[272,1152]{1,0:T(8,128)(2,1)} %gate.16), channel_id=1, source_target_pairs={{0,4},{2,6},{4,0},{6,2},{1,5},{3,7},{5,1},{7,3},{8,12},{10,14},{12... | collective-permute-start | bytes 1880072 | tf_op jit(solution)/shard_map/ppermute | solution.py:804
  121.2 60.6 %collective-permute-start.4 = (bf16[272,1152]{1,0:T(8,128)(2,1)}, bf16[272,1152]{1,0:T(8,128)(2,1)}, u32[]{:S(2)}, u32[]{:S(2)}) collective-permute-start(bf16[272,1152]{1,0:T(8,128)(2,1)} %gate.16), channel_id=1, source_target_pairs={{0,6},{2,0},{4,2},{6,4},{1,7},{3,1},{5,3},{7,5},{8,14},{10,8},{12,... | collective-permute-start | bytes 1880072 | tf_op jit(solution)/shard_map/ppermute | solution.py:804
  129.2 53.8 %collective-permute-start.5 = (bf16[512,1088]{0,1:T(8,128)(2,1)}, bf16[512,1088]{0,1:T(8,128)(2,1)}, u32[]{:S(2)}, u32[]{:S(2)}) collective-permute-start(bf16[512,1088]{0,1:T(8,128)(2,1)} %copy.115), channel_id=1, source_target_pairs={{0,1},{1,0},{2,3},{3,2},{4,5},{5,4},{6,7},{7,6},{8,9},{9,8},{10,11... | collective-permute-start | bytes 3342344 | tf_op jit(solution)/shard_map/ppermute | solution.py:799
  191.1 72.8 %collective-permute-start.6 = (bf16[1088,1152]{1,0:T(8,128)(2,1)}, bf16[1088,1152]{1,0:T(8,128)(2,1)}, u32[]{:S(2)}, u32[]{:S(2)}) collective-permute-start(bf16[1088,1152]{1,0:T(8,128)(2,1)} %gate.18), channel_id=1, source_target_pairs={{0,1},{1,0},{2,3},{3,2},{4,5},{5,4},{6,7},{7,6},{8,9},{9,8},{10,11... | collective-permute-start | bytes 7520264 | tf_op jit(solution)/shard_map/ppermute | solution.py:799
  269.2 36.0 %collective-permute-start.7 = (bf16[1088,1152]{1,0:T(8,128)(2,1)}, bf16[1088,1152]{1,0:T(8,128)(2,1)}, u32[]{:S(2)}, u32[]{:S(2)}) collective-permute-start(bf16[1088,1152]{1,0:T(8,128)(2,1)} %get-tuple-element.166), channel_id=1, source_target_pairs={{0,8},{8,0},{16,24},{24,16},{1,9},{9,1},{17,25},{25,17},{2,10},{10... | collective-permute-start | bytes 7520264 | tf_op jit(solution)/shard_map/ppermute | solution.py:799
  269.2 43.8 %collective-permute-start.8 = (bf16[1088,1152]{1,0:T(8,128)(2,1)}, bf16[1088,1152]{1,0:T(8,128)(2,1)}, u32[]{:S(2)}, u32[]{:S(2)}) collective-permute-start(bf16[1088,1152]{1,0:T(8,128)(2,1)} %get-tuple-element.165), channel_id=1, source_target_pairs={{0,8},{8,0},{16,24},{24,16},{1,9},{9,1},{17,25},{25,17},{2,10},{10... | collective-permute-start | bytes 7520264 | tf_op jit(solution)/shard_map/ppermute | solution.py:799
  408.8 38.4 %collective-permute-start.10 = (bf16[4,136,4352]{2,1,0:T(8,128)(2,1)}, bf16[4,136,4352]{2,1,0:T(8,128)(2,1)}, u32[]{:S(2)}, u32[]{:S(2)}) collective-permute-start(bf16[4,136,4352]{2,1,0:T(8,128)(2,1)} %get-tuple-element.68), channel_id=1, source_target_pairs={{0,8},{8,0},{16,24},{24,16},{1,9},{9,1},{17,25},{25,17},{2,10},{10... | collective-permute-start | bytes 14204936 | tf_op jit(solution)/shard_map/ppermute | solution.py:799
  411.0 31.2 %collective-permute-start.9 = (bf16[512,1088]{0,1:T(8,128)(2,1)S(1)}, bf16[512,1088]{0,1:T(8,128)(2,1)}, u32[]{:S(2)}, u32[]{:S(2)}) collective-permute-start(bf16[512,1088]{0,1:T(8,128)(2,1)S(1)} %copy.124), channel_id=1, source_target_pairs={{0,1},{1,0},{2,3},{3,2},{4,5},{5,4},{6,7},{7,6},{8,9},{9,8},{10,11... | collective-permute-start | bytes 3342344 | tf_op jit(solution)/shard_map/ppermute | solution.py:799
  453.6 56.4 %collective-permute-start.11 = (bf16[4,136,2048]{2,1,0:T(8,128)(2,1)}, bf16[4,136,2048]{2,1,0:T(8,128)(2,1)}, u32[]{:S(2)}, u32[]{:S(2)}) collective-permute-start(bf16[4,136,2048]{2,1,0:T(8,128)(2,1)} %gate.20), channel_id=1, source_target_pairs={{0,8},{8,0},{16,24},{24,16},{1,9},{9,1},{17,25},{25,17},{2,10},{10... | collective-permute-start | bytes 6684680 | tf_op jit(solution)/shard_map/ppermute | solution.py:799
  456.7 58.1 %collective-permute-start.12 = (bf16[4,136,2304]{2,1,0:T(8,128)(2,1)}, bf16[4,136,2304]{2,1,0:T(8,128)(2,1)S(1)}, u32[]{:S(2)}, u32[]{:S(2)}) collective-permute-start(bf16[4,136,2304]{2,1,0:T(8,128)(2,1)} %gate.21), channel_id=1, source_target_pairs={{0,16},{8,24},{16,0},{24,8},{1,17},{9,25},{17,1},{25,9},{2,18},{10... | collective-permute-start | bytes 7520264 | tf_op jit(solution)/shard_map/ppermute | solution.py:799
  516.8 31.3 %collective-permute-start.13 = (bf16[4,136,2304]{2,1,0:T(8,128)(2,1)}, bf16[4,136,2304]{2,1,0:T(8,128)(2,1)}, u32[]{:S(2)}, u32[]{:S(2)}) collective-permute-start(bf16[4,136,2304]{2,1,0:T(8,128)(2,1)} %gate.22), channel_id=1, source_target_pairs={{0,8},{8,0},{16,24},{24,16},{1,9},{9,1},{17,25},{25,17},{2,10},{10... | collective-permute-start | bytes 7520264 | tf_op jit(solution)/shard_map/ppermute | solution.py:799
  560.6 105.1 %collective-permute-start.15 = (bf16[4,136,2720]{2,1,0:T(8,128)(2,1)}, bf16[4,136,2720]{2,1,0:T(8,128)(2,1)}, u32[]{:S(2)}, u32[]{:S(2)}) collective-permute-start(bf16[4,136,2720]{2,1,0:T(8,128)(2,1)} %broadcast_select_fusion), channel_id=1, source_target_pairs={{0,1},{1,0},{2,3},{3,2},{4,5},{5,4},{6,7},{7,6},{8,9},{9,8},{10,11... | collective-permute-start | bytes 8878088 | tf_op jit(solution)/shard_map/ppermute | solution.py:799
  562.6 76.5 %collective-permute-start.16 = (bf16[136,2304]{1,0:T(8,128)(2,1)}, bf16[136,2304]{1,0:T(8,128)(2,1)}, u32[]{:S(2)}, u32[]{:S(2)}) collective-permute-start(bf16[136,2304]{1,0:T(8,128)(2,1)} %get-tuple-element.197), channel_id=1, source_target_pairs={{0,2},{2,4},{4,6},{6,0},{1,3},{3,5},{5,7},{7,1},{8,10},{10,12},{12... | collective-permute-start | bytes 1880072 | tf_op jit(solution)/shard_map/ppermute | solution.py:804
  565.9 73.3 %collective-permute-start.17 = (bf16[136,2304]{1,0:T(8,128)(2,1)}, bf16[136,2304]{1,0:T(8,128)(2,1)}, u32[]{:S(2)}, u32[]{:S(2)}) collective-permute-start(bf16[136,2304]{1,0:T(8,128)(2,1)} %get-tuple-element.199), channel_id=1, source_target_pairs={{0,4},{2,6},{4,0},{6,2},{1,5},{3,7},{5,1},{7,3},{8,12},{10,14},{12... | collective-permute-start | bytes 1880072 | tf_op jit(solution)/shard_map/ppermute | solution.py:804
  567.6 71.5 %collective-permute-start.18 = (bf16[136,2304]{1,0:T(8,128)(2,1)}, bf16[136,2304]{1,0:T(8,128)(2,1)}, u32[]{:S(2)}, u32[]{:S(2)}) collective-permute-start(bf16[136,2304]{1,0:T(8,128)(2,1)} %get-tuple-element.198), channel_id=1, source_target_pairs={{0,6},{2,0},{4,2},{6,4},{1,7},{3,1},{5,3},{7,5},{8,14},{10,8},{12,... | collective-permute-start | bytes 1880072 | tf_op jit(solution)/shard_map/ppermute | solution.py:804
  670.7 56.9 %collective-permute-start.19 = (bf16[136,2720]{1,0:T(8,128)(2,1)}, bf16[136,2720]{1,0:T(8,128)(2,1)S(1)}, u32[]{:S(2)}, u32[]{:S(2)}) collective-permute-start(bf16[136,2720]{1,0:T(8,128)(2,1)} %get-tuple-element.189), channel_id=1, source_target_pairs={{0,2},{2,4},{4,6},{6,0},{1,3},{3,5},{5,7},{7,1},{8,10},{10,12},{12... | collective-permute-start | bytes 2219528 | tf_op jit(solution)/shard_map/ppermute | solution.py:804
  671.5 56.1 %collective-permute-start.20 = (bf16[136,2720]{1,0:T(8,128)(2,1)}, bf16[136,2720]{1,0:T(8,128)(2,1)S(1)}, u32[]{:S(2)}, u32[]{:S(2)}) collective-permute-start(bf16[136,2720]{1,0:T(8,128)(2,1)} %get-tuple-element.191), channel_id=1, source_target_pairs={{0,4},{2,6},{4,0},{6,2},{1,5},{3,7},{5,1},{7,3},{8,12},{10,14},{12... | collective-permute-start | bytes 2219528 | tf_op jit(solution)/shard_map/ppermute | solution.py:804
  672.7 54.9 %collective-permute-start.21 = (bf16[136,2720]{1,0:T(8,128)(2,1)S(1)}, bf16[136,2720]{1,0:T(8,128)(2,1)}, u32[]{:S(2)}, u32[]{:S(2)}) collective-permute-start(bf16[136,2720]{1,0:T(8,128)(2,1)S(1)} %get-tuple-element.190), channel_id=1, source_target_pairs={{0,6},{2,0},{4,2},{6,4},{1,7},{3,1},{5,3},{7,5},{8,14},{10,8},{12,... | collective-permute-start | bytes 2219528 | tf_op jit(solution)/shard_map/ppermute | solution.py:804
  774.7 49.0 %collective-permute-start.25 = (bf16[4,136,1792]{2,1,0:T(8,128)(2,1)}, bf16[4,136,1792]{2,1,0:T(8,128)(2,1)}, u32[]{:S(2)}, u32[]{:S(2)}) collective-permute-start(bf16[4,136,1792]{2,1,0:T(8,128)(2,1)} %get-tuple-element.167.refs_14_), channel_id=1, source_target_pairs={{0,16},{8,24},{16,0},{24,8},{1,17},{9,25},{17,1},{25,9},{2,18},{10... | collective-permute-start | bytes 5849096 | tf_op jit(solution)/shard_map/ppermute | solution.py:799
  815.6 52.8 %collective-permute-start.24 = (bf16[1024,1088]{0,1:T(8,128)(2,1)}, bf16[1024,1088]{0,1:T(8,128)(2,1)}, u32[]{:S(2)}, u32[]{:S(2)}) collective-permute-start(bf16[1024,1088]{0,1:T(8,128)(2,1)} %copy.129), channel_id=1, source_target_pairs={{0,1},{1,0},{2,3},{3,2},{4,5},{5,4},{6,7},{7,6},{8,9},{9,8},{10,11... | collective-permute-start | bytes 6684680 | tf_op jit(solution)/shard_map/ppermute | solution.py:799
  827.0 47.7 %collective-permute-start.40 = (bf16[136,1152]{1,0:T(8,128)(2,1)}, bf16[136,1152]{1,0:T(8,128)(2,1)}, u32[]{:S(2)}, u32[]{:S(2)}) collective-permute-start(bf16[136,1152]{1,0:T(8,128)(2,1)} %gate.31), channel_id=1, source_target_pairs={{0,1},{1,0},{2,3},{3,2},{4,5},{5,4},{6,7},{7,6},{8,9},{9,8},{10,11... | collective-permute-start | bytes 940040 | tf_op jit(solution)/shard_map/ppermute | solution.py:799
  829.6 47.1 %collective-permute-start.26 = (bf16[136,1792]{1,0:T(8,128)(2,1)}, bf16[136,1792]{1,0:T(8,128)(2,1)}, u32[]{:S(2)}, u32[]{:S(2)}) collective-permute-start(bf16[136,1792]{1,0:T(8,128)(2,1)} %get-tuple-element.208), channel_id=1, source_target_pairs={{0,2},{2,4},{4,6},{6,0},{1,3},{3,5},{5,7},{7,1},{8,10},{10,12},{12... | collective-permute-start | bytes 1462280 | tf_op jit(solution)/shard_map/ppermute | solution.py:804
  839.7 37.0 %collective-permute-start.27 = (bf16[136,1792]{1,0:T(8,128)(2,1)}, bf16[136,1792]{1,0:T(8,128)(2,1)}, u32[]{:S(2)}, u32[]{:S(2)}) collective-permute-start(bf16[136,1792]{1,0:T(8,128)(2,1)} %get-tuple-element.210), channel_id=1, source_target_pairs={{0,4},{2,6},{4,0},{6,2},{1,5},{3,7},{5,1},{7,3},{8,12},{10,14},{12... | collective-permute-start | bytes 1462280 | tf_op jit(solution)/shard_map/ppermute | solution.py:804
  841.1 35.6 %collective-permute-start.28 = (bf16[136,1792]{1,0:T(8,128)(2,1)S(1)}, bf16[136,1792]{1,0:T(8,128)(2,1)}, u32[]{:S(2)}, u32[]{:S(2)}) collective-permute-start(bf16[136,1792]{1,0:T(8,128)(2,1)S(1)} %get-tuple-element.209), channel_id=1, source_target_pairs={{0,6},{2,0},{4,2},{6,4},{1,7},{3,1},{5,3},{7,5},{8,14},{10,8},{12,... | collective-permute-start | bytes 1462280 | tf_op jit(solution)/shard_map/ppermute | solution.py:804
  880.8 48.9 %collective-permute-start.38 = (bf16[136,2720]{1,0:T(8,128)(2,1)}, bf16[136,2720]{1,0:T(8,128)(2,1)}, u32[]{:S(2)}, u32[]{:S(2)}) collective-permute-start(bf16[136,2720]{1,0:T(8,128)(2,1)} %gate.30), channel_id=1, source_target_pairs={{0,16},{8,24},{16,0},{24,8},{1,17},{9,25},{17,1},{25,9},{2,18},{10... | collective-permute-start | bytes 2219528 | tf_op jit(solution)/shard_map/ppermute | solution.py:799
  881.9 38.4 %collective-permute-start.35 = (bf16[136,896]{1,0:T(8,128)(2,1)}, bf16[136,896]{1,0:T(8,128)(2,1)}, u32[]{:S(2)}, u32[]{:S(2)}) collective-permute-start(bf16[136,896]{1,0:T(8,128)(2,1)} %broadcast_select_fusion.15), channel_id=1, source_target_pairs={{0,1},{1,0},{2,3},{3,2},{4,5},{5,4},{6,7},{7,6},{8,9},{9,8},{10,11... | collective-permute-start | bytes 731144 | tf_op jit(solution)/shard_map/ppermute | solution.py:799
  (133 other events, 1620.8 us)
Sparse Core Ops, SparseCore 0:
  11.5 74.2 all-gather.6
  88.7 104.1 all-gather.8
  195.8 104.8 all-gather.10

commit v6 on v5

--- a/solution.py
+++ b/solution.py
@@ -507,8 +507,7 @@
 def up_back_last_kernel(
     half, act_turned, cot, slope, up, down, so_far, norm, pace, gain, mixed_a, mixed_b, out_w, *rest
 ):
-    d_resid, d_mixed_a, d_mixed_b, keep, give, out_keep, out_give, bias_grad, lines = rest[-11:-2]
-    d_branch, piece = rest[-2:]
+    d_resid, d_branch, d_mixed_a, d_mixed_b, keep, give, out_keep, out_give, bias_grad, lines, piece = rest[-11:]
     step = pl.program_id(0)
     rows, width = cot.shape
     first = mixed_a.shape[1]
@@ -581,9 +580,9 @@
             fixed((width, width)),
         ]
         operands += [so_far, norm, pace, gain.reshape(1, width), *mixed, out_w]
-        out_specs += [steady(m.shape) for m in mixed]
-        out_shape += [like(m.shape, jnp.bfloat16) for m in mixed]
-        scratch = [pltpu.VMEM((rows, width), jnp.bfloat16), pltpu.VMEM((width, TILE), jnp.float32)]
+        out_specs += [steady((rows, width))] + [steady(m.shape) for m in mixed]
+        out_shape += [like((rows, width), jnp.bfloat16)] + [like(m.shape, jnp.bfloat16) for m in mixed]
+        scratch = [pltpu.VMEM((width, TILE), jnp.float32)]
     out_specs += [split] * 2
     out_shape += [like((count, block, inner), jnp.bfloat16)] * 2
     if final is not None:
@@ -615,8 +614,11 @@
 
 
 def tokens_back_kernel(*refs):
-    grads, weights, norm = refs[0:6], refs[6:12], refs[12]
+    grads, weights, rows = refs[0:6], refs[6:12], refs[12]
     out, lines = refs[-2:]
+    values = rows[...].astype(jnp.float32)
+    centred = values - jnp.mean(values, axis=1, keepdims=True)
+    normed = centred * lax.rsqrt(jnp.mean(centred * centred, axis=1, keepdims=True) + epsilon)
     total = sum(nt(grad[...], weight[...]) for grad, weight in zip(grads, weights))
     out[...] = total.astype(out.dtype)
 
@@ -624,12 +626,12 @@
     def _():
         lines[...] = jnp.zeros_like(lines)
 
-    lines[0:1, :] += jnp.sum(total * norm[...].astype(jnp.float32), axis=0, keepdims=True)
+    lines[0:1, :] += jnp.sum(total * normed, axis=0, keepdims=True)
     lines[1:2, :] += jnp.sum(total, axis=0, keepdims=True)
 
 
-def tokens_back(grads, weights, norm, size, after=()):
-    total, width = norm.shape
+def tokens_back(grads, weights, rows, size, after=()):
+    total, width = rows.shape
     flat_grads, flat_weights = [g for group in grads for g in group], [w for group in weights for w in group]
     tall = pl.BlockSpec((size, width), lambda t: (t, 0))
     return pl.pallas_call(
@@ -649,7 +651,7 @@
         ),
         cost_estimate=busy(20),
         name="tokens_back",
-    )(*flat_grads, *flat_weights, norm, *after)
+    )(*flat_grads, *flat_weights, rows, *after)
 
 
 def weights_back_kernel(half, turned, *refs, tiles):
@@ -804,19 +806,6 @@
     return lax.ppermute(value, axis, [(i, (i + step) % count) for i in range(count)])
 
 
-def total_over(value, axes):
-    for axis in axes:
-        count = lax.axis_size(axis)
-        if count & (count - 1):
-            value = lax.psum(value, axis)
-            continue
-        bit = 1
-        while bit < count:
-            value = value + swap(value, axis, bit)
-            bit *= 2
-    return value
-
-
 def by_halves(half_width):
     return lax.axis_size("dp") == 4 and lax.axis_size("gy") == 2 and half_width > GROUP
 
@@ -954,9 +943,9 @@
     return value[..., :size], value[..., size:]
 
 
-def overlap_join(value, columns):
+def overlap_join(value, columns, end=()):
     size = value.shape[-1]
-    other = swap(value, "dp", 2)
+    other = gate(swap(value, "dp", 2), end)
     own_first = lax.axis_index("dp") // 2 == 0
     first, second = jnp.where(own_first, value, other), jnp.where(own_first, other, value)
     return jnp.concatenate([first, second[..., 2 * size - columns :]], axis=-1)
@@ -973,23 +962,19 @@
     return total.astype(jnp.bfloat16)
 
 
-def copies_step(value):
-    bit = 2
-    while bit < lax.axis_size("dp"):
-        value = add(value, swap(value, "dp", bit))
-        bit *= 2
-    return value
-
-
-def join_step(value):
+def join_step(value, end=()):
     columns = value.shape[-1]
-    return pair_rows(value, swap(value, "dp", 1)).reshape(-1, columns).astype(jnp.float32)
-
-
-def side_exchange(first, second, begin=()):
+    return pair_rows(value, gate(swap(value, "dp", 1), end)).reshape(-1, columns).astype(jnp.float32)
+
+
+def side_parts(first, second):
     first_side = lax.axis_index("gy") == 0
-    keep = jnp.where(first_side, first, second)
-    return add(keep, swap(gate(jnp.where(first_side, second, first), begin), "gy", 1))
+    return jnp.where(first_side, first, second), jnp.where(first_side, second, first)
+
+
+def side_exchange(first, second):
+    keep, give = side_parts(first, second)
+    return add(keep, swap(give, "gy", 1))
 
 
 def projection_sides(first, rest):
@@ -1094,10 +1079,10 @@
     def given_rows(own):
         return lax.dynamic_slice_in_dim(own, block - kept_at, block, 0)
 
-    def back_home(done, end=()):
+    def back_home(done):
         if not halved:
             return done
-        kept, home = done[:block], gate(swap(done[block:], "gy", 1), end)
+        kept, home = done[:block], swap(done[block:], "gy", 1)
         return jnp.concatenate([jnp.where(is_long, kept, home), jnp.where(is_long, home, kept)], axis=0)
 
     own_prompt = prompt.reshape(shard, width)
@@ -1140,8 +1125,19 @@
     tokens = jnp.concatenate(
         [lax.dynamic_slice_in_dim(whole_prompt, places[n], block, 0) for n in range(2)] + [branch], axis=0
     )
+    all_turned, cotangent_turned = act_all.T, cotangent.T
     hidden, slope, result, act_turned, norm_two, pace_two = mlp_forward(
-        mixed, tokens, out_full, out_bias, mlp_gain, mlp_shift, up_full, up_bias, down_full, down_bias
+        mixed,
+        tokens,
+        out_full,
+        out_bias,
+        mlp_gain,
+        mlp_shift,
+        up_full,
+        up_bias,
+        down_full,
+        down_bias,
+        (all_turned, cotangent_turned),
     )
     count = lax.axis_size("gx")
     half = jnp.reshape(half_index() if halved else 0, (1,)).astype(jnp.int32)
@@ -1149,7 +1145,7 @@
     part = tiles // 2
     prompt_out = back_home(result[:shard]).reshape(groups, shard, width)
     continuation_out = result[shard:].reshape(1, length, width)
-    down_keep, down_give = down_back(half, count, cotangent.T, hidden)
+    down_keep, down_give = down_back(half, count, cotangent_turned, hidden)
     after = ()
     if halved:
         down_flow = core_step(down_keep, down_give)
@@ -1157,7 +1153,7 @@
     so_far, up_keep, up_give, up_bias_grad = up_back(
         half, count, (0, part), act_turned, cotangent, slope, up_full, down_full
     )
-    d_resid, *d_mixed, keep_rest, give_rest, out_keep, out_give, bias_rest, lines = up_back(
+    d_resid, d_branch, *d_mixed, keep_rest, give_rest, out_keep, out_give, bias_rest, lines = up_back(
         half,
         count,
         (part, tiles),
@@ -1193,29 +1189,32 @@
                 jnp.concatenate([up_flow[..., side:], out_flow[..., width // 2 :]], axis=-1),
             )
             down_flow = blocks_step(down_flow)
-            d_home = gate(d_resid.astype(jnp.bfloat16), (d_parts[1][0],))
-            after = (up_flow, down_flow, d_home)
+            after = (up_flow, down_flow)
         if halved and number == 0:
             up_flow = blocks_step(up_flow)
-            home = back_home(d_home[:shard], (d_parts[0][0],)).astype(jnp.float32)
-            after = (up_flow,)
-    keep_a, give_a, bias_a, keep_b, give_b, bias_b = weights_back(half, count, act_all.T, d_parts, after)
+            down_keep, down_give = side_parts(*two(down_flow))
+            home_give = gate(d_branch[block:shard], (d_parts[0][0],))
+            after = (up_flow, down_give, home_give)
+    keep_a, give_a, bias_a, keep_b, give_b, bias_b = weights_back(half, count, all_turned, d_parts, after)
     if halved:
         sides = projection_sides(core_step(keep_a, give_a), core_step(keep_b, give_b))
         parts = chips_parts(sides)
-        after = parts
+        up_flow = add(up_flow, gate(swap(up_flow, "dp", 2), (keep_a,)))
+        down_flow = add(down_keep, gate(swap(down_give, "gy", 1), (keep_a,)))
+        home = gate(swap(home_give, "gy", 1), (keep_a,)).astype(jnp.float32)
+        after = (*parts, up_flow, down_flow)
     else:
         after = (keep_a,)
-    d_act_all, act_lines = tokens_back(d_parts, weights, norm_all.astype(jnp.bfloat16), length, after)
+    d_act_all, act_lines = tokens_back(d_parts, weights, all_rows, length, after)
     attn_gain_grad, attn_shift_grad = act_lines[0], act_lines[1]
     others = others_tokens(d_act_all[:prompt_len])
     if halved:
         qkv_flow = chips_step(parts, (d_act_all,))
-        down_flow = side_exchange(*two(down_flow), (qkv_flow,))
+        up_total = join_step(up_flow, (d_act_all,))
+        down_flow = overlap_join(down_flow, side, (d_act_all,))
         qkv_flow = blocks_step(qkv_flow)
         others = gate(others, (qkv_flow,))
-        summed = qkv_flow
-        up_flow = gate(up_flow, (summed,))
+        down_total = join_step(gate(down_flow, (qkv_flow,)))
     size = bias_b.shape[1] // 3
     query_bias_grad, value_bias_grad = (
         jnp.concatenate(
@@ -1226,9 +1225,7 @@
     if halved:
         qkv_flow = side_exchange(*two(qkv_flow))
         qkv_total = join_projections(join_step(overlap_join(qkv_flow, sides[0].shape[-1])), width)
-        up_total = join_step(copies_step(up_flow))
         up_total, out_total = up_total[:, :side], up_total[:, side:]
-        down_total = join_step(overlap_join(down_flow, side))
     else:
         whole_a, whole_b = both_halves(keep_a, give_a), both_halves(keep_b, give_b)
         qkv_grad = jnp.concatenate(
@@ -1253,9 +1250,8 @@
         )
     prompt_resid = d_resid[:shard]
     if halved:
-        kept = jnp.where(is_long, prompt_resid[:block], home[:block]), jnp.where(
-            is_long, home[block:], prompt_resid[:block]
-        )
+        kept = prompt_resid[:block]
+        kept = jnp.where(is_long, kept, home), jnp.where(is_long, home, kept)
         prompt_resid = jnp.concatenate(kept, axis=0)
     own_rows = jnp.concatenate([own_prompt, branch], axis=0)
     own_grad = jnp.concatenate(
@@ -1276,8 +1272,7 @@
         up_bias_grad.reshape(-1),
         down_bias_grad,
     )
-    joined = gate(jnp.concatenate(vectors), (summed,) if halved else ())
-    joined = total_over(joined, ("dp", "gy", "gx"))
+    joined = jnp.sum(lax.all_gather(jnp.concatenate(vectors), ("dp", "gx", "gy")), axis=0)
     totals = []
     at = 0
     for vector in vectors:

time: 965 us -> 917 us (0.950)
  waiting for transfers between devices: 140 us -> 114 us
  starting transfers between devices: 69.2 us -> 45.2 us
  other arithmetic: 135 us -> 124 us
    ppermute x31 -> x26, waiting for transfers between devices: 112 us -> 54.6 us  [swap(): return lax.ppermute(value, axis, [(i, i ^ bit) for i in range(count)])]
    ppermute x12, waiting for transfers between devices: 0.03 us -> 50.1 us  [ahead(): lax.ppermute(value, axis, [(i, (i + step) % count) for i in range(count)])]
    all_gather x3, waiting for transfers between devices: 28.1 us -> 9.56 us  [gather_quarters(): raw = lax.all_gather(mine, ('dp', 'gx', 'gy'))]
    ppermute x31 -> x26, starting transfers between devices: 40.9 us -> 23.9 us  [swap(): return lax.ppermute(value, axis, [(i, i ^ bit) for i in range(count)])]
    unnamed x236 -> x259, local copies, waits for them, and re-layouts: 45.7 us -> 45.7 us
  transfers between devices with their start and end apart: 46 -> 42, of which waited for: 12 -> 8; matrix products, arithmetic and copies ran while one was open for 25% -> 27% of each run, Pallas kernels for 31% -> 36%
where the time goes in v6:
time: 917 us; the launch traced here: 907 us
  Pallas kernels  414 us (45%)
  local copies, waits for them, and re-layouts  153 us (17%)
  other arithmetic  124 us (14%)
  waiting for transfers between devices  114 us (12%)
  starting transfers between devices  45.2 us (5%)
  matrix products  37.9 us (4%)
  between operations  17.9 us (2%)
    pallas_call x2, Pallas kernels, attention_backward(): pl.pallas_call(functools.partial(backward_kernel, block=block, branch=bra...  104 us
    pallas_call x2, Pallas kernels, up_back(): pl.pallas_call(up_back_first_kernel if final is None else up_back_last_ke...  82.6 us
    pallas_call x2, Pallas kernels, attention_forward(): pl.pallas_call(functools.partial(forward_kernel, block=block, branch=bran...  74.1 us
    pallas_call x1, Pallas kernels, mlp_forward(): pl.pallas_call(mlp_forward_kernel, grid=(inner // TILE,), in_specs=[fixed...  64.9 us
    ppermute x26, waiting for transfers between devices, swap(): return lax.ppermute(value, axis, [(i, i ^ bit) for i in range(count)])  54.6 us
    ppermute x12, waiting for transfers between devices, ahead(): lax.ppermute(value, axis, [(i, (i + step) % count) for i in range(count)])  50.1 us
    unnamed x259, local copies, waits for them, and re-layouts  45.7 us
    dot_general x6, matrix products, dot(): return jnp.dot(a, b, preferred_element_type=jnp.float32)  37.9 us
  transfers between devices with their start and end apart: 42, of which 8 were waited for; matrix products, arithmetic and copies ran while one was open for 27% of the time, Pallas kernels for 36%

profile of v6, /device:TPU:0, one launch (start us, length us, event | category | flops | bytes accessed | tf_op | source)
XLA Modules:
  0.0 906.5 jit_solution(6912222713758120825)
XLA Ops:
  26.5 49.1 %collective-permute-done = s32[1]{0:T(128)} collective-permute-done((s32[1]{0:T(128)}, s32[1]{0:T(128)}, u32[]{:S(2)}, u32[]{:S(2)}) %collective-permute-start) | collective-permute-done | bytes 36 | tf_op jit(solution)/shard_map/ppermute | solution.py:801
  103.2 8.5 copy.128.rest_0_.turned
  115.3 8.3 pad_maximum_fusion.3
  138.4 6.1 fusion.8.q
  144.5 7.0 convolution_convert_fusion.1.k
  151.5 6.9 fusion.9.v
  158.5 33.1 %attention_forward.2 = (bf16[1280,512]{1,0:T(8,128)(2,1)S(1)}, f32[4,8,1280]{2,1,0:T(8,128)S(1)}) custom-call(s32[3]{0:T(128)S(1)} %pad_add_fusion.pos, bf16[2304,512]{1,0:T(8,128)(2,1)S(1)} %fusion.8.q, bf16[2304,512]{1,0:T(8,128)(2,1)S(1)} %convolution_convert_fusion.1.k, bf16[2304,512]{1,0:T(8,128)(2,1)S(1)} %fusion.9.v), custom_call_target="tpu_custom_call" | custom-call | flops 28000000000 | bytes 28000000 | tf_op jit(solution)/shard_map/attention_forward/pallas_call | solution.py:169
  202.0 6.2 fusion.37
  208.2 5.4 copy.129.rest_1_.cot_turned
  213.6 5.0 fusion.39
  221.3 7.8 convolution_convert_fusion.k
  229.2 4.9 add_convert_fusion.3.q
  234.1 5.3 add_convert_fusion.2.v
  239.4 41.0 %attention_forward.3 = (bf16[1280,576]{1,0:T(8,128)(2,1)S(1)}, f32[5,8,1280]{2,1,0:T(8,128)S(1)}) custom-call(s32[3]{0:T(128)S(1)} %pad_add_fusion.pos, bf16[2304,576]{1,0:T(8,128)(2,1)S(1)} %add_convert_fusion.3.q, bf16[2304,576]{1,0:T(8,128)(2,1)S(1)} %convolution_convert_fusion.k, bf16[2304,576]{1,0:T(8,128)(2,1)S(1)} %add_convert_fusion.2.v), custom_call_target="tpu_custom_call" | custom-call | flops 35000000512 | bytes 35000000 | tf_op jit(solution)/shard_map/attention_forward/pallas_call | solution.py:169
  285.0 5.5 broadcast_select_fusion.2
  293.9 9.6 %all-gather.14.cloned.1.call-done = bf16[8704,512]{1,0:T(8,128)(2,1)} async-done(((bf16[272,512]{1,0:T(8,128)(2,1)}), bf16[8704,512]{1,0:T(8,128)(2,1)}) %all-gather.14.cloned.1.call-update) | async-done | bytes 8912912 | tf_op jit(solution)/shard_map/all_gather | solution.py:832
  322.3 64.9 %mlp_forward.1 = (bf16[1280,4352]{1,0:T(8,128)(2,1)}, bf16[1280,4352]{1,0:T(8,128)(2,1)}, bf16[1280,1088]{1,0:T(8,128)(2,1)}, bf16[1088,1280]{1,0:T(8,128)(2,1)}...) custom-call(bf16[1280,512]{1,0:T(8,128)(2,1)S(1)} %copy-done.19, bf16[1280,576]{1,0:T(8,128)(2,1)} %copy-done.10, ...), custom_call_target="tpu_custom_call" | custom-call | flops 49999998976 | bytes 50000000 | tf_op jit(solution)/shard_map/mlp_forward/pallas_call | solution.py:409
  387.2 20.1 %down_back.1 = (bf16[4,136,4352]{2,1,0:T(8,128)(2,1)S(1)}, bf16[4,136,4352]{2,1,0:T(8,128)(2,1)}) custom-call(s32[1]{0:T(128)} %bitcast.48.half, bf16[1088,1280]{1,0:T(8,128)(2,1)S(1)} %copy-done.8, bf16[1280,4352]{1,0:T(8,128)(2,1)} %get-tuple-element.67.hidden), custom_call_target="tpu_custom_call" | custom-call | flops 15000000512 | bytes 15000000 | tf_op jit(solution)/shard_map/down_back/pallas_call | solution.py:470
  413.0 29.8 %up_back_first.1 = (f32[1280,1088]{1,0:T(8,128)}, bf16[4,136,2048]{2,1,0:T(8,128)(2,1)}, bf16[4,136,2048]{2,1,0:T(8,128)(2,1)}, f32[1,2048]{1,0:T(1,128)}) custom-call(s32[1]{0:T(128)} %bitcast.48.half, bf16[1088,1280]{1,0:T(8,128)(2,1)} %get-tuple-element.62.act_turned, bf16[1280,1088]{1,0:T(8,128)(2,1)} %get-tuple-element.193.refs_2_.cot, ...), custom_call_target="tpu_custom_call" | custom-call | flops 30000001024 | bytes 30000000 | tf_op jit(solution)/shard_map/up_back_first/pallas_call | solution.py:598
  456.8 52.8 %up_back_last.1 = (f32[1280,1088]{1,0:T(8,128)}, bf16[1280,1088]{1,0:T(8,128)(2,1)}, bf16[1280,512]{1,0:T(8,128)(2,1)}, bf16[1280,576]{1,0:T(8,128)(2,1)}, bf16[...) custom-call(s32[1]{0:T(128)} %bitcast.48.half, ...), custom_call_target="tpu_custom_call" | custom-call | flops 49999998976 | bytes 50000000 | tf_op jit(solution)/shard_map/up_back_last/pallas_call | solution.py:598
  553.4 4.6 collective-permute-start.18
  559.1 57.5 %attention_backward.3 = (bf16[2304,576]{1,0:T(8,128)(2,1)S(1)}, bf16[2304,576]{1,0:T(8,128)(2,1)S(1)}, bf16[2304,576]{1,0:T(8,128)(2,1)}) custom-call(s32[3]{0:T(128)S(1)} %copy-done.26, bf16[2304,576]{1,0:T(8,128)(2,1)} %copy-done.32, bf16[2304,576]{1,0:T(8,128)(2,1)} %copy-done.31, bf16[2304,576]{1,0:T(8,128)(2,1)} %copy-done.33, ...), custom_call_target="tpu_custom_call" | custom-call | flops 49999998976 | bytes 50000000 | tf_op jit(solution)/shard_map/attention_backward/pallas_call | solution.py:305
  630.4 46.6 %attention_backward.2 = (bf16[2304,512]{1,0:T(8,128)(2,1)S(1)}, bf16[2304,512]{1,0:T(8,128)(2,1)S(1)}, bf16[2304,512]{1,0:T(8,128)(2,1)S(1)}) custom-call(s32[3]{0:T(128)S(1)} %copy-done.26, bf16[2304,512]{1,0:T(8,128)(2,1)S(1)} %copy-done.29, bf16[2304,512]{1,0:T(8,128)(2,1)} %copy-done.27, bf16[2304,512]{1,0:T(8,128)(2,1)} %copy-done.30, ...), custom_call_target="tpu_custom_call" | custom-call | flops 40000000000 | bytes 40000000 | tf_op jit(solution)/shard_map/attention_backward/pallas_call | solution.py:305
  683.6 4.5 collective-permute-start.31
  688.1 7.8 collective-permute-done.20
  698.7 31.1 %weights_back.1 = (bf16[4,136,1536]{2,1,0:T(8,128)(2,1)}, bf16[4,136,1536]{2,1,0:T(8,128)(2,1)}, f32[1,1536]{1,0:T(1,128)S(1)}, bf16[4,136,2304]{2,1,0:T(8,128)(...) custom-call(s32[1]{0:T(128)} %bitcast.48.half, bf16[1088,2304]{1,0:T(8,128)(2,1)} %copy.128.rest_0_.turned, ...), custom_call_target="tpu_custom_call" | custom-call | flops 24999999488 | bytes 25000000 | tf_op jit(solution)/shard_map/weights_back/pallas_call | solution.py:697
  755.6 30.3 %tokens_back.1 = (bf16[2304,1088]{1,0:T(8,128)(2,1)}, f32[8,1088]{1,0:T(8,128)S(1)}) custom-call(bf16[2304,512]{1,0:T(8,128)(2,1)} %copy-done.9, bf16[2304,512]{1,0:T(8,128)(2,1)} %copy-done.36, bf16[2304,512]{1,0:T(8,128)(2,1)} %copy-done.37, bf16[2304,576]{1,0:T(8,128)(2,1)} %copy-done.34, bf16[2304,576]{1,0:T(8,128)(2,1)} %copy-done.35, ...), custom_call_target="tpu_custom_call" | custom-call | flops 20000000000 | bytes 20000000 | tf_op jit(solution)/shard_map/tokens_back/pallas_call | solution.py:637
  785.9 4.9 slice.402
  798.5 4.3 copy.135
  816.7 8.8 collective-permute-done.30
  825.4 33.5 %collective-permute-done.29 = bf16[136,1792]{1,0:T(8,128)(2,1)S(1)} collective-permute-done((bf16[136,1792]{1,0:T(8,128)(2,1)S(1)}, bf16[136,1792]{1,0:T(8,128)(2,1)S(1)}, u32[]{:S(2)}, u32[]{:S(2)}) %collective-permute-start.29) | collective-permute-done | bytes 487456 | tf_op jit(solution)/shard_map/ppermute | solution.py:806
  875.2 6.8 rows_back.1
  (502 shorter events, 270.6 us)
Async XLA Ops:
  7.2 116.4 %all-gather.10.cloned.1.call-start = ((), (), s32[]{:S(2)}) async-start(), calls=%async_computation | async-start | bytes 4595712 | tf_op jit(solution)/shard_map/all_gather | solution.py:832
  9.5 204.1 %all-gather.12.cloned.1.call-start = ((), (), s32[]{:S(2)}) async-start(), calls=%async_computation.1 | async-start | bytes 6893568 | tf_op jit(solution)/shard_map/all_gather | solution.py:832
  11.7 291.7 %all-gather.14.cloned.1.call-start = ((), (), s32[]{:S(2)}) async-start(), calls=%async_computation.2 | async-start | bytes 9191424 | tf_op jit(solution)/shard_map/all_gather | solution.py:832
  11.7 73.3 %collective-permute-start.1 = (bf16[1024,1088]{0,1:T(8,128)(2,1)}, bf16[1024,1088]{0,1:T(8,128)(2,1)}, u32[]{:S(2)}, u32[]{:S(2)}) collective-permute-start(bf16[1024,1088]{0,1:T(8,128)(2,1)} %bitcast.5), channel_id=1, source_target_pairs={{0,1},{1,0},{2,3},{3,2},{4,5},{5,4},{6,7},{7,6},{8,9},{9,8},{10,11... | collective-permute-start | bytes 6684680 | tf_op jit(solution)/shard_map/ppermute | solution.py:801
  14.7 60.9 %collective-permute-start = (s32[1]{0:T(128)}, s32[1]{0:T(128)}, u32[]{:S(2)}, u32[]{:S(2)}) collective-permute-start(s32[1]{0:T(128)} %param.20), channel_id=1, source_target_pairs={{0,1},{1,0},{2,3},{3,2},{4,5},{5,4},{6,7},{7,6},{8,9},{9,8},{10,11... | collective-permute-start | bytes 20 | tf_op jit(solution)/shard_map/ppermute | solution.py:801
  16.8 868.4 %all-gather.16.cloned.1.call-start = ((), (), s32[]{:S(2)}) async-start(), calls=%async_computation.3 | async-start | bytes 1723392 | tf_op jit(solution)/shard_map/all_gather | solution.py:1275
  123.6 70.7 %collective-permute-start.2 = (bf16[272,1152]{1,0:T(8,128)(2,1)}, bf16[272,1152]{1,0:T(8,128)(2,1)}, u32[]{:S(2)}, u32[]{:S(2)}) collective-permute-start(bf16[272,1152]{1,0:T(8,128)(2,1)} %gate.18), channel_id=1, source_target_pairs={{0,2},{2,4},{4,6},{6,0},{1,3},{3,5},{5,7},{7,1},{8,10},{10,12},{12... | collective-permute-start | bytes 1880072 | tf_op jit(solution)/shard_map/ppermute | solution.py:806
  125.3 71.0 %collective-permute-start.3 = (bf16[272,1152]{1,0:T(8,128)(2,1)}, bf16[272,1152]{1,0:T(8,128)(2,1)}, u32[]{:S(2)}, u32[]{:S(2)}) collective-permute-start(bf16[272,1152]{1,0:T(8,128)(2,1)} %gate.18), channel_id=1, source_target_pairs={{0,4},{2,6},{4,0},{6,2},{1,5},{3,7},{5,1},{7,3},{8,12},{10,14},{12... | collective-permute-start | bytes 1880072 | tf_op jit(solution)/shard_map/ppermute | solution.py:806
  128.1 70.2 %collective-permute-start.4 = (bf16[272,1152]{1,0:T(8,128)(2,1)}, bf16[272,1152]{1,0:T(8,128)(2,1)}, u32[]{:S(2)}, u32[]{:S(2)}) collective-permute-start(bf16[272,1152]{1,0:T(8,128)(2,1)} %gate.18), channel_id=1, source_target_pairs={{0,6},{2,0},{4,2},{6,4},{1,7},{3,1},{5,3},{7,5},{8,14},{10,8},{12,... | collective-permute-start | bytes 1880072 | tf_op jit(solution)/shard_map/ppermute | solution.py:806
  136.1 64.2 %collective-permute-start.5 = (bf16[512,1088]{0,1:T(8,128)(2,1)}, bf16[512,1088]{0,1:T(8,128)(2,1)}, u32[]{:S(2)}, u32[]{:S(2)}) collective-permute-start(bf16[512,1088]{0,1:T(8,128)(2,1)} %copy.119), channel_id=1, source_target_pairs={{0,1},{1,0},{2,3},{3,2},{4,5},{5,4},{6,7},{7,6},{8,9},{9,8},{10,11... | collective-permute-start | bytes 3342344 | tf_op jit(solution)/shard_map/ppermute | solution.py:801
  208.2 76.8 %collective-permute-start.6 = (bf16[1088,1152]{1,0:T(8,128)(2,1)}, bf16[1088,1152]{1,0:T(8,128)(2,1)}, u32[]{:S(2)}, u32[]{:S(2)}) collective-permute-start(bf16[1088,1152]{1,0:T(8,128)(2,1)} %gate.20), channel_id=1, source_target_pairs={{0,1},{1,0},{2,3},{3,2},{4,5},{5,4},{6,7},{7,6},{8,9},{9,8},{10,11... | collective-permute-start | bytes 7520264 | tf_op jit(solution)/shard_map/ppermute | solution.py:801
  290.5 21.4 %collective-permute-start.8 = (bf16[1088,1152]{1,0:T(8,128)(2,1)}, bf16[1088,1152]{1,0:T(8,128)(2,1)}, u32[]{:S(2)}, u32[]{:S(2)}) collective-permute-start(bf16[1088,1152]{1,0:T(8,128)(2,1)} %get-tuple-element.167), channel_id=1, source_target_pairs={{0,8},{8,0},{16,24},{24,16},{1,9},{9,1},{17,25},{25,17},{2,10},{10... | collective-permute-start | bytes 7520264 | tf_op jit(solution)/shard_map/ppermute | solution.py:801
  409.5 38.3 %collective-permute-start.10 = (bf16[4,136,4352]{2,1,0:T(8,128)(2,1)}, bf16[4,136,4352]{2,1,0:T(8,128)(2,1)}, u32[]{:S(2)}, u32[]{:S(2)}) collective-permute-start(bf16[4,136,4352]{2,1,0:T(8,128)(2,1)} %get-tuple-element.69), channel_id=1, source_target_pairs={{0,8},{8,0},{16,24},{24,16},{1,9},{9,1},{17,25},{25,17},{2,10},{10... | collective-permute-start | bytes 14204936 | tf_op jit(solution)/shard_map/ppermute | solution.py:801
  411.8 31.1 %collective-permute-start.9 = (bf16[512,1088]{0,1:T(8,128)(2,1)S(1)}, bf16[512,1088]{0,1:T(8,128)(2,1)}, u32[]{:S(2)}, u32[]{:S(2)}) collective-permute-start(bf16[512,1088]{0,1:T(8,128)(2,1)S(1)} %copy.130), channel_id=1, source_target_pairs={{0,1},{1,0},{2,3},{3,2},{4,5},{5,4},{6,7},{7,6},{8,9},{9,8},{10,11... | collective-permute-start | bytes 3342344 | tf_op jit(solution)/shard_map/ppermute | solution.py:801
  455.6 58.2 %collective-permute-start.12 = (bf16[4,136,2304]{2,1,0:T(8,128)(2,1)}, bf16[4,136,2304]{2,1,0:T(8,128)(2,1)}, u32[]{:S(2)}, u32[]{:S(2)}) collective-permute-start(bf16[4,136,2304]{2,1,0:T(8,128)(2,1)} %gate.23), channel_id=1, source_target_pairs={{0,16},{8,24},{16,0},{24,8},{1,17},{9,25},{17,1},{25,9},{2,18},{10... | collective-permute-start | bytes 7520264 | tf_op jit(solution)/shard_map/ppermute | solution.py:801
  456.8 52.8 %collective-permute-start.11 = (bf16[4,136,2048]{2,1,0:T(8,128)(2,1)}, bf16[4,136,2048]{2,1,0:T(8,128)(2,1)}, u32[]{:S(2)}, u32[]{:S(2)}) collective-permute-start(bf16[4,136,2048]{2,1,0:T(8,128)(2,1)} %gate.22), channel_id=1, source_target_pairs={{0,8},{8,0},{16,24},{24,16},{1,9},{9,1},{17,25},{25,17},{2,10},{10... | collective-permute-start | bytes 6684680 | tf_op jit(solution)/shard_map/ppermute | solution.py:801
  552.2 69.1 %collective-permute-start.15 = (bf16[4,136,2720]{2,1,0:T(8,128)(2,1)}, bf16[4,136,2720]{2,1,0:T(8,128)(2,1)}, u32[]{:S(2)}, u32[]{:S(2)}) collective-permute-start(bf16[4,136,2720]{2,1,0:T(8,128)(2,1)} %broadcast_select_fusion), channel_id=1, source_target_pairs={{0,1},{1,0},{2,3},{3,2},{4,5},{5,4},{6,7},{7,6},{8,9},{9,8},{10,11... | collective-permute-start | bytes 8878088 | tf_op jit(solution)/shard_map/ppermute | solution.py:801
  553.4 63.3 %collective-permute-start.18 = (bf16[136,2304]{1,0:T(8,128)(2,1)S(1)}, bf16[136,2304]{1,0:T(8,128)(2,1)S(1)}, u32[]{:S(2)}, u32[]{:S(2)}) collective-permute-start(bf16[136,2304]{1,0:T(8,128)(2,1)S(1)} %get-tuple-element.198), channel_id=1, source_target_pairs={{0,6},{2,0},{4,2},{6,4},{1,7},{3,1},{5,3},{7,5},{8,14},{10,8},{12,... | collective-permute-start | bytes 1880072 | tf_op jit(solution)/shard_map/ppermute | solution.py:806
  558.0 58.7 %collective-permute-start.17 = (bf16[136,2304]{1,0:T(8,128)(2,1)S(1)}, bf16[136,2304]{1,0:T(8,128)(2,1)S(1)}, u32[]{:S(2)}, u32[]{:S(2)}) collective-permute-start(bf16[136,2304]{1,0:T(8,128)(2,1)S(1)} %get-tuple-element.199), channel_id=1, source_target_pairs={{0,4},{2,6},{4,0},{6,2},{1,5},{3,7},{5,1},{7,3},{8,12},{10,14},{12... | collective-permute-start | bytes 1880072 | tf_op jit(solution)/shard_map/ppermute | solution.py:806
  558.0 58.7 %collective-permute-start.16 = (bf16[136,2304]{1,0:T(8,128)(2,1)S(1)}, bf16[136,2304]{1,0:T(8,128)(2,1)S(1)}, u32[]{:S(2)}, u32[]{:S(2)}) collective-permute-start(bf16[136,2304]{1,0:T(8,128)(2,1)S(1)} %get-tuple-element.197), channel_id=1, source_target_pairs={{0,2},{2,4},{4,6},{6,0},{1,3},{3,5},{5,7},{7,1},{8,10},{10,12},{12... | collective-permute-start | bytes 1880072 | tf_op jit(solution)/shard_map/ppermute | solution.py:806
  617.1 113.2 %collective-permute-start.25 = (bf16[136,1152]{1,0:T(8,128)(2,1)S(1)}, bf16[136,1152]{1,0:T(8,128)(2,1)S(1)}, u32[]{:S(2)}, u32[]{:S(2)}) collective-permute-start(bf16[136,1152]{1,0:T(8,128)(2,1)S(1)} %broadcast_select_fusion.12.refs_7_), channel_id=1, source_target_pairs={{0,1},{1,0},{2,3},{3,2},{4,5},{5,4},{6,7},{7,6},{8,9},{9,8},{10,11... | collective-permute-start | bytes 940040 | tf_op jit(solution)/shard_map/ppermute | solution.py:801
  625.4 62.7 %collective-permute-start.21 = (bf16[136,2720]{1,0:T(8,128)(2,1)}, bf16[136,2720]{1,0:T(8,128)(2,1)}, u32[]{:S(2)}, u32[]{:S(2)}) collective-permute-start(bf16[136,2720]{1,0:T(8,128)(2,1)} %get-tuple-element.190), channel_id=1, source_target_pairs={{0,6},{2,0},{4,2},{6,4},{1,7},{3,1},{5,3},{7,5},{8,14},{10,8},{12,... | collective-permute-start | bytes 2219528 | tf_op jit(solution)/shard_map/ppermute | solution.py:806
  629.6 66.2 %collective-permute-start.20 = (bf16[136,2720]{1,0:T(8,128)(2,1)}, bf16[136,2720]{1,0:T(8,128)(2,1)}, u32[]{:S(2)}, u32[]{:S(2)}) collective-permute-start(bf16[136,2720]{1,0:T(8,128)(2,1)} %get-tuple-element.191), channel_id=1, source_target_pairs={{0,4},{2,6},{4,0},{6,2},{1,5},{3,7},{5,1},{7,3},{8,12},{10,14},{12... | collective-permute-start | bytes 2219528 | tf_op jit(solution)/shard_map/ppermute | solution.py:806
  630.0 65.9 %collective-permute-start.19 = (bf16[136,2720]{1,0:T(8,128)(2,1)}, bf16[136,2720]{1,0:T(8,128)(2,1)}, u32[]{:S(2)}, u32[]{:S(2)}) collective-permute-start(bf16[136,2720]{1,0:T(8,128)(2,1)} %get-tuple-element.189), channel_id=1, source_target_pairs={{0,2},{2,4},{4,6},{6,0},{1,3},{3,5},{5,7},{7,1},{8,10},{10,12},{12... | collective-permute-start | bytes 2219528 | tf_op jit(solution)/shard_map/ppermute | solution.py:806
  683.6 50.1 %collective-permute-start.31 = (bf16[512,1088]{0,1:T(8,128)(2,1)}, bf16[512,1088]{0,1:T(8,128)(2,1)}, u32[]{:S(2)}, u32[]{:S(2)}) collective-permute-start(bf16[512,1088]{0,1:T(8,128)(2,1)} %copy.137), channel_id=1, source_target_pairs={{0,1},{1,0},{2,3},{3,2},{4,5},{5,4},{6,7},{7,6},{8,9},{9,8},{10,11... | collective-permute-start | bytes 3342344 | tf_op jit(solution)/shard_map/ppermute | solution.py:801
  698.1 43.3 %collective-permute-start.24 = (bf16[136,2720]{1,0:T(8,128)(2,1)S(1)}, bf16[136,2720]{1,0:T(8,128)(2,1)}, u32[]{:S(2)}, u32[]{:S(2)}) collective-permute-start(bf16[136,2720]{1,0:T(8,128)(2,1)S(1)} %fusion.21.refs_6_), channel_id=1, source_target_pairs={{0,16},{8,24},{16,0},{24,8},{1,17},{9,25},{17,1},{25,9},{2,18},{10... | collective-permute-start | bytes 2219528 | tf_op jit(solution)/shard_map/ppermute | solution.py:801
  732.1 72.7 %collective-permute-start.36 = (bf16[136,1152]{1,0:T(8,128)(2,1)S(1)}, bf16[136,1152]{1,0:T(8,128)(2,1)S(1)}, u32[]{:S(2)}, u32[]{:S(2)}) collective-permute-start(bf16[136,1152]{1,0:T(8,128)(2,1)S(1)} %add_convert_fusion.12.refs_16_), channel_id=1, source_target_pairs={{0,16},{8,24},{16,0},{24,8},{1,17},{9,25},{17,1},{25,9},{2,18},{10... | collective-permute-start | bytes 940040 | tf_op jit(solution)/shard_map/ppermute | solution.py:801
  742.7 50.0 %collective-permute-start.35 = (bf16[136,2720]{1,0:T(8,128)(2,1)S(1)}, bf16[136,2720]{1,0:T(8,128)(2,1)}, u32[]{:S(2)}, u32[]{:S(2)}) collective-permute-start(bf16[136,2720]{1,0:T(8,128)(2,1)S(1)} %add_convert_fusion.11.refs_15_), channel_id=1, source_target_pairs={{0,8},{8,0},{16,24},{24,16},{1,9},{9,1},{17,25},{25,17},{2,10},{10... | collective-permute-start | bytes 2219528 | tf_op jit(solution)/shard_map/ppermute | solution.py:801
  753.5 55.5 %collective-permute-start.27 = (bf16[4,136,1792]{2,1,0:T(8,128)(2,1)}, bf16[4,136,1792]{2,1,0:T(8,128)(2,1)}, u32[]{:S(2)}, u32[]{:S(2)}) collective-permute-start(bf16[4,136,1792]{2,1,0:T(8,128)(2,1)} %get-tuple-element.169.refs_14_), channel_id=1, source_target_pairs={{0,16},{8,24},{16,0},{24,8},{1,17},{9,25},{17,1},{25,9},{2,18},{10... | collective-permute-start | bytes 5849096 | tf_op jit(solution)/shard_map/ppermute | solution.py:801
  802.8 59.2 %collective-permute-start.26 = (bf16[1024,1088]{0,1:T(8,128)(2,1)}, bf16[1024,1088]{0,1:T(8,128)(2,1)}, u32[]{:S(2)}, u32[]{:S(2)}) collective-permute-start(bf16[1024,1088]{0,1:T(8,128)(2,1)} %copy.135), channel_id=1, source_target_pairs={{0,1},{1,0},{2,3},{3,2},{4,5},{5,4},{6,7},{7,6},{8,9},{9,8},{10,11... | collective-permute-start | bytes 6684680 | tf_op jit(solution)/shard_map/ppermute | solution.py:801
  811.2 47.8 %collective-permute-start.29 = (bf16[136,1792]{1,0:T(8,128)(2,1)S(1)}, bf16[136,1792]{1,0:T(8,128)(2,1)S(1)}, u32[]{:S(2)}, u32[]{:S(2)}) collective-permute-start(bf16[136,1792]{1,0:T(8,128)(2,1)S(1)} %get-tuple-element.210), channel_id=1, source_target_pairs={{0,4},{2,6},{4,0},{6,2},{1,5},{3,7},{5,1},{7,3},{8,12},{10,14},{12... | collective-permute-start | bytes 1462280 | tf_op jit(solution)/shard_map/ppermute | solution.py:806
  813.8 45.2 %collective-permute-start.28 = (bf16[136,1792]{1,0:T(8,128)(2,1)S(1)}, bf16[136,1792]{1,0:T(8,128)(2,1)S(1)}, u32[]{:S(2)}, u32[]{:S(2)}) collective-permute-start(bf16[136,1792]{1,0:T(8,128)(2,1)S(1)} %get-tuple-element.208), channel_id=1, source_target_pairs={{0,2},{2,4},{4,6},{6,0},{1,3},{3,5},{5,7},{7,1},{8,10},{10,12},{12... | collective-permute-start | bytes 1462280 | tf_op jit(solution)/shard_map/ppermute | solution.py:806
  (140 other events, 1457.5 us)
Sparse Core Ops, SparseCore 0:
  11.5 74.2 all-gather.9
  88.7 102.9 all-gather.11
  194.6 108.7 all-gather.13
  805.0 77.0 all-gather.15

commit v7 on v6

--- a/solution.py
+++ b/solution.py
@@ -620,7 +620,9 @@
     centred = values - jnp.mean(values, axis=1, keepdims=True)
     normed = centred * lax.rsqrt(jnp.mean(centred * centred, axis=1, keepdims=True) + epsilon)
     total = sum(nt(grad[...], weight[...]) for grad, weight in zip(grads, weights))
-    out[...] = total.astype(out.dtype)
+    width = total.shape[1]
+    out[:, :width] = total.astype(out.dtype)
+    out[:, width:] = jnp.zeros((out.shape[0], out.shape[1] - width), out.dtype)
 
     @pl.when(pl.program_id(0) == 0)
     def _():
@@ -634,6 +636,7 @@
     total, width = rows.shape
     flat_grads, flat_weights = [g for group in grads for g in group], [w for group in weights for w in group]
     tall = pl.BlockSpec((size, width), lambda t: (t, 0))
+    wide = pl.cdiv(width, 128) * 128
     return pl.pallas_call(
         tokens_back_kernel,
         grid=(total // size,),
@@ -641,9 +644,9 @@
         + [fixed(w.shape) for w in flat_weights]
         + [tall]
         + [pl.BlockSpec(memory_space=pl.ANY)] * len(after),
-        out_specs=[tall, steady((8, width))],
+        out_specs=[pl.BlockSpec((size, wide), lambda t: (t, 0)), steady((8, width))],
         out_shape=[
-            jax.ShapeDtypeStruct((total, width), jnp.bfloat16),
+            jax.ShapeDtypeStruct((total, wide), jnp.bfloat16),
             jax.ShapeDtypeStruct((8, width), jnp.float32),
         ],
         compiler_params=pltpu.CompilerParams(
@@ -720,7 +723,9 @@
     centred = values - jnp.mean(values, axis=1, keepdims=True)
     pace = lax.rsqrt(jnp.mean(centred * centred, axis=1, keepdims=True) + epsilon)
     normed = centred * pace
-    grad = own[...].astype(jnp.float32) + jnp.where(step == last, 0.0, others[...].astype(jnp.float32))
+    width = values.shape[1]
+    received = jnp.where(step == last, 0.0, others[:, :width].astype(jnp.float32))
+    grad = own[:, :width].astype(jnp.float32) + received
     scaled = grad * gain[...]
     inner = (
         scaled
@@ -739,7 +744,8 @@
 
 
 def rows_back(others, own, rows, resid, gain, branch):
-    total, width = own.shape
+    total, width = rows.shape
+    wide = own.shape[1]
     shard = total - branch
     steps = shard // branch
     tall = pl.BlockSpec((branch, width), lambda t: (t, 0))
@@ -747,8 +753,8 @@
         rows_back_kernel,
         grid=(steps + 1,),
         in_specs=[
-            pl.BlockSpec((branch, width), lambda t: (jnp.minimum(t, steps - 1), 0)),
-            tall,
+            pl.BlockSpec((branch, wide), lambda t: (jnp.minimum(t, steps - 1), 0)),
+            pl.BlockSpec((branch, wide), lambda t: (t, 0)),
             tall,
             tall,
             fixed((1, width)),

time: 917 us -> 912 us (level)
  local copies, waits for them, and re-layouts: 153 us -> 137 us
  waiting for transfers between devices: 114 us -> 124 us
    unnamed x259 -> x257, local copies, waits for them, and re-layouts: 45.7 us -> 46.1 us
  transfers between devices with their start and end apart: 42 -> 42, of which waited for: 8 -> 8; matrix products, arithmetic and copies ran while one was open for 27% -> 25% of each run, Pallas kernels for 36% -> 37%
where the time goes in v7:
time: 912 us; the launch traced here: 904 us
  Pallas kernels  416 us (46%)
  local copies, waits for them, and re-layouts  137 us (15%)
  other arithmetic  126 us (14%)
  waiting for transfers between devices  124 us (14%)
  starting transfers between devices  46.1 us (5%)
  matrix products  37.9 us (4%)
  between operations  17.7 us (2%)
    pallas_call x2, Pallas kernels, attention_backward(): pl.pallas_call(functools.partial(backward_kernel, block=block, branch=bra...  104 us
    pallas_call x2, Pallas kernels, up_back(): pl.pallas_call(up_back_first_kernel if final is None else up_back_last_ke...  82.6 us
    pallas_call x2, Pallas kernels, attention_forward(): pl.pallas_call(functools.partial(forward_kernel, block=block, branch=bran...  74.1 us
    pallas_call x1, Pallas kernels, mlp_forward(): pl.pallas_call(mlp_forward_kernel, grid=(inner // TILE,), in_specs=[fixed...  64.9 us
    ppermute x26, waiting for transfers between devices, swap(): return lax.ppermute(value, axis, [(i, i ^ bit) for i in range(count)])  61.6 us
    ppermute x12, waiting for transfers between devices, ahead(): lax.ppermute(value, axis, [(i, (i + step) % count) for i in range(count)])  52.1 us
    unnamed x257, local copies, waits for them, and re-layouts  46.1 us
    dot_general x6, matrix products, dot(): return jnp.dot(a, b, preferred_element_type=jnp.float32)  37.9 us
  transfers between devices with their start and end apart: 42, of which 8 were waited for; matrix products, arithmetic and copies ran while one was open for 25% of the time, Pallas kernels for 37%

profile of v7, /device:TPU:0, one launch (start us, length us, event | category | flops | bytes accessed | tf_op | source)
XLA Modules:
  0.0 904.2 jit_solution(6817865207787277084)
XLA Ops:
  26.5 49.1 %collective-permute-done = s32[1]{0:T(128)} collective-permute-done((s32[1]{0:T(128)}, s32[1]{0:T(128)}, u32[]{:S(2)}, u32[]{:S(2)}) %collective-permute-start) | collective-permute-done | bytes 36 | tf_op jit(solution)/shard_map/ppermute | solution.py:807
  102.9 8.5 copy.128.rest_0_.turned
  114.9 8.3 pad_maximum_fusion.3
  138.1 6.1 fusion.8.q
  144.3 7.0 convolution_convert_fusion.1.k
  151.3 6.9 fusion.9.v
  158.2 33.1 %attention_forward.2 = (bf16[1280,512]{1,0:T(8,128)(2,1)S(1)}, f32[4,8,1280]{2,1,0:T(8,128)S(1)}) custom-call(s32[3]{0:T(128)S(1)} %pad_add_fusion.pos, bf16[2304,512]{1,0:T(8,128)(2,1)S(1)} %fusion.8.q, bf16[2304,512]{1,0:T(8,128)(2,1)S(1)} %convolution_convert_fusion.1.k, bf16[2304,512]{1,0:T(8,128)(2,1)S(1)} %fusion.9.v), custom_call_target="tpu_custom_call" | custom-call | flops 28000000000 | bytes 28000000 | tf_op jit(solution)/shard_map/attention_forward/pallas_call | solution.py:169
  201.7 6.2 fusion.37
  207.9 5.4 copy.129.rest_1_.cot_turned
  213.2 5.1 fusion.39
  221.0 7.8 convolution_convert_fusion.k
  228.9 4.9 add_convert_fusion.3.q
  233.8 5.3 add_convert_fusion.2.v
  239.1 41.0 %attention_forward.3 = (bf16[1280,576]{1,0:T(8,128)(2,1)S(1)}, f32[5,8,1280]{2,1,0:T(8,128)S(1)}) custom-call(s32[3]{0:T(128)S(1)} %pad_add_fusion.pos, bf16[2304,576]{1,0:T(8,128)(2,1)S(1)} %add_convert_fusion.3.q, bf16[2304,576]{1,0:T(8,128)(2,1)S(1)} %convolution_convert_fusion.k, bf16[2304,576]{1,0:T(8,128)(2,1)S(1)} %add_convert_fusion.2.v), custom_call_target="tpu_custom_call" | custom-call | flops 35000000512 | bytes 35000000 | tf_op jit(solution)/shard_map/attention_forward/pallas_call | solution.py:169
  284.4 5.5 broadcast_select_fusion.2
  293.2 10.3 %all-gather.14.cloned.1.call-done = bf16[8704,512]{1,0:T(8,128)(2,1)} async-done(((bf16[272,512]{1,0:T(8,128)(2,1)}), bf16[8704,512]{1,0:T(8,128)(2,1)}) %all-gather.14.cloned.1.call-update) | async-done | bytes 8912912 | tf_op jit(solution)/shard_map/all_gather | solution.py:838
  322.3 64.9 %mlp_forward.1 = (bf16[1280,4352]{1,0:T(8,128)(2,1)}, bf16[1280,4352]{1,0:T(8,128)(2,1)}, bf16[1280,1088]{1,0:T(8,128)(2,1)}, bf16[1088,1280]{1,0:T(8,128)(2,1)}...) custom-call(bf16[1280,512]{1,0:T(8,128)(2,1)S(1)} %copy-done.18, bf16[1280,576]{1,0:T(8,128)(2,1)} %copy-done.9, ...), custom_call_target="tpu_custom_call" | custom-call | flops 49999998976 | bytes 50000000 | tf_op jit(solution)/shard_map/mlp_forward/pallas_call | solution.py:409
  387.3 20.1 %down_back.1 = (bf16[4,136,4352]{2,1,0:T(8,128)(2,1)S(1)}, bf16[4,136,4352]{2,1,0:T(8,128)(2,1)}) custom-call(s32[1]{0:T(128)} %bitcast.48.half, bf16[1088,1280]{1,0:T(8,128)(2,1)S(1)} %copy-done.7, bf16[1280,4352]{1,0:T(8,128)(2,1)} %get-tuple-element.67.hidden), custom_call_target="tpu_custom_call" | custom-call | flops 15000000512 | bytes 15000000 | tf_op jit(solution)/shard_map/down_back/pallas_call | solution.py:470
  412.9 29.8 %up_back_first.1 = (f32[1280,1088]{1,0:T(8,128)}, bf16[4,136,2048]{2,1,0:T(8,128)(2,1)}, bf16[4,136,2048]{2,1,0:T(8,128)(2,1)}, f32[1,2048]{1,0:T(1,128)}) custom-call(s32[1]{0:T(128)} %bitcast.48.half, bf16[1088,1280]{1,0:T(8,128)(2,1)} %get-tuple-element.62.act_turned, bf16[1280,1088]{1,0:T(8,128)(2,1)} %get-tuple-element.193.refs_2_.cot, ...), custom_call_target="tpu_custom_call" | custom-call | flops 30000001024 | bytes 30000000 | tf_op jit(solution)/shard_map/up_back_first/pallas_call | solution.py:598
  456.9 52.8 %up_back_last.1 = (f32[1280,1088]{1,0:T(8,128)}, bf16[1280,1088]{1,0:T(8,128)(2,1)}, bf16[1280,512]{1,0:T(8,128)(2,1)}, bf16[1280,576]{1,0:T(8,128)(2,1)}, bf16[...) custom-call(s32[1]{0:T(128)} %bitcast.48.half, ...), custom_call_target="tpu_custom_call" | custom-call | flops 49999998976 | bytes 50000000 | tf_op jit(solution)/shard_map/up_back_last/pallas_call | solution.py:598
  545.9 4.3 pad_maximum_fusion.1.rest_1_
  553.5 4.5 collective-permute-start.18
  558.9 57.6 %attention_backward.3 = (bf16[2304,576]{1,0:T(8,128)(2,1)S(1)}, bf16[2304,576]{1,0:T(8,128)(2,1)S(1)}, bf16[2304,576]{1,0:T(8,128)(2,1)}) custom-call(s32[3]{0:T(128)S(1)} %copy-done.25, bf16[2304,576]{1,0:T(8,128)(2,1)} %copy-done.31, bf16[2304,576]{1,0:T(8,128)(2,1)} %copy-done.30, bf16[2304,576]{1,0:T(8,128)(2,1)} %copy-done.32, ...), custom_call_target="tpu_custom_call" | custom-call | flops 49999998976 | bytes 50000000 | tf_op jit(solution)/shard_map/attention_backward/pallas_call | solution.py:305
  625.5 4.7 collective-permute-start.21
  631.3 46.6 %attention_backward.2 = (bf16[2304,512]{1,0:T(8,128)(2,1)S(1)}, bf16[2304,512]{1,0:T(8,128)(2,1)S(1)}, bf16[2304,512]{1,0:T(8,128)(2,1)S(1)}) custom-call(s32[3]{0:T(128)S(1)} %copy-done.25, bf16[2304,512]{1,0:T(8,128)(2,1)S(1)} %copy-done.28, bf16[2304,512]{1,0:T(8,128)(2,1)} %copy-done.26, bf16[2304,512]{1,0:T(8,128)(2,1)} %copy-done.29, ...), custom_call_target="tpu_custom_call" | custom-call | flops 40000000000 | bytes 40000000 | tf_op jit(solution)/shard_map/attention_backward/pallas_call | solution.py:305
  687.8 8.0 collective-permute-done.20
  698.6 31.1 %weights_back.1 = (bf16[4,136,1536]{2,1,0:T(8,128)(2,1)}, bf16[4,136,1536]{2,1,0:T(8,128)(2,1)}, f32[1,1536]{1,0:T(1,128)S(1)}, bf16[4,136,2304]{2,1,0:T(8,128)(...) custom-call(s32[1]{0:T(128)} %bitcast.48.half, bf16[1088,2304]{1,0:T(8,128)(2,1)} %copy.128.rest_0_.turned, ...), custom_call_target="tpu_custom_call" | custom-call | flops 24999999488 | bytes 25000000 | tf_op jit(solution)/shard_map/weights_back/pallas_call | solution.py:700
  755.6 30.3 %tokens_back.1 = (bf16[2304,1152]{1,0:T(8,128)(2,1)}, f32[8,1088]{1,0:T(8,128)S(1)}) custom-call(bf16[2304,512]{1,0:T(8,128)(2,1)} %copy-done.8, bf16[2304,512]{1,0:T(8,128)(2,1)} %copy-done.35, bf16[2304,512]{1,0:T(8,128)(2,1)} %copy-done.36, bf16[2304,576]{1,0:T(8,128)(2,1)} %copy-done.33, bf16[2304,576]{1,0:T(8,128)(2,1)} %copy-done.34, ...), custom_call_target="tpu_custom_call" | custom-call | flops 20000000000 | bytes 20000000 | tf_op jit(solution)/shard_map/tokens_back/pallas_call | solution.py:640
  809.0 10.0 %collective-permute-done.30 = bf16[136,1792]{1,0:T(8,128)(2,1)S(1)} collective-permute-done((bf16[136,1792]{1,0:T(8,128)(2,1)S(1)}, bf16[136,1792]{1,0:T(8,128)(2,1)S(1)}, u32[]{:S(2)}, u32[]{:S(2)}) %collective-permute-start.30) | collective-permute-done | bytes 487456 | tf_op jit(solution)/shard_map/ppermute | solution.py:812
  819.0 34.1 %collective-permute-done.29 = bf16[136,1792]{1,0:T(8,128)(2,1)S(1)} collective-permute-done((bf16[136,1792]{1,0:T(8,128)(2,1)S(1)}, bf16[136,1792]{1,0:T(8,128)(2,1)S(1)}, u32[]{:S(2)}, u32[]{:S(2)}) %collective-permute-start.29) | collective-permute-done | bytes 487456 | tf_op jit(solution)/shard_map/ppermute | solution.py:812
  856.2 8.8 collective-permute-done.32
  871.4 8.4 rows_back.1
  (498 shorter events, 260.4 us)
Async XLA Ops:
  7.2 116.1 %all-gather.10.cloned.1.call-start = ((), (), s32[]{:S(2)}) async-start(), calls=%async_computation | async-start | bytes 4595712 | tf_op jit(solution)/shard_map/all_gather | solution.py:838
  9.5 203.7 %all-gather.12.cloned.1.call-start = ((), (), s32[]{:S(2)}) async-start(), calls=%async_computation.1 | async-start | bytes 6893568 | tf_op jit(solution)/shard_map/all_gather | solution.py:838
  11.7 291.8 %all-gather.14.cloned.1.call-start = ((), (), s32[]{:S(2)}) async-start(), calls=%async_computation.2 | async-start | bytes 9191424 | tf_op jit(solution)/shard_map/all_gather | solution.py:838
  11.7 73.0 %collective-permute-start.1 = (bf16[1024,1088]{0,1:T(8,128)(2,1)}, bf16[1024,1088]{0,1:T(8,128)(2,1)}, u32[]{:S(2)}, u32[]{:S(2)}) collective-permute-start(bf16[1024,1088]{0,1:T(8,128)(2,1)} %bitcast.5), channel_id=1, source_target_pairs={{0,1},{1,0},{2,3},{3,2},{4,5},{5,4},{6,7},{7,6},{8,9},{9,8},{10,11... | collective-permute-start | bytes 6684680 | tf_op jit(solution)/shard_map/ppermute | solution.py:807
  14.7 60.9 %collective-permute-start = (s32[1]{0:T(128)}, s32[1]{0:T(128)}, u32[]{:S(2)}, u32[]{:S(2)}) collective-permute-start(s32[1]{0:T(128)} %param.20), channel_id=1, source_target_pairs={{0,1},{1,0},{2,3},{3,2},{4,5},{5,4},{6,7},{7,6},{8,9},{9,8},{10,11... | collective-permute-start | bytes 20 | tf_op jit(solution)/shard_map/ppermute | solution.py:807
  16.8 866.1 %all-gather.16.cloned.1.call-start = ((), (), s32[]{:S(2)}) async-start(), calls=%async_computation.3 | async-start | bytes 1723392 | tf_op jit(solution)/shard_map/all_gather | solution.py:1281
  123.3 70.7 %collective-permute-start.2 = (bf16[272,1152]{1,0:T(8,128)(2,1)}, bf16[272,1152]{1,0:T(8,128)(2,1)}, u32[]{:S(2)}, u32[]{:S(2)}) collective-permute-start(bf16[272,1152]{1,0:T(8,128)(2,1)} %gate.18), channel_id=1, source_target_pairs={{0,2},{2,4},{4,6},{6,0},{1,3},{3,5},{5,7},{7,1},{8,10},{10,12},{12... | collective-permute-start | bytes 1880072 | tf_op jit(solution)/shard_map/ppermute | solution.py:812
  125.0 70.9 %collective-permute-start.3 = (bf16[272,1152]{1,0:T(8,128)(2,1)}, bf16[272,1152]{1,0:T(8,128)(2,1)}, u32[]{:S(2)}, u32[]{:S(2)}) collective-permute-start(bf16[272,1152]{1,0:T(8,128)(2,1)} %gate.18), channel_id=1, source_target_pairs={{0,4},{2,6},{4,0},{6,2},{1,5},{3,7},{5,1},{7,3},{8,12},{10,14},{12... | collective-permute-start | bytes 1880072 | tf_op jit(solution)/shard_map/ppermute | solution.py:812
  127.9 70.1 %collective-permute-start.4 = (bf16[272,1152]{1,0:T(8,128)(2,1)}, bf16[272,1152]{1,0:T(8,128)(2,1)}, u32[]{:S(2)}, u32[]{:S(2)}) collective-permute-start(bf16[272,1152]{1,0:T(8,128)(2,1)} %gate.18), channel_id=1, source_target_pairs={{0,6},{2,0},{4,2},{6,4},{1,7},{3,1},{5,3},{7,5},{8,14},{10,8},{12,... | collective-permute-start | bytes 1880072 | tf_op jit(solution)/shard_map/ppermute | solution.py:812
  135.9 64.1 %collective-permute-start.5 = (bf16[512,1088]{0,1:T(8,128)(2,1)}, bf16[512,1088]{0,1:T(8,128)(2,1)}, u32[]{:S(2)}, u32[]{:S(2)}) collective-permute-start(bf16[512,1088]{0,1:T(8,128)(2,1)} %copy.119), channel_id=1, source_target_pairs={{0,1},{1,0},{2,3},{3,2},{4,5},{5,4},{6,7},{7,6},{8,9},{9,8},{10,11... | collective-permute-start | bytes 3342344 | tf_op jit(solution)/shard_map/ppermute | solution.py:807
  207.9 76.5 %collective-permute-start.6 = (bf16[1088,1152]{1,0:T(8,128)(2,1)}, bf16[1088,1152]{1,0:T(8,128)(2,1)}, u32[]{:S(2)}, u32[]{:S(2)}) collective-permute-start(bf16[1088,1152]{1,0:T(8,128)(2,1)} %gate.20), channel_id=1, source_target_pairs={{0,1},{1,0},{2,3},{3,2},{4,5},{5,4},{6,7},{7,6},{8,9},{9,8},{10,11... | collective-permute-start | bytes 7520264 | tf_op jit(solution)/shard_map/ppermute | solution.py:807
  409.6 38.2 %collective-permute-start.10 = (bf16[4,136,4352]{2,1,0:T(8,128)(2,1)}, bf16[4,136,4352]{2,1,0:T(8,128)(2,1)}, u32[]{:S(2)}, u32[]{:S(2)}) collective-permute-start(bf16[4,136,4352]{2,1,0:T(8,128)(2,1)} %get-tuple-element.69), channel_id=1, source_target_pairs={{0,8},{8,0},{16,24},{24,16},{1,9},{9,1},{17,25},{25,17},{2,10},{10... | collective-permute-start | bytes 14204936 | tf_op jit(solution)/shard_map/ppermute | solution.py:807
  411.8 30.9 %collective-permute-start.9 = (bf16[512,1088]{0,1:T(8,128)(2,1)S(1)}, bf16[512,1088]{0,1:T(8,128)(2,1)}, u32[]{:S(2)}, u32[]{:S(2)}) collective-permute-start(bf16[512,1088]{0,1:T(8,128)(2,1)S(1)} %copy.130), channel_id=1, source_target_pairs={{0,1},{1,0},{2,3},{3,2},{4,5},{5,4},{6,7},{7,6},{8,9},{9,8},{10,11... | collective-permute-start | bytes 3342344 | tf_op jit(solution)/shard_map/ppermute | solution.py:807
  455.5 58.4 %collective-permute-start.12 = (bf16[4,136,2304]{2,1,0:T(8,128)(2,1)}, bf16[4,136,2304]{2,1,0:T(8,128)(2,1)}, u32[]{:S(2)}, u32[]{:S(2)}) collective-permute-start(bf16[4,136,2304]{2,1,0:T(8,128)(2,1)} %gate.23), channel_id=1, source_target_pairs={{0,16},{8,24},{16,0},{24,8},{1,17},{9,25},{17,1},{25,9},{2,18},{10... | collective-permute-start | bytes 7520264 | tf_op jit(solution)/shard_map/ppermute | solution.py:807
  456.9 52.8 %collective-permute-start.11 = (bf16[4,136,2048]{2,1,0:T(8,128)(2,1)}, bf16[4,136,2048]{2,1,0:T(8,128)(2,1)}, u32[]{:S(2)}, u32[]{:S(2)}) collective-permute-start(bf16[4,136,2048]{2,1,0:T(8,128)(2,1)} %gate.22), channel_id=1, source_target_pairs={{0,8},{8,0},{16,24},{24,16},{1,9},{9,1},{17,25},{25,17},{2,10},{10... | collective-permute-start | bytes 6684680 | tf_op jit(solution)/shard_map/ppermute | solution.py:807
  552.2 69.1 %collective-permute-start.15 = (bf16[4,136,2720]{2,1,0:T(8,128)(2,1)}, bf16[4,136,2720]{2,1,0:T(8,128)(2,1)}, u32[]{:S(2)}, u32[]{:S(2)}) collective-permute-start(bf16[4,136,2720]{2,1,0:T(8,128)(2,1)} %broadcast_select_fusion), channel_id=1, source_target_pairs={{0,1},{1,0},{2,3},{3,2},{4,5},{5,4},{6,7},{7,6},{8,9},{9,8},{10,11... | collective-permute-start | bytes 8878088 | tf_op jit(solution)/shard_map/ppermute | solution.py:807
  553.5 63.0 %collective-permute-start.18 = (bf16[136,2304]{1,0:T(8,128)(2,1)S(1)}, bf16[136,2304]{1,0:T(8,128)(2,1)S(1)}, u32[]{:S(2)}, u32[]{:S(2)}) collective-permute-start(bf16[136,2304]{1,0:T(8,128)(2,1)S(1)} %get-tuple-element.198), channel_id=1, source_target_pairs={{0,6},{2,0},{4,2},{6,4},{1,7},{3,1},{5,3},{7,5},{8,14},{10,8},{12,... | collective-permute-start | bytes 1880072 | tf_op jit(solution)/shard_map/ppermute | solution.py:812
  557.9 58.6 %collective-permute-start.17 = (bf16[136,2304]{1,0:T(8,128)(2,1)S(1)}, bf16[136,2304]{1,0:T(8,128)(2,1)S(1)}, u32[]{:S(2)}, u32[]{:S(2)}) collective-permute-start(bf16[136,2304]{1,0:T(8,128)(2,1)S(1)} %get-tuple-element.199), channel_id=1, source_target_pairs={{0,4},{2,6},{4,0},{6,2},{1,5},{3,7},{5,1},{7,3},{8,12},{10,14},{12... | collective-permute-start | bytes 1880072 | tf_op jit(solution)/shard_map/ppermute | solution.py:812
  558.1 58.4 %collective-permute-start.16 = (bf16[136,2304]{1,0:T(8,128)(2,1)S(1)}, bf16[136,2304]{1,0:T(8,128)(2,1)S(1)}, u32[]{:S(2)}, u32[]{:S(2)}) collective-permute-start(bf16[136,2304]{1,0:T(8,128)(2,1)S(1)} %get-tuple-element.197), channel_id=1, source_target_pairs={{0,2},{2,4},{4,6},{6,0},{1,3},{3,5},{5,7},{7,1},{8,10},{10,12},{12... | collective-permute-start | bytes 1880072 | tf_op jit(solution)/shard_map/ppermute | solution.py:812
  616.9 113.3 %collective-permute-start.25 = (bf16[136,1152]{1,0:T(8,128)(2,1)S(1)}, bf16[136,1152]{1,0:T(8,128)(2,1)S(1)}, u32[]{:S(2)}, u32[]{:S(2)}) collective-permute-start(bf16[136,1152]{1,0:T(8,128)(2,1)S(1)} %broadcast_select_fusion.12.refs_7_), channel_id=1, source_target_pairs={{0,1},{1,0},{2,3},{3,2},{4,5},{5,4},{6,7},{7,6},{8,9},{9,8},{10,11... | collective-permute-start | bytes 940040 | tf_op jit(solution)/shard_map/ppermute | solution.py:807
  625.5 62.3 %collective-permute-start.21 = (bf16[136,2720]{1,0:T(8,128)(2,1)}, bf16[136,2720]{1,0:T(8,128)(2,1)}, u32[]{:S(2)}, u32[]{:S(2)}) collective-permute-start(bf16[136,2720]{1,0:T(8,128)(2,1)} %get-tuple-element.190), channel_id=1, source_target_pairs={{0,6},{2,0},{4,2},{6,4},{1,7},{3,1},{5,3},{7,5},{8,14},{10,8},{12,... | collective-permute-start | bytes 2219528 | tf_op jit(solution)/shard_map/ppermute | solution.py:812
  630.2 65.7 %collective-permute-start.20 = (bf16[136,2720]{1,0:T(8,128)(2,1)}, bf16[136,2720]{1,0:T(8,128)(2,1)}, u32[]{:S(2)}, u32[]{:S(2)}) collective-permute-start(bf16[136,2720]{1,0:T(8,128)(2,1)} %get-tuple-element.191), channel_id=1, source_target_pairs={{0,4},{2,6},{4,0},{6,2},{1,5},{3,7},{5,1},{7,3},{8,12},{10,14},{12... | collective-permute-start | bytes 2219528 | tf_op jit(solution)/shard_map/ppermute | solution.py:812
  630.2 65.7 %collective-permute-start.19 = (bf16[136,2720]{1,0:T(8,128)(2,1)}, bf16[136,2720]{1,0:T(8,128)(2,1)}, u32[]{:S(2)}, u32[]{:S(2)}) collective-permute-start(bf16[136,2720]{1,0:T(8,128)(2,1)} %get-tuple-element.189), channel_id=1, source_target_pairs={{0,2},{2,4},{4,6},{6,0},{1,3},{3,5},{5,7},{7,1},{8,10},{10,12},{12... | collective-permute-start | bytes 2219528 | tf_op jit(solution)/shard_map/ppermute | solution.py:812
  684.4 49.2 %collective-permute-start.31 = (bf16[512,1088]{0,1:T(8,128)(2,1)}, bf16[512,1088]{0,1:T(8,128)(2,1)}, u32[]{:S(2)}, u32[]{:S(2)}) collective-permute-start(bf16[512,1088]{0,1:T(8,128)(2,1)} %copy.135), channel_id=1, source_target_pairs={{0,1},{1,0},{2,3},{3,2},{4,5},{5,4},{6,7},{7,6},{8,9},{9,8},{10,11... | collective-permute-start | bytes 3342344 | tf_op jit(solution)/shard_map/ppermute | solution.py:807
  698.0 43.3 %collective-permute-start.24 = (bf16[136,2720]{1,0:T(8,128)(2,1)S(1)}, bf16[136,2720]{1,0:T(8,128)(2,1)}, u32[]{:S(2)}, u32[]{:S(2)}) collective-permute-start(bf16[136,2720]{1,0:T(8,128)(2,1)S(1)} %fusion.21.refs_6_), channel_id=1, source_target_pairs={{0,16},{8,24},{16,0},{24,8},{1,17},{9,25},{17,1},{25,9},{2,18},{10... | collective-permute-start | bytes 2219528 | tf_op jit(solution)/shard_map/ppermute | solution.py:807
  732.0 64.6 %collective-permute-start.36 = (bf16[136,1152]{1,0:T(8,128)(2,1)S(1)}, bf16[136,1152]{1,0:T(8,128)(2,1)S(1)}, u32[]{:S(2)}, u32[]{:S(2)}) collective-permute-start(bf16[136,1152]{1,0:T(8,128)(2,1)S(1)} %add_convert_fusion.12.refs_16_), channel_id=1, source_target_pairs={{0,16},{8,24},{16,0},{24,8},{1,17},{9,25},{17,1},{25,9},{2,18},{10... | collective-permute-start | bytes 940040 | tf_op jit(solution)/shard_map/ppermute | solution.py:807
  742.7 43.1 %collective-permute-start.35 = (bf16[136,2720]{1,0:T(8,128)(2,1)S(1)}, bf16[136,2720]{1,0:T(8,128)(2,1)S(1)}, u32[]{:S(2)}, u32[]{:S(2)}) collective-permute-start(bf16[136,2720]{1,0:T(8,128)(2,1)S(1)} %add_convert_fusion.11.refs_15_), channel_id=1, source_target_pairs={{0,8},{8,0},{16,24},{24,16},{1,9},{9,1},{17,25},{25,17},{2,10},{10... | collective-permute-start | bytes 2219528 | tf_op jit(solution)/shard_map/ppermute | solution.py:807
  753.5 49.2 %collective-permute-start.27 = (bf16[4,136,1792]{2,1,0:T(8,128)(2,1)}, bf16[4,136,1792]{2,1,0:T(8,128)(2,1)}, u32[]{:S(2)}, u32[]{:S(2)}) collective-permute-start(bf16[4,136,1792]{2,1,0:T(8,128)(2,1)} %get-tuple-element.169.refs_14_), channel_id=1, source_target_pairs={{0,16},{8,24},{16,0},{24,8},{1,17},{9,25},{17,1},{25,9},{2,18},{10... | collective-permute-start | bytes 5849096 | tf_op jit(solution)/shard_map/ppermute | solution.py:807
  794.2 62.0 %collective-permute-start.26 = (bf16[1024,1152]{1,0:T(8,128)(2,1)}, bf16[1024,1152]{1,0:T(8,128)(2,1)}, u32[]{:S(2)}, u32[]{:S(2)}) collective-permute-start(bf16[1024,1152]{1,0:T(8,128)(2,1)} %constant_dynamic-slice_fusion.1), channel_id=1, source_target_pairs={{0,1},{1,0},{2,3},{3,2},{4,5},{5,4},{6,7},{7,6},{8,9},{9,8},{10,11... | collective-permute-start | bytes 7077896 | tf_op jit(solution)/shard_map/ppermute | solution.py:807
  804.9 48.2 %collective-permute-start.29 = (bf16[136,1792]{1,0:T(8,128)(2,1)S(1)}, bf16[136,1792]{1,0:T(8,128)(2,1)S(1)}, u32[]{:S(2)}, u32[]{:S(2)}) collective-permute-start(bf16[136,1792]{1,0:T(8,128)(2,1)S(1)} %get-tuple-element.210), channel_id=1, source_target_pairs={{0,4},{2,6},{4,0},{6,2},{1,5},{3,7},{5,1},{7,3},{8,12},{10,14},{12... | collective-permute-start | bytes 1462280 | tf_op jit(solution)/shard_map/ppermute | solution.py:812
  807.0 46.1 %collective-permute-start.28 = (bf16[136,1792]{1,0:T(8,128)(2,1)S(1)}, bf16[136,1792]{1,0:T(8,128)(2,1)S(1)}, u32[]{:S(2)}, u32[]{:S(2)}) collective-permute-start(bf16[136,1792]{1,0:T(8,128)(2,1)S(1)} %get-tuple-element.208), channel_id=1, source_target_pairs={{0,2},{2,4},{4,6},{6,0},{1,3},{3,5},{5,7},{7,1},{8,10},{10,12},{12... | collective-permute-start | bytes 1462280 | tf_op jit(solution)/shard_map/ppermute | solution.py:812
  856.1 23.8 %collective-permute-start.37 = (bf16[136,2176]{1,0:T(8,128)(2,1)}, bf16[136,2176]{1,0:T(8,128)(2,1)}, u32[]{:S(2)}, u32[]{:S(2)}) collective-permute-start(bf16[136,2176]{1,0:T(8,128)(2,1)} %gate.35), channel_id=1, source_target_pairs={{0,8},{8,0},{16,24},{24,16},{1,9},{9,1},{17,25},{25,17},{2,10},{10... | collective-permute-start | bytes 1775624 | tf_op jit(solution)/shard_map/ppermute | solution.py:807
  (139 other events, 1431.6 us)
Sparse Core Ops, SparseCore 0:
  11.5 74.2 all-gather.9
  88.7 102.9 all-gather.11
  194.7 108.7 all-gather.13
  796.7 74.5 all-gather.15
